TPU v7x, 32 devices: a whole 2x2x4 slice. The times are simulated.
32 devices in a mesh: seq: 8 (over y, x, core), fsdp: 4 (over z).
Axes of the slice: x: 2, y: 2, z: 4, core: 2. Of those that a mesh axis runs over, the one named last changes fastest.
Arguments:
- tokens: bfloat16 [4, 1024, 2048], P('fsdp', 'seq'), may hold values from -6 to 6
- positions: int32 [4, 1024], P('fsdp', 'seq'), may hold values from 0 to 511, as said below
- w_query: bfloat16 [2048, 2048], P('fsdp'), may hold values from -0.125 to 0.125
- w_key: bfloat16 [2048, 256], P('fsdp'), may hold values from -0.125 to 0.125
- w_value: bfloat16 [2048, 256], P('fsdp'), may hold values from -0.125 to 0.125
- w_out: bfloat16 [2048, 2048], P('fsdp'), may hold values from -2 to 2
- gain_attn: bfloat16 [2048], P('fsdp'), may hold values from 0.099609375 to 1.8984375
- w_gate: bfloat16 [2048, 5632], P('fsdp'), may hold values from -0.125 to 0.125
- w_up: bfloat16 [2048, 5632], P('fsdp'), may hold values from -0.125 to 0.125
- w_down: bfloat16 [5632, 2048], P('fsdp'), may hold values from -0.078125 to 0.078125
- gain_mlp: bfloat16 [2048], P('fsdp'), may hold values from 0.099609375 to 1.8984375
- cotangent: bfloat16 [4, 1024, 2048], P('fsdp', 'seq'), may hold values from -6 to 6
Outputs:
- layer_out: bfloat16 [4, 1024, 2048], P('fsdp', 'seq')
- grad_tokens: float32 [4, 1024, 2048], P('fsdp', 'seq')
- grad_query: float32 [2048, 2048], P('fsdp')
- grad_key: float32 [2048, 256], P('fsdp')
- grad_value: float32 [2048, 256], P('fsdp')
- grad_out: float32 [2048, 2048], P('fsdp')
- grad_gain_attn: float32 [2048], P('fsdp')
- grad_gate: float32 [2048, 5632], P('fsdp')
- grad_up: float32 [2048, 5632], P('fsdp')
- grad_down: float32 [5632, 2048], P('fsdp')
- grad_gain_mlp: float32 [2048], P('fsdp')
Inputs may be any that keep to these rules, and one draw needn't show every extreme that they name: `positions`: within each sequence a position is 0 where a document starts and rises by one from token to token inside a document; documents start at the first token, at token 512 and at some later tokens, and the first document spans tokens 0 to 511.
All inputs are finite; a program needn't handle non-finite values.
Results may differ from a plain program's by a relative error of at most 0.018.
Values may be sent and summed in bfloat16 or wider, within the bound.
No kernel may reach another device: no remote copies, remote signals or barrier semaphores. Data moves between devices by JAX's collectives and lax.ppermute only.
A program may use at most 640 MiB of HBM per device.

v0:
```python
import math

import jax
import jax.numpy as jnp
from jax import lax
from jax.sharding import PartitionSpec as P

HEADS = 32
KV_HEADS = 4
HEAD_DIM = 64


EPS = 1e-05
ROPE_BASE = 10000.0


def rope_tables(positions, head_size):
    half_dim = head_size // 2
    freqs_base = jnp.exp(
        jnp.arange(half_dim, dtype=jnp.float32) * (-2.0 * math.log(ROPE_BASE) / head_size)
    )
    angles = positions.astype(jnp.float32)[..., None] * freqs_base
    return (jnp.cos(angles), jnp.sin(angles))


def rotate(values, cosine, sine_table):
    half_dim = values.shape[-1] // 2
    lower_half = values[..., :half_dim]
    upper_half = values[..., half_dim:]
    cos_part = cosine[:, None, :]
    sin_part = sine_table[:, None, :]
    return jnp.concatenate(
        [
            lower_half * cos_part - upper_half * sin_part,
            upper_half * cos_part + lower_half * sin_part,
        ],
        axis=-1,
    )


def unrotate(values, cosine, sine_table):
    half_dim = values.shape[-1] // 2
    lower_half = values[..., :half_dim]
    upper_half = values[..., half_dim:]
    cos_part = cosine[:, None, :]
    sin_part = sine_table[:, None, :]
    return jnp.concatenate(
        [
            lower_half * cos_part + upper_half * sin_part,
            upper_half * cos_part - lower_half * sin_part,
        ],
        axis=-1,
    )


def norm_back(grad_normed, normed, inverse):
    return inverse * (grad_normed - normed * jnp.mean(grad_normed * normed, axis=-1, keepdims=True))


def spread_rows(left_rows, right_rows, groups, shards):
    tok_rows = left_rows.shape[0]
    split_left = left_rows.reshape(tok_rows, shards, groups, -1)
    product = jnp.einsum(
        "tfsr,tc->sfrc", split_left, right_rows, preferred_element_type=jnp.float32
    )
    return product.reshape(-1, right_rows.shape[1])


def spread_vector(vector, groups, shards):
    return jnp.transpose(vector.reshape(shards, groups, -1), (1, 0, 2)).reshape(-1)


def on_device(
    tokens,
    positions,
    w_query,
    w_key,
    w_value,
    w_out,
    gain_attn,
    w_gate,
    w_up,
    w_down,
    gain_mlp,
    cotangent,
):
    groups = lax.axis_size("seq")
    shards = lax.axis_size("fsdp")
    tok_rows = tokens.shape[1]
    heads_dev = HEADS // groups
    kv_copies = groups // KV_HEADS
    seq_len = tok_rows * groups
    scale = HEAD_DIM ** (-0.5)
    stream = tokens[0].astype(jnp.float32)
    cosine, sine_table = rope_tables(positions[0], HEAD_DIM)
    query_full, key_full, value_full, out_full, gain_in = (
        lax.all_gather(w_query, "fsdp", axis=0, tiled=True),
        lax.all_gather(w_key, "fsdp", axis=0, tiled=True),
        lax.all_gather(w_value, "fsdp", axis=0, tiled=True),
        lax.all_gather(w_out, "fsdp", axis=0, tiled=True),
        lax.all_gather(gain_attn, "fsdp", axis=0, tiled=True),
    )
    inverse_in = lax.rsqrt(jnp.mean(stream * stream, axis=-1, keepdims=True) + EPS)
    unit_in = stream * inverse_in
    normed_in = (unit_in * gain_in).astype(jnp.bfloat16)
    query_pre = jnp.dot(normed_in, query_full, preferred_element_type=jnp.float32).reshape(
        tok_rows, HEADS, HEAD_DIM
    )
    key_pre = jnp.dot(normed_in, key_full, preferred_element_type=jnp.float32).reshape(
        tok_rows, KV_HEADS, HEAD_DIM
    )
    value_rows = (
        jnp.dot(normed_in, value_full, preferred_element_type=jnp.float32)
        .astype(jnp.bfloat16)
        .reshape(tok_rows, KV_HEADS, HEAD_DIM)
    )
    query_rot = (
        rotate(query_pre, cosine, sine_table)
        .astype(jnp.bfloat16)
        .reshape(tok_rows, groups, heads_dev * HEAD_DIM)
    )
    key_rot = rotate(key_pre, cosine, sine_table).astype(jnp.bfloat16)
    kv_send = jnp.concatenate(
        [jnp.repeat(key_rot, kv_copies, axis=1), jnp.repeat(value_rows, kv_copies, axis=1)], axis=-1
    )
    query_heads, kv_heads = (
        lax.all_to_all(query_rot, "seq", split_axis=1, concat_axis=0, tiled=True),
        lax.all_to_all(kv_send, "seq", split_axis=1, concat_axis=0, tiled=True),
    )
    query_all = query_heads.reshape(seq_len, heads_dev, HEAD_DIM)
    key_all = kv_heads[:, 0, :HEAD_DIM]
    value_all = kv_heads[:, 0, HEAD_DIM:]
    block = 512
    blocks = seq_len // block
    key_index = jnp.arange(seq_len, dtype=jnp.int32)
    starts = jnp.arange(blocks, dtype=jnp.int32) * block
    query_blocks = query_all.reshape(blocks, block, heads_dev, HEAD_DIM)

    def block_scores(query_block, start):
        scores = (
            jnp.einsum("qhd,kd->hqk", query_block, key_all, preferred_element_type=jnp.float32)
            * scale
        )
        causal = key_index[None, :] <= (start + jnp.arange(block, dtype=jnp.int32))[:, None]
        return jnp.where(causal[None], scores, -jnp.inf)

    def attend(block_args):
        query_block, start = block_args
        scores = block_scores(query_block, start)
        row_max = jnp.max(scores, axis=-1)
        unnormed = jnp.exp(scores - row_max[..., None])
        row_sum = jnp.sum(unnormed, axis=-1)
        accum = jnp.einsum(
            "hqk,kd->qhd",
            unnormed.astype(jnp.bfloat16),
            value_all,
            preferred_element_type=jnp.float32,
        )
        return (accum / jnp.transpose(row_sum)[:, :, None], row_max, row_sum)

    out_blocks, max_blocks, sum_blocks = lax.map(attend, (query_blocks, starts))
    attended_send = out_blocks.astype(jnp.bfloat16).reshape(seq_len, 1, heads_dev * HEAD_DIM)
    attended_tok = lax.all_to_all(
        attended_send, "seq", split_axis=0, concat_axis=1, tiled=True
    ).reshape(tok_rows, HEADS * HEAD_DIM)
    gate_full, upper_full, down_full, gain_mid = (
        lax.all_gather(w_gate, "fsdp", axis=0, tiled=True),
        lax.all_gather(w_up, "fsdp", axis=0, tiled=True),
        lax.all_gather(w_down, "fsdp", axis=0, tiled=True),
        lax.all_gather(gain_mlp, "fsdp", axis=0, tiled=True),
    )
    middle = stream + jnp.dot(attended_tok, out_full, preferred_element_type=jnp.float32)
    inverse_mid = lax.rsqrt(jnp.mean(middle * middle, axis=-1, keepdims=True) + EPS)
    unit_mid = middle * inverse_mid
    normed_mid = (unit_mid * gain_mid).astype(jnp.bfloat16)
    gate_pre = jnp.dot(normed_mid, gate_full, preferred_element_type=jnp.float32)
    upper_pre = jnp.dot(normed_mid, upper_full, preferred_element_type=jnp.float32)
    sigmoid_gate = jax.nn.sigmoid(gate_pre)
    activated = gate_pre * sigmoid_gate
    hidden = (activated * upper_pre).astype(jnp.bfloat16)
    layer_out = (middle + jnp.dot(hidden, down_full, preferred_element_type=jnp.float32)).astype(
        jnp.bfloat16
    )
    gate_back, upper_back, down_back, gain_mid_back = (
        lax.all_gather(w_gate, "fsdp", axis=0, tiled=True),
        lax.all_gather(w_up, "fsdp", axis=0, tiled=True),
        lax.all_gather(w_down, "fsdp", axis=0, tiled=True),
        lax.all_gather(gain_mlp, "fsdp", axis=0, tiled=True),
    )
    grad_layer = cotangent[0]
    grad_hidden = jnp.einsum("tc,fc->tf", grad_layer, down_back, preferred_element_type=jnp.float32)
    grad_gate_pre = (
        grad_hidden * upper_pre * (sigmoid_gate * (1.0 + gate_pre * (1.0 - sigmoid_gate)))
    ).astype(jnp.bfloat16)
    grad_upper = (grad_hidden * activated).astype(jnp.bfloat16)
    grad_normed_mid = jnp.einsum(
        "tf,cf->tc", grad_gate_pre, gate_back, preferred_element_type=jnp.float32
    )
    grad_normed_mid = grad_normed_mid + jnp.einsum(
        "tf,cf->tc", grad_upper, upper_back, preferred_element_type=jnp.float32
    )
    grad_gain_mid = jnp.sum(grad_normed_mid * unit_mid, axis=0)
    grad_middle = norm_back(
        grad_normed_mid * gain_mid_back, unit_mid, inverse_mid
    ) + grad_layer.astype(jnp.float32)
    mlp_terms = (
        spread_rows(normed_mid, grad_gate_pre, groups, shards),
        spread_rows(normed_mid, grad_upper, groups, shards),
        spread_rows(hidden, grad_layer, groups, shards),
        spread_vector(grad_gain_mid, groups, shards),
    )
    mlp_parts = (
        lax.psum_scatter(mlp_terms[0], ("seq", "fsdp"), scatter_dimension=0, tiled=True),
        lax.psum_scatter(mlp_terms[1], ("seq", "fsdp"), scatter_dimension=0, tiled=True),
        lax.psum_scatter(mlp_terms[2], ("seq", "fsdp"), scatter_dimension=0, tiled=True),
        lax.psum_scatter(mlp_terms[3], ("seq", "fsdp"), scatter_dimension=0, tiled=True),
    )
    grad_gate, grad_up, grad_down, grad_gain_mlp = (
        lax.all_gather(mlp_parts[0].astype(jnp.bfloat16), "seq", axis=0, tiled=True).astype(
            jnp.float32
        ),
        lax.all_gather(mlp_parts[1].astype(jnp.bfloat16), "seq", axis=0, tiled=True).astype(
            jnp.float32
        ),
        lax.all_gather(mlp_parts[2].astype(jnp.bfloat16), "seq", axis=0, tiled=True).astype(
            jnp.float32
        ),
        lax.all_gather(mlp_parts[3].astype(jnp.bfloat16), "seq", axis=0, tiled=True).astype(
            jnp.float32
        ),
    )
    query_back, key_back, value_back, out_back, gain_in_back = (
        lax.all_gather(w_query, "fsdp", axis=0, tiled=True),
        lax.all_gather(w_key, "fsdp", axis=0, tiled=True),
        lax.all_gather(w_value, "fsdp", axis=0, tiled=True),
        lax.all_gather(w_out, "fsdp", axis=0, tiled=True),
        lax.all_gather(gain_attn, "fsdp", axis=0, tiled=True),
    )
    grad_proj = grad_middle.astype(jnp.bfloat16)
    grad_attended = jnp.einsum(
        "tc,oc->to", grad_proj, out_back, preferred_element_type=jnp.float32
    ).astype(jnp.bfloat16)
    grad_heads = lax.all_to_all(
        grad_attended.reshape(tok_rows, groups, heads_dev * HEAD_DIM),
        "seq",
        split_axis=1,
        concat_axis=0,
        tiled=True,
    )
    grad_blocks = grad_heads.reshape(blocks, block, heads_dev, HEAD_DIM)

    def retrace(carried, block_args):
        query_block, grad_block, out_block, row_max, row_sum, start = block_args
        scores = block_scores(query_block, start)
        unnormed = jnp.exp(scores - row_max[..., None])
        grad_out_f = grad_block.astype(jnp.float32)
        grad_accum = (grad_out_f / jnp.transpose(row_sum)[:, :, None]).astype(jnp.bfloat16)
        grad_probs = jnp.einsum(
            "qhd,kd->hqk", grad_accum, value_all, preferred_element_type=jnp.float32
        )
        shift = jnp.transpose(jnp.sum(grad_out_f * out_block, axis=-1)) / row_sum
        grad_scores = (unnormed * (grad_probs - shift[..., None])).astype(jnp.bfloat16)
        grad_query_block = (
            jnp.einsum("hqk,kd->qhd", grad_scores, key_all, preferred_element_type=jnp.float32)
            * scale
        )
        grad_keys = (
            carried[0]
            + jnp.einsum(
                "hqk,qhd->kd", grad_scores, query_block, preferred_element_type=jnp.float32
            )
            * scale
        )
        grad_values = carried[1] + jnp.einsum(
            "hqk,qhd->kd",
            unnormed.astype(jnp.bfloat16),
            grad_accum,
            preferred_element_type=jnp.float32,
        )
        return ((grad_keys, grad_values), grad_query_block.astype(jnp.bfloat16))

    zeros_kv = jnp.zeros((seq_len, HEAD_DIM), jnp.float32)
    (grad_keys, grad_values), grad_query_blocks = lax.scan(
        retrace,
        (zeros_kv, zeros_kv),
        (query_blocks, grad_blocks, out_blocks, max_blocks, sum_blocks, starts),
    )
    grad_query_send = grad_query_blocks.reshape(seq_len, 1, heads_dev * HEAD_DIM)
    grad_kv_send = (
        jnp.concatenate([grad_keys, grad_values], axis=-1)
        .astype(jnp.bfloat16)
        .reshape(seq_len, 1, 2 * HEAD_DIM)
    )
    grad_query_tok, grad_kv_tok = (
        lax.all_to_all(grad_query_send, "seq", split_axis=0, concat_axis=1, tiled=True),
        lax.all_to_all(grad_kv_send, "seq", split_axis=0, concat_axis=1, tiled=True),
    )
    grad_query_rot = grad_query_tok.reshape(tok_rows, HEADS, HEAD_DIM).astype(jnp.float32)
    grad_kv = jnp.sum(
        grad_kv_tok.astype(jnp.float32).reshape(tok_rows, KV_HEADS, kv_copies, 2 * HEAD_DIM), axis=2
    )
    grad_q = (
        unrotate(grad_query_rot, cosine, sine_table)
        .astype(jnp.bfloat16)
        .reshape(tok_rows, HEADS * HEAD_DIM)
    )
    grad_k = (
        unrotate(grad_kv[..., :HEAD_DIM], cosine, sine_table)
        .astype(jnp.bfloat16)
        .reshape(tok_rows, KV_HEADS * HEAD_DIM)
    )
    grad_v = grad_kv[..., HEAD_DIM:].astype(jnp.bfloat16).reshape(tok_rows, KV_HEADS * HEAD_DIM)
    grad_normed_in = jnp.einsum("to,co->tc", grad_q, query_back, preferred_element_type=jnp.float32)
    grad_normed_in = grad_normed_in + jnp.einsum(
        "to,co->tc", grad_k, key_back, preferred_element_type=jnp.float32
    )
    grad_normed_in = grad_normed_in + jnp.einsum(
        "to,co->tc", grad_v, value_back, preferred_element_type=jnp.float32
    )
    grad_gain_in = jnp.sum(grad_normed_in * unit_in, axis=0)
    grad_stream = norm_back(grad_normed_in * gain_in_back, unit_in, inverse_in) + grad_middle
    attn_terms = (
        spread_rows(normed_in, grad_q, groups, shards),
        spread_rows(normed_in, grad_k, groups, shards),
        spread_rows(normed_in, grad_v, groups, shards),
        spread_rows(attended_tok, grad_proj, groups, shards),
        spread_vector(grad_gain_in, groups, shards),
    )
    attn_parts = (
        lax.psum_scatter(attn_terms[0], ("seq", "fsdp"), scatter_dimension=0, tiled=True),
        lax.psum_scatter(attn_terms[1], ("seq", "fsdp"), scatter_dimension=0, tiled=True),
        lax.psum_scatter(attn_terms[2], ("seq", "fsdp"), scatter_dimension=0, tiled=True),
        lax.psum_scatter(attn_terms[3], ("seq", "fsdp"), scatter_dimension=0, tiled=True),
        lax.psum_scatter(attn_terms[4], ("seq", "fsdp"), scatter_dimension=0, tiled=True),
    )
    grad_query, grad_key, grad_value, grad_out, grad_gain_attn = (
        lax.all_gather(attn_parts[0].astype(jnp.bfloat16), "seq", axis=0, tiled=True).astype(
            jnp.float32
        ),
        lax.all_gather(attn_parts[1].astype(jnp.bfloat16), "seq", axis=0, tiled=True).astype(
            jnp.float32
        ),
        lax.all_gather(attn_parts[2].astype(jnp.bfloat16), "seq", axis=0, tiled=True).astype(
            jnp.float32
        ),
        lax.all_gather(attn_parts[3].astype(jnp.bfloat16), "seq", axis=0, tiled=True).astype(
            jnp.float32
        ),
        lax.all_gather(attn_parts[4].astype(jnp.bfloat16), "seq", axis=0, tiled=True).astype(
            jnp.float32
        ),
    )
    return (
        layer_out[None],
        grad_stream[None],
        grad_query,
        grad_key,
        grad_value,
        grad_out,
        grad_gain_attn,
        grad_gate,
        grad_up,
        grad_down,
        grad_gain_mlp,
    )


def solution(mesh):
    placed = (
        P("fsdp", "seq", None),
        P("fsdp", "seq"),
        P("fsdp", None),
        P("fsdp", None),
        P("fsdp", None),
        P("fsdp", None),
        P("fsdp"),
        P("fsdp", None),
        P("fsdp", None),
        P("fsdp", None),
        P("fsdp"),
        P("fsdp", "seq", None),
    )
    return jax.shard_map(
        on_device,
        mesh=mesh,
        in_specs=placed,
        out_specs=(
            P("fsdp", "seq", None),
            P("fsdp", "seq", None),
            P("fsdp", None),
            P("fsdp", None),
            P("fsdp", None),
            P("fsdp", None),
            P("fsdp"),
            P("fsdp", None),
            P("fsdp", None),
            P("fsdp", None),
            P("fsdp"),
        ),
        check_vma=False,
    )
```

profile of v0, /device:TPU:0, one launch (start us, length us, event | category | flops | bytes accessed | tf_op | source)
XLA Modules:
  0.0 5733.7 jit_solution(6325863598085468374)
XLA Ops:
  11.9 13.7 all-gather
  26.0 14.2 all-gather.19.cloned.1.call-done
  42.0 27.3 all-gather.17.cloned.1.call-done
  75.8 144.2 %all-gather.15.cloned.1.call-done = bf16[2048,2048]{1,0:T(8,128)(2,1)} async-done(((bf16[512,2048]{1,0:T(8,128)(2,1)}), bf16[2048,2048]{1,0:T(8,128)(2,1)}) %all-gather.15.cloned.1.call-update) | async-done | bytes 8388624 | tf_op jit(solution)/shard_map/all_gather | solution.py:97
  220.0 12.4 copy.134
  244.1 9.1 all-to-all-done
  255.6 15.9 while.30
  288.3 12.4 all-gather.1
  305.2 64.2 %all-gather.21.cloned.1.call-done = bf16[2048,2048]{1,0:T(8,128)(2,1)} async-done(((bf16[512,2048]{1,0:T(8,128)(2,1)}), bf16[2048,2048]{1,0:T(8,128)(2,1)}) %all-gather.21.cloned.1.call-update) | async-done | bytes 8388624 | tf_op jit(solution)/shard_map/all_gather | solution.py:100
  374.4 385.9 %all-gather.23.cloned.1.call-done = bf16[2048,5632]{1,0:T(8,128)(2,1)} async-done(((bf16[512,5632]{1,0:T(8,128)(2,1)}), bf16[2048,5632]{1,0:T(8,128)(2,1)}) %all-gather.23.cloned.1.call-update) | async-done | bytes 23068688 | tf_op jit(solution)/shard_map/all_gather | solution.py:167
  760.3 13.3 fusion.108
  773.6 377.5 %all-gather.25.cloned.1.call-done = bf16[2048,5632]{1,0:T(8,128)(2,1)} async-done(((bf16[512,5632]{1,0:T(8,128)(2,1)}), bf16[2048,5632]{1,0:T(8,128)(2,1)}) %all-gather.25.cloned.1.call-update) | async-done | bytes 23068688 | tf_op jit(solution)/shard_map/all_gather | solution.py:168
  1151.1 13.2 fusion.109
  1164.3 377.8 %all-gather.27.cloned.1.call-done = bf16[5632,2048]{1,0:T(8,128)(2,1)} async-done(((bf16[1408,2048]{1,0:T(8,128)(2,1)}), bf16[5632,2048]{1,0:T(8,128)(2,1)}) %all-gather.27.cloned.1.call-update) | async-done | bytes 23068688 | tf_op jit(solution)/shard_map/all_gather | solution.py:169
  1542.1 14.7 multiply_convert_fusion
  1556.9 12.6 fusion.110
  1569.5 13.9 multiply_reduce_fusion
  1605.0 11.8 all-to-all-done.3
  1617.4 37.3 while.31
  1661.1 14.0 all_to_all.81
  1686.5 18.2 fusion.112
  1704.7 34.5 copy.171
  1740.6 18.3 fusion.113
  1758.9 34.7 copy.172
  1796.2 18.0 convolution_bitcast_fusion.1
  1814.2 33.6 copy.174
  1850.8 10.3 all_to_all.82
  1866.5 88.7 %reduce-scatter.14.cloned.1.call-done = f32[64,2048]{1,0:T(8,128)} async-done(((f32[2048,2048]{1,0:T(8,128)}), f32[64,2048]{1,0:T(8,128)}) %reduce-scatter.14.cloned.1.call-update) | async-done | bytes 524304 | tf_op jit(solution)/shard_map/reduce_scatter | solution.py:333
  1957.0 363.8 %reduce-scatter.8.cloned.1.call-done = f32[64,2048]{1,0:T(8,128)} async-done(((f32[2048,2048]{1,0:T(8,128)}), f32[64,2048]{1,0:T(8,128)}) %reduce-scatter.8.cloned.1.call-update) | async-done | bytes 524304 | tf_op jit(solution)/shard_map/reduce_scatter | solution.py:330
  2322.6 970.6 %reduce-scatter.16.cloned.1.call-done = f32[64,5632]{1,0:T(8,128)} async-done(((f32[2048,5632]{1,0:T(8,128)}), f32[64,5632]{1,0:T(8,128)}) %reduce-scatter.16.cloned.1.call-update) | async-done | bytes 1441808 | tf_op jit(solution)/shard_map/reduce_scatter | solution.py:213
  3295.6 972.7 %reduce-scatter.18.cloned.1.call-done = f32[64,5632]{1,0:T(8,128)} async-done(((f32[2048,5632]{1,0:T(8,128)}), f32[64,5632]{1,0:T(8,128)}) %reduce-scatter.18.cloned.1.call-update) | async-done | bytes 1441808 | tf_op jit(solution)/shard_map/reduce_scatter | solution.py:214
  4270.9 972.4 %reduce-scatter.20.cloned.1.call-done = f32[176,2048]{1,0:T(8,128)} async-done(((f32[5632,2048]{1,0:T(8,128)}), f32[176,2048]{1,0:T(8,128)}) %reduce-scatter.20.cloned.1.call-update) | async-done | bytes 1441808 | tf_op jit(solution)/shard_map/reduce_scatter | solution.py:215
  5247.1 11.6 fusion.66
  5258.8 6.5 fusion.111
  5266.6 40.9 all-reduce.4
  5308.1 13.5 all-reduce.5
  5324.1 61.6 %reduce-scatter.10.cloned.1.call-done = f32[64,256]{1,0:T(8,128)} async-done(((f32[2048,256]{1,0:T(8,128)}), f32[64,256]{1,0:T(8,128)}) %reduce-scatter.10.cloned.1.call-update) | async-done | bytes 65552 | tf_op jit(solution)/shard_map/reduce_scatter | solution.py:331
  5386.5 8.1 all_gather.73
  5395.4 128.2 %reduce-scatter.12.cloned.1.call-done = f32[64,256]{1,0:T(8,128)} async-done(((f32[2048,256]{1,0:T(8,128)}), f32[64,256]{1,0:T(8,128)}) %reduce-scatter.12.cloned.1.call-update) | async-done | bytes 65552 | tf_op jit(solution)/shard_map/reduce_scatter | solution.py:332
  5524.4 8.8 all_gather.74
  5534.1 17.5 all-gather.31.cloned.1.call-done
  5555.6 26.1 all-gather.29.cloned.1.call-done
  5585.9 41.5 all-gather.33.cloned.1.call-done
  5627.4 8.6 convert_element_type.284
  5636.0 37.1 all-gather.35.cloned.1.call-done
  5673.1 8.6 convert_element_type.286
  5681.6 36.7 all-gather.37.cloned.1.call-done
  5718.3 8.7 convert_element_type.288
  (297 shorter events, 185.4 us)
Async XLA Ops:
  7.2 33.1 all-gather.19.cloned.1.call-start
  7.9 61.4 %all-gather.17.cloned.1.call-start = ((), (), s32[]{:S(2)}) async-start(), calls=%async_computation.14 | async-start | bytes 1310720 | tf_op jit(solution)/shard_map/all_gather | solution.py:98
  8.7 211.4 %all-gather.15.cloned.1.call-start = ((), (), s32[]{:S(2)}) async-start(), calls=%async_computation.13 | async-start | bytes 10485760 | tf_op jit(solution)/shard_map/all_gather | solution.py:97
  9.4 360.0 %all-gather.21.cloned.1.call-start = ((), (), s32[]{:S(2)}) async-start(), calls=%async_computation.16 | async-start | bytes 10485760 | tf_op jit(solution)/shard_map/all_gather | solution.py:100
  10.0 15.7 copy-start.2
  10.0 15.9 copy-start.44
  10.0 750.3 %all-gather.23.cloned.1.call-start = ((), (), s32[]{:S(2)}) async-start(), calls=%async_computation.17 | async-start | bytes 28835840 | tf_op jit(solution)/shard_map/all_gather | solution.py:167
  10.6 1140.5 %all-gather.25.cloned.1.call-start = ((), (), s32[]{:S(2)}) async-start(), calls=%async_computation.18 | async-start | bytes 28835840 | tf_op jit(solution)/shard_map/all_gather | solution.py:168
  11.2 1531.0 %all-gather.27.cloned.1.call-start = ((), (), s32[]{:S(2)}) async-start(), calls=%async_computation.19 | async-start | bytes 28835840 | tf_op jit(solution)/shard_map/all_gather | solution.py:169
  25.6 206.8 %copy-start.35 = (f32[4,1,512]{2,1,0:T(1,128)}, f32[4,1,512]{2,1,0:T(1,128)S(1)}, u32[]{:S(2)}) copy-start(f32[4,1,512]{2,1,0:T(1,128)S(1)} %convert_element_type.299) | copy-start | bytes 24580
  25.9 206.6 %copy-start.39 = (f32[128]{0:T(128)}, f32[128]{0:T(128)S(1)}, u32[]{:S(2)}) copy-start(f32[128]{0:T(128)S(1)} %add_rsqrt_fusion.1) | copy-start | bytes 1540
  26.0 212.4 %copy-start.29 = (f32[128,32]{0,1:T(8,128)}, f32[128,32]{0,1:T(8,128)S(1)}, u32[]{:S(2)}) copy-start(f32[128,32]{0,1:T(8,128)S(1)} %get-tuple-element.343) | copy-start | bytes 49156
  26.0 212.4 %copy-start.32 = (f32[128,32]{0,1:T(8,128)}, f32[128,32]{0,1:T(8,128)S(1)}, u32[]{:S(2)}) copy-start(f32[128,32]{0,1:T(8,128)S(1)} %get-tuple-element.344) | copy-start | bytes 49156
  72.1 167.3 %all-to-all-start.1 = ((bf16[128,8,128]{0,2,1:T(8,128)(2,1)}), bf16[128,8,128]{0,2,1:T(8,128)(2,1)S(1)}, u32[]{:S(2)}, u32[]{:S(2)}) async-start(bf16[128,8,128]{0,2,1:T(8,128)(2,1)} %pad_maximum_fusion.1), calls=%async_computation.1 | async-start | bytes 524288 | tf_op jit(solution)/shard_map/all_to_all | solution.py:128
  239.5 13.7 all-to-all-start
  271.5 97.9 %copy-start.11 = (f32[2,512,4,64]{1,3,2,0:T(8,128)}, f32[2,512,4,64]{1,3,2,0:T(8,128)S(1)}, u32[]{:S(2)}) copy-start(f32[2,512,4,64]{1,3,2,0:T(8,128)S(1)} %get-tuple-element.523) | copy-start | bytes 3145732
  271.5 16.7 copy-start.43
  284.1 16.7 all-to-all-start.2
  288.2 1666.9 %reduce-scatter.14.cloned.1.call-start = ((), (), s32[]{:S(2)}) async-start(), calls=%async_computation.24 | async-start | bytes 17301504 | tf_op jit(solution)/shard_map/reduce_scatter | solution.py:333
  305.2 69.0 %copy-start.18 = (bf16[128,8,1,256]{0,3,1,2:T(8,128)(2,1)}, bf16[128,8,1,256]{0,3,1,2:T(8,128)(2,1)S(1)}, u32[]{:S(2)}) copy-start(bf16[128,8,1,256]{0,3,1,2:T(8,128)(2,1)S(1)} %copy.144) | copy-start | bytes 1572868
  374.2 1209.2 %copy-start.5 = (f32[128,2048]{1,0:T(8,128)}, f32[128,2048]{1,0:T(8,128)S(1)}, u32[]{:S(2)}) copy-start(f32[128,2048]{1,0:T(8,128)S(1)} %get-tuple-element.346) | copy-start | bytes 3145732
  374.4 776.8 %copy-start.9 = (bf16[128,2048]{1,0:T(8,128)(2,1)}, bf16[128,2048]{1,0:T(8,128)(2,1)S(1)}, u32[]{:S(2)}) copy-start(bf16[128,2048]{1,0:T(8,128)(2,1)S(1)} %multiply_convert_fusion.3) | copy-start | bytes 1572868
  773.6 768.5 %copy-start.24 = (bf16[1,128,2048]{2,1,0:T(8,128)(2,1)S(1)}, bf16[1,128,2048]{2,1,0:T(8,128)(2,1)}, u32[]{:S(2)}) copy-start(bf16[1,128,2048]{2,1,0:T(8,128)(2,1)} %param.27) | copy-start | bytes 1572868
  1569.5 15.6 copy-start.19
  1593.9 23.5 copy-start.12
  1601.3 15.5 all-to-all-start.3
  1604.9 715.8 %reduce-scatter.8.cloned.1.call-start = ((), (), s32[]{:S(2)}) async-start(), calls=%async_computation.20 | async-start | bytes 17301504 | tf_op jit(solution)/shard_map/reduce_scatter | solution.py:330
  1654.7 21.7 copy-start.16
  1654.7 21.4 copy-start.30
  1654.7 21.5 copy-start.33
  1654.7 21.7 copy-start.3
  1654.7 21.7 copy-start.36
  1654.7 21.7 copy-start.40
  1685.0 1608.3 %reduce-scatter.16.cloned.1.call-start = ((), (), s32[]{:S(2)}) async-start(), calls=%async_computation.26 | async-start | bytes 47579136 | tf_op jit(solution)/shard_map/reduce_scatter | solution.py:213
  1739.2 2529.1 %reduce-scatter.18.cloned.1.call-start = ((), (), s32[]{:S(2)}) async-start(), calls=%async_computation.28 | async-start | bytes 47579136 | tf_op jit(solution)/shard_map/reduce_scatter | solution.py:214
  1793.6 3449.7 %reduce-scatter.20.cloned.1.call-start = ((), (), s32[]{:S(2)}) async-start(), calls=%async_computation.30 | async-start | bytes 47579136 | tf_op jit(solution)/shard_map/reduce_scatter | solution.py:215
  1847.8 14.4 copy-start.37
  1847.9 3537.8 %reduce-scatter.10.cloned.1.call-start = ((), (), s32[]{:S(2)}) async-start(), calls=%async_computation.22 | async-start | bytes 2162688 | tf_op jit(solution)/shard_map/reduce_scatter | solution.py:331
  1864.2 3659.4 %reduce-scatter.12.cloned.1.call-start = ((), (), s32[]{:S(2)}) async-start(), calls=%async_computation.23 | async-start | bytes 2162688 | tf_op jit(solution)/shard_map/reduce_scatter | solution.py:332
  1864.9 3380.8 %copy-start.45 = (u32[32]{0:T(128)S(1)}, u32[32]{0:T(128)}, u32[]{:S(2)}) copy-start(u32[32]{0:T(128)} %constant.68) | copy-start | bytes 388
  1864.9 3382.0 %copy-start.38 = (f32[2048]{0:T(1024)S(1)}, f32[2048]{0:T(1024)}, u32[]{:S(2)}) copy-start(f32[2048]{0:T(1024)} %get-tuple-element.274) | copy-start | bytes 24580
  1864.9 3382.2 %copy-start.6 = (f32[128,2048]{1,0:T(8,128)S(1)}, f32[128,2048]{1,0:T(8,128)}, u32[]{:S(2)}) copy-start(f32[128,2048]{1,0:T(8,128)} %copy-done.5) | copy-start | bytes 3145732
  1866.4 3685.1 %all-gather.31.cloned.1.call-start = ((), (), s32[]{:S(2)}) async-start(), calls=%async_computation.25 | async-start | bytes 2359296 | tf_op jit(solution)/shard_map/all_gather | solution.py:346
  1957.0 3624.8 %all-gather.29.cloned.1.call-start = ((), (), s32[]{:S(2)}) async-start(), calls=%async_computation.21 | async-start | bytes 2359296 | tf_op jit(solution)/shard_map/all_gather | solution.py:337
  2322.6 3304.8 %all-gather.33.cloned.1.call-start = ((), (), s32[]{:S(2)}) async-start(), calls=%async_computation.27 | async-start | bytes 6488064 | tf_op jit(solution)/shard_map/all_gather | solution.py:219
  3295.6 2377.5 %all-gather.35.cloned.1.call-start = ((), (), s32[]{:S(2)}) async-start(), calls=%async_computation.29 | async-start | bytes 6488064 | tf_op jit(solution)/shard_map/all_gather | solution.py:222
  4270.7 1447.6 %all-gather.37.cloned.1.call-start = ((), (), s32[]{:S(2)}) async-start(), calls=%async_computation.31 | async-start | bytes 6488064 | tf_op jit(solution)/shard_map/all_gather | solution.py:225
  5258.8 64.0 %copy-start.8 = (f32[128,2048]{1,0:T(8,128)S(1)}, f32[128,2048]{1,0:T(8,128)}, u32[]{:S(2)}) copy-start(f32[128,2048]{1,0:T(8,128)} %copy-done.7) | copy-start | bytes 3145732
  (25 other events, 154.1 us)
Sparse Core Ops, SparseCore 0:
  9.6 30.6 all-gather.18
  41.8 27.4 all-gather.16
  70.9 149.1 all-gather.14
  221.4 147.9 all-gather.20
  370.9 389.3 all-gather.22
  761.7 389.3 all-gather.24
  1152.7 389.3 all-gather.26
  1594.0 361.0 reduce-scatter.13
  1957.4 363.2 reduce-scatter.7
  2322.9 970.2 reduce-scatter.15
  3295.6 972.7 reduce-scatter.17
  4270.5 972.7 reduce-scatter.19
  5246.2 139.4 reduce-scatter.9
  5388.4 135.1 reduce-scatter.11
  5525.3 26.1 all-gather.30
  5553.8 27.8 all-gather.28
  5584.1 43.3 all-gather.32
  5629.7 43.3 all-gather.34
  5675.0 43.3 all-gather.36
where the time goes:
time: 5740 us; the launch traced here: 5730 us
  waiting for transfers between devices  5130 us (89%)
  matrix products  206 us (4%)
  local copies, waits for them, and re-layouts  165 us (3%)
  blocking collectives  122 us (2%)
  other arithmetic  74.5 us (1%)
    reduce_scatter x1, waiting for transfers between devices, on_device(): lax.psum_scatter(mlp_terms[1], ('seq', 'fsdp'), scatter_dimension=0, tile...  973 us
    reduce_scatter x1, waiting for transfers between devices, on_device(): lax.psum_scatter(mlp_terms[2], ('seq', 'fsdp'), scatter_dimension=0, tile...  972 us
    reduce_scatter x1, waiting for transfers between devices, on_device(): lax.psum_scatter(mlp_terms[0], ('seq', 'fsdp'), scatter_dimension=0, tile...  971 us
    all_gather x1, waiting for transfers between devices, on_device(): lax.all_gather(w_gate, 'fsdp', axis=0, tiled=True)  386 us
    all_gather x1, waiting for transfers between devices, on_device(): lax.all_gather(w_down, 'fsdp', axis=0, tiled=True)  378 us
    all_gather x1, waiting for transfers between devices, on_device(): lax.all_gather(w_up, 'fsdp', axis=0, tiled=True)  378 us
    reduce_scatter x1, waiting for transfers between devices, on_device(): lax.psum_scatter(attn_terms[0], ('seq', 'fsdp'), scatter_dimension=0, til...  364 us
    all_gather x1, waiting for transfers between devices, on_device(): lax.all_gather(w_query, 'fsdp', axis=0, tiled=True)  144 us
  transfers between devices with their start and end apart: 23, of which 21 were waited for; matrix products, arithmetic and copies ran while one was open for 7% of the time, Pallas kernels for 0%

commit v1 on v0

v1 whole, which is shorter than its diff:
```python
import math

import jax
import jax.numpy as jnp
from jax import lax
from jax.sharding import PartitionSpec as P

HEADS = 32
KV_HEADS = 4
HEAD_DIM = 64


EPS = 1e-05
ROPE_BASE = 10000.0


def rope_tables(positions, head_size):
    half_dim = head_size // 2
    freqs_base = jnp.exp(
        jnp.arange(half_dim, dtype=jnp.float32) * (-2.0 * math.log(ROPE_BASE) / head_size)
    )
    angles = positions.astype(jnp.float32)[..., None] * freqs_base
    return (jnp.cos(angles), jnp.sin(angles))


def rotate(values, cosine, sine_table):
    half_dim = values.shape[-1] // 2
    lower_half = values[..., :half_dim]
    upper_half = values[..., half_dim:]
    cos_part = cosine[:, None, :]
    sin_part = sine_table[:, None, :]
    return jnp.concatenate(
        [
            lower_half * cos_part - upper_half * sin_part,
            upper_half * cos_part + lower_half * sin_part,
        ],
        axis=-1,
    )


def unrotate(values, cosine, sine_table):
    return rotate(values, cosine, -sine_table)


def norm_back(grad_normed, normed, inverse):
    return inverse * (grad_normed - normed * jnp.mean(grad_normed * normed, axis=-1, keepdims=True))


def dot(left, right, dims):
    return lax.dot_general(left, right, ((dims[0], dims[1]), ((), ())), preferred_element_type=jnp.float32)


def swap(value, mask):
    return lax.ppermute(value, "seq", [(i, i ^ mask) for i in range(lax.axis_size("seq"))])


def seq_gather(part):
    n = lax.axis_size("seq")
    if n == 8:
        half = part.shape[0] // 2
        by_x, by_y = swap(part, 2), swap(part, 4)
        far = jnp.concatenate([swap(by_x[:half], 4), swap(by_y[half:], 2)])
        mine = jnp.stack([part, by_x, by_y, far])
    else:
        mine, mask = part[None], 2
        while mask < n:
            mine = jnp.concatenate([mine, swap(mine, mask)])
            mask *= 2
    return jnp.concatenate([mine, swap(mine, 1)])


def seq_scatter(parts):
    n = lax.axis_size("seq")

    def add(own, other):
        return own.astype(jnp.float32) + other.astype(jnp.float32)

    low = jnp.bfloat16
    mine = add(parts[: n // 2], swap(parts[n // 2 :], 1))
    if n == 8:
        half = parts.shape[1] // 2
        far = mine[3].astype(low)
        from_x, from_y = swap(far[:half], 2), swap(far[half:], 4)
        to_y = jnp.concatenate([add(mine[2][:half], from_x), mine[2][half:]]).astype(low)
        to_x = jnp.concatenate([mine[1][:half], add(mine[1][half:], from_y)]).astype(low)
        return mine[0] + swap(to_x, 2).astype(jnp.float32) + swap(to_y, 4).astype(jnp.float32)
    mask = n // 2
    while mask > 1:
        count = mine.shape[0] // 2
        mine = add(mine[:count], swap(mine[count:].astype(low), mask))
        mask //= 2
    return mine[0]


def flips(stacked, axis):
    shape, n, bit = stacked.shape, stacked.shape[axis], 1
    place = lax.axis_index("seq")
    while bit < n:
        split = stacked.reshape(shape[:axis] + (n // (2 * bit), 2, bit) + shape[axis + 1 :])
        stacked = jnp.where((place & bit) != 0, jnp.flip(split, axis + 1), split).reshape(shape)
        bit *= 2
    return stacked


def to_absolute(slots, axis=0):
    shape, n = slots.shape, slots.shape[axis]
    split = slots.reshape(shape[:axis] + (2, n // 2) + shape[axis + 1 :])
    return flips(jnp.swapaxes(split, axis, axis + 1).reshape(shape), axis)


def to_slots(absolute, axis=0):
    shape, n = absolute.shape, absolute.shape[axis]
    split = flips(absolute, axis).reshape(shape[:axis] + (n // 2, 2) + shape[axis + 1 :])
    return jnp.swapaxes(split, axis, axis + 1).reshape(shape)


def seq_exchange(slots):
    n = lax.axis_size("seq")
    masks = [((k << 1) & (n - 1)) | (k // (n // 2)) for k in range(n)]
    return jnp.stack([slots[k] if mask == 0 else swap(slots[k], mask) for k, mask in enumerate(masks)])


def columns_of(weight, place, groups, shards):
    width = weight.shape[1] // (groups * shards)
    return jnp.concatenate(
        [
            lax.dynamic_slice_in_dim(weight, (f * groups + place) * width, width, 1)
            for f in range(shards)
        ],
        axis=1,
    )


def on_device(
    tokens,
    positions,
    w_query,
    w_key,
    w_value,
    w_out,
    gain_attn,
    w_gate,
    w_up,
    w_down,
    gain_mlp,
    cotangent,
):
    low, wide = jnp.bfloat16, jnp.float32
    groups = lax.axis_size("seq")
    shards = lax.axis_size("fsdp")
    place = lax.axis_index("seq")
    shard = lax.axis_index("fsdp")
    tok_rows, width = tokens.shape[1:]
    shard_rows = w_query.shape[0]
    heads_dev = HEADS // groups
    kv_copies = groups // KV_HEADS
    seq_len = tok_rows * groups
    q_cols = heads_dev * HEAD_DIM
    out_cols = width // groups
    ff = w_gate.shape[1]
    ff_dev = ff // groups
    scale = HEAD_DIM ** (-0.5)

    def z_gather(part):
        return lax.all_gather(part, "fsdp", axis=0, tiled=True)

    def z_scatter(part):
        return lax.psum_scatter(part, "fsdp", scatter_dimension=0, tiled=True)

    def columns(weight, start, count):
        return lax.dynamic_slice_in_dim(weight, start, count, 1)

    kv_head = place // kv_copies
    attn_full = z_gather(
        jnp.concatenate(
            [
                columns(w_query, place * q_cols, q_cols),
                columns(w_key, kv_head * HEAD_DIM, HEAD_DIM),
                columns(w_value, kv_head * HEAD_DIM, HEAD_DIM),
            ],
            axis=1,
        )
    )
    out_part = z_gather(columns(w_out, place * out_cols, out_cols))
    gate_full = z_gather(columns_of(w_gate, place, groups, shards))
    up_full = z_gather(columns_of(w_up, place, groups, shards))
    down_rows = w_down.shape[0] // groups
    down_full = z_gather(lax.dynamic_slice_in_dim(w_down, place * down_rows, down_rows, 0))
    gains = lax.all_gather(jnp.stack([gain_attn, gain_mlp]), "fsdp", axis=1, tiled=True)
    gain_in, gain_mid = gains[0].astype(wide), gains[1].astype(wide)

    own = tokens[0]
    stream = seq_gather(own).reshape(seq_len, width).astype(wide)
    dy = seq_gather(cotangent[0]).reshape(seq_len, width)
    where = seq_gather(positions).reshape(seq_len)
    cosine, sine_table = rope_tables(where, HEAD_DIM)
    inverse_all = lax.rsqrt(jnp.mean(stream * stream, axis=-1, keepdims=True) + EPS)
    normed_in = (stream * inverse_all * gain_in).astype(low)
    qkv = jnp.dot(normed_in, attn_full, preferred_element_type=wide)
    query_rot = rotate(qkv[:, :q_cols].reshape(seq_len, heads_dev, HEAD_DIM), cosine, sine_table)
    key_rot = rotate(qkv[:, None, q_cols : q_cols + HEAD_DIM], cosine, sine_table)
    qkv_rot = jnp.concatenate(
        [query_rot.reshape(seq_len, q_cols), key_rot[:, 0], qkv[:, q_cols + HEAD_DIM :]], axis=1
    ).astype(low)
    qkv_all = to_absolute(qkv_rot.reshape(groups, tok_rows, -1)).reshape(seq_len, -1)
    query_all = qkv_all[:, :q_cols].reshape(seq_len, heads_dev, HEAD_DIM)
    key_all = qkv_all[:, q_cols : q_cols + HEAD_DIM]
    value_all = qkv_all[:, q_cols + HEAD_DIM :]

    block = 512
    blocks = seq_len // block
    key_index = jnp.arange(seq_len, dtype=jnp.int32)
    starts = jnp.arange(blocks, dtype=jnp.int32) * block
    query_blocks = query_all.reshape(blocks, block, heads_dev, HEAD_DIM)

    def block_scores(query_block, start):
        scores = (
            jnp.einsum("qhd,kd->hqk", query_block, key_all, preferred_element_type=jnp.float32)
            * scale
        )
        causal = key_index[None, :] <= (start + jnp.arange(block, dtype=jnp.int32))[:, None]
        return jnp.where(causal[None], scores, -jnp.inf)

    def attend(block_args):
        query_block, start = block_args
        scores = block_scores(query_block, start)
        row_max = jnp.max(scores, axis=-1)
        unnormed = jnp.exp(scores - row_max[..., None])
        row_sum = jnp.sum(unnormed, axis=-1)
        accum = jnp.einsum(
            "hqk,kd->qhd",
            unnormed.astype(jnp.bfloat16),
            value_all,
            preferred_element_type=jnp.float32,
        )
        return (accum / jnp.transpose(row_sum)[:, :, None], row_max, row_sum)

    out_blocks, max_blocks, sum_blocks = lax.map(attend, (query_blocks, starts))
    attended_send = out_blocks.astype(low).reshape(groups, tok_rows, q_cols)
    attended_tok = (
        to_absolute(seq_exchange(to_slots(attended_send))).transpose(1, 0, 2).reshape(tok_rows, -1)
    )

    out_slots = seq_gather(out_part)
    stream_own = own.astype(wide)
    projected = jnp.einsum("to,soc->tsc", attended_tok, out_slots, preferred_element_type=wide)
    middle = stream_own + to_absolute(projected, 1).reshape(tok_rows, width)
    inverse_mid = lax.rsqrt(jnp.mean(middle * middle, axis=-1, keepdims=True) + EPS)
    unit_mid = middle * inverse_mid
    normed_mid = seq_gather((unit_mid * gain_mid).astype(low)).reshape(seq_len, width)

    gate_pre = jnp.dot(normed_mid, gate_full, preferred_element_type=wide)
    upper_pre = jnp.dot(normed_mid, up_full, preferred_element_type=wide)
    sigmoid_gate = jax.nn.sigmoid(gate_pre)
    activated = gate_pre * sigmoid_gate
    hidden = (activated * upper_pre).astype(low)
    down_term = jnp.dot(hidden, down_full, preferred_element_type=wide).astype(low)
    layer_out = (middle + seq_scatter(down_term.reshape(groups, tok_rows, width))).astype(low)

    grad_hidden = dot(dy, down_full, ((1,), (1,)))
    grad_gate_pre = (
        grad_hidden * upper_pre * (sigmoid_gate * (1.0 + gate_pre * (1.0 - sigmoid_gate)))
    ).astype(low)
    grad_upper = (grad_hidden * activated).astype(low)
    grad_normed_mid = (
        dot(grad_gate_pre, gate_full, ((1,), (1,))) + dot(grad_upper, up_full, ((1,), (1,)))
    ).astype(low)
    grad_normed_mid = seq_scatter(grad_normed_mid.reshape(groups, tok_rows, width))
    grad_layer = cotangent[0].astype(wide)
    grad_gain_mid = jnp.sum(grad_normed_mid * unit_mid, axis=0)
    grad_middle = norm_back(grad_normed_mid * gain_mid, unit_mid, inverse_mid) + grad_layer
    down_sum = z_scatter(dot(hidden, dy, ((0,), (0,))).astype(low))
    gate_sum = z_scatter(dot(normed_mid, grad_gate_pre, ((0,), (0,))).astype(low))
    up_sum = z_scatter(dot(normed_mid, grad_upper, ((0,), (0,))).astype(low))

    grad_proj = to_slots(grad_middle.astype(low).reshape(tok_rows, groups, out_cols), 1)
    grad_attended = jnp.einsum("tsc,soc->to", grad_proj, out_slots, preferred_element_type=wide)
    grad_attended = to_slots(grad_attended.astype(low).reshape(tok_rows, groups, q_cols), 1)
    grad_heads = to_absolute(seq_exchange(grad_attended.transpose(1, 0, 2)))
    grad_blocks = grad_heads.reshape(blocks, block, heads_dev, HEAD_DIM)

    def retrace(carried, block_args):
        query_block, grad_block, out_block, row_max, row_sum, start = block_args
        scores = block_scores(query_block, start)
        unnormed = jnp.exp(scores - row_max[..., None])
        grad_out_f = grad_block.astype(jnp.float32)
        grad_accum = (grad_out_f / jnp.transpose(row_sum)[:, :, None]).astype(jnp.bfloat16)
        grad_probs = jnp.einsum(
            "qhd,kd->hqk", grad_accum, value_all, preferred_element_type=jnp.float32
        )
        shift = jnp.transpose(jnp.sum(grad_out_f * out_block, axis=-1)) / row_sum
        grad_scores = (unnormed * (grad_probs - shift[..., None])).astype(jnp.bfloat16)
        grad_query_block = (
            jnp.einsum("hqk,kd->qhd", grad_scores, key_all, preferred_element_type=jnp.float32)
            * scale
        )
        grad_keys = (
            carried[0]
            + jnp.einsum(
                "hqk,qhd->kd", grad_scores, query_block, preferred_element_type=jnp.float32
            )
            * scale
        )
        grad_values = carried[1] + jnp.einsum(
            "hqk,qhd->kd",
            unnormed.astype(jnp.bfloat16),
            grad_accum,
            preferred_element_type=jnp.float32,
        )
        return ((grad_keys, grad_values), grad_query_block.astype(jnp.bfloat16))

    zeros_kv = jnp.zeros((seq_len, HEAD_DIM), jnp.float32)
    (grad_keys, grad_values), grad_query_blocks = lax.scan(
        retrace,
        (zeros_kv, zeros_kv),
        (query_blocks, grad_blocks, out_blocks, max_blocks, sum_blocks, starts),
    )
    grad_all = jnp.concatenate(
        [
            grad_query_blocks.reshape(seq_len, q_cols),
            grad_keys.astype(low),
            grad_values.astype(low),
        ],
        axis=1,
    )
    grad_all = to_slots(grad_all.reshape(groups, tok_rows, -1)).reshape(seq_len, -1).astype(wide)
    grad_q = unrotate(
        grad_all[:, :q_cols].reshape(seq_len, heads_dev, HEAD_DIM), cosine, sine_table
    )
    grad_k = unrotate(grad_all[:, None, q_cols : q_cols + HEAD_DIM], cosine, sine_table)
    grad_qkv = jnp.concatenate(
        [grad_q.reshape(seq_len, q_cols), grad_k[:, 0], grad_all[:, q_cols + HEAD_DIM :]], axis=1
    ).astype(low)
    grad_normed_in = dot(grad_qkv, attn_full, ((1,), (1,))).astype(low)
    grad_normed_in = seq_scatter(grad_normed_in.reshape(groups, tok_rows, width))
    inverse_in = lax.rsqrt(jnp.mean(stream_own * stream_own, axis=-1, keepdims=True) + EPS)
    unit_in = stream_own * inverse_in
    grad_gain_in = jnp.sum(grad_normed_in * unit_in, axis=0)
    grad_stream = norm_back(grad_normed_in * gain_in, unit_in, inverse_in) + grad_middle

    attended_all = seq_gather(attended_tok).reshape(seq_len, -1)
    grad_proj_cols = seq_exchange(grad_proj.transpose(1, 0, 2)).reshape(seq_len, out_cols)
    attn_sum = z_scatter(
        jnp.concatenate(
            [
                dot(normed_in, grad_qkv, ((0,), (0,))).astype(low),
                dot(attended_all, grad_proj_cols, ((0,), (0,))).astype(low),
            ],
            axis=1,
        )
    )

    def spread_columns(part, pieces):
        slots = to_absolute(seq_gather(part)).astype(wide)
        split = slots.reshape(groups, part.shape[0], pieces, -1)
        return split.transpose(1, 2, 0, 3).reshape(part.shape[0], -1)

    grad_down = to_absolute(seq_gather(down_sum)).reshape(w_down.shape).astype(wide)
    grad_gate = spread_columns(gate_sum, shards)
    grad_up = spread_columns(up_sum, shards)
    attn_slots = to_absolute(seq_gather(attn_sum)).astype(wide)

    def flat(part):
        return part.transpose(1, 0, 2).reshape(shard_rows, -1)

    grad_query = flat(attn_slots[:, :, :q_cols])
    grad_kv = attn_slots[:, :, q_cols : q_cols + 2 * HEAD_DIM].reshape(
        KV_HEADS, kv_copies, shard_rows, 2 * HEAD_DIM
    )
    grad_kv = jnp.sum(grad_kv, axis=1)
    grad_key = flat(grad_kv[:, :, :HEAD_DIM])
    grad_value = flat(grad_kv[:, :, HEAD_DIM:])
    grad_out = flat(attn_slots[:, :, q_cols + 2 * HEAD_DIM :])
    gain_sums = lax.psum(jnp.stack([grad_gain_in, grad_gain_mid]), ("seq", "fsdp"))
    gain_sums = lax.dynamic_slice_in_dim(gain_sums, shard * shard_rows, shard_rows, 1)
    return (
        layer_out[None],
        grad_stream[None],
        grad_query,
        grad_key,
        grad_value,
        grad_out,
        gain_sums[0],
        grad_gate,
        grad_up,
        grad_down,
        gain_sums[1],
    )


def solution(mesh):
    placed = (
        P("fsdp", "seq", None),
        P("fsdp", "seq"),
        P("fsdp", None),
        P("fsdp", None),
        P("fsdp", None),
        P("fsdp", None),
        P("fsdp"),
        P("fsdp", None),
        P("fsdp", None),
        P("fsdp", None),
        P("fsdp"),
        P("fsdp", "seq", None),
    )
    return jax.shard_map(
        on_device,
        mesh=mesh,
        in_specs=placed,
        out_specs=(
            P("fsdp", "seq", None),
            P("fsdp", "seq", None),
            P("fsdp", None),
            P("fsdp", None),
            P("fsdp", None),
            P("fsdp", None),
            P("fsdp"),
            P("fsdp", None),
            P("fsdp", None),
            P("fsdp", None),
            P("fsdp"),
        ),
        check_vma=False,
    )
```

time: 5740 us -> 815 us (0.14)
  waiting for transfers between devices: 5130 us -> 111 us
  other arithmetic: 74.5 us -> 162 us
  matrix products: 206 us -> 121 us
  local copies, waits for them, and re-layouts: 165 us -> 236 us
  starting transfers between devices: 16.3 us -> 76.9 us
    reduce_scatter x7 -> x4, waiting for transfers between devices: 3560 us -> 0.03 us  [z_scatter(): return lax.psum_scatter(part, 'fsdp', scatter_dimension=0, tiled=True)]
    all_gather x12 -> x5, waiting for transfers between devices: 1550 us -> 10.6 us  [z_gather(): return lax.all_gather(part, 'fsdp', axis=0, tiled=True)]
    transpose x9 -> x5, local copies, waits for them, and re-layouts: 118 us -> 1.28 us  [the longest x3 0.97 us: flat(): return part.transpose(1, 0, 2).reshape(shard_rows, -1)]
    ppermute x0 -> x85, waiting for transfers between devices: none -> 100 us  [swap(): lax.ppermute(value, 'seq', [(i, i ^ mask) for i in range(lax.axis_size('s...]
    ppermute x0 -> x85, starting transfers between devices: none -> 76.6 us  [swap(): lax.ppermute(value, 'seq', [(i, i ^ mask) for i in range(lax.axis_size('s...]
    psum x0 -> x1, blocking collectives: none -> 71.7 us  [on_device(): lax.psum(jnp.stack([grad_gain_in, grad_gain_mid]), ('seq', 'fsdp'))]
    unnamed x106 -> x215, local copies, waits for them, and re-layouts: 14 us -> 85 us
  transfers between devices with their start and end apart: 23 -> 94, of which waited for: 21 -> 35; matrix products, arithmetic and copies ran while one was open for 7% -> 58% of each run, Pallas kernels for 0% -> 0%
where the time goes in v1:
time: 815 us; the launch traced here: 808 us
  local copies, waits for them, and re-layouts  236 us (29%)
  other arithmetic  162 us (20%)
  matrix products  121 us (15%)
  waiting for transfers between devices  111 us (14%)
  blocking collectives  84.1 us (10%)
  starting transfers between devices  76.9 us (9%)
  between operations  16.3 us (2%)
    ppermute x85, waiting for transfers between devices, swap(): lax.ppermute(value, 'seq', [(i, i ^ mask) for i in range(lax.axis_size('s...  100 us
    unnamed x215, local copies, waits for them, and re-layouts  85 us
    ppermute x85, starting transfers between devices, swap(): lax.ppermute(value, 'seq', [(i, i ^ mask) for i in range(lax.axis_size('s...  76.6 us
    psum x1, blocking collectives, on_device(): lax.psum(jnp.stack([grad_gain_in, grad_gain_mid]), ('seq', 'fsdp'))  71.7 us
    dot_general x9, matrix products, dot(): lax.dot_general(left, right, ((dims[0], dims[1]), ((), ())), preferred_el...  43.7 us
    select_n x35, other arithmetic, flips(): jnp.where(place & bit != 0, jnp.flip(split, axis + 1), split).reshape(shape)  42.7 us
    concatenate x10, local copies, waits for them, and re-layouts, seq_gather(): return jnp.concatenate([mine, swap(mine, 1)])  26.9 us
    another operation x19, other arithmetic, seq_gather(): mine = jnp.stack([part, by_x, by_y, far])  26.8 us
  transfers between devices with their start and end apart: 94, of which 35 were waited for; matrix products, arithmetic and copies ran while one was open for 58% of the time, Pallas kernels for 0%

profile of v1, /device:TPU:0, one launch (start us, length us, event | category | flops | bytes accessed | tf_op | source)
XLA Modules:
  0.0 807.5 jit_solution(6574702042329566771)
XLA Ops:
  30.2 12.4 %all_gather.18 = bf16[2,2048]{1,0:T(2,128)(2,1)S(1)} all-gather(bf16[2,512]{1,0:T(2,128)(2,1)S(1)} %pad_maximum_fusion.26), channel_id=1, replica_groups=mesh['seq'=8,'fsdp'=4] {'fsdp'}, dimensions={1}, use_global_device_ids=true | all-gather | bytes 10240 | tf_op jit(solution)/shard_map/all_gather | solution.py:189
  75.5 17.6 %collective-permute-done.17 = bf16[2048,256]{1,0:T(8,128)(2,1)S(1)} collective-permute-done((bf16[2048,256]{1,0:T(8,128)(2,1)}, bf16[2048,256]{1,0:T(8,128)(2,1)S(1)}, u32[]{:S(2)}, u32[]{:S(2)}) %collective-permute-start.17) | collective-permute-done | bytes 1048608 | tf_op jit(solution)/shard_map/ppermute | solution.py:54
  103.1 5.2 fusion.65
  108.3 4.5 fusion.130
  132.6 3.6 pad_maximum_fusion
  136.2 17.1 %while.30 = (s32[]{:T(128)}, f32[2,512,4,64]{1,3,2,0:T(8,128)S(1)}, f32[2,4,512]{2,1,0:T(4,128)}, f32[2,4,512]{2,1,0:T(4,128)S(1)}, s32[2]{0:T(128)S(1)}, /*inde...) while((s32[]{:T(128)}, f32[2,512,4,64]{1,3,2,0:T(8,128)S(1)}, ...), condition=%wide.region_4.5_spmd.clone, body=%wide.region_1.4_spmd.clone.sunk | while | flops 560591360 | bytes 28389504 | solution.py:238
  156.1 4.0 rev.115
  184.1 4.5 constant_dynamic-update-slice_fusion.18
  188.5 4.7 convolution_bitcast_fusion.3
  206.4 6.5 collective-permute-done.22
  239.3 8.0 fusion.131
  247.2 8.2 %fusion.132 = f32[1024,704]{0,1:T(8,128)} fusion(bf16[1024,2048]{1,0:T(8,128)(2,1)} %bitcast.60, bf16[2048,704]{1,0:T(8,128)(2,1)} %all-gather.12.cloned.1.call-done), kind=kOutput, calls=%fused_computation.396 | convolution fusion | flops 2952790016 | bytes 9961472 | tf_op jit(solution)/shard_map/dot_general | solution.py:253
  255.4 10.6 %all-gather.14.cloned.1.call-done = bf16[704,2048]{1,0:T(8,128)(2,1)} async-done(((bf16[176,2048]{1,0:T(8,128)(2,1)}), bf16[704,2048]{1,0:T(8,128)(2,1)}) %all-gather.14.cloned.1.call-update) | async-done | bytes 2883600 | tf_op jit(solution)/shard_map/all_gather | solution.py:165
  266.0 10.4 %multiply_convert_fusion = (bf16[1024,704]{0,1:T(8,128)(2,1)}, bf16[1024,704]{0,1:T(8,128)(2,1)S(1)}, bf16[1024,704]{0,1:T(8,128)(2,1)}) fusion(f32[1024,704]{0,1:T(8,128)} %fusion.131, f32[1024,704]{0,1:T(8,128)} %fusion.132, bf16[1024,2048]{1,0:T(8,128)(2,1)} %bitcast.75, bf16[704,2048]{1,0:T(8,128)(2,1)} %all-gather.14.cloned.1.call-done), kind=kOutput, calls=%fused_computation.99 | convolution fusion | flops 2963603456 | bytes 17170432 | tf_op jit(solution)/shard_map/dot_general | solution.py:50
  277.5 6.7 convolution_convert_fusion.3
  305.7 4.2 add_convert_fusion
  313.7 3.7 convolution_convert_fusion.1
  320.4 6.8 convolution_convert_fusion.2
  355.1 6.7 convolution_convert_fusion.4
  367.2 5.6 collective-permute-done.30
  374.1 4.1 fusion.124
  383.2 6.3 fusion.68
  409.5 39.9 %while.31 = (s32[]{:T(128)}, f32[1024,64]{0,1:T(8,128)S(1)}, f32[1024,64]{0,1:T(8,128)S(1)}, bf16[2,512,4,64]{1,3,2,0:T(8,128)(2,1)}, s32[2]{0:T(128)S(1)}, /*in...) while((s32[]{:T(128)}, f32[1024,64]{0,1:T(8,128)S(1)}, ...), condition=%wide.region_10.11_spmd.clone, body=%wide.region_8.10_spmd.clone.sunk | while | flops 1365443072 | bytes 101691760 | solution.py:313
  412.8 5.4 fusion.199
  421.2 5.9 fusion.201
  432.6 5.4 fusion.199
  441.1 5.9 fusion.201
  452.1 5.8 rev.130
  487.5 5.1 collective-permute-done.49
  507.0 3.7 collective-permute-done.52
  515.6 71.7 %psum.7 = f32[2,2048]{1,0:T(2,128)S(1)} all-reduce(f32[2,2048]{1,0:T(2,128)S(1)} %pad_maximum_fusion.25), channel_id=1, replica_groups=mesh['seq'=8,'fsdp'=4] {'seq','fsdp'}, use_global_device_ids=true, to_apply=%region_16.17 | all-reduce | flops 4096 | bytes 32768 | tf_op jit(solution)/shard_map/psum | solution.py:374
  600.7 6.8 collective-permute-done.80
  638.5 10.4 %collective-permute-done.66 = bf16[512,640]{0,1:T(8,128)(2,1)S(1)} collective-permute-done((bf16[512,640]{0,1:T(8,128)(2,1)}, bf16[512,640]{0,1:T(8,128)(2,1)S(1)}, u32[]{:S(2)}, u32[]{:S(2)}) %collective-permute-start.66) | collective-permute-done | bytes 655392 | tf_op jit(solution)/shard_map/ppermute | solution.py:54
  651.2 6.7 collective-permute-done.68
  669.0 6.1 convert_bitcast_fusion.1
  675.1 11.0 %copy.212 = f32[512,4,8,176]{0,3,2,1:T(8,128)} copy(f32[512,4,8,176]{0,3,1,2:T(8,128)} %convert_bitcast_fusion.1) | data formatting | bytes 23068672 | tf_op jit(solution)/shard_map/reshape | solution.py:356
  686.0 12.1 %copy.218 = f32[512,5632]{1,0:T(8,128)} copy(f32[512,5632]{0,1:T(8,128)} %bitcast.692) | data formatting | bytes 23068672
  701.8 6.1 reverse_select_fusion.5
  711.0 3.9 constant_dynamic-update-slice_fusion.72
  714.8 7.1 reverse_select_fusion.2
  722.0 4.1 reverse_select_fusion.1
  726.0 6.1 convert_bitcast_fusion
  732.1 10.8 %copy.214 = f32[512,4,8,176]{0,3,2,1:T(8,128)} copy(f32[512,4,8,176]{0,3,1,2:T(8,128)} %convert_bitcast_fusion) | data formatting | bytes 23068672 | tf_op jit(solution)/shard_map/reshape | solution.py:356
  742.9 12.1 %copy.219 = f32[512,5632]{1,0:T(8,128)} copy(f32[512,5632]{0,1:T(8,128)} %bitcast.693) | data formatting | bytes 23068672
  760.3 6.4 bitcast_convert_fusion
  772.0 7.9 copy.206
  779.9 5.3 reverse_select_fusion.10
  795.6 5.0 copy.228
  (677 shorter events, 409.9 us)
Async XLA Ops:
  7.2 58.2 %all-gather.8.cloned.1.call-start = ((), (), s32[]{:S(2)}) async-start(), calls=%async_computation.5 | async-start | bytes 1310720 | tf_op jit(solution)/shard_map/all_gather | solution.py:165
  9.5 98.8 %all-gather.6.cloned.1.call-start = ((), (), s32[]{:S(2)}) async-start(), calls=%async_computation.4 | async-start | bytes 1966080 | tf_op jit(solution)/shard_map/all_gather | solution.py:165
  12.6 226.7 %all-gather.10.cloned.1.call-start = ((), (), s32[]{:S(2)}) async-start(), calls=%async_computation.6 | async-start | bytes 3932160 | tf_op jit(solution)/shard_map/all_gather | solution.py:165
  17.0 230.2 %all-gather.12.cloned.1.call-start = ((), (), s32[]{:S(2)}) async-start(), calls=%async_computation.7 | async-start | bytes 3932160 | tf_op jit(solution)/shard_map/all_gather | solution.py:165
  18.4 247.6 %all-gather.14.cloned.1.call-start = ((), (), s32[]{:S(2)}) async-start(), calls=%async_computation.8 | async-start | bytes 3604480 | tf_op jit(solution)/shard_map/all_gather | solution.py:165
  18.5 32.6 %collective-permute-start = (bf16[128,2048]{1,0:T(8,128)(2,1)S(1)}, bf16[128,2048]{1,0:T(8,128)(2,1)}, u32[]{:S(2)}, u32[]{:S(2)}) collective-permute-start(bf16[128,2048]{1,0:T(8,128)(2,1)S(1)} %bitcast.694), channel_id=1, source_target_pairs={{0,8},{4,12},{8,0},{12,4},{16,24},{20,28},{24,16},{28,20},{1,9},{5... | collective-permute-start | bytes 1572872 | tf_op jit(solution)/shard_map/ppermute | solution.py:54
  21.5 28.1 %collective-permute-start.1 = (bf16[128,2048]{1,0:T(8,128)(2,1)S(1)}, bf16[128,2048]{1,0:T(8,128)(2,1)}, u32[]{:S(2)}, u32[]{:S(2)}) collective-permute-start(bf16[128,2048]{1,0:T(8,128)(2,1)S(1)} %bitcast.695), channel_id=1, source_target_pairs={{0,16},{4,20},{8,24},{12,28},{16,0},{20,4},{24,8},{28,12},{1,17},{... | collective-permute-start | bytes 1572872 | tf_op jit(solution)/shard_map/ppermute | solution.py:54
  23.0 21.5 %collective-permute-start.5 = (s32[1,128]{1,0:T(1,128)S(1)}, s32[1,128]{1,0:T(1,128)S(1)}, u32[]{:S(2)}, u32[]{:S(2)}) collective-permute-start(s32[1,128]{1,0:T(1,128)S(1)} %copy-done.68), channel_id=1, source_target_pairs={{0,8},{4,12},{8,0},{12,4},{16,24},{20,28},{24,16},{28,20},{1,9},{5... | collective-permute-start | bytes 1544 | tf_op jit(solution)/shard_map/ppermute | solution.py:54
  23.6 22.4 %collective-permute-start.6 = (s32[1,128]{1,0:T(1,128)S(1)}, s32[1,128]{1,0:T(1,128)S(1)}, u32[]{:S(2)}, u32[]{:S(2)}) collective-permute-start(s32[1,128]{1,0:T(1,128)S(1)} %copy-done.68), channel_id=1, source_target_pairs={{0,16},{4,20},{8,24},{12,28},{16,0},{20,4},{24,8},{28,12},{1,17},{... | collective-permute-start | bytes 1544 | tf_op jit(solution)/shard_map/ppermute | solution.py:54
  23.6 32.8 %collective-permute-start.31 = (bf16[128,2048]{1,0:T(8,128)(2,1)S(1)}, bf16[128,2048]{1,0:T(8,128)(2,1)}, u32[]{:S(2)}, u32[]{:S(2)}) collective-permute-start(bf16[128,2048]{1,0:T(8,128)(2,1)S(1)} %bitcast.731), channel_id=1, source_target_pairs={{0,8},{4,12},{8,0},{12,4},{16,24},{20,28},{24,16},{28,20},{1,9},{5... | collective-permute-start | bytes 1572872 | tf_op jit(solution)/shard_map/ppermute | solution.py:54
  27.6 470.3 %reduce-scatter.7.cloned.1.call-start = ((), (), s32[]{:S(2)}) async-start(), calls=%async_computation.10 | async-start | bytes 3604480 | tf_op jit(solution)/shard_map/reduce_scatter | solution.py:168
  63.5 33.3 %collective-permute-start.4 = (bf16[4,128,2048]{2,1,0:T(8,128)(2,1)}, bf16[4,128,2048]{2,1,0:T(8,128)(2,1)}, u32[]{:S(2)}, u32[]{:S(2)}) collective-permute-start(bf16[4,128,2048]{2,1,0:T(8,128)(2,1)} %pad_maximum_fusion.6), channel_id=1, source_target_pairs={{0,4},{4,0},{8,12},{12,8},{16,20},{20,16},{24,28},{28,24},{1,5},{5... | collective-permute-start | bytes 6291464 | tf_op jit(solution)/shard_map/ppermute | solution.py:54
  65.4 29.0 %collective-permute-start.16 = (bf16[2048,256]{1,0:T(8,128)(2,1)}, bf16[2048,256]{1,0:T(8,128)(2,1)S(1)}, u32[]{:S(2)}, u32[]{:S(2)}) collective-permute-start(bf16[2048,256]{1,0:T(8,128)(2,1)} %all-gather.8.cloned.1.call-done), channel_id=1, source_target_pairs={{0,8},{4,12},{8,0},{12,4},{16,24},{20,28},{24,16},{28,20},{1,9},{5... | collective-permute-start | bytes 3145736 | tf_op jit(solution)/shard_map/ppermute | solution.py:54
  67.7 25.5 %collective-permute-start.17 = (bf16[2048,256]{1,0:T(8,128)(2,1)}, bf16[2048,256]{1,0:T(8,128)(2,1)S(1)}, u32[]{:S(2)}, u32[]{:S(2)}) collective-permute-start(bf16[2048,256]{1,0:T(8,128)(2,1)} %all-gather.8.cloned.1.call-done), channel_id=1, source_target_pairs={{0,16},{4,20},{8,24},{12,28},{16,0},{20,4},{24,8},{28,12},{1,17},{... | collective-permute-start | bytes 3145736 | tf_op jit(solution)/shard_map/ppermute | solution.py:54
  94.1 37.2 %collective-permute-start.19 = (bf16[1024,256]{1,0:T(8,128)(2,1)}, bf16[1024,256]{1,0:T(8,128)(2,1)}, u32[]{:S(2)}, u32[]{:S(2)}) collective-permute-start(bf16[1024,256]{1,0:T(8,128)(2,1)} %slice.533), channel_id=1, source_target_pairs={{0,8},{4,12},{8,0},{12,4},{16,24},{20,28},{24,16},{28,20},{1,9},{5... | collective-permute-start | bytes 1572872 | tf_op jit(solution)/shard_map/ppermute | solution.py:54
  95.3 36.0 %collective-permute-start.18 = (bf16[1024,256]{1,0:T(8,128)(2,1)}, bf16[1024,256]{1,0:T(8,128)(2,1)}, u32[]{:S(2)}, u32[]{:S(2)}) collective-permute-start(bf16[1024,256]{1,0:T(8,128)(2,1)} %slice.532), channel_id=1, source_target_pairs={{0,16},{4,20},{8,24},{12,28},{16,0},{20,4},{24,8},{28,12},{1,17},{... | collective-permute-start | bytes 1572872 | tf_op jit(solution)/shard_map/ppermute | solution.py:54
  136.2 47.8 %collective-permute-start.20 = (bf16[4,2048,256]{2,1,0:T(8,128)(2,1)}, bf16[4,2048,256]{2,1,0:T(8,128)(2,1)}, u32[]{:S(2)}, u32[]{:S(2)}) collective-permute-start(bf16[4,2048,256]{2,1,0:T(8,128)(2,1)} %pad_maximum_fusion), channel_id=1, source_target_pairs={{0,4},{4,0},{8,12},{12,8},{16,20},{20,16},{24,28},{28,24},{1,5},{5... | collective-permute-start | bytes 12582920 | tf_op jit(solution)/shard_map/ppermute | solution.py:54
  201.8 26.2 %collective-permute-start.35 = (bf16[4,128,2048]{2,1,0:T(8,128)(2,1)}, bf16[4,128,2048]{2,1,0:T(8,128)(2,1)}, u32[]{:S(2)}, u32[]{:S(2)}) collective-permute-start(bf16[4,128,2048]{2,1,0:T(8,128)(2,1)} %pad_maximum_fusion.8), channel_id=1, source_target_pairs={{0,4},{4,0},{8,12},{12,8},{16,20},{20,16},{24,28},{28,24},{1,5},{5... | collective-permute-start | bytes 6291464 | tf_op jit(solution)/shard_map/ppermute | solution.py:54
  232.0 57.8 %collective-permute-start.53 = (bf16[128,2048]{1,0:T(8,128)(2,1)}, bf16[128,2048]{1,0:T(8,128)(2,1)}, u32[]{:S(2)}, u32[]{:S(2)}) collective-permute-start(bf16[128,2048]{1,0:T(8,128)(2,1)} %bitcast.267), channel_id=1, source_target_pairs={{0,8},{4,12},{8,0},{12,4},{16,24},{20,28},{24,16},{28,20},{1,9},{5... | collective-permute-start | bytes 1572872 | tf_op jit(solution)/shard_map/ppermute | solution.py:54
  232.6 54.7 %collective-permute-start.54 = (bf16[128,2048]{1,0:T(8,128)(2,1)}, bf16[128,2048]{1,0:T(8,128)(2,1)}, u32[]{:S(2)}, u32[]{:S(2)}) collective-permute-start(bf16[128,2048]{1,0:T(8,128)(2,1)} %bitcast.267), channel_id=1, source_target_pairs={{0,16},{4,20},{8,24},{12,28},{16,0},{20,4},{24,8},{28,12},{1,17},{... | collective-permute-start | bytes 1572872 | tf_op jit(solution)/shard_map/ppermute | solution.py:54
  284.2 218.3 %reduce-scatter.9.cloned.1.call-start = ((), (), s32[]{:S(2)}) async-start(), calls=%async_computation.11 | async-start | bytes 3604480 | tf_op jit(solution)/shard_map/reduce_scatter | solution.py:168
  302.2 28.1 %collective-permute-start.57 = (bf16[4,128,2048]{2,1,0:T(8,128)(2,1)}, bf16[4,128,2048]{2,1,0:T(8,128)(2,1)}, u32[]{:S(2)}, u32[]{:S(2)}) collective-permute-start(bf16[4,128,2048]{2,1,0:T(8,128)(2,1)} %pad_maximum_fusion.9), channel_id=1, source_target_pairs={{0,4},{4,0},{8,12},{12,8},{16,20},{20,16},{24,28},{28,24},{1,5},{5... | collective-permute-start | bytes 6291464 | tf_op jit(solution)/shard_map/ppermute | solution.py:54
  312.6 20.8 %collective-permute-start.36 = (bf16[4,128,2048]{2,1,0:T(8,128)(2,1)}, bf16[4,128,2048]{2,1,0:T(8,128)(2,1)}, u32[]{:S(2)}, u32[]{:S(2)}) collective-permute-start(bf16[4,128,2048]{2,1,0:T(8,128)(2,1)} %bitcast.77), channel_id=1, source_target_pairs={{0,4},{4,0},{8,12},{12,8},{16,20},{20,16},{24,28},{28,24},{1,5},{5... | collective-permute-start | bytes 6291464 | tf_op jit(solution)/shard_map/ppermute | solution.py:54
  327.2 177.6 %reduce-scatter.11.cloned.1.call-start = ((), (), s32[]{:S(2)}) async-start(), calls=%async_computation.12 | async-start | bytes 3604480 | tf_op jit(solution)/shard_map/reduce_scatter | solution.py:168
  353.7 19.2 %collective-permute-start.30 = (bf16[128,2048]{1,0:T(8,128)(2,1)}, bf16[128,2048]{1,0:T(8,128)(2,1)}, u32[]{:S(2)}, u32[]{:S(2)}) collective-permute-start(bf16[128,2048]{1,0:T(8,128)(2,1)} %pad_maximum_fusion.15), channel_id=1, source_target_pairs={{0,16},{4,20},{8,24},{12,28},{16,0},{20,4},{24,8},{28,12},{1,17},{... | collective-permute-start | bytes 1572872 | tf_op jit(solution)/shard_map/ppermute | solution.py:54
  354.7 19.4 %collective-permute-start.28 = (bf16[128,2048]{1,0:T(8,128)(2,1)}, bf16[128,2048]{1,0:T(8,128)(2,1)}, u32[]{:S(2)}, u32[]{:S(2)}) collective-permute-start(bf16[128,2048]{1,0:T(8,128)(2,1)} %pad_maximum_fusion.14), channel_id=1, source_target_pairs={{0,8},{4,12},{8,0},{12,4},{16,24},{20,28},{24,16},{28,20},{1,9},{5... | collective-permute-start | bytes 1572872 | tf_op jit(solution)/shard_map/ppermute | solution.py:54
  361.9 268.5 %reduce-scatter.5.cloned.1.call-start = ((), (), s32[]{:S(2)}) async-start(), calls=%async_computation.9 | async-start | bytes 3276800 | tf_op jit(solution)/shard_map/reduce_scatter | solution.py:168
  401.5 65.9 %collective-permute-start.58 = (bf16[128,256]{0,1:T(8,128)(2,1)}, bf16[128,256]{0,1:T(8,128)(2,1)}, u32[]{:S(2)}, u32[]{:S(2)}) collective-permute-start(bf16[128,256]{0,1:T(8,128)(2,1)} %get-tuple-element.433), channel_id=1, source_target_pairs={{0,8},{4,12},{8,0},{12,4},{16,24},{20,28},{24,16},{28,20},{1,9},{5... | collective-permute-start | bytes 196616 | tf_op jit(solution)/shard_map/ppermute | solution.py:54
  402.9 68.1 %collective-permute-start.59 = (bf16[128,256]{0,1:T(8,128)(2,1)}, bf16[128,256]{0,1:T(8,128)(2,1)}, u32[]{:S(2)}, u32[]{:S(2)}) collective-permute-start(bf16[128,256]{0,1:T(8,128)(2,1)} %get-tuple-element.432), channel_id=1, source_target_pairs={{0,16},{4,20},{8,24},{12,28},{16,0},{20,4},{24,8},{28,12},{1,17},{... | collective-permute-start | bytes 196616 | tf_op jit(solution)/shard_map/ppermute | solution.py:54
  404.5 67.3 %collective-permute-start.60 = (bf16[128,256]{0,1:T(8,128)(2,1)}, bf16[128,256]{0,1:T(8,128)(2,1)}, u32[]{:S(2)}, u32[]{:S(2)}) collective-permute-start(bf16[128,256]{0,1:T(8,128)(2,1)} %get-tuple-element.431), channel_id=1, source_target_pairs={{0,24},{4,28},{8,16},{12,20},{16,8},{20,12},{24,0},{28,4},{1,25},{... | collective-permute-start | bytes 196616 | tf_op jit(solution)/shard_map/ppermute | solution.py:54
  405.2 68.3 %collective-permute-start.61 = (bf16[128,256]{0,1:T(8,128)(2,1)}, bf16[128,256]{0,1:T(8,128)(2,1)}, u32[]{:S(2)}, u32[]{:S(2)}) collective-permute-start(bf16[128,256]{0,1:T(8,128)(2,1)} %get-tuple-element.430), channel_id=1, source_target_pairs={{0,4},{4,0},{8,12},{12,8},{16,20},{20,16},{24,28},{28,24},{1,5},{5... | collective-permute-start | bytes 196616 | tf_op jit(solution)/shard_map/ppermute | solution.py:54
  405.3 69.1 %collective-permute-start.62 = (bf16[128,256]{0,1:T(8,128)(2,1)}, bf16[128,256]{0,1:T(8,128)(2,1)}, u32[]{:S(2)}, u32[]{:S(2)}) collective-permute-start(bf16[128,256]{0,1:T(8,128)(2,1)} %get-tuple-element.429), channel_id=1, source_target_pairs={{0,12},{4,8},{8,4},{12,0},{16,28},{20,24},{24,20},{28,16},{1,13},{... | collective-permute-start | bytes 196616 | tf_op jit(solution)/shard_map/ppermute | solution.py:54
  500.0 94.4 %collective-permute-start.70 = (bf16[512,704]{0,1:T(8,128)(2,1)}, bf16[512,704]{0,1:T(8,128)(2,1)S(1)}, u32[]{:S(2)}, u32[]{:S(2)}) collective-permute-start(bf16[512,704]{0,1:T(8,128)(2,1)} %reduce-scatter.7.cloned.1.call-done), channel_id=1, source_target_pairs={{0,8},{4,12},{8,0},{12,4},{16,24},{20,28},{24,16},{28,20},{1,9},{5... | collective-permute-start | bytes 2162696 | tf_op jit(solution)/shard_map/ppermute | solution.py:54
  501.4 86.5 %collective-permute-start.71 = (bf16[512,704]{0,1:T(8,128)(2,1)}, bf16[512,704]{0,1:T(8,128)(2,1)}, u32[]{:S(2)}, u32[]{:S(2)}) collective-permute-start(bf16[512,704]{0,1:T(8,128)(2,1)} %reduce-scatter.7.cloned.1.call-done), channel_id=1, source_target_pairs={{0,16},{4,20},{8,24},{12,28},{16,0},{20,4},{24,8},{28,12},{1,17},{... | collective-permute-start | bytes 2162696 | tf_op jit(solution)/shard_map/ppermute | solution.py:54
  504.5 93.0 %collective-permute-start.75 = (bf16[512,704]{0,1:T(8,128)(2,1)}, bf16[512,704]{0,1:T(8,128)(2,1)S(1)}, u32[]{:S(2)}, u32[]{:S(2)}) collective-permute-start(bf16[512,704]{0,1:T(8,128)(2,1)} %reduce-scatter.9.cloned.1.call-done), channel_id=1, source_target_pairs={{0,8},{4,12},{8,0},{12,4},{16,24},{20,28},{24,16},{28,20},{1,9},{5... | collective-permute-start | bytes 2162696 | tf_op jit(solution)/shard_map/ppermute | solution.py:54
  510.7 83.8 %collective-permute-start.76 = (bf16[512,704]{0,1:T(8,128)(2,1)}, bf16[512,704]{0,1:T(8,128)(2,1)}, u32[]{:S(2)}, u32[]{:S(2)}) collective-permute-start(bf16[512,704]{0,1:T(8,128)(2,1)} %reduce-scatter.9.cloned.1.call-done), channel_id=1, source_target_pairs={{0,16},{4,20},{8,24},{12,28},{16,0},{20,4},{24,8},{28,12},{1,17},{... | collective-permute-start | bytes 2162696 | tf_op jit(solution)/shard_map/ppermute | solution.py:54
  512.5 85.8 %collective-permute-start.81 = (bf16[176,2048]{1,0:T(8,128)(2,1)}, bf16[176,2048]{1,0:T(8,128)(2,1)S(1)}, u32[]{:S(2)}, u32[]{:S(2)}) collective-permute-start(bf16[176,2048]{1,0:T(8,128)(2,1)} %reduce-scatter.11.cloned.1.call-done), channel_id=1, source_target_pairs={{0,16},{4,20},{8,24},{12,28},{16,0},{20,4},{24,8},{28,12},{1,17},{... | collective-permute-start | bytes 2162696 | tf_op jit(solution)/shard_map/ppermute | solution.py:54
  587.9 19.5 %collective-permute-start.80 = (bf16[176,2048]{1,0:T(8,128)(2,1)}, bf16[176,2048]{1,0:T(8,128)(2,1)S(1)}, u32[]{:S(2)}, u32[]{:S(2)}) collective-permute-start(bf16[176,2048]{1,0:T(8,128)(2,1)} %reduce-scatter.11.cloned.1.call-done), channel_id=1, source_target_pairs={{0,8},{4,12},{8,0},{12,4},{16,24},{20,28},{24,16},{28,20},{1,9},{5... | collective-permute-start | bytes 2162696 | tf_op jit(solution)/shard_map/ppermute | solution.py:54
  594.3 20.9 %collective-permute-start.73 = (bf16[256,704]{0,1:T(8,128)(2,1)S(1)}, bf16[256,704]{0,1:T(8,128)(2,1)S(1)}, u32[]{:S(2)}, u32[]{:S(2)}) collective-permute-start(bf16[256,704]{0,1:T(8,128)(2,1)S(1)} %slice.599), channel_id=1, source_target_pairs={{0,8},{4,12},{8,0},{12,4},{16,24},{20,28},{24,16},{28,20},{1,9},{5... | collective-permute-start | bytes 1081352 | tf_op jit(solution)/shard_map/ppermute | solution.py:54
  594.5 22.8 %collective-permute-start.72 = (bf16[256,704]{0,1:T(8,128)(2,1)S(1)}, bf16[256,704]{0,1:T(8,128)(2,1)S(1)}, u32[]{:S(2)}, u32[]{:S(2)}) collective-permute-start(bf16[256,704]{0,1:T(8,128)(2,1)S(1)} %slice.598), channel_id=1, source_target_pairs={{0,16},{4,20},{8,24},{12,28},{16,0},{20,4},{24,8},{28,12},{1,17},{... | collective-permute-start | bytes 1081352 | tf_op jit(solution)/shard_map/ppermute | solution.py:54
  597.6 25.3 %collective-permute-start.78 = (bf16[256,704]{0,1:T(8,128)(2,1)S(1)}, bf16[256,704]{0,1:T(8,128)(2,1)S(1)}, u32[]{:S(2)}, u32[]{:S(2)}) collective-permute-start(bf16[256,704]{0,1:T(8,128)(2,1)S(1)} %slice.601), channel_id=1, source_target_pairs={{0,8},{4,12},{8,0},{12,4},{16,24},{20,28},{24,16},{28,20},{1,9},{5... | collective-permute-start | bytes 1081352 | tf_op jit(solution)/shard_map/ppermute | solution.py:54
  598.3 24.6 %collective-permute-start.77 = (bf16[256,704]{0,1:T(8,128)(2,1)S(1)}, bf16[256,704]{0,1:T(8,128)(2,1)S(1)}, u32[]{:S(2)}, u32[]{:S(2)}) collective-permute-start(bf16[256,704]{0,1:T(8,128)(2,1)S(1)} %slice.600), channel_id=1, source_target_pairs={{0,16},{4,20},{8,24},{12,28},{16,0},{20,4},{24,8},{28,12},{1,17},{... | collective-permute-start | bytes 1081352 | tf_op jit(solution)/shard_map/ppermute | solution.py:54
  607.5 20.9 %collective-permute-start.83 = (bf16[88,2048]{1,0:T(8,128)(2,1)S(1)}, bf16[88,2048]{1,0:T(8,128)(2,1)S(1)}, u32[]{:S(2)}, u32[]{:S(2)}) collective-permute-start(bf16[88,2048]{1,0:T(8,128)(2,1)S(1)} %slice.603), channel_id=1, source_target_pairs={{0,8},{4,12},{8,0},{12,4},{16,24},{20,28},{24,16},{28,20},{1,9},{5... | collective-permute-start | bytes 1081352 | tf_op jit(solution)/shard_map/ppermute | solution.py:54
  620.8 41.8 %collective-permute-start.74 = (bf16[4,512,704]{1,2,0:T(8,128)(2,1)}, bf16[4,512,704]{1,2,0:T(8,128)(2,1)}, u32[]{:S(2)}, u32[]{:S(2)}) collective-permute-start(bf16[4,512,704]{1,2,0:T(8,128)(2,1)} %pad_maximum_fusion.1), channel_id=1, source_target_pairs={{0,4},{4,0},{8,12},{12,8},{16,20},{20,16},{24,28},{28,24},{1,5},{5... | collective-permute-start | bytes 8650760 | tf_op jit(solution)/shard_map/ppermute | solution.py:54
  626.1 72.1 %collective-permute-start.79 = (bf16[4,512,704]{1,2,0:T(8,128)(2,1)}, bf16[4,512,704]{1,2,0:T(8,128)(2,1)}, u32[]{:S(2)}, u32[]{:S(2)}) collective-permute-start(bf16[4,512,704]{1,2,0:T(8,128)(2,1)} %pad_maximum_fusion.2), channel_id=1, source_target_pairs={{0,4},{4,0},{8,12},{12,8},{16,20},{20,16},{24,28},{28,24},{1,5},{5... | collective-permute-start | bytes 8650760 | tf_op jit(solution)/shard_map/ppermute | solution.py:54
  630.4 80.6 %collective-permute-start.84 = (bf16[4,176,2048]{2,1,0:T(8,128)(2,1)}, bf16[4,176,2048]{2,1,0:T(8,128)(2,1)}, u32[]{:S(2)}, u32[]{:S(2)}) collective-permute-start(bf16[4,176,2048]{2,1,0:T(8,128)(2,1)} %pad_maximum_fusion.3), channel_id=1, source_target_pairs={{0,4},{4,0},{8,12},{12,8},{16,20},{20,16},{24,28},{28,24},{1,5},{5... | collective-permute-start | bytes 8650760 | tf_op jit(solution)/shard_map/ppermute | solution.py:54
  630.4 19.2 %collective-permute-start.65 = (bf16[512,640]{0,1:T(8,128)(2,1)}, bf16[512,640]{0,1:T(8,128)(2,1)S(1)}, u32[]{:S(2)}, u32[]{:S(2)}) collective-permute-start(bf16[512,640]{0,1:T(8,128)(2,1)} %reduce-scatter.5.cloned.1.call-done), channel_id=1, source_target_pairs={{0,8},{4,12},{8,0},{12,4},{16,24},{20,28},{24,16},{28,20},{1,9},{5... | collective-permute-start | bytes 1966088 | tf_op jit(solution)/shard_map/ppermute | solution.py:54
  660.2 106.5 %collective-permute-start.69 = (bf16[4,512,640]{1,2,0:T(8,128)(2,1)}, bf16[4,512,640]{1,2,0:T(8,128)(2,1)}, u32[]{:S(2)}, u32[]{:S(2)}) collective-permute-start(bf16[4,512,640]{1,2,0:T(8,128)(2,1)} %pad_maximum_fusion.5), channel_id=1, source_target_pairs={{0,4},{4,0},{8,12},{12,8},{16,20},{20,16},{24,28},{28,24},{1,5},{5... | collective-permute-start | bytes 7864328 | tf_op jit(solution)/shard_map/ppermute | solution.py:54
  (136 other events, 1143.8 us)
Sparse Core Ops, SparseCore 0:
  10.2 30.7 all-gather.7
  42.5 36.5 all-gather.5
  80.7 62.4 all-gather.9
  144.6 62.0 all-gather.11
  208.1 57.8 all-gather.13
  284.3 54.8 reduce-scatter.6
  341.5 56.0 reduce-scatter.8
  399.9 56.0 reduce-scatter.10
  487.6 50.3 reduce-scatter.4

commit v2 on v1

v2 whole, which is shorter than its diff:
```python
import math

import jax
import jax.numpy as jnp
from jax import lax
from jax.experimental import pallas as pl
from jax.experimental.pallas import tpu as pltpu
from jax.sharding import PartitionSpec as P

HEADS = 32
KV_HEADS = 4
HEAD_DIM = 64


EPS = 1e-05
ROPE_BASE = 10000.0


def rope_tables(positions, head_size):
    half_dim = head_size // 2
    lane = jnp.arange(128)
    freqs = jnp.exp(
        (lane % half_dim).astype(jnp.float32) * (-2.0 * math.log(ROPE_BASE) / head_size)
    )
    angles = positions.astype(jnp.float32)[..., None] * freqs
    sign = jnp.where(lane % head_size < half_dim, -1.0, 1.0)
    return jnp.cos(angles), jnp.sin(angles) * sign


def norm_back(grad_normed, normed, inverse):
    return inverse * (grad_normed - normed * jnp.mean(grad_normed * normed, axis=-1, keepdims=True))


def dot(left, right, dims):
    return lax.dot_general(left, right, ((dims[0], dims[1]), ((), ())), preferred_element_type=jnp.float32)


def swap(value, mask):
    return lax.ppermute(value, "seq", [(i, i ^ mask) for i in range(lax.axis_size("seq"))])


def place_pieces(pieces, places, shape):
    cols = shape[2]
    tile = 512 if cols % 512 == 0 else cols

    def kernel(*refs):
        for piece, (slot, row), ref in zip(pieces, places, refs):
            refs[-1][slot, row : row + piece.shape[0]] = ref[...]

    return pl.pallas_call(
        kernel,
        grid=(cols // tile,),
        out_shape=jax.ShapeDtypeStruct(shape, pieces[0].dtype),
        in_specs=[pl.BlockSpec((piece.shape[0], tile), lambda i: (0, i)) for piece in pieces],
        out_specs=pl.BlockSpec(shape[:2] + (tile,), lambda i: (0, 0, i)),
        compiler_params=pltpu.CompilerParams(vmem_limit_bytes=48 * 2**20),
        cost_estimate=pl.CostEstimate(flops=0, bytes_accessed=math.prod(shape) * 4, transcendentals=0),
    )(*pieces)


def even_pieces(part, *meanwhile):
    half = part.shape[0] // 32 * 16
    by_x, by_y = lax.optimization_barrier((swap(part, 2), swap(part, 4), meanwhile))[:2]
    far = lax.optimization_barrier((swap(by_x[:half], 4), swap(by_y[half:], 2)))
    return (part, by_x, by_y, *far), ((0, 0), (1, 0), (2, 0), (3, 0), (3, half))


def doubled(part):
    mine, mask = part[None], 2
    while mask < lax.axis_size("seq"):
        mine = jnp.concatenate([mine, swap(mine, mask)])
        mask *= 2
    return mine


def seq_halves(part, *meanwhile):
    if lax.axis_size("seq") == 8 and part.shape[0] % 16 == 0:
        pieces, places = even_pieces(part, *meanwhile)
        mine = place_pieces(pieces, places, (4,) + part.shape)
    else:
        mine = doubled(part)
    return mine, swap(mine, 1)


def after(value, *earlier):
    return lax.optimization_barrier((value, *earlier))[0]


def seq_gather(part, *meanwhile):
    mine, other = seq_halves(part, *meanwhile)
    if part.shape[0] % 16:
        return jnp.concatenate([mine, other])
    half, rows, cols = mine.shape
    tile = 512 if cols % 512 == 0 else cols

    def kernel(mine_ref, other_ref, out_ref):
        out_ref[:half] = mine_ref[...]
        out_ref[half:] = other_ref[...]

    return pl.pallas_call(
        kernel,
        grid=(cols // tile,),
        out_shape=jax.ShapeDtypeStruct((2 * half, rows, cols), part.dtype),
        in_specs=[pl.BlockSpec((half, rows, tile), lambda i: (0, 0, i))] * 2,
        out_specs=pl.BlockSpec((2 * half, rows, tile), lambda i: (0, 0, i)),
        cost_estimate=pl.CostEstimate(flops=0, bytes_accessed=mine.size * 8, transcendentals=0),
    )(mine, other)


def ring_sum(value):
    n = lax.axis_size("fsdp")
    moving = value
    for _ in range(n - 1):
        moving = lax.ppermute(moving, "fsdp", [(i, (i + 1) % n) for i in range(n)])
        value = value + moving
    return value


def ordered(place, even, odd, body):
    core = place & 1
    pl.when(core == 0)(lambda: body(even, odd))
    pl.when(core == 1)(lambda: body(odd, even))


def put_columns(even, odd, place, pieces, w_gate, w_up):
    half, rows, cols = even.shape
    n, w = 2 * half, cols // (2 * pieces)
    tile = 64

    def kernel(place_ref, even_ref, odd_ref, w_gate_ref, w_up_ref, gate_ref, up_ref, sums_ref):
        chip = place_ref[0] // 2

        def body(first, second):
            blocks = [(second if t % 2 else first)[(t // 2) ^ chip] for t in range(n)]
            sums = jnp.zeros((tile, 1), jnp.float32)
            for target, weight, start in ((gate_ref, w_gate_ref, 0), (up_ref, w_up_ref, cols // 2)):
                for f in range(pieces):
                    at, to = start + f * w, slice(f * n * w, (f + 1) * n * w)
                    row = jnp.concatenate([block[:, at : at + w] for block in blocks], axis=1)
                    row = row.astype(jnp.float32)
                    target[:, to] = row
                    sums += jnp.sum(row * weight[:, to].astype(jnp.float32), axis=1, keepdims=True)
            sums_ref[...] = sums

        ordered(place_ref[0], even_ref, odd_ref, body)

    spec = pl.BlockSpec((half, tile, cols), lambda i: (0, i, 0))
    wide = jax.ShapeDtypeStruct((rows, pieces * n * w), jnp.float32)
    return pl.pallas_call(
        kernel,
        grid=(rows // tile,),
        out_shape=(wide, wide, jax.ShapeDtypeStruct((rows, 1), jnp.float32)),
        in_specs=[pl.BlockSpec(memory_space=pltpu.SMEM), spec, spec]
        + [pl.BlockSpec((tile, pieces * n * w), lambda i: (i, 0))] * 2,
        out_specs=[pl.BlockSpec((tile, pieces * n * w), lambda i: (i, 0))] * 2
        + [pl.BlockSpec((tile, 1), lambda i: (i, 0))],
        compiler_params=pltpu.CompilerParams(vmem_limit_bytes=48 * 2**20),
        cost_estimate=pl.CostEstimate(flops=0, bytes_accessed=even.size * 12, transcendentals=0),
    )(place, even, odd, w_gate, w_up)


def put_rows(even, odd, place):
    half, rows, cols = even.shape
    tile = 256

    def kernel(place_ref, even_ref, odd_ref, out_ref):
        chip = place_ref[0] // 2

        def body(first, second):
            for t in range(2 * half):
                block = (second if t % 2 else first)[(t // 2) ^ chip]
                out_ref[t * rows : (t + 1) * rows, :] = block.astype(jnp.float32)

        ordered(place_ref[0], even_ref, odd_ref, body)

    spec = pl.BlockSpec((half, rows, tile), lambda i: (0, 0, i))
    return pl.pallas_call(
        kernel,
        grid=(cols // tile,),
        out_shape=jax.ShapeDtypeStruct((2 * half * rows, cols), jnp.float32),
        in_specs=[pl.BlockSpec(memory_space=pltpu.SMEM), spec, spec],
        out_specs=pl.BlockSpec((2 * half * rows, tile), lambda i: (0, i)),
        compiler_params=pltpu.CompilerParams(vmem_limit_bytes=48 * 2**20),
        cost_estimate=pl.CostEstimate(flops=0, bytes_accessed=even.size * 12, transcendentals=0),
    )(place, even, odd)


def put_attention(even, odd, place, weights, q_cols, out_cols):
    half, rows, cols = even.shape
    n, tile = 2 * half, 128
    copies = n // KV_HEADS
    sizes = (n * q_cols, KV_HEADS * HEAD_DIM, KV_HEADS * HEAD_DIM, n * out_cols)

    def kernel(place_ref, even_ref, odd_ref, wq_ref, wk_ref, wv_ref, *refs):
        query_ref, key_ref, value_ref, out_ref, sums_ref = refs
        chip = place_ref[0] // 2

        def body(first, second):
            blocks = [
                (second if t % 2 else first)[(t // 2) ^ chip].astype(jnp.float32) for t in range(n)
            ]
            for t, block in enumerate(blocks):
                query_ref[:, t * q_cols : (t + 1) * q_cols] = block[:, :q_cols]
                out_ref[:, t * out_cols : (t + 1) * out_cols] = block[:, cols - out_cols :]
            sums = [
                sum(block[:, q_cols : q_cols + 2 * HEAD_DIM] for block in blocks[h * copies : (h + 1) * copies])
                for h in range(KV_HEADS)
            ]
            key_ref[...] = jnp.concatenate([part[:, :HEAD_DIM] for part in sums], axis=1)
            value_ref[...] = jnp.concatenate([part[:, HEAD_DIM:] for part in sums], axis=1)
            sums_ref[...] = sum(
                jnp.sum(ref[...] * weight[...].astype(jnp.float32), axis=1, keepdims=True)
                for ref, weight in ((query_ref, wq_ref), (key_ref, wk_ref), (value_ref, wv_ref))
            )

        ordered(place_ref[0], even_ref, odd_ref, body)

    spec = pl.BlockSpec((half, tile, cols), lambda i: (0, i, 0))
    return pl.pallas_call(
        kernel,
        grid=(rows // tile,),
        out_shape=[jax.ShapeDtypeStruct((rows, size), jnp.float32) for size in (*sizes, 1)],
        in_specs=[pl.BlockSpec(memory_space=pltpu.SMEM), spec, spec]
        + [pl.BlockSpec((tile, size), lambda i: (i, 0)) for size in sizes[:3]],
        out_specs=[pl.BlockSpec((tile, size), lambda i: (i, 0)) for size in (*sizes, 1)],
        compiler_params=pltpu.CompilerParams(vmem_limit_bytes=48 * 2**20),
        cost_estimate=pl.CostEstimate(flops=0, bytes_accessed=even.size * 12, transcendentals=0),
    )(place, even, odd, *weights)


def seq_scatter(even, odd):
    n = lax.axis_size("seq")

    def add(own, other):
        return own.astype(jnp.float32) + other.astype(jnp.float32)

    low = jnp.bfloat16
    mine = add(even, swap(odd, 1))
    if n == 8:
        half = even.shape[1] // 2
        far = mine[3].astype(low)
        from_x, from_y = swap(far[:half], 2), swap(far[half:], 4)
        to_y = jnp.concatenate([add(mine[2][:half], from_x), mine[2][half:]]).astype(low)
        to_x = jnp.concatenate([mine[1][:half], add(mine[1][half:], from_y)]).astype(low)
        return mine[0] + swap(to_x, 2).astype(jnp.float32) + swap(to_y, 4).astype(jnp.float32)
    mask = n // 2
    while mask > 1:
        count = mine.shape[0] // 2
        mine = add(mine[:count], swap(mine[count:].astype(low), mask))
        mask //= 2
    return mine[0]


def slot_of(mask, n):
    return (mask >> 1) + (mask & 1) * (n // 2)


def split_columns(parts, place, n):
    rows = parts[0].shape[0]
    sizes = [part.shape[1] // n for part in parts]
    half, cols = n // 2, sum(sizes)

    def kernel(place_ref, *refs):
        for core, ref in enumerate(refs[-2:]):
            for k in range(half):
                block, at = place_ref[0] ^ (2 * k + core), 0
                for size, part_ref in zip(sizes, refs):
                    start = pl.multiple_of(block * size, size)
                    ref[k, :, at : at + size] = part_ref[:, pl.ds(start, size)]
                    at += size

    vmem = pl.BlockSpec(memory_space=pltpu.VMEM)
    return pl.pallas_call(
        kernel,
        out_shape=[jax.ShapeDtypeStruct((half, rows, cols), parts[0].dtype)] * 2,
        in_specs=[pl.BlockSpec(memory_space=pltpu.SMEM)] + [vmem] * len(parts),
        out_specs=[vmem] * 2,
    )(place, *parts)


def seq_exchange(even, odd):
    half, rows, cols = even.shape
    other = swap(odd, 1)

    def kernel(even_ref, other_ref, *refs):
        for k, ref in enumerate(refs):
            ref[0] = even_ref[k]
            ref[1] = other_ref[k]

    vmem = pl.BlockSpec(memory_space=pltpu.VMEM)
    pairs = pl.pallas_call(
        kernel,
        out_shape=[jax.ShapeDtypeStruct((2, rows, cols), even.dtype)] * half,
        in_specs=[vmem] * 2,
        out_specs=[vmem] * half,
    )(even, other)
    return [pair if k == 0 else swap(pair, 2 * k) for k, pair in enumerate(pairs)]


def join_columns(pairs, place):
    n, (_, rows, cols) = 2 * len(pairs), pairs[0].shape

    def kernel(place_ref, *refs):
        for k, ref in enumerate(refs[:-1]):
            for core in range(2):
                start = pl.multiple_of((place_ref[0] ^ (2 * k + core)) * cols, cols)
                refs[-1][:, pl.ds(start, cols)] = ref[core]

    vmem = pl.BlockSpec(memory_space=pltpu.VMEM)
    return pl.pallas_call(
        kernel,
        out_shape=jax.ShapeDtypeStruct((rows, n * cols), pairs[0].dtype),
        in_specs=[pl.BlockSpec(memory_space=pltpu.SMEM)] + [vmem] * len(pairs),
        out_specs=vmem,
    )(place, *pairs)


def join_weight(even, odd, place):
    half, rows, cols = even.shape
    n, tile = 2 * half, 512

    def kernel(place_ref, even_ref, odd_ref, out_ref):
        for ref, core in ((even_ref, 0), (odd_ref, 1)):
            for k in range(half):
                start = pl.multiple_of((place_ref[0] ^ (2 * k + core)) * cols, cols)
                out_ref[:, pl.ds(start, cols)] = ref[k]

    spec = pl.BlockSpec((half, tile, cols), lambda i: (0, i, 0))
    return pl.pallas_call(
        kernel,
        grid=(rows // tile,),
        out_shape=jax.ShapeDtypeStruct((rows, n * cols), even.dtype),
        in_specs=[pl.BlockSpec(memory_space=pltpu.SMEM), spec, spec],
        out_specs=pl.BlockSpec((tile, n * cols), lambda i: (i, 0)),
        compiler_params=pltpu.CompilerParams(vmem_limit_bytes=48 * 2**20),
        cost_estimate=pl.CostEstimate(flops=0, bytes_accessed=even.size * 8, transcendentals=0),
    )(place, even, odd)


def lanes(shape):
    return lax.broadcasted_iota(jnp.int32, shape, 1)


def halves_swapped(value):
    first = lanes(value.shape) % HEAD_DIM < HEAD_DIM // 2
    size = value.shape[1]
    left, right = pltpu.roll(value, size - HEAD_DIM // 2, 1), pltpu.roll(value, HEAD_DIM // 2, 1)
    return jnp.where(first, left, right)


def turned(value, cosine, sine):
    parts = [
        value[:, i : i + 128] * cosine + halves_swapped(value[:, i : i + 128]) * sine
        for i in range(0, value.shape[1], 128)
    ]
    return jnp.concatenate(parts, axis=1)


def key_copies(key_value):
    first = lanes(key_value.shape) < HEAD_DIM
    turned_over = pltpu.roll(key_value, HEAD_DIM, 1)
    keys = jnp.where(first, key_value, turned_over)
    values = jnp.where(first, turned_over, key_value)
    return keys, values, first


def only(value, head):
    first = lanes(value.shape) < HEAD_DIM
    return jnp.where(first if head == 0 else ~first, value, jnp.zeros_like(value))


def matmul(left, right, dims):
    return lax.dot_general(left, right, (dims, ((), ())), preferred_element_type=jnp.float32)


ROWS_OF = ((1,), (1,))
PLAIN = ((1,), (0,))
COLUMNS_OF = ((0,), (0,))
MASKED = -1e30


def attention(qkv, cosine, sine, place, heads_dev):
    n, rows, cols = qkv.shape
    length, q_cols = n * rows, heads_dev * HEAD_DIM
    block = 256
    low, wide = jnp.bfloat16, jnp.float32

    def kernel(place_ref, qkv_ref, cos_ref, sin_ref, *refs):
        even_ref, odd_ref, out_ref, rot_ref, top_ref, sum_ref = refs
        for t in range(n):
            slot = slot_of(place_ref[0] ^ t, n)
            value = qkv_ref[slot]
            moved = turned(value[:, : q_cols + 128], cos_ref[slot], sin_ref[slot])
            key_value = jnp.where(
                lanes((rows, 128)) < HEAD_DIM, moved[:, q_cols:], value[:, q_cols:]
            )
            at = slice(t * rows, (t + 1) * rows)
            rot_ref[at, :q_cols] = moved[:, :q_cols].astype(low)
            rot_ref[at, q_cols:] = key_value.astype(low)
        for i in range(length // block):
            span = (i + 1) * block
            key_value = rot_ref[:span, q_cols:]
            keys, values, _ = key_copies(key_value)
            held = [only(values, 0), only(values, 1)]
            shape = (block, span)
            seen = lax.broadcasted_iota(jnp.int32, shape, 1) <= i * block + (
                lax.broadcasted_iota(jnp.int32, shape, 0)
            )
            at = slice(i * block, (i + 1) * block)
            for pair in range(q_cols // 128):
                query = rot_ref[at, pair * 128 : (pair + 1) * 128] * jnp.asarray(0.125, low)
                total = None
                for head in range(2):
                    scores = matmul(only(query, head), keys, ROWS_OF)
                    scores = jnp.where(seen, scores, MASKED)
                    top = jnp.max(scores, axis=1, keepdims=True)
                    unnormed = jnp.exp(scores - top)
                    row_sum = jnp.sum(unnormed, axis=1, keepdims=True)
                    part = matmul(unnormed.astype(low), held[head], PLAIN) / row_sum
                    top_ref[2 * pair + head, at, :] = top
                    sum_ref[2 * pair + head, at, :] = row_sum
                    total = part if total is None else total + part
                out_ref[at, pair * 128 : (pair + 1) * 128] = total
        for core, ref in ((0, even_ref), (1, odd_ref)):
            for k in range(n // 2):
                start = pl.multiple_of((place_ref[0] ^ (2 * k + core)) * rows, rows)
                ref[k] = out_ref[pl.ds(start, rows), :].astype(low)

    vmem = pl.BlockSpec(memory_space=pltpu.VMEM)
    results = pl.pallas_call(
        kernel,
        out_shape=[jax.ShapeDtypeStruct((n // 2, rows, q_cols), low)] * 2
        + [
            jax.ShapeDtypeStruct((length, q_cols), wide),
            jax.ShapeDtypeStruct((length, q_cols + 2 * HEAD_DIM), low),
            jax.ShapeDtypeStruct((heads_dev, length, 1), wide),
            jax.ShapeDtypeStruct((heads_dev, length, 1), wide),
        ],
        in_specs=[pl.BlockSpec(memory_space=pltpu.SMEM)] + [vmem] * 3,
        out_specs=[vmem] * 6,
        compiler_params=pltpu.CompilerParams(vmem_limit_bytes=48 * 2**20),
        cost_estimate=pl.CostEstimate(
            flops=2 * length * length * 128 * heads_dev,
            bytes_accessed=qkv.size * 8,
            transcendentals=length * length * heads_dev // 2,
        ),
    )(place, qkv, cosine, sine)
    return results[:2], *results[2:]


def attention_back(grads, rotated, out, tops, sums, cosine, sine, place):
    n, (_, rows, all_cols) = 2 * len(grads), grads[0].shape
    length, cols = rotated.shape
    q_cols = cols - 2 * HEAD_DIM
    heads_dev = q_cols // HEAD_DIM
    block = 256
    low, wide = jnp.bfloat16, jnp.float32

    def kernel(place_ref, rot_ref, out_ref, top_ref, sum_ref, cos_ref, sin_ref, *refs):
        grad_refs = refs[: n // 2]
        result_ref, others_ref, grad_ref, dq_ref, dk_ref, dv_ref = refs[n // 2 :]
        for k, ref in enumerate(grad_refs):
            for core in range(2):
                start = pl.multiple_of((place_ref[0] ^ (2 * k + core)) * rows, rows)
                grad_ref[pl.ds(start, rows), :] = ref[core, :, :q_cols]
                others_ref[core * (n // 2) + k] = ref[core, :, q_cols:]
        dk_ref[...] = jnp.zeros_like(dk_ref)
        dv_ref[...] = jnp.zeros_like(dv_ref)
        for i in range(length // block):
            span = (i + 1) * block
            keys, values, _ = key_copies(rot_ref[:span, q_cols:])
            held = [only(keys, 0), only(keys, 1)]
            shape = (block, span)
            seen = lax.broadcasted_iota(jnp.int32, shape, 1) <= i * block + (
                lax.broadcasted_iota(jnp.int32, shape, 0)
            )
            at = slice(i * block, (i + 1) * block)
            dk = dv = None
            for pair in range(q_cols // 128):
                pair_at = slice(pair * 128, (pair + 1) * 128)
                query = rot_ref[at, pair_at] * jnp.asarray(0.125, low)
                grad = grad_ref[at, pair_at].astype(wide)
                product = grad * out_ref[at, pair_at]
                dq = None
                for head in range(2):
                    row_sum = sum_ref[2 * pair + head, at, :]
                    own_query = only(query, head)
                    own_grad = only((grad / row_sum).astype(low), head)
                    scores = jnp.where(seen, matmul(own_query, keys, ROWS_OF), MASKED)
                    unnormed = jnp.exp(scores - top_ref[2 * pair + head, at, :])
                    shift = jnp.sum(only(product, head), axis=1, keepdims=True) / row_sum
                    grad_probs = matmul(own_grad, values, ROWS_OF)
                    grad_scores = (unnormed * (grad_probs - shift)).astype(low)
                    dq_part = matmul(grad_scores, held[head], PLAIN)
                    dk_part = matmul(grad_scores, own_query, COLUMNS_OF)
                    dv_part = matmul(unnormed.astype(low), own_grad, COLUMNS_OF)
                    dq = dq_part if dq is None else dq + dq_part
                    dk = dk_part if dk is None else dk + dk_part
                    dv = dv_part if dv is None else dv + dv_part
                dq_ref[at, pair_at] = dq * 0.125
            dk_ref[:span, :] += dk
            dv_ref[:span, :] += dv
        for t in range(n):
            slot = slot_of(place_ref[0] ^ t, n)
            at = slice(t * rows, (t + 1) * rows)
            dk, dv = dk_ref[at, :], dv_ref[at, :]
            first = lanes(dk.shape) < HEAD_DIM
            dk, dv = dk + pltpu.roll(dk, HEAD_DIM, 1), dv + pltpu.roll(dv, HEAD_DIM, 1)
            moved = turned(
                jnp.concatenate([dq_ref[at, :], dk], axis=1), cos_ref[slot], -sin_ref[slot]
            )
            result_ref[slot, :, :q_cols] = moved[:, :q_cols].astype(low)
            result_ref[slot, :, q_cols:] = jnp.where(first, moved[:, q_cols:], dv).astype(low)

    vmem = pl.BlockSpec(memory_space=pltpu.VMEM)
    return pl.pallas_call(
        kernel,
        out_shape=[
            jax.ShapeDtypeStruct((n, rows, cols), low),
            jax.ShapeDtypeStruct((n, rows, all_cols - q_cols), low),
        ],
        in_specs=[pl.BlockSpec(memory_space=pltpu.SMEM)] + [vmem] * (6 + n // 2),
        out_specs=[vmem] * 2,
        scratch_shapes=[
            pltpu.VMEM((length, q_cols), low),
            pltpu.VMEM((length, q_cols), wide),
            pltpu.VMEM((length, 128), wide),
            pltpu.VMEM((length, 128), wide),
        ],
        compiler_params=pltpu.CompilerParams(vmem_limit_bytes=48 * 2**20),
        cost_estimate=pl.CostEstimate(
            flops=5 * length * length * 128 * heads_dev,
            bytes_accessed=rotated.size * 8,
            transcendentals=length * length * heads_dev // 2,
        ),
    )(place, rotated, out, tops, sums, cosine, sine, *grads)


def silu_parts(gate):
    sigmoid_gate = 1.0 / (1.0 + jnp.exp(-gate))
    return sigmoid_gate, gate * sigmoid_gate


def hidden_units(normed, weights):
    rows, width = normed.shape
    cols = weights.shape[1]
    tile, ff_dev = 256, cols // 2

    def kernel(normed_ref, weights_ref, pre_ref, hidden_ref):
        pre = matmul(normed_ref[...], weights_ref[...], PLAIN)
        pre_ref[...] = pre
        hidden_ref[...] = (silu_parts(pre[:, :ff_dev])[1] * pre[:, ff_dev:]).astype(jnp.bfloat16)

    return pl.pallas_call(
        kernel,
        grid=(rows // tile,),
        out_shape=[
            jax.ShapeDtypeStruct((rows, cols), jnp.float32),
            jax.ShapeDtypeStruct((rows, ff_dev), jnp.bfloat16),
        ],
        in_specs=[
            pl.BlockSpec((tile, width), lambda i: (i, 0)),
            pl.BlockSpec((width, cols), lambda i: (0, 0)),
        ],
        out_specs=[
            pl.BlockSpec((tile, cols), lambda i: (i, 0)),
            pl.BlockSpec((tile, ff_dev), lambda i: (i, 0)),
        ],
        compiler_params=pltpu.CompilerParams(vmem_limit_bytes=48 * 2**20),
        cost_estimate=pl.CostEstimate(
            flops=2 * rows * width * cols, bytes_accessed=rows * cols * 8, transcendentals=rows * ff_dev
        ),
    )(normed, weights)


def hidden_back(dy, down, pre):
    rows, width = dy.shape
    ff_dev = down.shape[0]
    tile = 256

    def kernel(dy_ref, down_ref, pre_ref, out_ref):
        grad_hidden = matmul(dy_ref[...], down_ref[...], ROWS_OF)
        gate, upper = pre_ref[:, :ff_dev], pre_ref[:, ff_dev:]
        sigmoid_gate, activated = silu_parts(gate)
        grad_gate = grad_hidden * upper * (sigmoid_gate * (1.0 + gate * (1.0 - sigmoid_gate)))
        both = jnp.concatenate([grad_gate, grad_hidden * activated], axis=1)
        out_ref[...] = both.astype(jnp.bfloat16)

    return pl.pallas_call(
        kernel,
        grid=(rows // tile,),
        out_shape=jax.ShapeDtypeStruct((rows, 2 * ff_dev), jnp.bfloat16),
        in_specs=[
            pl.BlockSpec((tile, width), lambda i: (i, 0)),
            pl.BlockSpec((ff_dev, width), lambda i: (0, 0)),
            pl.BlockSpec((tile, 2 * ff_dev), lambda i: (i, 0)),
        ],
        out_specs=pl.BlockSpec((tile, 2 * ff_dev), lambda i: (i, 0)),
        compiler_params=pltpu.CompilerParams(vmem_limit_bytes=48 * 2**20),
        cost_estimate=pl.CostEstimate(
            flops=2 * rows * width * ff_dev, bytes_accessed=rows * ff_dev * 16, transcendentals=rows * ff_dev
        ),
    )(dy, down, pre)


def attention_terms(normed, grad_qkv, attended, grad_proj):
    rows, width = normed.shape
    sizes = grad_qkv.shape[1], grad_proj.shape[1]
    tile = 512

    def kernel(normed_ref, grad_qkv_ref, attended_ref, grad_proj_ref, out_ref):
        low = jnp.bfloat16
        out_ref[:, : sizes[0]] = matmul(normed_ref[...], grad_qkv_ref[...], COLUMNS_OF).astype(low)
        out_ref[:, sizes[0] :] = matmul(attended_ref[...], grad_proj_ref[...], COLUMNS_OF).astype(low)

    return pl.pallas_call(
        kernel,
        grid=(width // tile,),
        out_shape=jax.ShapeDtypeStruct((width, sum(sizes)), jnp.bfloat16),
        in_specs=[
            pl.BlockSpec((rows, tile), lambda i: (0, i)),
            pl.BlockSpec((rows, sizes[0]), lambda i: (0, 0)),
            pl.BlockSpec((rows, tile), lambda i: (0, i)),
            pl.BlockSpec((rows, sizes[1]), lambda i: (0, 0)),
        ],
        out_specs=pl.BlockSpec((tile, sum(sizes)), lambda i: (i, 0)),
        compiler_params=pltpu.CompilerParams(vmem_limit_bytes=48 * 2**20),
        cost_estimate=pl.CostEstimate(
            flops=2 * rows * width * sum(sizes), bytes_accessed=rows * width * 4, transcendentals=0
        ),
    )(normed, grad_qkv, attended, grad_proj)


def stage(sure, body, *args):
    shapes = jax.eval_shape(body, *args)

    def nothing(*_):
        return jax.tree.map(lambda leaf: jnp.zeros(leaf.shape, leaf.dtype), shapes)

    return lax.cond(sure, body, nothing, *args)


def columns_of(weight, place, groups, shards):
    width = weight.shape[1] // (groups * shards)
    return jnp.concatenate(
        [
            lax.dynamic_slice_in_dim(weight, (f * groups + place) * width, width, 1)
            for f in range(shards)
        ],
        axis=1,
    )


def on_device(
    tokens,
    positions,
    w_query,
    w_key,
    w_value,
    w_out,
    gain_attn,
    w_gate,
    w_up,
    w_down,
    gain_mlp,
    cotangent,
):
    low, wide = jnp.bfloat16, jnp.float32
    groups = lax.axis_size("seq")
    shards = lax.axis_size("fsdp")
    place = lax.axis_index("seq")
    shard = lax.axis_index("fsdp")
    tok_rows, width = tokens.shape[1:]
    shard_rows = w_query.shape[0]
    heads_dev = HEADS // groups
    kv_copies = groups // KV_HEADS
    seq_len = tok_rows * groups
    q_cols = heads_dev * HEAD_DIM
    out_cols = width // groups
    ff = w_gate.shape[1]
    ff_dev = ff // groups
    scale = HEAD_DIM ** (-0.5)

    def z_gather(part):
        return lax.all_gather(part, "fsdp", axis=0, tiled=True)

    def z_scatter(part):
        return lax.psum_scatter(part, "fsdp", scatter_dimension=0, tiled=True)

    def columns(weight, start, count):
        return lax.dynamic_slice_in_dim(weight, start, count, 1)

    place_arg = place.reshape(1).astype(jnp.int32)
    kv_head = place // kv_copies
    attn_full = z_gather(
        jnp.concatenate(
            [
                columns(w_query, place * q_cols, q_cols),
                columns(w_key, kv_head * HEAD_DIM, HEAD_DIM),
                columns(w_value, kv_head * HEAD_DIM, HEAD_DIM),
                columns(w_out, place * out_cols, out_cols),
            ],
            axis=1,
        )
    )
    attn_full, out_part = attn_full[:, :-out_cols], attn_full[:, -out_cols:]
    mlp_full = z_gather(
        jnp.concatenate(
            [columns_of(w_gate, place, groups, shards), columns_of(w_up, place, groups, shards)],
            axis=1,
        )
    )
    down_rows = w_down.shape[0] // groups
    down_full = z_gather(lax.dynamic_slice_in_dim(w_down, place * down_rows, down_rows, 0))
    sure = positions[0, 0] >= 0
    own = tokens[0]
    gains_own = jnp.stack([gain_attn, gain_mlp]).astype(wide)

    def inputs_stage(own, positions, gains_own):
        gains = lax.dynamic_update_slice(
            jnp.zeros((2, width), wide), gains_own, (0, shard * shard_rows)
        )
        gains = ring_sum(gains)
        where = seq_gather(positions).reshape(seq_len)
        stream = seq_gather(own, gains, where).reshape(seq_len, width).astype(wide)
        cosine, sine = rope_tables(where, HEAD_DIM)
        cosine, sine = cosine.reshape(groups, tok_rows, 128), sine.reshape(groups, tok_rows, 128)
        inverse_all = lax.rsqrt(jnp.mean(stream * stream, axis=-1, keepdims=True) + EPS)
        normed_in = (stream * inverse_all * gains[0]).astype(low)
        return gains, cosine, sine, normed_in

    gains, cosine, sine, normed_in = stage(sure, inputs_stage, own, positions, gains_own)
    gain_in, gain_mid = gains

    def attention_stage(own, cotangent, normed_in, attn_full, out_part, cosine, sine, gain_mid):
        qkv = jnp.dot(normed_in, attn_full, preferred_element_type=wide)
        attended_send, *kept = attention(
            qkv.reshape(groups, tok_rows, -1), cosine, sine, place_arg, heads_dev
        )
        attended_tok = join_columns(seq_exchange(*attended_send), place_arg)
        out_even, out_odd = seq_halves(out_part, attended_send[0])
        out_full = join_weight(out_even, out_odd, place_arg)
        dy = seq_gather(after(cotangent, out_even)).reshape(seq_len, width)
        middle = own.astype(wide) + jnp.dot(attended_tok, out_full, preferred_element_type=wide)
        inverse_mid = lax.rsqrt(jnp.mean(middle * middle, axis=-1, keepdims=True) + EPS)
        unit_mid = middle * inverse_mid
        normed_mid = seq_gather((unit_mid * gain_mid).astype(low)).reshape(seq_len, width)
        return attended_tok, out_full, middle, normed_mid, dy, kept

    attended_tok, out_full, middle, normed_mid, dy, kept = stage(
        sure, attention_stage, own, cotangent[0], normed_in, attn_full, out_part, cosine, sine, gain_mid
    )

    def hidden_stage(normed_mid, mlp_full, dy, attended_tok):
        mlp_pre, hidden = hidden_units(normed_mid, mlp_full)
        attended_all = seq_gather(attended_tok, hidden).reshape(seq_len, -1)
        return attended_all, mlp_pre, hidden, dot(hidden, dy, ((0,), (0,))).astype(low)

    attended_all, mlp_pre, hidden, down_grad = stage(
        sure, hidden_stage, normed_mid, mlp_full, dy, attended_tok
    )
    down_sum = z_scatter(down_grad)
    grad_mlp = hidden_back(after(dy, down_grad), down_full, mlp_pre)
    halves = (slice(0, seq_len // 2), slice(seq_len // 2, None))

    def by_halves(product):
        return [product(at).astype(low).reshape(groups // 2, tok_rows, width) for at in halves]

    mlp_grad = dot(normed_mid, grad_mlp, ((0,), (0,))).astype(low)
    mlp_sum = z_scatter(mlp_grad)

    def middle_stage(
        grad_mlp, mlp_full, hidden, down_full, middle, dy_own, gain_mid, out_full, mlp_grad
    ):
        inverse_mid = lax.rsqrt(jnp.mean(middle * middle, axis=-1, keepdims=True) + EPS)
        unit_mid = middle * inverse_mid
        terms = by_halves(lambda at: dot(grad_mlp[at], mlp_full, ((1,), (1,))))
        grad_normed_mid = seq_scatter(*terms)
        grad_middle = norm_back(grad_normed_mid * gain_mid, unit_mid, inverse_mid)
        grad_middle = grad_middle + dy_own.astype(wide)
        grad_proj = grad_middle.astype(low)
        grad_attended = dot(grad_proj, out_full, ((1,), (1,))).astype(low)
        grad_even, grad_odd = split_columns((grad_attended, grad_proj), place_arg, groups)
        later = after(hidden, tuple(terms))
        down_terms = by_halves(
            lambda at: jnp.dot(later[at], down_full, preferred_element_type=wide)
        )
        layer_out = (middle + seq_scatter(*down_terms)).astype(low)
        return grad_middle, layer_out, grad_even, grad_odd

    grad_middle, layer_out, grad_even, grad_odd = stage(
        sure, middle_stage, grad_mlp, mlp_full, hidden, down_full, middle, cotangent[0], gain_mid, out_full,
        mlp_grad[:16],
    )

    def back_stage(
        grad_even, grad_odd, attended_all, normed_in, attn_full, cosine, sine, kept, down_sum
    ):
        wide_out, rotated, tops, sums = kept
        grad_pairs = seq_exchange(grad_even, grad_odd)
        grad_qkv, grad_proj_cols = attention_back(
            grad_pairs, rotated, wide_out, tops, sums, cosine, sine, place_arg
        )
        grad_qkv = grad_qkv.reshape(seq_len, -1)
        grad_proj_cols = grad_proj_cols.reshape(seq_len, out_cols)
        attn_terms = attention_terms(normed_in, grad_qkv, attended_all, grad_proj_cols)
        terms_in = by_halves(lambda at: dot(grad_qkv[at], attn_full, ((1,), (1,))))
        down_even, down_odd = seq_halves(after(down_sum, tuple(grad_pairs)), attn_terms)
        return attn_terms, terms_in, down_even, down_odd

    attn_terms, terms_in, down_even, down_odd = stage(
        sure, back_stage, grad_even, grad_odd, attended_all, normed_in, attn_full, cosine, sine, kept,
        after(down_sum, grad_even),
    )

    attn_sum = z_scatter(attn_terms)

    def tokens_stage(own, even, odd, gain_in, grad_middle, down_even, down_odd, mlp_sum):
        grad_normed_in = seq_scatter(even, odd)
        stream_own = own.astype(wide)
        inverse_in = lax.rsqrt(jnp.mean(stream_own * stream_own, axis=-1, keepdims=True) + EPS)
        unit_in = stream_own * inverse_in
        grad_stream = norm_back(grad_normed_in * gain_in, unit_in, inverse_in) + grad_middle
        grad_down = put_rows(down_even, down_odd, place_arg)
        return grad_stream, grad_down, *seq_halves(mlp_sum, grad_down)

    grad_stream, grad_down, mlp_even, mlp_odd = stage(
        sure, tokens_stage, own, *terms_in, gain_in, grad_middle, down_even, down_odd,
        after(mlp_sum, attn_terms),
    )

    def last_stage(mlp_even, mlp_odd, w_gate, w_up, attn_sum):
        grads = put_columns(mlp_even, mlp_odd, place_arg, shards, w_gate, w_up)
        return grads, seq_halves(attn_sum, grads)

    (grad_gate, grad_up, rows_mid), attn_halves = stage(
        sure, last_stage, mlp_even, mlp_odd, w_gate, w_up, attn_sum
    )
    grad_query, grad_key, grad_value, grad_out, rows_in = put_attention(
        *attn_halves,
        place_arg,
        (w_query, w_key, w_value),
        q_cols,
        out_cols,
    )
    return (
        layer_out[None],
        grad_stream[None],
        grad_query,
        grad_key,
        grad_value,
        grad_out,
        rows_in[:, 0] / gain_attn.astype(wide),
        grad_gate,
        grad_up,
        grad_down,
        rows_mid[:, 0] / gain_mlp.astype(wide),
    )


def solution(mesh):
    placed = (
        P("fsdp", "seq", None),
        P("fsdp", "seq"),
        P("fsdp", None),
        P("fsdp", None),
        P("fsdp", None),
        P("fsdp", None),
        P("fsdp"),
        P("fsdp", None),
        P("fsdp", None),
        P("fsdp", None),
        P("fsdp"),
        P("fsdp", "seq", None),
    )
    return jax.shard_map(
        on_device,
        mesh=mesh,
        in_specs=placed,
        out_specs=(
            P("fsdp", "seq", None),
            P("fsdp", "seq", None),
            P("fsdp", None),
            P("fsdp", None),
            P("fsdp", None),
            P("fsdp", None),
            P("fsdp"),
            P("fsdp", None),
            P("fsdp", None),
            P("fsdp", None),
            P("fsdp"),
        ),
        check_vma=False,
    )
```

time: 815 us -> 545 us (0.67)
  local copies, waits for them, and re-layouts: 236 us -> 23.9 us
  other arithmetic: 162 us -> 24.4 us
  Pallas kernels: 0 us -> 132 us
  waiting for transfers between devices: 111 us -> 223 us
  blocking collectives: 84.1 us -> 0 us
  matrix products: 121 us -> 57.4 us
  starting transfers between devices: 76.9 us -> 59.6 us
    pallas_call x0 -> x25, Pallas kernels: none -> 132 us  [the longest x1 21.4 us: put_columns(): pl.pallas_call(kernel, grid=(rows // tile,), out_shape=(wide, wide, jax.S...]
    ppermute x85 -> x66, waiting for transfers between devices: 100 us -> 193 us  [swap(): lax.ppermute(value, 'seq', [(i, i ^ mask) for i in range(lax.axis_size('s...]
    unnamed x215 -> x28, local copies, waits for them, and re-layouts: 85 us -> 2.76 us
    psum x1 -> x0, blocking collectives: 71.7 us -> none  [on_device(): lax.psum(jnp.stack([grad_gain_in, grad_gain_mid]), ('seq', 'fsdp'))]
    dot_general x20 -> x4, matrix products: 77.4 us -> 15.5 us  [the longest x2 5.9 us: middle_stage(): jnp.dot(later[at], down_full, preferred_element_type=wide)]
    select_n x35 -> x1, other arithmetic: 42.7 us -> 0.01 us  [rope_tables(): sign = jnp.where(lane % head_size < half_dim, -1.0, 1.0)]
    another operation x30 -> x3, other arithmetic: 30.7 us -> 0.34 us  [the longest x19 26.8 us: seq_gather(): mine = jnp.stack([part, by_x, by_y, far])]
    reshape x6 -> x0, local copies, waits for them, and re-layouts: 29.8 us -> none  [the longest x2 21.8 us: spread_columns(): return split.transpose(1, 2, 0, 3).reshape(part.shape[0], -1)]
  transfers between devices with their start and end apart: 94 -> 75, of which waited for: 35 -> 50; matrix products, arithmetic and copies ran while one was open for 58% -> 17% of each run, Pallas kernels for 0% -> 23%
where the time goes in v2:
time: 545 us; the launch traced here: 537 us
  waiting for transfers between devices  223 us (41%)
  Pallas kernels  132 us (24%)
  starting transfers between devices  59.6 us (11%)
  matrix products  57.4 us (11%)
  other arithmetic  24.4 us (4%)
  local copies, waits for them, and re-layouts  23.9 us (4%)
  between operations  14.6 us (3%)
    ppermute x66, waiting for transfers between devices, swap(): lax.ppermute(value, 'seq', [(i, i ^ mask) for i in range(lax.axis_size('s...  193 us
    ppermute x66, starting transfers between devices, swap(): lax.ppermute(value, 'seq', [(i, i ^ mask) for i in range(lax.axis_size('s...  56.1 us
    dot_general x7, matrix products, dot(): lax.dot_general(left, right, ((dims[0], dims[1]), ((), ())), preferred_el...  41.9 us
    pallas_call x1, Pallas kernels, put_columns(): pl.pallas_call(kernel, grid=(rows // tile,), out_shape=(wide, wide, jax.S...  21.4 us
    pallas_call x4, Pallas kernels, seq_gather(): pl.pallas_call(kernel, grid=(cols // tile,), out_shape=jax.ShapeDtypeStru...  19.1 us
    pallas_call x8, Pallas kernels, place_pieces(): pl.pallas_call(kernel, grid=(cols // tile,), out_shape=jax.ShapeDtypeStru...  12.8 us
    pallas_call x1, Pallas kernels, attention_back(): pl.pallas_call(kernel, out_shape=[jax.ShapeDtypeStruct((n, rows, cols), l...  12.6 us
    ppermute x3, waiting for transfers between devices, ring_sum(): moving = lax.ppermute(moving, 'fsdp', [(i, (i + 1) % n) for i in range(n)])  12.1 us
  transfers between devices with their start and end apart: 75, of which 50 were waited for; matrix products, arithmetic and copies ran while one was open for 17% of the time, Pallas kernels for 23%

profile of v2, /device:TPU:0, one launch (start us, length us, event | category | flops | bytes accessed | tf_op | source)
XLA Modules:
  0.0 536.8 jit_solution(6340405473270696313)
XLA Ops:
  18.2 53.4 %conditional.7 = (f32[2,2048]{1,0:T(2,128)}, f32[8,128,128]{2,1,0:T(8,128)}, f32[8,128,128]{2,1,0:T(8,128)}, bf16[1024,2048]{1,0:T(8,128)(2,1)}, f32[1,2048]{1,0:T(1,128)S(1)}, /*index=5*/f32[1,2048]{1,0:T(1,128)}) conditional(s32[]{:T(128)} %bitcast.45, () %tuple.97, (s32[]{:T(128)}, f32[2,512]{1,0:T(2,128)S(1)}, s32[1,128]{1,0:T(1,128)S(1)}, ...), branch_computations={%region_0.1_spmd, %region_1.3_spmd} | conditional | flops 14959876 | bytes 67566192 | solution.py:640
  21.3 3.9 collective-permute-done.15
  31.2 5.7 %collective-permute-done.17 = f32[2,2048]{1,0:T(2,128)S(1)} collective-permute-done((f32[2,2048]{1,0:T(2,128)S(1)}, f32[2,2048]{1,0:T(2,128)S(1)}, u32[]{:S(2)}, u32[]{:S(2)}) %collective-permute-start.17) | collective-permute-done | bytes 16416 | tf_op jit(solution)/shard_map/cond/branch_1_fun/ppermute | solution.py:114
  41.3 4.4 collective-permute-done.24.refs_4_
  59.7 4.7 branch_1_fun.24
  74.4 116.4 %conditional.8 = (bf16[128,2048]{1,0:T(8,128)(2,1)S(1)}, bf16[2048,2048]{1,0:T(8,128)(2,1)}, f32[128,2048]{1,0:T(8,128)S(1)}, bf16[1024,2048]{1,0:T(8,128)(2,1)}...) conditional(s32[]{:T(128)} %bitcast.45, () %tuple.96, ...), branch_computations={%region_3.4_spmd, %region_4.6_spmd} | conditional | flops 3759931648 | bytes 186133664 | solution.py:640
  77.2 4.8 fusion.47
  82.0 9.7 %branch_1_fun.25 = (bf16[4,128,256]{2,1,0:T(8,128)(2,1)S(1)}, bf16[4,128,256]{2,1,0:T(8,128)(2,1)S(1)}, f32[1024,256]{1,0:T(8,128)}, bf16[1024,384]{1,0:T(8,128)...) custom-call(s32[1]{0:T(128)} %get-tuple-element.122.place_ref, f32[8,128,384]{2,1,0:T(8,128)S(1)} %bitcast.155, ...), custom_call_target="tpu_custom_call" | custom-call | flops 1073741824 | bytes 3145728 | tf_op jit(solution)/shard_map/cond/branch_1_fun/pallas_call | solution.py:430
  91.7 9.7 %collective-permute-done.31.refs_2_ = bf16[2048,256]{1,0:T(8,128)(2,1)S(1)} collective-permute-done((bf16[2048,256]{1,0:T(8,128)(2,1)S(1)}, bf16[2048,256]{1,0:T(8,128)(2,1)S(1)}, u32[]{:S(2)}, u32[]{:S(2)}) %collective-permute-start.31) | collective-permute-done | bytes 1048608 | tf_op jit(solution)/shard_map/cond/branch_1_fun/ppermute | solution.py:39
  103.9 11.0 %collective-permute-done.33.refs_4_ = bf16[1024,256]{1,0:T(8,128)(2,1)S(1)} collective-permute-done((bf16[1024,256]{1,0:T(8,128)(2,1)S(1)}, bf16[1024,256]{1,0:T(8,128)(2,1)S(1)}, u32[]{:S(2)}, u32[]{:S(2)}) %collective-permute-start.33) | collective-permute-done | bytes 524320 | tf_op jit(solution)/shard_map/cond/branch_1_fun/ppermute | solution.py:39
  117.9 6.1 %collective-permute-done.26.other_ref = bf16[4,128,256]{2,1,0:T(8,128)(2,1)S(1)} collective-permute-done((bf16[4,128,256]{2,1,0:T(8,128)(2,1)S(1)}, bf16[4,128,256]{2,1,0:T(8,128)(2,1)S(1)}, u32[]{:S(2)}, u32[]{:S(2)}) %collective-permute-start.26) | collective-permute-done | bytes 262176 | tf_op jit(solution)/shard_map/cond/branch_1_fun/ppermute | solution.py:39
  142.7 6.3 %branch_1_fun.29 = bf16[2048,2048]{1,0:T(8,128)(2,1)} custom-call(s32[1]{0:T(128)} %get-tuple-element.122.place_ref, bf16[4,2048,256]{2,1,0:T(8,128)(2,1)S(1)} %copy-done, bf16[4,2048,256]{2,1,0:T(8,128)(2,1)} %collective-permute-done.34.odd_ref), custom_call_target="tpu_custom_call" | custom-call | bytes 16777216 | tf_op jit(solution)/shard_map/cond/branch_1_fun/pallas_call | solution.py:329
  149.0 4.8 multiply_reduce_fusion.1
  158.2 10.7 %collective-permute-done.36.refs_2_ = bf16[128,2048]{1,0:T(8,128)(2,1)S(1)} collective-permute-done((bf16[128,2048]{1,0:T(8,128)(2,1)S(1)}, bf16[128,2048]{1,0:T(8,128)(2,1)S(1)}, u32[]{:S(2)}, u32[]{:S(2)}) %collective-permute-start.36) | collective-permute-done | bytes 524320 | tf_op jit(solution)/shard_map/cond/branch_1_fun/ppermute | solution.py:39
  181.1 4.8 branch_1_fun.33
  185.9 4.8 branch_1_fun.31
  190.8 38.7 %conditional.9 = (bf16[1024,2048]{1,0:T(8,128)(2,1)}, f32[1024,1408]{1,0:T(8,128)}, bf16[1024,704]{1,0:T(8,128)(2,1)}, bf16[704,2048]{1,0:T(8,128)(2,1)}) conditional(s32[]{:T(128)} %bitcast.45, () %tuple.100, (bf16[128,2048]{1,0:T(8,128)(2,1)S(1)}, bf16[1024,2048]{1,0:T(8,128)(2,1)}, bf16[2048,1408]{1,0:T(8,128)(2,1)}, ...), branch_computations={%region_6.7_spmd, %region_7.8_spmd} | conditional | flops 8859811840 | bytes 65143072 | solution.py:640
  193.1 11.9 %branch_1_fun.34 = (f32[1024,1408]{1,0:T(8,128)}, bf16[1024,704]{1,0:T(8,128)(2,1)}) custom-call(bf16[1024,2048]{1,0:T(8,128)(2,1)} %get-tuple-element.155.normed_ref, bf16[2048,1408]{1,0:T(8,128)(2,1)} %get-tuple-element.156.weights_ref), custom_call_target="tpu_custom_call" | custom-call | flops 5905580032 | bytes 11534336 | tf_op jit(solution)/shard_map/cond/branch_1_fun/pallas_call | solution.py:554
  207.7 5.9 %collective-permute-done.48.refs_4_ = bf16[64,2048]{1,0:T(8,128)(2,1)S(1)} collective-permute-done((bf16[64,2048]{1,0:T(8,128)(2,1)S(1)}, bf16[64,2048]{1,0:T(8,128)(2,1)S(1)}, u32[]{:S(2)}, u32[]{:S(2)}) %collective-permute-start.48) | collective-permute-done | bytes 262176 | tf_op jit(solution)/shard_map/cond/branch_1_fun/ppermute | solution.py:39
  215.3 8.1 %convolution_convert_fusion = bf16[704,2048]{1,0:T(8,128)(2,1)} fusion(bf16[1024,704]{1,0:T(8,128)(2,1)} %get-tuple-element.414, bf16[1024,2048]{1,0:T(8,128)(2,1)} %get-tuple-element.163), kind=kOutput, calls=%fused_computation.24 | convolution fusion | flops 2954231808 | bytes 8519680 | tf_op jit(solution)/shard_map/cond/branch_1_fun/dot_general | solution.py:35
  224.8 4.7 branch_1_fun.36
  229.6 5.4 all-gather.8.cloned.1.call-done.down_ref
  234.9 8.1 %shard_map.203 = bf16[1024,1408]{1,0:T(8,128)(2,1)S(1)} custom-call(bf16[1024,2048]{1,0:T(8,128)(2,1)} %get-tuple-element.290.dy_ref, bf16[704,2048]{1,0:T(8,128)(2,1)} %all-gather.8.cloned.1.call-done.down_ref, f32[1024,1408]{1,0:T(8,128)} %get-tuple-element.291.pre_ref), custom_call_target="tpu_custom_call" | custom-call | flops 2952790016 | bytes 11534336 | tf_op jit(solution)/shard_map/pallas_call | solution.py:589
  244.7 10.8 %convolution_convert_fusion.8 = bf16[2048,1408]{1,0:T(8,128)(2,1)} fusion(bf16[1024,2048]{1,0:T(8,128)(2,1)} %get-tuple-element.288, bf16[1024,1408]{1,0:T(8,128)(2,1)S(1)} %shard_map.203), kind=kOutput, calls=%fused_computation.109 | convolution fusion | flops 5908463616 | bytes 12845056 | tf_op jit(solution)/shard_map/dot_general | solution.py:35
  255.5 67.9 %conditional.10 = (f32[128,2048]{1,0:T(8,128)}, bf16[4,128,512]{2,1,0:T(8,128)(2,1)}, bf16[4,128,512]{2,1,0:T(8,128)(2,1)}, bf16[1,128,2048]{2,1,0:T(8,128)(2,1)}) conditional(s32[]{:T(128)} %bitcast.45, () %tuple.95, (f32[128,2048]{1,0:T(8,128)S(1)}, bf16[1024,1408]{1,0:T(8,128)(2,1)}, bf16[2048,1408]{1,0:T(8,128)(2,1)}, f32[1,2048]{1,0:T(1,128)S(1)}, ...), branch_computations={%region_8.9_spmd, %region_9.12_spmd} | conditional | flops 9958064128 | bytes 164910112 | solution.py:640
  256.0 6.7 %convolution_convert_fusion.3 = bf16[512,2048]{1,0:T(8,128)(2,1)S(1)} fusion(bf16[2048,1408]{1,0:T(8,128)(2,1)} %get-tuple-element.166, bf16[1024,1408]{1,0:T(8,128)(2,1)} %get-tuple-element.165), kind=kOutput, calls=%fused_computation.29 | convolution fusion | flops 2953838592 | bytes 9306112 | tf_op jit(solution)/shard_map/cond/branch_1_fun/dot_general | solution.py:35
  279.7 3.9 collective-permute-done.53
  293.1 8.8 %collective-permute-done.54 = bf16[128,2048]{1,0:T(8,128)(2,1)S(1)} collective-permute-done((bf16[128,2048]{1,0:T(8,128)(2,1)S(1)}, bf16[128,2048]{1,0:T(8,128)(2,1)S(1)}, u32[]{:S(2)}, u32[]{:S(2)}) %collective-permute-start.54) | collective-permute-done | bytes 524320 | tf_op jit(solution)/shard_map/cond/branch_1_fun/ppermute | solution.py:39
  302.3 9.6 %collective-permute-done.59 = bf16[128,2048]{1,0:T(8,128)(2,1)S(1)} collective-permute-done((bf16[128,2048]{1,0:T(8,128)(2,1)S(1)}, bf16[128,2048]{1,0:T(8,128)(2,1)S(1)}, u32[]{:S(2)}, u32[]{:S(2)}) %collective-permute-start.59) | collective-permute-done | bytes 524320 | tf_op jit(solution)/shard_map/cond/branch_1_fun/ppermute | solution.py:39
  313.9 7.2 %convolution_convert_fusion.5.refs_0_ = bf16[128,2048]{1,0:T(8,128)(2,1)} fusion(bf16[128,2048]{1,0:T(8,128)(2,1)S(1)} %get-tuple-element.325.refs_1_, bf16[2048,2048]{1,0:T(8,128)(2,1)} %get-tuple-element.170), kind=kOutput, calls=%fused_computation.31 | convolution fusion | flops 1074003968 | bytes 9437184 | tf_op jit(solution)/shard_map/cond/branch_1_fun/dot_general | solution.py:35
  323.5 61.7 %conditional.11 = (bf16[2048,640]{1,0:T(8,128)(2,1)}, bf16[4,128,2048]{2,1,0:T(8,128)(2,1)}, bf16[4,128,2048]{2,1,0:T(8,128)(2,1)}, bf16[4,176,2048]{2,1,0:T(8,128)(2,1)}, bf16[4,176,2048]{2,1,0:T(8,128)(2,1)}) conditional(s32[]{:T(128)} %bitcast.45, () %tuple.105, (bf16[4,128,512]{2,1,0:T(8,128)(2,1)}, bf16[4,128,512]{2,1,0:T(8,128)(2,1)}, ...), branch_computations={%region_13.14_spmd, %region_14.15_spmd} | conditional | flops 6981419008 | bytes 59900388 | solution.py:640
  332.3 5.9 %collective-permute-done.61.refs_1_ = bf16[2,128,512]{2,1,0:T(8,128)(2,1)S(1)} collective-permute-done((bf16[2,128,512]{2,1,0:T(8,128)(2,1)}, bf16[2,128,512]{2,1,0:T(8,128)(2,1)S(1)}, u32[]{:S(2)}, u32[]{:S(2)}) %collective-permute-start.61) | collective-permute-done | bytes 262176 | tf_op jit(solution)/shard_map/cond/branch_1_fun/ppermute | solution.py:39
  338.2 5.7 %collective-permute-done.63.refs_3_ = bf16[2,128,512]{2,1,0:T(8,128)(2,1)S(1)} collective-permute-done((bf16[2,128,512]{2,1,0:T(8,128)(2,1)}, bf16[2,128,512]{2,1,0:T(8,128)(2,1)S(1)}, u32[]{:S(2)}, u32[]{:S(2)}) %collective-permute-start.63) | collective-permute-done | bytes 262176 | tf_op jit(solution)/shard_map/cond/branch_1_fun/ppermute | solution.py:39
  347.2 12.6 %branch_1_fun.39 = (bf16[8,128,384]{2,1,0:T(8,128)(2,1)S(1)}, bf16[8,128,256]{2,1,0:T(8,128)(2,1)S(1)}) custom-call(s32[1]{0:T(128)} %get-tuple-element.177.place_ref, bf16[1024,384]{1,0:T(8,128)(2,1)} %get-tuple-element.178.rot_ref, f32[1024,256]{1,0:T(8,128)} %get-tuple-element.179.out_ref, f32[4,1024,1]{2,1,0:T(8,128)} %get-tuple-element.180.top_ref, ...), custom_call_target="tpu_custom_call" | custom-call | flops 2684354560 | bytes 3145728 | tf_op jit(solution)/shard_map/cond/branch_1_fun/pallas_call | solution.py:516
  359.8 7.5 %branch_1_fun.40 = bf16[2048,640]{1,0:T(8,128)(2,1)} custom-call(bf16[1024,2048]{1,0:T(8,128)(2,1)} %get-tuple-element.176.normed_ref, bf16[1024,384]{1,0:T(8,128)(2,1)S(1)} %bitcast.153, bf16[1024,2048]{1,0:T(8,128)(2,1)} %get-tuple-element.191.attended_ref, bf16[1024,256]{1,0:T(8,128)(2,1)S(1)} %bitcast.154), custom_call_target="tpu_custom_call" | custom-call | flops 2684354560 | bytes 8388608 | tf_op jit(solution)/shard_map/cond/branch_1_fun/pallas_call | solution.py:616
  369.3 6.5 %collective-permute-done.66.refs_3_ = bf16[80,2048]{1,0:T(8,128)(2,1)S(1)} collective-permute-done((bf16[80,2048]{1,0:T(8,128)(2,1)S(1)}, bf16[80,2048]{1,0:T(8,128)(2,1)S(1)}, u32[]{:S(2)}, u32[]{:S(2)}) %collective-permute-start.66) | collective-permute-done | bytes 327712 | tf_op jit(solution)/shard_map/cond/branch_1_fun/ppermute | solution.py:39
  385.2 11.7 %reduce-scatter.6.cloned.1.call-done = bf16[512,1408]{1,0:T(8,128)(2,1)} async-done(((bf16[2048,1408]{1,0:T(8,128)(2,1)}), bf16[512,1408]{1,0:T(8,128)(2,1)}) %reduce-scatter.6.cloned.1.call-update) | async-done | bytes 1441808 | tf_op jit(solution)/shard_map/reduce_scatter | solution.py:688
  396.9 85.5 %conditional.12 = (f32[1408,2048]{1,0:T(8,128)}, bf16[4,512,1408]{2,1,0:T(8,128)(2,1)}, bf16[4,512,1408]{2,1,0:T(8,128)(2,1)}, f32[1,128,2048]{2,1,0:T(8,128)}) conditional(s32[]{:T(128)} %bitcast.45, () %tuple.104, (s32[1]{0:T(128)}, bf16[4,176,2048]{2,1,0:T(8,128)(2,1)}, bf16[4,176,2048]{2,1,0:T(8,128)(2,1)}, bf16[512,1408]{1,0:T(8,128)(2,1)}, ...), branch_computations={%region_16.17_spmd, %region_17.20_spmd} | conditional | flops 13107328 | bytes 117199816 | solution.py:640
  399.8 8.6 %branch_1_fun.42 = f32[1408,2048]{1,0:T(8,128)} custom-call(s32[1]{0:T(128)} %get-tuple-element.200.place_ref, bf16[4,176,2048]{2,1,0:T(8,128)(2,1)} %get-tuple-element.201.even_ref, bf16[4,176,2048]{2,1,0:T(8,128)(2,1)} %get-tuple-element.202.odd_ref), custom_call_target="tpu_custom_call" | custom-call | bytes 17301504 | tf_op jit(solution)/shard_map/cond/branch_1_fun/pallas_call | solution.py:177
  408.4 22.0 %collective-permute-done.6.refs_2_ = bf16[512,1408]{1,0:T(8,128)(2,1)S(1)} collective-permute-done((bf16[512,1408]{1,0:T(8,128)(2,1)}, bf16[512,1408]{1,0:T(8,128)(2,1)S(1)}, u32[]{:S(2)}, u32[]{:S(2)}) %collective-permute-start.6) | collective-permute-done | bytes 1441824 | tf_op jit(solution)/shard_map/cond/branch_1_fun/ppermute | solution.py:39
  433.9 14.8 %collective-permute-done.8.refs_4_ = bf16[256,1408]{1,0:T(8,128)(2,1)S(1)} collective-permute-done((bf16[256,1408]{1,0:T(8,128)(2,1)S(1)}, bf16[256,1408]{1,0:T(8,128)(2,1)S(1)}, u32[]{:S(2)}, u32[]{:S(2)}) %collective-permute-start.8) | collective-permute-done | bytes 720928 | tf_op jit(solution)/shard_map/cond/branch_1_fun/ppermute | solution.py:39
  456.8 7.5 %collective-permute-done.13 = bf16[64,2048]{1,0:T(8,128)(2,1)S(1)} collective-permute-done((bf16[64,2048]{1,0:T(8,128)(2,1)S(1)}, bf16[64,2048]{1,0:T(8,128)(2,1)S(1)}, u32[]{:S(2)}, u32[]{:S(2)}) %collective-permute-start.13) | collective-permute-done | bytes 262176 | tf_op jit(solution)/shard_map/cond/branch_1_fun/ppermute | solution.py:39
  467.2 10.9 %collective-permute-done.14 = bf16[128,2048]{1,0:T(8,128)(2,1)S(1)} collective-permute-done((bf16[128,2048]{1,0:T(8,128)(2,1)S(1)}, bf16[128,2048]{1,0:T(8,128)(2,1)S(1)}, u32[]{:S(2)}, u32[]{:S(2)}) %collective-permute-start.14) | collective-permute-done | bytes 524320 | tf_op jit(solution)/shard_map/cond/branch_1_fun/ppermute | solution.py:39
  482.4 39.1 %conditional.13 = (f32[512,5632]{1,0:T(8,128)}, f32[512,5632]{1,0:T(8,128)}, bf16[4,512,640]{2,1,0:T(8,128)(2,1)}, bf16[4,512,640]{2,1,0:T(8,128)(2,1)}, f32[512]{0:T(512)S(1)}) conditional(s32[]{:T(128)} %bitcast.45, () %tuple.110, (s32[1]{0:T(128)}, bf16[4,512,1408]{2,1,0:T(8,128)(2,1)}, bf16[4,512,1408]{2,1,0:T(8,128)(2,1)}, ...), branch_computations={%region_21.22_spmd, %region_22.23_spmd} | conditional | bytes 62132496 | solution.py:640
  485.3 21.4 %branch_1_fun.44 = (f32[512,5632]{1,0:T(8,128)}, f32[512,5632]{1,0:T(8,128)}, f32[512,1]{1,0:T(8,128)S(1)}) custom-call(s32[1]{0:T(128)} %get-tuple-element.213.place_ref, bf16[4,512,1408]{2,1,0:T(8,128)(2,1)} %get-tuple-element.214.even_ref, bf16[4,512,1408]{2,1,0:T(8,128)(2,1)} %get-tuple-element.215.odd_ref, ...), custom_call_target="tpu_custom_call" | custom-call | bytes 34603008 | tf_op jit(solution)/shard_map/cond/branch_1_fun/pallas_call | solution.py:149
  508.1 6.1 %collective-permute-done.3.refs_4_ = bf16[256,640]{1,0:T(8,128)(2,1)S(1)} collective-permute-done((bf16[256,640]{1,0:T(8,128)(2,1)S(1)}, bf16[256,640]{1,0:T(8,128)(2,1)S(1)}, u32[]{:S(2)}, u32[]{:S(2)}) %collective-permute-start.3) | collective-permute-done | bytes 327712 | tf_op jit(solution)/shard_map/cond/branch_1_fun/ppermute | solution.py:39
  516.4 5.1 collective-permute-done.4
  522.1 6.9 %shard_map.204 = (f32[512,2048]{1,0:T(8,128)}, f32[512,256]{1,0:T(8,128)}, f32[512,256]{1,0:T(8,128)}, f32[512,2048]{1,0:T(8,128)}, f32[512,1]{1,0:T(8,128)S(1)}) custom-call(s32[1]{0:T(128)} %bitcast.47.place_ref, bf16[4,512,640]{2,1,0:T(8,128)(2,1)} %get-tuple-element.314.even_ref, bf16[4,512,640]{2,1,0:T(8,128)(2,1)} %get-tuple-element.315.odd_ref, ...), custom_call_target="tpu_custom_call" | custom-call | bytes 15728640 | tf_op jit(solution)/shard_map/pallas_call | solution.py:219
  (307 shorter events, 184.3 us)
Async XLA Ops:
  7.2 64.4 %all-gather.4.cloned.1.call-start = ((), (), s32[]{:S(2)}) async-start(), calls=%async_computation.3 | async-start | bytes 3276800 | tf_op jit(solution)/shard_map/all_gather | solution.py:685
  10.5 180.3 %all-gather.6.cloned.1.call-start = ((), (), s32[]{:S(2)}) async-start(), calls=%async_computation.4 | async-start | bytes 7208960 | tf_op jit(solution)/shard_map/all_gather | solution.py:685
  15.9 219.1 %all-gather.8.cloned.1.call-start = ((), (), s32[]{:S(2)}) async-start(), calls=%async_computation.5 | async-start | bytes 3604480 | tf_op jit(solution)/shard_map/all_gather | solution.py:685
  18.0 305.4 %reduce-scatter.4.cloned.1.call-start = ((), (), s32[]{:S(2)}) async-start(), calls=%async_computation.6 | async-start | bytes 3604480 | tf_op jit(solution)/shard_map/reduce_scatter | solution.py:688
  25.2 12.8 %collective-permute-start.22 = (bf16[128,2048]{1,0:T(8,128)(2,1)S(1)}, bf16[128,2048]{1,0:T(8,128)(2,1)S(1)}, u32[]{:S(2)}, u32[]{:S(2)}) collective-permute-start(bf16[128,2048]{1,0:T(8,128)(2,1)S(1)} %get-tuple-element.117.refs_0_), channel_id=1, source_target_pairs={{0,16},{4,20},{8,24},{12,28},{16,0},{20,4},{24,8},{28,12},{1,17},{... | collective-permute-start | bytes 1572872 | tf_op jit(solution)/shard_map/cond/branch_1_fun/ppermute | solution.py:39
  26.9 12.3 %collective-permute-start.21 = (bf16[128,2048]{1,0:T(8,128)(2,1)S(1)}, bf16[128,2048]{1,0:T(8,128)(2,1)S(1)}, u32[]{:S(2)}, u32[]{:S(2)}) collective-permute-start(bf16[128,2048]{1,0:T(8,128)(2,1)S(1)} %get-tuple-element.117.refs_0_), channel_id=1, source_target_pairs={{0,8},{4,12},{8,0},{12,4},{16,24},{20,28},{24,16},{28,20},{1,9},{5... | collective-permute-start | bytes 1572872 | tf_op jit(solution)/shard_map/cond/branch_1_fun/ppermute | solution.py:39
  47.6 12.1 %collective-permute-start.25 = (bf16[4,128,2048]{2,1,0:T(8,128)(2,1)S(1)}, bf16[4,128,2048]{2,1,0:T(8,128)(2,1)}, u32[]{:S(2)}, u32[]{:S(2)}) collective-permute-start(bf16[4,128,2048]{2,1,0:T(8,128)(2,1)S(1)} %branch_1_fun.23.mine_ref), channel_id=1, source_target_pairs={{0,4},{4,0},{8,12},{12,8},{16,20},{20,16},{24,28},{28,24},{1,5},{5... | collective-permute-start | bytes 6291464 | tf_op jit(solution)/shard_map/cond/branch_1_fun/ppermute | solution.py:39
  76.1 25.3 %collective-permute-start.31 = (bf16[2048,256]{1,0:T(8,128)(2,1)S(1)}, bf16[2048,256]{1,0:T(8,128)(2,1)S(1)}, u32[]{:S(2)}, u32[]{:S(2)}) collective-permute-start(bf16[2048,256]{1,0:T(8,128)(2,1)S(1)} %slice.180.refs_0_), channel_id=1, source_target_pairs={{0,16},{4,20},{8,24},{12,28},{16,0},{20,4},{24,8},{28,12},{1,17},{... | collective-permute-start | bytes 3145736 | tf_op jit(solution)/shard_map/cond/branch_1_fun/ppermute | solution.py:39
  76.7 25.0 %collective-permute-start.30 = (bf16[2048,256]{1,0:T(8,128)(2,1)S(1)}, bf16[2048,256]{1,0:T(8,128)(2,1)S(1)}, u32[]{:S(2)}, u32[]{:S(2)}) collective-permute-start(bf16[2048,256]{1,0:T(8,128)(2,1)S(1)} %slice.180.refs_0_), channel_id=1, source_target_pairs={{0,8},{4,12},{8,0},{12,4},{16,24},{20,28},{24,16},{28,20},{1,9},{5... | collective-permute-start | bytes 3145736 | tf_op jit(solution)/shard_map/cond/branch_1_fun/ppermute | solution.py:39
  101.7 13.1 %collective-permute-start.33 = (bf16[1024,256]{1,0:T(8,128)(2,1)S(1)}, bf16[1024,256]{1,0:T(8,128)(2,1)S(1)}, u32[]{:S(2)}, u32[]{:S(2)}) collective-permute-start(bf16[1024,256]{1,0:T(8,128)(2,1)S(1)} %slice.182), channel_id=1, source_target_pairs={{0,8},{4,12},{8,0},{12,4},{16,24},{20,28},{24,16},{28,20},{1,9},{5... | collective-permute-start | bytes 1572872 | tf_op jit(solution)/shard_map/cond/branch_1_fun/ppermute | solution.py:39
  102.3 12.8 %collective-permute-start.32 = (bf16[1024,256]{1,0:T(8,128)(2,1)S(1)}, bf16[1024,256]{1,0:T(8,128)(2,1)S(1)}, u32[]{:S(2)}, u32[]{:S(2)}) collective-permute-start(bf16[1024,256]{1,0:T(8,128)(2,1)S(1)} %slice.181), channel_id=1, source_target_pairs={{0,16},{4,20},{8,24},{12,28},{16,0},{20,4},{24,8},{28,12},{1,17},{... | collective-permute-start | bytes 1572872 | tf_op jit(solution)/shard_map/cond/branch_1_fun/ppermute | solution.py:39
  117.4 23.1 %collective-permute-start.34 = (bf16[4,2048,256]{2,1,0:T(8,128)(2,1)}, bf16[4,2048,256]{2,1,0:T(8,128)(2,1)}, u32[]{:S(2)}, u32[]{:S(2)}) collective-permute-start(bf16[4,2048,256]{2,1,0:T(8,128)(2,1)} %branch_1_fun.28.even_ref), channel_id=1, source_target_pairs={{0,4},{4,0},{8,12},{12,8},{16,20},{20,16},{24,28},{28,24},{1,5},{5... | collective-permute-start | bytes 12582920 | tf_op jit(solution)/shard_map/cond/branch_1_fun/ppermute | solution.py:39
  138.5 17.7 %collective-permute-start.41 = (bf16[128,2048]{1,0:T(8,128)(2,1)S(1)}, bf16[128,2048]{1,0:T(8,128)(2,1)S(1)}, u32[]{:S(2)}, u32[]{:S(2)}) collective-permute-start(bf16[128,2048]{1,0:T(8,128)(2,1)S(1)} %get-tuple-element.145.refs_0_), channel_id=1, source_target_pairs={{0,16},{4,20},{8,24},{12,28},{16,0},{20,4},{24,8},{28,12},{1,17},{... | collective-permute-start | bytes 1572872 | tf_op jit(solution)/shard_map/cond/branch_1_fun/ppermute | solution.py:39
  140.0 16.2 %collective-permute-start.40 = (bf16[128,2048]{1,0:T(8,128)(2,1)S(1)}, bf16[128,2048]{1,0:T(8,128)(2,1)S(1)}, u32[]{:S(2)}, u32[]{:S(2)}) collective-permute-start(bf16[128,2048]{1,0:T(8,128)(2,1)S(1)} %get-tuple-element.145.refs_0_), channel_id=1, source_target_pairs={{0,8},{4,12},{8,0},{12,4},{16,24},{20,28},{24,16},{28,20},{1,9},{5... | collective-permute-start | bytes 1572872 | tf_op jit(solution)/shard_map/cond/branch_1_fun/ppermute | solution.py:39
  154.0 14.9 %collective-permute-start.36 = (bf16[128,2048]{1,0:T(8,128)(2,1)S(1)}, bf16[128,2048]{1,0:T(8,128)(2,1)S(1)}, u32[]{:S(2)}, u32[]{:S(2)}) collective-permute-start(bf16[128,2048]{1,0:T(8,128)(2,1)S(1)} %multiply_convert_fusion.refs_0_), channel_id=1, source_target_pairs={{0,16},{4,20},{8,24},{12,28},{16,0},{20,4},{24,8},{28,12},{1,17},{... | collective-permute-start | bytes 1572872 | tf_op jit(solution)/shard_map/cond/branch_1_fun/ppermute | solution.py:39
  155.2 14.9 %collective-permute-start.35 = (bf16[128,2048]{1,0:T(8,128)(2,1)S(1)}, bf16[128,2048]{1,0:T(8,128)(2,1)S(1)}, u32[]{:S(2)}, u32[]{:S(2)}) collective-permute-start(bf16[128,2048]{1,0:T(8,128)(2,1)S(1)} %multiply_convert_fusion.refs_0_), channel_id=1, source_target_pairs={{0,8},{4,12},{8,0},{12,4},{16,24},{20,28},{24,16},{28,20},{1,9},{5... | collective-permute-start | bytes 1572872 | tf_op jit(solution)/shard_map/cond/branch_1_fun/ppermute | solution.py:39
  156.2 19.5 %collective-permute-start.43 = (bf16[64,2048]{1,0:T(8,128)(2,1)S(1)}, bf16[64,2048]{1,0:T(8,128)(2,1)S(1)}, u32[]{:S(2)}, u32[]{:S(2)}) collective-permute-start(bf16[64,2048]{1,0:T(8,128)(2,1)S(1)} %slice.186), channel_id=1, source_target_pairs={{0,8},{4,12},{8,0},{12,4},{16,24},{20,28},{24,16},{28,20},{1,9},{5... | collective-permute-start | bytes 786440 | tf_op jit(solution)/shard_map/cond/branch_1_fun/ppermute | solution.py:39
  157.4 18.3 %collective-permute-start.42 = (bf16[64,2048]{1,0:T(8,128)(2,1)S(1)}, bf16[64,2048]{1,0:T(8,128)(2,1)S(1)}, u32[]{:S(2)}, u32[]{:S(2)}) collective-permute-start(bf16[64,2048]{1,0:T(8,128)(2,1)S(1)} %slice.185), channel_id=1, source_target_pairs={{0,16},{4,20},{8,24},{12,28},{16,0},{20,4},{24,8},{28,12},{1,17},{... | collective-permute-start | bytes 786440 | tf_op jit(solution)/shard_map/cond/branch_1_fun/ppermute | solution.py:39
  170.1 9.0 %collective-permute-start.38 = (bf16[64,2048]{1,0:T(8,128)(2,1)S(1)}, bf16[64,2048]{1,0:T(8,128)(2,1)S(1)}, u32[]{:S(2)}, u32[]{:S(2)}) collective-permute-start(bf16[64,2048]{1,0:T(8,128)(2,1)S(1)} %slice.184), channel_id=1, source_target_pairs={{0,8},{4,12},{8,0},{12,4},{16,24},{20,28},{24,16},{28,20},{1,9},{5... | collective-permute-start | bytes 786440 | tf_op jit(solution)/shard_map/cond/branch_1_fun/ppermute | solution.py:39
  191.0 14.4 %collective-permute-start.46 = (bf16[128,2048]{1,0:T(8,128)(2,1)S(1)}, bf16[128,2048]{1,0:T(8,128)(2,1)S(1)}, u32[]{:S(2)}, u32[]{:S(2)}) collective-permute-start(bf16[128,2048]{1,0:T(8,128)(2,1)S(1)} %get-tuple-element.154.refs_0_), channel_id=1, source_target_pairs={{0,16},{4,20},{8,24},{12,28},{16,0},{20,4},{24,8},{28,12},{1,17},{... | collective-permute-start | bytes 1572872 | tf_op jit(solution)/shard_map/cond/branch_1_fun/ppermute | solution.py:39
  191.7 14.1 %collective-permute-start.45 = (bf16[128,2048]{1,0:T(8,128)(2,1)S(1)}, bf16[128,2048]{1,0:T(8,128)(2,1)S(1)}, u32[]{:S(2)}, u32[]{:S(2)}) collective-permute-start(bf16[128,2048]{1,0:T(8,128)(2,1)S(1)} %get-tuple-element.154.refs_0_), channel_id=1, source_target_pairs={{0,8},{4,12},{8,0},{12,4},{16,24},{20,28},{24,16},{28,20},{1,9},{5... | collective-permute-start | bytes 1572872 | tf_op jit(solution)/shard_map/cond/branch_1_fun/ppermute | solution.py:39
  229.5 167.3 %reduce-scatter.6.cloned.1.call-start = ((), (), s32[]{:S(2)}) async-start(), calls=%async_computation.7 | async-start | bytes 7208960 | tf_op jit(solution)/shard_map/reduce_scatter | solution.py:688
  255.5 226.9 %reduce-scatter.8.cloned.1.call-start = ((), (), s32[]{:S(2)}) async-start(), calls=%async_computation.8 | async-start | bytes 3276800 | tf_op jit(solution)/shard_map/reduce_scatter | solution.py:688
  262.8 10.4 %collective-permute-start.50 = (bf16[4,128,2048]{2,1,0:T(8,128)(2,1)S(1)}, bf16[4,128,2048]{2,1,0:T(8,128)(2,1)S(1)}, u32[]{:S(2)}, u32[]{:S(2)}) collective-permute-start(bf16[4,128,2048]{2,1,0:T(8,128)(2,1)S(1)} %bitcast.175), channel_id=1, source_target_pairs={{0,4},{4,0},{8,12},{12,8},{16,20},{20,16},{24,28},{28,24},{1,5},{5... | collective-permute-start | bytes 6291464 | tf_op jit(solution)/shard_map/cond/branch_1_fun/ppermute | solution.py:39
  274.4 9.2 %collective-permute-start.53 = (bf16[64,2048]{1,0:T(8,128)(2,1)S(1)}, bf16[64,2048]{1,0:T(8,128)(2,1)S(1)}, u32[]{:S(2)}, u32[]{:S(2)}) collective-permute-start(bf16[64,2048]{1,0:T(8,128)(2,1)S(1)} %get-tuple-element.359), channel_id=1, source_target_pairs={{0,8},{4,12},{8,0},{12,4},{16,24},{20,28},{24,16},{28,20},{1,9},{5... | collective-permute-start | bytes 786440 | tf_op jit(solution)/shard_map/cond/branch_1_fun/ppermute | solution.py:39
  275.9 9.2 %collective-permute-start.51 = (bf16[64,2048]{1,0:T(8,128)(2,1)S(1)}, bf16[64,2048]{1,0:T(8,128)(2,1)S(1)}, u32[]{:S(2)}, u32[]{:S(2)}) collective-permute-start(bf16[64,2048]{1,0:T(8,128)(2,1)S(1)} %get-tuple-element.360), channel_id=1, source_target_pairs={{0,16},{4,20},{8,24},{12,28},{16,0},{20,4},{24,8},{28,12},{1,17},{... | collective-permute-start | bytes 786440 | tf_op jit(solution)/shard_map/cond/branch_1_fun/ppermute | solution.py:39
  278.5 10.7 %collective-permute-start.58 = (bf16[64,2048]{1,0:T(8,128)(2,1)S(1)}, bf16[64,2048]{1,0:T(8,128)(2,1)S(1)}, u32[]{:S(2)}, u32[]{:S(2)}) collective-permute-start(bf16[64,2048]{1,0:T(8,128)(2,1)S(1)} %get-tuple-element.355), channel_id=1, source_target_pairs={{0,8},{4,12},{8,0},{12,4},{16,24},{20,28},{24,16},{28,20},{1,9},{5... | collective-permute-start | bytes 786440 | tf_op jit(solution)/shard_map/cond/branch_1_fun/ppermute | solution.py:39
  279.1 11.6 %collective-permute-start.56 = (bf16[64,2048]{1,0:T(8,128)(2,1)S(1)}, bf16[64,2048]{1,0:T(8,128)(2,1)S(1)}, u32[]{:S(2)}, u32[]{:S(2)}) collective-permute-start(bf16[64,2048]{1,0:T(8,128)(2,1)S(1)} %get-tuple-element.356), channel_id=1, source_target_pairs={{0,16},{4,20},{8,24},{12,28},{16,0},{20,4},{24,8},{28,12},{1,17},{... | collective-permute-start | bytes 786440 | tf_op jit(solution)/shard_map/cond/branch_1_fun/ppermute | solution.py:39
  285.2 16.7 %collective-permute-start.54 = (bf16[128,2048]{1,0:T(8,128)(2,1)S(1)}, bf16[128,2048]{1,0:T(8,128)(2,1)S(1)}, u32[]{:S(2)}, u32[]{:S(2)}) collective-permute-start(bf16[128,2048]{1,0:T(8,128)(2,1)S(1)} %pad_maximum_fusion.1), channel_id=1, source_target_pairs={{0,16},{4,20},{8,24},{12,28},{16,0},{20,4},{24,8},{28,12},{1,17},{... | collective-permute-start | bytes 1572872 | tf_op jit(solution)/shard_map/cond/branch_1_fun/ppermute | solution.py:39
  286.8 15.1 %collective-permute-start.52 = (bf16[128,2048]{1,0:T(8,128)(2,1)S(1)}, bf16[128,2048]{1,0:T(8,128)(2,1)S(1)}, u32[]{:S(2)}, u32[]{:S(2)}) collective-permute-start(bf16[128,2048]{1,0:T(8,128)(2,1)S(1)} %pad_maximum_fusion), channel_id=1, source_target_pairs={{0,8},{4,12},{8,0},{12,4},{16,24},{20,28},{24,16},{28,20},{1,9},{5... | collective-permute-start | bytes 1572872 | tf_op jit(solution)/shard_map/cond/branch_1_fun/ppermute | solution.py:39
  290.9 21.0 %collective-permute-start.59 = (bf16[128,2048]{1,0:T(8,128)(2,1)S(1)}, bf16[128,2048]{1,0:T(8,128)(2,1)S(1)}, u32[]{:S(2)}, u32[]{:S(2)}) collective-permute-start(bf16[128,2048]{1,0:T(8,128)(2,1)S(1)} %pad_maximum_fusion.3), channel_id=1, source_target_pairs={{0,16},{4,20},{8,24},{12,28},{16,0},{20,4},{24,8},{28,12},{1,17},{... | collective-permute-start | bytes 1572872 | tf_op jit(solution)/shard_map/cond/branch_1_fun/ppermute | solution.py:39
  292.5 19.5 %collective-permute-start.57 = (bf16[128,2048]{1,0:T(8,128)(2,1)S(1)}, bf16[128,2048]{1,0:T(8,128)(2,1)S(1)}, u32[]{:S(2)}, u32[]{:S(2)}) collective-permute-start(bf16[128,2048]{1,0:T(8,128)(2,1)S(1)} %pad_maximum_fusion.2), channel_id=1, source_target_pairs={{0,8},{4,12},{8,0},{12,4},{16,24},{20,28},{24,16},{28,20},{1,9},{5... | collective-permute-start | bytes 1572872 | tf_op jit(solution)/shard_map/cond/branch_1_fun/ppermute | solution.py:39
  328.8 9.4 %collective-permute-start.61 = (bf16[2,128,512]{2,1,0:T(8,128)(2,1)}, bf16[2,128,512]{2,1,0:T(8,128)(2,1)S(1)}, u32[]{:S(2)}, u32[]{:S(2)}) collective-permute-start(bf16[2,128,512]{2,1,0:T(8,128)(2,1)} %get-tuple-element.187), channel_id=1, source_target_pairs={{0,8},{4,12},{8,0},{12,4},{16,24},{20,28},{24,16},{28,20},{1,9},{5... | collective-permute-start | bytes 786440 | tf_op jit(solution)/shard_map/cond/branch_1_fun/ppermute | solution.py:39
  329.4 8.8 %collective-permute-start.62 = (bf16[2,128,512]{2,1,0:T(8,128)(2,1)}, bf16[2,128,512]{2,1,0:T(8,128)(2,1)S(1)}, u32[]{:S(2)}, u32[]{:S(2)}) collective-permute-start(bf16[2,128,512]{2,1,0:T(8,128)(2,1)} %get-tuple-element.188), channel_id=1, source_target_pairs={{0,16},{4,20},{8,24},{12,28},{16,0},{20,4},{24,8},{28,12},{1,17},{... | collective-permute-start | bytes 786440 | tf_op jit(solution)/shard_map/cond/branch_1_fun/ppermute | solution.py:39
  330.8 13.1 %collective-permute-start.63 = (bf16[2,128,512]{2,1,0:T(8,128)(2,1)}, bf16[2,128,512]{2,1,0:T(8,128)(2,1)S(1)}, u32[]{:S(2)}, u32[]{:S(2)}) collective-permute-start(bf16[2,128,512]{2,1,0:T(8,128)(2,1)} %get-tuple-element.189), channel_id=1, source_target_pairs={{0,24},{4,28},{8,16},{12,20},{16,8},{20,12},{24,0},{28,4},{1,25},{... | collective-permute-start | bytes 786440 | tf_op jit(solution)/shard_map/cond/branch_1_fun/ppermute | solution.py:39
  343.9 23.4 %collective-permute-start.65 = (bf16[176,2048]{1,0:T(8,128)(2,1)}, bf16[176,2048]{1,0:T(8,128)(2,1)S(1)}, u32[]{:S(2)}, u32[]{:S(2)}) collective-permute-start(bf16[176,2048]{1,0:T(8,128)(2,1)} %get-tuple-element.195.refs_0_), channel_id=1, source_target_pairs={{0,16},{4,20},{8,24},{12,28},{16,0},{20,4},{24,8},{28,12},{1,17},{... | collective-permute-start | bytes 2162696 | tf_op jit(solution)/shard_map/cond/branch_1_fun/ppermute | solution.py:39
  344.7 22.6 %collective-permute-start.64 = (bf16[176,2048]{1,0:T(8,128)(2,1)}, bf16[176,2048]{1,0:T(8,128)(2,1)S(1)}, u32[]{:S(2)}, u32[]{:S(2)}) collective-permute-start(bf16[176,2048]{1,0:T(8,128)(2,1)} %get-tuple-element.195.refs_0_), channel_id=1, source_target_pairs={{0,8},{4,12},{8,0},{12,4},{16,24},{20,28},{24,16},{28,20},{1,9},{5... | collective-permute-start | bytes 2162696 | tf_op jit(solution)/shard_map/cond/branch_1_fun/ppermute | solution.py:39
  367.4 9.7 %collective-permute-start.67 = (bf16[96,2048]{1,0:T(8,128)(2,1)S(1)}, bf16[96,2048]{1,0:T(8,128)(2,1)S(1)}, u32[]{:S(2)}, u32[]{:S(2)}) collective-permute-start(bf16[96,2048]{1,0:T(8,128)(2,1)S(1)} %slice.224), channel_id=1, source_target_pairs={{0,8},{4,12},{8,0},{12,4},{16,24},{20,28},{24,16},{28,20},{1,9},{5... | collective-permute-start | bytes 1179656 | tf_op jit(solution)/shard_map/cond/branch_1_fun/ppermute | solution.py:39
  396.9 33.6 %collective-permute-start.6 = (bf16[512,1408]{1,0:T(8,128)(2,1)}, bf16[512,1408]{1,0:T(8,128)(2,1)S(1)}, u32[]{:S(2)}, u32[]{:S(2)}) collective-permute-start(bf16[512,1408]{1,0:T(8,128)(2,1)} %get-tuple-element.203.refs_0_), channel_id=1, source_target_pairs={{0,16},{4,20},{8,24},{12,28},{16,0},{20,4},{24,8},{28,12},{1,17},{... | collective-permute-start | bytes 4325384 | tf_op jit(solution)/shard_map/cond/branch_1_fun/ppermute | solution.py:39
  398.4 33.3 %collective-permute-start.5 = (bf16[512,1408]{1,0:T(8,128)(2,1)}, bf16[512,1408]{1,0:T(8,128)(2,1)S(1)}, u32[]{:S(2)}, u32[]{:S(2)}) collective-permute-start(bf16[512,1408]{1,0:T(8,128)(2,1)} %get-tuple-element.203.refs_0_), channel_id=1, source_target_pairs={{0,8},{4,12},{8,0},{12,4},{16,24},{20,28},{24,16},{28,20},{1,9},{5... | collective-permute-start | bytes 4325384 | tf_op jit(solution)/shard_map/cond/branch_1_fun/ppermute | solution.py:39
  431.8 16.9 %collective-permute-start.8 = (bf16[256,1408]{1,0:T(8,128)(2,1)S(1)}, bf16[256,1408]{1,0:T(8,128)(2,1)S(1)}, u32[]{:S(2)}, u32[]{:S(2)}) collective-permute-start(bf16[256,1408]{1,0:T(8,128)(2,1)S(1)} %slice.226), channel_id=1, source_target_pairs={{0,8},{4,12},{8,0},{12,4},{16,24},{20,28},{24,16},{28,20},{1,9},{5... | collective-permute-start | bytes 2162696 | tf_op jit(solution)/shard_map/cond/branch_1_fun/ppermute | solution.py:39
  433.3 16.6 %collective-permute-start.7 = (bf16[256,1408]{1,0:T(8,128)(2,1)S(1)}, bf16[256,1408]{1,0:T(8,128)(2,1)S(1)}, u32[]{:S(2)}, u32[]{:S(2)}) collective-permute-start(bf16[256,1408]{1,0:T(8,128)(2,1)S(1)} %slice.225), channel_id=1, source_target_pairs={{0,16},{4,20},{8,24},{12,28},{16,0},{20,4},{24,8},{28,12},{1,17},{... | collective-permute-start | bytes 2162696 | tf_op jit(solution)/shard_map/cond/branch_1_fun/ppermute | solution.py:39
  433.9 19.0 %collective-permute-start.10 = (bf16[4,128,2048]{2,1,0:T(8,128)(2,1)}, bf16[4,128,2048]{2,1,0:T(8,128)(2,1)S(1)}, u32[]{:S(2)}, u32[]{:S(2)}) collective-permute-start(bf16[4,128,2048]{2,1,0:T(8,128)(2,1)} %get-tuple-element.210), channel_id=1, source_target_pairs={{0,4},{4,0},{8,12},{12,8},{16,20},{20,16},{24,28},{28,24},{1,5},{5... | collective-permute-start | bytes 6291464 | tf_op jit(solution)/shard_map/cond/branch_1_fun/ppermute | solution.py:39
  452.9 29.5 %collective-permute-start.9 = (bf16[4,512,1408]{2,1,0:T(8,128)(2,1)}, bf16[4,512,1408]{2,1,0:T(8,128)(2,1)}, u32[]{:S(2)}, u32[]{:S(2)}) collective-permute-start(bf16[4,512,1408]{2,1,0:T(8,128)(2,1)} %branch_1_fun.43), channel_id=1, source_target_pairs={{0,4},{4,0},{8,12},{12,8},{16,20},{20,16},{24,28},{28,24},{1,5},{5... | collective-permute-start | bytes 17301512 | tf_op jit(solution)/shard_map/cond/branch_1_fun/ppermute | solution.py:39
  464.7 13.3 %collective-permute-start.14 = (bf16[128,2048]{1,0:T(8,128)(2,1)S(1)}, bf16[128,2048]{1,0:T(8,128)(2,1)S(1)}, u32[]{:S(2)}, u32[]{:S(2)}) collective-permute-start(bf16[128,2048]{1,0:T(8,128)(2,1)S(1)} %pad_maximum_fusion.5), channel_id=1, source_target_pairs={{0,16},{4,20},{8,24},{12,28},{16,0},{20,4},{24,8},{28,12},{1,17},{... | collective-permute-start | bytes 1572872 | tf_op jit(solution)/shard_map/cond/branch_1_fun/ppermute | solution.py:39
  465.5 13.0 %collective-permute-start.12 = (bf16[128,2048]{1,0:T(8,128)(2,1)S(1)}, bf16[128,2048]{1,0:T(8,128)(2,1)S(1)}, u32[]{:S(2)}, u32[]{:S(2)}) collective-permute-start(bf16[128,2048]{1,0:T(8,128)(2,1)S(1)} %pad_maximum_fusion.4), channel_id=1, source_target_pairs={{0,8},{4,12},{8,0},{12,4},{16,24},{20,28},{24,16},{28,20},{1,9},{5... | collective-permute-start | bytes 1572872 | tf_op jit(solution)/shard_map/cond/branch_1_fun/ppermute | solution.py:39
  482.4 24.4 %collective-permute-start.1 = (bf16[512,640]{1,0:T(8,128)(2,1)}, bf16[512,640]{1,0:T(8,128)(2,1)S(1)}, u32[]{:S(2)}, u32[]{:S(2)}) collective-permute-start(bf16[512,640]{1,0:T(8,128)(2,1)} %get-tuple-element.220.refs_0_), channel_id=1, source_target_pairs={{0,16},{4,20},{8,24},{12,28},{16,0},{20,4},{24,8},{28,12},{1,17},{... | collective-permute-start | bytes 1966088 | tf_op jit(solution)/shard_map/cond/branch_1_fun/ppermute | solution.py:39
  483.9 22.9 %collective-permute-start = (bf16[512,640]{1,0:T(8,128)(2,1)}, bf16[512,640]{1,0:T(8,128)(2,1)S(1)}, u32[]{:S(2)}, u32[]{:S(2)}) collective-permute-start(bf16[512,640]{1,0:T(8,128)(2,1)} %get-tuple-element.220.refs_0_), channel_id=1, source_target_pairs={{0,8},{4,12},{8,0},{12,4},{16,24},{20,28},{24,16},{28,20},{1,9},{5... | collective-permute-start | bytes 1966088 | tf_op jit(solution)/shard_map/cond/branch_1_fun/ppermute | solution.py:39
  (69 other events, 782.8 us)
Sparse Core Ops, SparseCore 0:
  10.6 58.1 all-gather.3
  70.4 105.4 all-gather.5
  177.4 57.4 all-gather.7
  237.1 54.8 reduce-scatter.3
  294.7 102.1 reduce-scatter.5
  399.6 52.6 reduce-scatter.7

commit v3 on v2

--- a/solution.py
+++ b/solution.py
@@ -58,36 +58,70 @@
     )(*pieces)
 
 
-def even_pieces(part, *meanwhile):
-    half = part.shape[0] // 32 * 16
-    by_x, by_y = lax.optimization_barrier((swap(part, 2), swap(part, 4), meanwhile))[:2]
-    far = lax.optimization_barrier((swap(by_x[:half], 4), swap(by_y[half:], 2)))
-    return (part, by_x, by_y, *far), ((0, 0), (1, 0), (2, 0), (3, 0), (3, half))
-
-
-def doubled(part):
+def after(value, *earlier):
+    return lax.optimization_barrier((value, *earlier))[0]
+
+
+def together(*chains):
+    results, values, live = [None] * len(chains), [None] * len(chains), list(range(len(chains)))
+    while live:
+        sent = {}
+        for i in live:
+            try:
+                sent[i] = chains[i].send(values[i])
+            except StopIteration as stop:
+                results[i] = stop.value
+        live = list(sent)
+        for i, value in lax.optimization_barrier(sent).items():
+            values[i] = value
+    return results
+
+
+def work(*parts):
+    results = []
+    for part in parts:
+        results.append((yield () if part is None else part()))
+    return results
+
+
+def held(value, steps):
+    for _ in range(steps):
+        value = yield value
+    return value
+
+
+def in_turn(*makers):
+    result = None
+    for maker in makers:
+        result = yield from maker(result)
+    return result
+
+
+def near_chain(part):
+    n = lax.axis_size("seq")
+    if n == 8 and part.shape[0] % 16 == 0:
+        half = part.shape[0] // 32 * 16
+        by_x, by_y = yield swap(part, 2), swap(part, 4)
+        far = yield swap(by_x[:half], 4), swap(by_y[half:], 2)
+        places = ((0, 0), (1, 0), (2, 0), (3, 0), (3, half))
+        return place_pieces((part, by_x, by_y, *far), places, (4,) + part.shape)
     mine, mask = part[None], 2
-    while mask < lax.axis_size("seq"):
-        mine = jnp.concatenate([mine, swap(mine, mask)])
+    while mask < n:
+        mine = jnp.concatenate([mine, (yield swap(mine, mask))])
         mask *= 2
     return mine
 
 
-def seq_halves(part, *meanwhile):
-    if lax.axis_size("seq") == 8 and part.shape[0] % 16 == 0:
-        pieces, places = even_pieces(part, *meanwhile)
-        mine = place_pieces(pieces, places, (4,) + part.shape)
-    else:
-        mine = doubled(part)
-    return mine, swap(mine, 1)
-
-
-def after(value, *earlier):
-    return lax.optimization_barrier((value, *earlier))[0]
-
-
-def seq_gather(part, *meanwhile):
-    mine, other = seq_halves(part, *meanwhile)
+def core_chain(mine):
+    return (yield mine, swap(mine, 1))
+
+
+def halves_chain(part):
+    return in_turn(lambda _: near_chain(part), core_chain)
+
+
+def gather_chain(part):
+    mine, other = yield from halves_chain(part)
     if part.shape[0] % 16:
         return jnp.concatenate([mine, other])
     half, rows, cols = mine.shape
@@ -107,13 +141,39 @@
     )(mine, other)
 
 
-def ring_sum(value):
+def ring_chain(value):
     n = lax.axis_size("fsdp")
     moving = value
     for _ in range(n - 1):
-        moving = lax.ppermute(moving, "fsdp", [(i, (i + 1) % n) for i in range(n)])
+        moving = yield lax.ppermute(moving, "fsdp", [(i, (i + 1) % n) for i in range(n)])
         value = value + moving
     return value
+
+
+def scatter_chain(make_odd, make_even):
+    n = lax.axis_size("seq")
+
+    def add(own, other):
+        return own.astype(jnp.float32) + other.astype(jnp.float32)
+
+    low = jnp.bfloat16
+    odd = make_odd()
+    even, other = yield make_even(), swap(odd, 1)
+    mine = add(even, other)
+    if n == 8:
+        half = even.shape[1] // 2
+        far = mine[3].astype(low)
+        from_x, from_y = yield swap(far[:half], 2), swap(far[half:], 4)
+        to_y = jnp.concatenate([add(mine[2][:half], from_x), mine[2][half:]]).astype(low)
+        to_x = jnp.concatenate([mine[1][:half], add(mine[1][half:], from_y)]).astype(low)
+        by_x, by_y = yield swap(to_x, 2), swap(to_y, 4)
+        return add(mine[0], by_x) + by_y.astype(jnp.float32)
+    mask = n // 2
+    while mask > 1:
+        count = mine.shape[0] // 2
+        mine = add(mine[:count], (yield swap(mine[count:].astype(low), mask)))
+        mask //= 2
+    return mine[0]
 
 
 def ordered(place, even, odd, body):
@@ -122,41 +182,33 @@
     pl.when(core == 1)(lambda: body(odd, even))
 
 
-def put_columns(even, odd, place, pieces, w_gate, w_up):
+def put_columns(even, odd, place, pieces, second):
     half, rows, cols = even.shape
     n, w = 2 * half, cols // (2 * pieces)
     tile = 64
 
-    def kernel(place_ref, even_ref, odd_ref, w_gate_ref, w_up_ref, gate_ref, up_ref, sums_ref):
+    def kernel(place_ref, even_ref, odd_ref, out_ref):
         chip = place_ref[0] // 2
 
-        def body(first, second):
-            blocks = [(second if t % 2 else first)[(t // 2) ^ chip] for t in range(n)]
-            sums = jnp.zeros((tile, 1), jnp.float32)
-            for target, weight, start in ((gate_ref, w_gate_ref, 0), (up_ref, w_up_ref, cols // 2)):
-                for f in range(pieces):
-                    at, to = start + f * w, slice(f * n * w, (f + 1) * n * w)
-                    row = jnp.concatenate([block[:, at : at + w] for block in blocks], axis=1)
-                    row = row.astype(jnp.float32)
-                    target[:, to] = row
-                    sums += jnp.sum(row * weight[:, to].astype(jnp.float32), axis=1, keepdims=True)
-            sums_ref[...] = sums
+        def body(first, other):
+            blocks = [(other if t % 2 else first)[(t // 2) ^ chip] for t in range(n)]
+            for f in range(pieces):
+                at = (second * pieces + f) * w
+                row = jnp.concatenate([block[:, at : at + w] for block in blocks], axis=1)
+                out_ref[:, f * n * w : (f + 1) * n * w] = row.astype(jnp.float32)
 
         ordered(place_ref[0], even_ref, odd_ref, body)
 
     spec = pl.BlockSpec((half, tile, cols), lambda i: (0, i, 0))
-    wide = jax.ShapeDtypeStruct((rows, pieces * n * w), jnp.float32)
     return pl.pallas_call(
         kernel,
         grid=(rows // tile,),
-        out_shape=(wide, wide, jax.ShapeDtypeStruct((rows, 1), jnp.float32)),
-        in_specs=[pl.BlockSpec(memory_space=pltpu.SMEM), spec, spec]
-        + [pl.BlockSpec((tile, pieces * n * w), lambda i: (i, 0))] * 2,
-        out_specs=[pl.BlockSpec((tile, pieces * n * w), lambda i: (i, 0))] * 2
-        + [pl.BlockSpec((tile, 1), lambda i: (i, 0))],
+        out_shape=jax.ShapeDtypeStruct((rows, pieces * n * w), jnp.float32),
+        in_specs=[pl.BlockSpec(memory_space=pltpu.SMEM), spec, spec],
+        out_specs=pl.BlockSpec((tile, pieces * n * w), lambda i: (i, 0)),
         compiler_params=pltpu.CompilerParams(vmem_limit_bytes=48 * 2**20),
-        cost_estimate=pl.CostEstimate(flops=0, bytes_accessed=even.size * 12, transcendentals=0),
-    )(place, even, odd, w_gate, w_up)
+        cost_estimate=pl.CostEstimate(flops=0, bytes_accessed=even.size * 8, transcendentals=0),
+    )(place, even, odd)
 
 
 def put_rows(even, odd, place):
@@ -185,14 +237,13 @@
     )(place, even, odd)
 
 
-def put_attention(even, odd, place, weights, q_cols, out_cols):
+def put_attention(even, odd, place, q_cols, out_cols):
     half, rows, cols = even.shape
-    n, tile = 2 * half, 128
+    n, tile = 2 * half, 64
     copies = n // KV_HEADS
     sizes = (n * q_cols, KV_HEADS * HEAD_DIM, KV_HEADS * HEAD_DIM, n * out_cols)
 
-    def kernel(place_ref, even_ref, odd_ref, wq_ref, wk_ref, wv_ref, *refs):
-        query_ref, key_ref, value_ref, out_ref, sums_ref = refs
+    def kernel(place_ref, even_ref, odd_ref, query_ref, key_ref, value_ref, out_ref):
         chip = place_ref[0] // 2
 
         def body(first, second):
@@ -208,10 +259,6 @@
             ]
             key_ref[...] = jnp.concatenate([part[:, :HEAD_DIM] for part in sums], axis=1)
             value_ref[...] = jnp.concatenate([part[:, HEAD_DIM:] for part in sums], axis=1)
-            sums_ref[...] = sum(
-                jnp.sum(ref[...] * weight[...].astype(jnp.float32), axis=1, keepdims=True)
-                for ref, weight in ((query_ref, wq_ref), (key_ref, wk_ref), (value_ref, wv_ref))
-            )
 
         ordered(place_ref[0], even_ref, odd_ref, body)
 
@@ -219,36 +266,12 @@
     return pl.pallas_call(
         kernel,
         grid=(rows // tile,),
-        out_shape=[jax.ShapeDtypeStruct((rows, size), jnp.float32) for size in (*sizes, 1)],
-        in_specs=[pl.BlockSpec(memory_space=pltpu.SMEM), spec, spec]
-        + [pl.BlockSpec((tile, size), lambda i: (i, 0)) for size in sizes[:3]],
-        out_specs=[pl.BlockSpec((tile, size), lambda i: (i, 0)) for size in (*sizes, 1)],
+        out_shape=[jax.ShapeDtypeStruct((rows, size), jnp.float32) for size in sizes],
+        in_specs=[pl.BlockSpec(memory_space=pltpu.SMEM), spec, spec],
+        out_specs=[pl.BlockSpec((tile, size), lambda i: (i, 0)) for size in sizes],
         compiler_params=pltpu.CompilerParams(vmem_limit_bytes=48 * 2**20),
         cost_estimate=pl.CostEstimate(flops=0, bytes_accessed=even.size * 12, transcendentals=0),
-    )(place, even, odd, *weights)
-
-
-def seq_scatter(even, odd):
-    n = lax.axis_size("seq")
-
-    def add(own, other):
-        return own.astype(jnp.float32) + other.astype(jnp.float32)
-
-    low = jnp.bfloat16
-    mine = add(even, swap(odd, 1))
-    if n == 8:
-        half = even.shape[1] // 2
-        far = mine[3].astype(low)
-        from_x, from_y = swap(far[:half], 2), swap(far[half:], 4)
-        to_y = jnp.concatenate([add(mine[2][:half], from_x), mine[2][half:]]).astype(low)
-        to_x = jnp.concatenate([mine[1][:half], add(mine[1][half:], from_y)]).astype(low)
-        return mine[0] + swap(to_x, 2).astype(jnp.float32) + swap(to_y, 4).astype(jnp.float32)
-    mask = n // 2
-    while mask > 1:
-        count = mine.shape[0] // 2
-        mine = add(mine[:count], swap(mine[count:].astype(low), mask))
-        mask //= 2
-    return mine[0]
+    )(place, even, odd)
 
 
 def slot_of(mask, n):
@@ -278,9 +301,9 @@
     )(place, *parts)
 
 
-def seq_exchange(even, odd):
+def exchange_chain(even, odd):
     half, rows, cols = even.shape
-    other = swap(odd, 1)
+    other = yield swap(odd, 1)
 
     def kernel(even_ref, other_ref, *refs):
         for k, ref in enumerate(refs):
@@ -294,7 +317,7 @@
         in_specs=[vmem] * 2,
         out_specs=[vmem] * half,
     )(even, other)
-    return [pair if k == 0 else swap(pair, 2 * k) for k, pair in enumerate(pairs)]
+    return (yield [pair if k == 0 else swap(pair, 2 * k) for k, pair in enumerate(pairs)])
 
 
 def join_columns(pairs, place):
@@ -603,32 +626,36 @@
     )(dy, down, pre)
 
 
-def attention_terms(normed, grad_qkv, attended, grad_proj):
-    rows, width = normed.shape
-    sizes = grad_qkv.shape[1], grad_proj.shape[1]
+def row_products(*pairs):
+    rows, width = pairs[0][0].shape
+    sizes = [right.shape[1] for _, right in pairs]
     tile = 512
 
-    def kernel(normed_ref, grad_qkv_ref, attended_ref, grad_proj_ref, out_ref):
-        low = jnp.bfloat16
-        out_ref[:, : sizes[0]] = matmul(normed_ref[...], grad_qkv_ref[...], COLUMNS_OF).astype(low)
-        out_ref[:, sizes[0] :] = matmul(attended_ref[...], grad_proj_ref[...], COLUMNS_OF).astype(low)
+    def kernel(*refs):
+        at = 0
+        for i, size in enumerate(sizes):
+            product = matmul(refs[2 * i][...], refs[2 * i + 1][...], COLUMNS_OF)
+            refs[-1][:, at : at + size] = product.astype(jnp.bfloat16)
+            at += size
 
     return pl.pallas_call(
         kernel,
         grid=(width // tile,),
         out_shape=jax.ShapeDtypeStruct((width, sum(sizes)), jnp.bfloat16),
         in_specs=[
-            pl.BlockSpec((rows, tile), lambda i: (0, i)),
-            pl.BlockSpec((rows, sizes[0]), lambda i: (0, 0)),
-            pl.BlockSpec((rows, tile), lambda i: (0, i)),
-            pl.BlockSpec((rows, sizes[1]), lambda i: (0, 0)),
+            spec
+            for size in sizes
+            for spec in (
+                pl.BlockSpec((rows, tile), lambda i: (0, i)),
+                pl.BlockSpec((rows, size), lambda i: (0, 0)),
+            )
         ],
         out_specs=pl.BlockSpec((tile, sum(sizes)), lambda i: (i, 0)),
         compiler_params=pltpu.CompilerParams(vmem_limit_bytes=48 * 2**20),
         cost_estimate=pl.CostEstimate(
             flops=2 * rows * width * sum(sizes), bytes_accessed=rows * width * 4, transcendentals=0
         ),
-    )(normed, grad_qkv, attended, grad_proj)
+    )(*[array for pair in pairs for array in pair])
 
 
 def stage(sure, body, *args):
@@ -692,37 +719,43 @@
 
     place_arg = place.reshape(1).astype(jnp.int32)
     kv_head = place // kv_copies
-    attn_full = z_gather(
-        jnp.concatenate(
-            [
-                columns(w_query, place * q_cols, q_cols),
-                columns(w_key, kv_head * HEAD_DIM, HEAD_DIM),
-                columns(w_value, kv_head * HEAD_DIM, HEAD_DIM),
-                columns(w_out, place * out_cols, out_cols),
-            ],
-            axis=1,
-        )
-    )
+    attn_own = jnp.concatenate(
+        [
+            columns(w_query, place * q_cols, q_cols),
+            columns(w_key, kv_head * HEAD_DIM, HEAD_DIM),
+            columns(w_value, kv_head * HEAD_DIM, HEAD_DIM),
+            columns(w_out, place * out_cols, out_cols),
+        ],
+        axis=1,
+    )
+    attn_full = z_gather(attn_own)
     attn_full, out_part = attn_full[:, :-out_cols], attn_full[:, -out_cols:]
-    mlp_full = z_gather(
-        jnp.concatenate(
-            [columns_of(w_gate, place, groups, shards), columns_of(w_up, place, groups, shards)],
-            axis=1,
-        )
-    )
+    mlp_own = jnp.concatenate(
+        [columns_of(w_gate, place, groups, shards), columns_of(w_up, place, groups, shards)], axis=1
+    )
+    mlp_full = z_gather(mlp_own)
     down_rows = w_down.shape[0] // groups
     down_full = z_gather(lax.dynamic_slice_in_dim(w_down, place * down_rows, down_rows, 0))
     sure = positions[0, 0] >= 0
     own = tokens[0]
     gains_own = jnp.stack([gain_attn, gain_mlp]).astype(wide)
 
+    halves = (slice(seq_len // 2, None), slice(0, seq_len // 2))
+
+    def by_halves(product):
+        def half(at):
+            return product(at).astype(low).reshape(groups // 2, tok_rows, width)
+
+        return scatter_chain(lambda: half(halves[0]), lambda: half(halves[1]))
+
     def inputs_stage(own, positions, gains_own):
         gains = lax.dynamic_update_slice(
             jnp.zeros((2, width), wide), gains_own, (0, shard * shard_rows)
         )
-        gains = ring_sum(gains)
-        where = seq_gather(positions).reshape(seq_len)
-        stream = seq_gather(own, gains, where).reshape(seq_len, width).astype(wide)
+        gains, where, stream = together(
+            ring_chain(gains), gather_chain(positions), gather_chain(own)
+        )
+        where, stream = where.reshape(seq_len), stream.reshape(seq_len, width).astype(wide)
         cosine, sine = rope_tables(where, HEAD_DIM)
         cosine, sine = cosine.reshape(groups, tok_rows, 128), sine.reshape(groups, tok_rows, 128)
         inverse_all = lax.rsqrt(jnp.mean(stream * stream, axis=-1, keepdims=True) + EPS)
@@ -733,115 +766,152 @@
     gain_in, gain_mid = gains
 
     def attention_stage(own, cotangent, normed_in, attn_full, out_part, cosine, sine, gain_mid):
-        qkv = jnp.dot(normed_in, attn_full, preferred_element_type=wide)
-        attended_send, *kept = attention(
-            qkv.reshape(groups, tok_rows, -1), cosine, sine, place_arg, heads_dev
+        def attend(_):
+            qkv = jnp.dot(normed_in, attn_full, preferred_element_type=wide)
+            return (
+                yield attention(
+                    qkv.reshape(groups, tok_rows, -1), cosine, sine, place_arg, heads_dev
+                )
+            )
+
+        def exchange(attended):
+            pairs = yield from exchange_chain(*attended[0])
+            return join_columns(pairs, place_arg), attended[1:]
+
+        def project(results):
+            attended_tok, kept = results
+            while not out_box:
+                yield ()
+            out_full = join_weight(*out_box[0], place_arg)
+            middle = own.astype(wide) + jnp.dot(attended_tok, out_full, preferred_element_type=wide)
+            inverse_mid = lax.rsqrt(jnp.mean(middle * middle, axis=-1, keepdims=True) + EPS)
+            normed_mid = yield from gather_chain((middle * inverse_mid * gain_mid).astype(low))
+            return attended_tok, out_full, middle, normed_mid.reshape(seq_len, width), kept
+
+        out_box = []
+
+        def weight():
+            out_box.append((yield from halves_chain(out_part)))
+
+        _, results, (_, dy) = together(
+            weight(),
+            in_turn(attend, exchange, project),
+            in_turn(lambda _: held(cotangent, 1), lambda later: pair_chain(gather_chain(later))),
         )
-        attended_tok = join_columns(seq_exchange(*attended_send), place_arg)
-        out_even, out_odd = seq_halves(out_part, attended_send[0])
-        out_full = join_weight(out_even, out_odd, place_arg)
-        dy = seq_gather(after(cotangent, out_even)).reshape(seq_len, width)
-        middle = own.astype(wide) + jnp.dot(attended_tok, out_full, preferred_element_type=wide)
+        return *results, dy.reshape(seq_len, width)
+
+    def pair_chain(chain):
+        return None, (yield from chain)
+
+    attended_tok, out_full, middle, normed_mid, kept, dy = stage(
+        sure, attention_stage, own, cotangent[0], normed_in, attn_full, out_part, cosine, sine, gain_mid
+    )
+
+    def hidden_stage(normed_mid, mlp_full, dy, attended_tok):
+        def products():
+            mlp_pre, hidden = yield hidden_units(normed_mid, mlp_full)
+            down_grad = yield dot(hidden, dy, ((0,), (0,))).astype(low)
+            return mlp_pre, hidden, down_grad
+
+        results, attended_all = together(products(), gather_chain(attended_tok))
+        return attended_all.reshape(seq_len, -1), *results
+
+    attended_all, mlp_pre, hidden, down_grad = stage(
+        sure, hidden_stage, normed_mid, mlp_full, dy, attended_tok
+    )
+    down_sum = z_scatter(down_grad)
+    grad_mlp = hidden_back(after(dy, down_grad), down_full, mlp_pre)
+
+    def middle_stage(grad_mlp, mlp_full, normed_mid, middle, dy_own, gain_mid, out_full):
         inverse_mid = lax.rsqrt(jnp.mean(middle * middle, axis=-1, keepdims=True) + EPS)
         unit_mid = middle * inverse_mid
-        normed_mid = seq_gather((unit_mid * gain_mid).astype(low)).reshape(seq_len, width)
-        return attended_tok, out_full, middle, normed_mid, dy, kept
-
-    attended_tok, out_full, middle, normed_mid, dy, kept = stage(
-        sure, attention_stage, own, cotangent[0], normed_in, attn_full, out_part, cosine, sine, gain_mid
-    )
-
-    def hidden_stage(normed_mid, mlp_full, dy, attended_tok):
-        mlp_pre, hidden = hidden_units(normed_mid, mlp_full)
-        attended_all = seq_gather(attended_tok, hidden).reshape(seq_len, -1)
-        return attended_all, mlp_pre, hidden, dot(hidden, dy, ((0,), (0,))).astype(low)
-
-    attended_all, mlp_pre, hidden, down_grad = stage(
-        sure, hidden_stage, normed_mid, mlp_full, dy, attended_tok
-    )
-    down_sum = z_scatter(down_grad)
-    grad_mlp = hidden_back(after(dy, down_grad), down_full, mlp_pre)
-    halves = (slice(0, seq_len // 2), slice(seq_len // 2, None))
-
-    def by_halves(product):
-        return [product(at).astype(low).reshape(groups // 2, tok_rows, width) for at in halves]
-
-    mlp_grad = dot(normed_mid, grad_mlp, ((0,), (0,))).astype(low)
-    mlp_sum = z_scatter(mlp_grad)
-
-    def middle_stage(
-        grad_mlp, mlp_full, hidden, down_full, middle, dy_own, gain_mid, out_full, mlp_grad
-    ):
-        inverse_mid = lax.rsqrt(jnp.mean(middle * middle, axis=-1, keepdims=True) + EPS)
-        unit_mid = middle * inverse_mid
-        terms = by_halves(lambda at: dot(grad_mlp[at], mlp_full, ((1,), (1,))))
-        grad_normed_mid = seq_scatter(*terms)
+        grad_normed_mid, results = together(
+            by_halves(lambda at: dot(grad_mlp[at], mlp_full, ((1,), (1,)))),
+            work(None, None, lambda: row_products((normed_mid, grad_mlp))),
+        )
         grad_middle = norm_back(grad_normed_mid * gain_mid, unit_mid, inverse_mid)
         grad_middle = grad_middle + dy_own.astype(wide)
         grad_proj = grad_middle.astype(low)
         grad_attended = dot(grad_proj, out_full, ((1,), (1,))).astype(low)
         grad_even, grad_odd = split_columns((grad_attended, grad_proj), place_arg, groups)
-        later = after(hidden, tuple(terms))
-        down_terms = by_halves(
-            lambda at: jnp.dot(later[at], down_full, preferred_element_type=wide)
-        )
-        layer_out = (middle + seq_scatter(*down_terms)).astype(low)
-        return grad_middle, layer_out, grad_even, grad_odd
-
-    grad_middle, layer_out, grad_even, grad_odd = stage(
-        sure, middle_stage, grad_mlp, mlp_full, hidden, down_full, middle, cotangent[0], gain_mid, out_full,
-        mlp_grad[:16],
-    )
+        return grad_middle, grad_even, grad_odd, results[-1]
+
+    grad_middle, grad_even, grad_odd, mlp_grad = stage(
+        sure, middle_stage, grad_mlp, mlp_full, normed_mid, middle, cotangent[0], gain_mid, out_full
+    )
+    mlp_sum = z_scatter(mlp_grad)
 
     def back_stage(
-        grad_even, grad_odd, attended_all, normed_in, attn_full, cosine, sine, kept, down_sum
+        grad_even, grad_odd, attended_all, normed_in, cosine, sine, kept, down_sum, own, attn_full,
+        gain_in, grad_middle, hidden, down_full, middle,
     ):
         wide_out, rotated, tops, sums = kept
-        grad_pairs = seq_exchange(grad_even, grad_odd)
-        grad_qkv, grad_proj_cols = attention_back(
-            grad_pairs, rotated, wide_out, tops, sums, cosine, sine, place_arg
+
+        def back(pairs):
+            grad_qkv, grad_proj_cols = yield attention_back(
+                pairs, rotated, wide_out, tops, sums, cosine, sine, place_arg
+            )
+            grad_qkv = grad_qkv.reshape(seq_len, -1)
+            terms = yield row_products(
+                (normed_in, grad_qkv), (attended_all, grad_proj_cols.reshape(seq_len, out_cols))
+            )
+            grad_normed_in = yield from by_halves(
+                lambda at: dot(grad_qkv[at], attn_full, ((1,), (1,)))
+            )
+            return grad_normed_in, terms
+
+        (grad_normed_in, attn_terms), down_halves, down_term = together(
+            in_turn(lambda _: exchange_chain(grad_even, grad_odd), back),
+            in_turn(lambda _: held(down_sum, 2), halves_chain),
+            in_turn(
+                lambda _: held(hidden, 2),
+                lambda later: by_halves(
+                    lambda at: jnp.dot(later[at], down_full, preferred_element_type=wide)
+                ),
+            ),
         )
-        grad_qkv = grad_qkv.reshape(seq_len, -1)
-        grad_proj_cols = grad_proj_cols.reshape(seq_len, out_cols)
-        attn_terms = attention_terms(normed_in, grad_qkv, attended_all, grad_proj_cols)
-        terms_in = by_halves(lambda at: dot(grad_qkv[at], attn_full, ((1,), (1,))))
-        down_even, down_odd = seq_halves(after(down_sum, tuple(grad_pairs)), attn_terms)
-        return attn_terms, terms_in, down_even, down_odd
-
-    attn_terms, terms_in, down_even, down_odd = stage(
-        sure, back_stage, grad_even, grad_odd, attended_all, normed_in, attn_full, cosine, sine, kept,
-        after(down_sum, grad_even),
-    )
-
-    attn_sum = z_scatter(attn_terms)
-
-    def tokens_stage(own, even, odd, gain_in, grad_middle, down_even, down_odd, mlp_sum):
-        grad_normed_in = seq_scatter(even, odd)
         stream_own = own.astype(wide)
         inverse_in = lax.rsqrt(jnp.mean(stream_own * stream_own, axis=-1, keepdims=True) + EPS)
         unit_in = stream_own * inverse_in
         grad_stream = norm_back(grad_normed_in * gain_in, unit_in, inverse_in) + grad_middle
-        grad_down = put_rows(down_even, down_odd, place_arg)
-        return grad_stream, grad_down, *seq_halves(mlp_sum, grad_down)
-
-    grad_stream, grad_down, mlp_even, mlp_odd = stage(
-        sure, tokens_stage, own, *terms_in, gain_in, grad_middle, down_even, down_odd,
-        after(mlp_sum, attn_terms),
-    )
-
-    def last_stage(mlp_even, mlp_odd, w_gate, w_up, attn_sum):
-        grads = put_columns(mlp_even, mlp_odd, place_arg, shards, w_gate, w_up)
-        return grads, seq_halves(attn_sum, grads)
-
-    (grad_gate, grad_up, rows_mid), attn_halves = stage(
-        sure, last_stage, mlp_even, mlp_odd, w_gate, w_up, attn_sum
-    )
-    grad_query, grad_key, grad_value, grad_out, rows_in = put_attention(
-        *attn_halves,
-        place_arg,
-        (w_query, w_key, w_value),
-        q_cols,
-        out_cols,
+        return grad_stream, attn_terms, (middle + down_term).astype(low), *down_halves
+
+    grad_stream, attn_terms, layer_out, down_even, down_odd = stage(
+        sure, back_stage, grad_even, grad_odd, attended_all, normed_in, cosine, sine, kept,
+        after(down_sum, grad_even), own, attn_full, gain_in, grad_middle, hidden, down_full, middle,
+    )
+
+    attn_sum = z_scatter(attn_terms)
+
+    def output_stage(down_even, down_odd, mlp_sum):
+        (grad_down,), mine = together(
+            work(lambda: put_rows(down_even, down_odd, place_arg)), near_chain(mlp_sum)
+        )
+        return grad_down, mine
+
+    grad_down, mine = stage(sure, output_stage, down_even, down_odd, after(mlp_sum, attn_terms))
+
+    def last_stage(mine, mlp_sum, mlp_own, attn_sum, attn_own):
+        def columns_put():
+            even, odd = yield from core_chain(mine)
+            gate = yield put_columns(even, odd, place_arg, shards, 0)
+            up = yield put_columns(even, odd, place_arg, shards, 1)
+            return gate, up
+
+        def sums_chain():
+            pairs = ((attn_sum[:, :-out_cols], attn_own[:, :-out_cols]), (mlp_sum, mlp_own))
+            sums = [jnp.sum(a.astype(wide) * b.astype(wide), axis=1) for a, b in pairs]
+            sums, mask = jnp.stack(sums), 1
+            while mask < groups:
+                sums = sums + (yield swap(sums, mask))
+                mask *= 2
+            return sums
+
+        puts, attn_halves, sums = together(columns_put(), halves_chain(attn_sum), sums_chain())
+        return *puts, sums, *put_attention(*attn_halves, place_arg, q_cols, out_cols)
+
+    grad_gate, grad_up, row_sums, grad_query, grad_key, grad_value, grad_out = stage(
+        sure, last_stage, mine, mlp_sum, mlp_own, after(attn_sum, grad_down), attn_own
     )
     return (
         layer_out[None],
@@ -850,11 +920,11 @@
         grad_key,
         grad_value,
         grad_out,
-        rows_in[:, 0] / gain_attn.astype(wide),
+        row_sums[0] / gain_attn.astype(wide),
         grad_gate,
         grad_up,
         grad_down,
-        rows_mid[:, 0] / gain_mlp.astype(wide),
+        row_sums[1] / gain_mlp.astype(wide),
     )
 
 

time: 545 us -> 517 us (0.949)
  waiting for transfers between devices: 223 us -> 192 us
  matrix products: 57.4 us -> 42.7 us
  Pallas kernels: 132 us -> 142 us
  starting transfers between devices: 59.6 us -> 68.6 us
  local copies, waits for them, and re-layouts: 23.9 us -> 18.3 us
    dot_general x7 -> x6, matrix products: 41.9 us -> 24.8 us  [dot(): lax.dot_general(left, right, ((dims[0], dims[1]), ((), ())), preferred_el...]
    ppermute x66 -> x69, waiting for transfers between devices: 193 us -> 182 us  [swap(): lax.ppermute(value, 'seq', [(i, i ^ mask) for i in range(lax.axis_size('s...]
    ppermute x3, waiting for transfers between devices: 12.1 us -> 2.32 us  [ring_chain(): lax.ppermute(moving, 'fsdp', [(i, (i + 1) % n) for i in range(n)])]
    reduce_scatter x3, waiting for transfers between devices: 11.7 us -> 2.17 us  [z_scatter(): return lax.psum_scatter(part, 'fsdp', scatter_dimension=0, tiled=True)]
    ppermute x66 -> x69, starting transfers between devices: 56.1 us -> 63.6 us  [swap(): lax.ppermute(value, 'seq', [(i, i ^ mask) for i in range(lax.axis_size('s...]
    pallas_call x8 -> x10, Pallas kernels: 52 us -> 59.4 us  [the longest x4 19.6 us: gather_chain(): pl.pallas_call(kernel, grid=(cols // tile,), out_shape=jax.ShapeDtypeStru...]
  transfers between devices with their start and end apart: 75 -> 78, of which waited for: 50 -> 47; matrix products, arithmetic and copies ran while one was open for 17% -> 16% of each run, Pallas kernels for 23% -> 27%
where the time goes in v3:
time: 517 us; the launch traced here: 509 us
  waiting for transfers between devices  192 us (37%)
  Pallas kernels  142 us (27%)
  starting transfers between devices  68.6 us (13%)
  matrix products  42.7 us (8%)
  other arithmetic  29.2 us (6%)
  local copies, waits for them, and re-layouts  18.3 us (4%)
  between operations  14.8 us (3%)
    ppermute x69, waiting for transfers between devices, swap(): lax.ppermute(value, 'seq', [(i, i ^ mask) for i in range(lax.axis_size('s...  182 us
    ppermute x69, starting transfers between devices, swap(): lax.ppermute(value, 'seq', [(i, i ^ mask) for i in range(lax.axis_size('s...  63.6 us
    dot_general x6, matrix products, dot(): lax.dot_general(left, right, ((dims[0], dims[1]), ((), ())), preferred_el...  24.8 us
    pallas_call x4, Pallas kernels, gather_chain(): pl.pallas_call(kernel, grid=(cols // tile,), out_shape=jax.ShapeDtypeStru...  19.6 us
    pallas_call x2, Pallas kernels, put_columns(): pl.pallas_call(kernel, grid=(rows // tile,), out_shape=jax.ShapeDtypeStru...  18.8 us
    pallas_call x2, Pallas kernels, row_products(): pl.pallas_call(kernel, grid=(width // tile,), out_shape=jax.ShapeDtypeStr...  17.1 us
    pallas_call x8, Pallas kernels, place_pieces(): pl.pallas_call(kernel, grid=(cols // tile,), out_shape=jax.ShapeDtypeStru...  14.6 us
    pallas_call x1, Pallas kernels, attention_back(): pl.pallas_call(kernel, out_shape=[jax.ShapeDtypeStruct((n, rows, cols), l...  12.8 us
  transfers between devices with their start and end apart: 78, of which 47 were waited for; matrix products, arithmetic and copies ran while one was open for 16% of the time, Pallas kernels for 27%

profile of v3, /device:TPU:0, one launch (start us, length us, event | category | flops | bytes accessed | tf_op | source)
XLA Modules:
  0.0 509.0 jit_solution(2035929166230723703)
XLA Ops:
  18.2 50.2 %conditional.7 = (f32[2,2048]{1,0:T(2,128)}, f32[8,128,128]{2,1,0:T(8,128)}, f32[8,128,128]{2,1,0:T(8,128)}, bf16[1024,2048]{1,0:T(8,128)(2,1)}, f32[1,2048]{1,0:T(1,128)S(1)}, /*index=5*/f32[1,2048]{1,0:T(1,128)}) conditional(s32[]{:T(128)} %bitcast.47, () %tuple.104, (s32[]{:T(128)}, f32[2,512]{1,0:T(2,128)S(1)}, s32[1,128]{1,0:T(1,128)S(1)}, ...), branch_computations={%region_0.1_spmd, %region_1.3_spmd} | conditional | flops 14957828 | bytes 78052016 | solution.py:667
  24.9 9.8 %collective-permute-done.5 = s32[1,1,128]{2,1,0:T(1,128)S(1)} collective-permute-done((s32[1,1,128]{2,1,0:T(1,128)S(1)}, s32[1,1,128]{2,1,0:T(1,128)S(1)}, u32[]{:S(2)}, u32[]{:S(2)}) %collective-permute-start.5) | collective-permute-done | bytes 544 | tf_op jit(solution)/shard_map/cond/branch_1_fun/ppermute | solution.py:39
  53.5 4.7 branch_1_fun.27
  61.6 3.7 fusion.1
  71.9 123.6 %conditional.8 = (bf16[128,2048]{1,0:T(8,128)(2,1)}, bf16[2048,2048]{1,0:T(8,128)(2,1)}, f32[128,2048]{1,0:T(8,128)}, bf16[1024,2048]{1,0:T(8,128)(2,1)}, f32[10...) conditional(s32[]{:T(128)} %bitcast.47, () %tuple.103, ...), branch_computations={%region_3.4_spmd, %region_4.6_spmd} | conditional | flops 3759931648 | bytes 181939232 | solution.py:667
  76.3 5.0 fusion.49
  81.4 9.7 %branch_1_fun.28 = (bf16[4,128,256]{2,1,0:T(8,128)(2,1)S(1)}, bf16[4,128,256]{2,1,0:T(8,128)(2,1)S(1)}, f32[1024,256]{1,0:T(8,128)}, bf16[1024,384]{1,0:T(8,128)...) custom-call(s32[1]{0:T(128)} %get-tuple-element.130.place_ref, f32[8,128,384]{2,1,0:T(8,128)S(1)} %bitcast.156, ...), custom_call_target="tpu_custom_call" | custom-call | flops 1073741824 | bytes 3145728 | tf_op jit(solution)/shard_map/cond/branch_1_fun/pallas_call | solution.py:453
  91.1 7.4 %collective-permute-done.16.refs_2_ = bf16[2048,256]{1,0:T(8,128)(2,1)S(1)} collective-permute-done((bf16[2048,256]{1,0:T(8,128)(2,1)S(1)}, bf16[2048,256]{1,0:T(8,128)(2,1)S(1)}, u32[]{:S(2)}, u32[]{:S(2)}) %collective-permute-start.16) | collective-permute-done | bytes 1048608 | tf_op jit(solution)/shard_map/cond/branch_1_fun/ppermute | solution.py:39
  105.4 9.3 %collective-permute-done.18.refs_4_ = bf16[1024,256]{1,0:T(8,128)(2,1)S(1)} collective-permute-done((bf16[1024,256]{1,0:T(8,128)(2,1)S(1)}, bf16[1024,256]{1,0:T(8,128)(2,1)S(1)}, u32[]{:S(2)}, u32[]{:S(2)}) %collective-permute-start.18) | collective-permute-done | bytes 524320 | tf_op jit(solution)/shard_map/cond/branch_1_fun/ppermute | solution.py:39
  115.9 8.6 %collective-permute-done.21.refs_2_ = bf16[128,2048]{1,0:T(8,128)(2,1)S(1)} collective-permute-done((bf16[128,2048]{1,0:T(8,128)(2,1)S(1)}, bf16[128,2048]{1,0:T(8,128)(2,1)S(1)}, u32[]{:S(2)}, u32[]{:S(2)}) %collective-permute-start.21) | collective-permute-done | bytes 524320 | tf_op jit(solution)/shard_map/cond/branch_1_fun/ppermute | solution.py:39
  136.1 8.5 %collective-permute-done.24.refs_2_ = bf16[2,128,256]{2,1,0:T(8,128)(2,1)S(1)} collective-permute-done((bf16[2,128,256]{2,1,0:T(8,128)(2,1)}, bf16[2,128,256]{2,1,0:T(8,128)(2,1)S(1)}, u32[]{:S(2)}, u32[]{:S(2)}) %collective-permute-start.24) | collective-permute-done | bytes 131104 | tf_op jit(solution)/shard_map/cond/branch_1_fun/ppermute | solution.py:39
  146.9 7.1 %branch_1_fun.32 = bf16[2048,2048]{1,0:T(8,128)(2,1)} custom-call(s32[1]{0:T(128)} %get-tuple-element.130.place_ref, bf16[4,2048,256]{2,1,0:T(8,128)(2,1)S(1)} %copy-done, bf16[4,2048,256]{2,1,0:T(8,128)(2,1)} %collective-permute-done.22.odd_ref), custom_call_target="tpu_custom_call" | custom-call | bytes 16777216 | tf_op jit(solution)/shard_map/cond/branch_1_fun/pallas_call | solution.py:352
  156.0 5.9 %multiply_reduce_fusion.1 = (f32[128]{0:T(128)S(1)}, f32[128,2048]{1,0:T(8,128)}) fusion(bf16[128,2048]{1,0:T(8,128)(2,1)} %branch_1_fun.31, bf16[2048,2048]{1,0:T(8,128)(2,1)} %branch_1_fun.32, bf16[128,2048]{1,0:T(8,128)(2,1)S(1)} %copy-done.13), kind=kOutput, calls=%fused_computation.22 | convolution fusion | flops 1074790272 | bytes 10486272 | tf_op jit(solution)/shard_map/cond/branch_1_fun/dot_general | solution.py:786
  164.7 12.1 %collective-permute-done.29.refs_2_ = bf16[128,2048]{1,0:T(8,128)(2,1)S(1)} collective-permute-done((bf16[128,2048]{1,0:T(8,128)(2,1)S(1)}, bf16[128,2048]{1,0:T(8,128)(2,1)S(1)}, u32[]{:S(2)}, u32[]{:S(2)}) %collective-permute-start.29) | collective-permute-done | bytes 524320 | tf_op jit(solution)/shard_map/cond/branch_1_fun/ppermute | solution.py:39
  179.6 4.7 collective-permute-done.32.refs_4_
  185.4 5.4 %branch_1_fun.36 = bf16[8,128,2048]{2,1,0:T(8,128)(2,1)} custom-call(bf16[4,128,2048]{2,1,0:T(8,128)(2,1)} %copy-done.1, bf16[4,128,2048]{2,1,0:T(8,128)(2,1)} %collective-permute-done.30.other_ref), custom_call_target="tpu_custom_call" | custom-call | bytes 8388608 | tf_op jit(solution)/shard_map/cond/branch_1_fun/pallas_call | solution.py:134
  190.8 4.7 branch_1_fun.35
  195.5 36.2 %conditional.9 = (bf16[1024,2048]{1,0:T(8,128)(2,1)}, f32[1024,1408]{1,0:T(8,128)}, bf16[1024,704]{1,0:T(8,128)(2,1)}, bf16[704,2048]{1,0:T(8,128)(2,1)}) conditional(s32[]{:T(128)} %bitcast.47, () %tuple.107, (bf16[1024,2048]{1,0:T(8,128)(2,1)}, bf16[2048,1408]{1,0:T(8,128)(2,1)}, bf16[128,2048]{1,0:T(8,128)(2,1)}, ...), branch_computations={%region_6.7_spmd, %region_7.8_spmd} | conditional | flops 8859811840 | bytes 56754436 | solution.py:667
  198.4 11.9 %branch_1_fun.37 = (f32[1024,1408]{1,0:T(8,128)}, bf16[1024,704]{1,0:T(8,128)(2,1)}) custom-call(bf16[1024,2048]{1,0:T(8,128)(2,1)} %get-tuple-element.180.normed_ref, bf16[2048,1408]{1,0:T(8,128)(2,1)} %get-tuple-element.181.weights_ref), custom_call_target="tpu_custom_call" | custom-call | flops 5905580032 | bytes 11534336 | tf_op jit(solution)/shard_map/cond/branch_1_fun/pallas_call | solution.py:577
  212.8 7.6 %convolution_convert_fusion = bf16[704,2048]{1,0:T(8,128)(2,1)} fusion(bf16[1024,704]{1,0:T(8,128)(2,1)} %get-tuple-element.481, bf16[1024,2048]{1,0:T(8,128)(2,1)} %get-tuple-element.187), kind=kOutput, calls=%fused_computation.24 | convolution fusion | flops 2954231808 | bytes 8519680 | tf_op jit(solution)/shard_map/cond/branch_1_fun/dot_general | solution.py:35
  222.6 4.3 collective-permute-done.38.other_ref
  226.9 4.8 branch_1_fun.39
  231.8 4.0 all-gather.8.cloned.1.call-done.down_ref
  235.8 8.3 %shard_map.203 = bf16[1024,1408]{1,0:T(8,128)(2,1)S(1)} custom-call(bf16[1024,2048]{1,0:T(8,128)(2,1)} %get-tuple-element.358.dy_ref, bf16[704,2048]{1,0:T(8,128)(2,1)} %all-gather.8.cloned.1.call-done.down_ref, f32[1024,1408]{1,0:T(8,128)} %get-tuple-element.359.pre_ref), custom_call_target="tpu_custom_call" | custom-call | flops 2952790016 | bytes 11534336 | tf_op jit(solution)/shard_map/pallas_call | solution.py:612
  244.1 46.1 %conditional.10 = (f32[128,2048]{1,0:T(8,128)S(1)}, bf16[4,128,512]{2,1,0:T(8,128)(2,1)S(1)}, bf16[4,128,512]{2,1,0:T(8,128)(2,1)}, bf16[2048,1408]{1,0:T(8,128)(2,1)}) conditional(s32[]{:T(128)} %bitcast.47, () %tuple.102, (f32[128,2048]{1,0:T(8,128)}, bf16[1024,1408]{1,0:T(8,128)(2,1)S(1)}, bf16[2048,1408]{1,0:T(8,128)(2,1)S(1)}, ...), branch_computations={%region_8.9_spmd, %region_9.12_spmd} | conditional | flops 12900106240 | bytes 79450888 | solution.py:667
  244.5 3.7 convolution_convert_fusion.1
  248.3 3.7 convolution_convert_fusion.2
  257.9 4.1 collective-permute-done.41
  265.4 9.6 %branch_1_fun.40 = bf16[2048,1408]{1,0:T(8,128)(2,1)} custom-call(bf16[1024,2048]{1,0:T(8,128)(2,1)} %get-tuple-element.201.refs_0_, bf16[1024,1408]{1,0:T(8,128)(2,1)S(1)} %get-tuple-element.195.refs_1_), custom_call_target="tpu_custom_call" | custom-call | flops 5905580032 | bytes 8388608 | tf_op jit(solution)/shard_map/cond/branch_1_fun/pallas_call | solution.py:641
  280.8 7.3 %convolution_convert_fusion.3.refs_0_ = bf16[128,2048]{1,0:T(8,128)(2,1)} fusion(bf16[128,2048]{1,0:T(8,128)(2,1)S(1)} %get-tuple-element.389.refs_1_, bf16[2048,2048]{1,0:T(8,128)(2,1)} %get-tuple-element.207), kind=kOutput, calls=%fused_computation.28 | convolution fusion | flops 1074003968 | bytes 9437184 | tf_op jit(solution)/shard_map/cond/branch_1_fun/dot_general | solution.py:35
  292.8 106.8 %conditional.11 = (bf16[2048,640]{1,0:T(8,128)(2,1)}, bf16[4,176,2048]{2,1,0:T(8,128)(2,1)}, bf16[4,176,2048]{2,1,0:T(8,128)(2,1)}, f32[1,128,2048]{2,1,0:T(8,128)}, bf16[1,128,2048]{2,1,0:T(8,128)(2,1)}) conditional(s32[]{:T(128)} %bitcast.47, () %tuple.101, (bf16[4,128,512]{2,1,0:T(8,128)(2,1)}, bf16[176,2048]{1,0:T(8,128)(2,1)}, ...), branch_computations={%region_13.14_spmd, %region_14.17_spmd} | conditional | flops 9958064128 | bytes 155342144 | solution.py:667
  301.0 5.9 %collective-permute-done.45.refs_1_ = bf16[2,128,512]{2,1,0:T(8,128)(2,1)S(1)} collective-permute-done((bf16[2,128,512]{2,1,0:T(8,128)(2,1)}, bf16[2,128,512]{2,1,0:T(8,128)(2,1)S(1)}, u32[]{:S(2)}, u32[]{:S(2)}) %collective-permute-start.45) | collective-permute-done | bytes 262176 | tf_op jit(solution)/shard_map/cond/branch_1_fun/ppermute | solution.py:39
  306.8 6.0 %collective-permute-done.46.refs_2_ = bf16[2,128,512]{2,1,0:T(8,128)(2,1)S(1)} collective-permute-done((bf16[2,128,512]{2,1,0:T(8,128)(2,1)}, bf16[2,128,512]{2,1,0:T(8,128)(2,1)S(1)}, u32[]{:S(2)}, u32[]{:S(2)}) %collective-permute-start.46) | collective-permute-done | bytes 262176 | tf_op jit(solution)/shard_map/cond/branch_1_fun/ppermute | solution.py:39
  312.9 3.9 convolution_convert_fusion.6
  319.1 12.8 %branch_1_fun.43 = (bf16[8,128,384]{2,1,0:T(8,128)(2,1)S(1)}, bf16[8,128,256]{2,1,0:T(8,128)(2,1)S(1)}) custom-call(s32[1]{0:T(128)} %get-tuple-element.212.place_ref, bf16[1024,384]{1,0:T(8,128)(2,1)} %get-tuple-element.213.rot_ref, f32[1024,256]{1,0:T(8,128)} %get-tuple-element.214.out_ref, f32[4,1024,1]{2,1,0:T(8,128)} %get-tuple-element.215.top_ref, ...), custom_call_target="tpu_custom_call" | custom-call | flops 2684354560 | bytes 3145728 | tf_op jit(solution)/shard_map/cond/branch_1_fun/pallas_call | solution.py:539
  342.7 7.4 %branch_1_fun.44 = bf16[2048,640]{1,0:T(8,128)(2,1)} custom-call(bf16[1024,2048]{1,0:T(8,128)(2,1)} %get-tuple-element.211.refs_0_, bf16[1024,384]{1,0:T(8,128)(2,1)S(1)} %bitcast.154, bf16[1024,2048]{1,0:T(8,128)(2,1)} %get-tuple-element.240.refs_2_, bf16[1024,256]{1,0:T(8,128)(2,1)S(1)} %bitcast.155), custom_call_target="tpu_custom_call" | custom-call | flops 2684354560 | bytes 8388608 | tf_op jit(solution)/shard_map/cond/branch_1_fun/pallas_call | solution.py:641
  361.8 10.4 %collective-permute-done.57 = bf16[128,2048]{1,0:T(8,128)(2,1)S(1)} collective-permute-done((bf16[128,2048]{1,0:T(8,128)(2,1)S(1)}, bf16[128,2048]{1,0:T(8,128)(2,1)S(1)}, u32[]{:S(2)}, u32[]{:S(2)}) %collective-permute-start.57) | collective-permute-done | bytes 524320 | tf_op jit(solution)/shard_map/cond/branch_1_fun/ppermute | solution.py:39
  376.5 4.9 collective-permute-done.60
  384.6 9.4 %collective-permute-done.61 = bf16[128,2048]{1,0:T(8,128)(2,1)S(1)} collective-permute-done((bf16[128,2048]{1,0:T(8,128)(2,1)S(1)}, bf16[128,2048]{1,0:T(8,128)(2,1)S(1)}, u32[]{:S(2)}, u32[]{:S(2)}) %collective-permute-start.61) | collective-permute-done | bytes 524320 | tf_op jit(solution)/shard_map/cond/branch_1_fun/ppermute | solution.py:39
  399.7 52.9 %conditional.12 = (f32[1408,2048]{1,0:T(8,128)}, bf16[4,512,1408]{2,1,0:T(8,128)(2,1)}) conditional(s32[]{:T(128)} %bitcast.47, () %tuple.114, (s32[1]{0:T(128)}, bf16[4,176,2048]{2,1,0:T(8,128)(2,1)}, bf16[4,176,2048]{2,1,0:T(8,128)(2,1)}, bf16[512,1408]{1,0:T(8,128)(2,1)}) %tuple.116), branch_computations={%region_18.19_spmd, %region_19.20_spmd} | conditional | bytes 54788300 | solution.py:667
  401.6 8.5 %branch_1_fun.46 = f32[1408,2048]{1,0:T(8,128)} custom-call(s32[1]{0:T(128)} %get-tuple-element.266.place_ref, bf16[4,176,2048]{2,1,0:T(8,128)(2,1)} %get-tuple-element.267.even_ref, bf16[4,176,2048]{2,1,0:T(8,128)(2,1)} %get-tuple-element.268.odd_ref), custom_call_target="tpu_custom_call" | custom-call | bytes 17301504 | tf_op jit(solution)/shard_map/cond/branch_1_fun/pallas_call | solution.py:229
  410.1 21.2 %collective-permute-done.1.refs_2_ = bf16[512,1408]{1,0:T(8,128)(2,1)S(1)} collective-permute-done((bf16[512,1408]{1,0:T(8,128)(2,1)}, bf16[512,1408]{1,0:T(8,128)(2,1)S(1)}, u32[]{:S(2)}, u32[]{:S(2)}) %collective-permute-start.1) | collective-permute-done | bytes 1441824 | tf_op jit(solution)/shard_map/cond/branch_1_fun/ppermute | solution.py:39
  434.7 13.6 %collective-permute-done.3.refs_4_ = bf16[256,1408]{1,0:T(8,128)(2,1)S(1)} collective-permute-done((bf16[256,1408]{1,0:T(8,128)(2,1)S(1)}, bf16[256,1408]{1,0:T(8,128)(2,1)S(1)}, u32[]{:S(2)}, u32[]{:S(2)}) %collective-permute-start.3) | collective-permute-done | bytes 720928 | tf_op jit(solution)/shard_map/cond/branch_1_fun/ppermute | solution.py:39
  453.1 47.4 %conditional.13 = (f32[512,5632]{1,0:T(8,128)}, f32[512,5632]{1,0:T(8,128)}, f32[2,512]{1,0:T(2,128)S(1)}, f32[512,2048]{1,0:T(8,128)}, f32[512,256]{1,0:T(8,128...) conditional(s32[]{:T(128)} %bitcast.47, () %tuple.113, (bf16[4,512,1408]{2,1,0:T(8,128)(2,1)}, ...), branch_computations={%region_21.22_spmd, %region_22.25_spmd} | conditional | flops 3676160 | bytes 116232632 | solution.py:667
  462.6 8.0 %collective-permute-done.65.refs_2_ = bf16[512,640]{1,0:T(8,128)(2,1)S(1)} collective-permute-done((bf16[512,640]{1,0:T(8,128)(2,1)}, bf16[512,640]{1,0:T(8,128)(2,1)S(1)}, u32[]{:S(2)}, u32[]{:S(2)}) %collective-permute-start.65) | collective-permute-done | bytes 655392 | tf_op jit(solution)/shard_map/cond/branch_1_fun/ppermute | solution.py:39
  474.5 9.4 %branch_1_fun.48 = f32[512,5632]{1,0:T(8,128)} custom-call(s32[1]{0:T(128)} %get-tuple-element.275.place_ref, bf16[4,512,1408]{2,1,0:T(8,128)(2,1)} %get-tuple-element.281.even_ref, bf16[4,512,1408]{2,1,0:T(8,128)(2,1)S(1)} %collective-permute-done.63.odd_ref), custom_call_target="tpu_custom_call" | custom-call | bytes 23068672 | tf_op jit(solution)/shard_map/cond/branch_1_fun/pallas_call | solution.py:203
  485.8 9.4 %branch_1_fun.49 = f32[512,5632]{1,0:T(8,128)} custom-call(s32[1]{0:T(128)} %get-tuple-element.275.place_ref, bf16[4,512,1408]{2,1,0:T(8,128)(2,1)} %get-tuple-element.281.even_ref, bf16[4,512,1408]{2,1,0:T(8,128)(2,1)S(1)} %collective-permute-done.63.odd_ref), custom_call_target="tpu_custom_call" | custom-call | bytes 23068672 | tf_op jit(solution)/shard_map/cond/branch_1_fun/pallas_call | solution.py:203
  495.2 5.3 %branch_1_fun.51 = (f32[512,2048]{1,0:T(8,128)}, f32[512,256]{1,0:T(8,128)}, f32[512,256]{1,0:T(8,128)}, f32[512,2048]{1,0:T(8,128)}) custom-call(s32[1]{0:T(128)} %get-tuple-element.275.place_ref, bf16[4,512,640]{2,1,0:T(8,128)(2,1)S(1)} %branch_1_fun.50.even_ref, bf16[4,512,640]{2,1,0:T(8,128)(2,1)S(1)} %collective-permute-done.70.odd_ref), custom_call_target="tpu_custom_call" | custom-call | bytes 15728640 | tf_op jit(solution)/shard_map/cond/branch_1_fun/pallas_call | solution.py:266
  (312 shorter events, 180.6 us)
Async XLA Ops:
  7.2 62.0 %all-gather.4.cloned.1.call-start = ((), (), s32[]{:S(2)}) async-start(), calls=%async_computation.3 | async-start | bytes 3276800 | tf_op jit(solution)/shard_map/all_gather | solution.py:712
  10.5 185.0 %all-gather.6.cloned.1.call-start = ((), (), s32[]{:S(2)}) async-start(), calls=%async_computation.4 | async-start | bytes 7208960 | tf_op jit(solution)/shard_map/all_gather | solution.py:712
  15.9 219.9 %all-gather.8.cloned.1.call-start = ((), (), s32[]{:S(2)}) async-start(), calls=%async_computation.5 | async-start | bytes 3604480 | tf_op jit(solution)/shard_map/all_gather | solution.py:712
  18.0 274.8 %reduce-scatter.4.cloned.1.call-start = ((), (), s32[]{:S(2)}) async-start(), calls=%async_computation.6 | async-start | bytes 3604480 | tf_op jit(solution)/shard_map/reduce_scatter | solution.py:715
  18.2 16.5 %collective-permute-start.7 = (bf16[128,2048]{1,0:T(8,128)(2,1)S(1)}, bf16[128,2048]{1,0:T(8,128)(2,1)S(1)}, u32[]{:S(2)}, u32[]{:S(2)}) collective-permute-start(bf16[128,2048]{1,0:T(8,128)(2,1)S(1)} %get-tuple-element.116.refs_0_), channel_id=1, source_target_pairs={{0,16},{4,20},{8,24},{12,28},{16,0},{20,4},{24,8},{28,12},{1,17},{... | collective-permute-start | bytes 1572872 | tf_op jit(solution)/shard_map/cond/branch_1_fun/ppermute | solution.py:39
  21.3 13.4 %collective-permute-start.6 = (bf16[128,2048]{1,0:T(8,128)(2,1)S(1)}, bf16[128,2048]{1,0:T(8,128)(2,1)S(1)}, u32[]{:S(2)}, u32[]{:S(2)}) collective-permute-start(bf16[128,2048]{1,0:T(8,128)(2,1)S(1)} %get-tuple-element.116.refs_0_), channel_id=1, source_target_pairs={{0,8},{4,12},{8,0},{12,4},{16,24},{20,28},{24,16},{28,20},{1,9},{5... | collective-permute-start | bytes 1572872 | tf_op jit(solution)/shard_map/cond/branch_1_fun/ppermute | solution.py:39
  22.7 11.9 %collective-permute-start.4 = (f32[2,2048]{1,0:T(2,128)S(1)}, f32[2,2048]{1,0:T(2,128)S(1)}, u32[]{:S(2)}, u32[]{:S(2)}) collective-permute-start(f32[2,2048]{1,0:T(2,128)S(1)} %constant_dynamic-update-slice_fusion), channel_id=1, source_target_pairs={{0,1},{1,2},{2,3},{3,0},{4,5},{5,6},{6,7},{7,4},{8,9},{9,10},{10,1... | collective-permute-start | bytes 49160 | tf_op jit(solution)/shard_map/cond/branch_1_fun/ppermute | solution.py:148
  73.5 24.9 %collective-permute-start.16 = (bf16[2048,256]{1,0:T(8,128)(2,1)S(1)}, bf16[2048,256]{1,0:T(8,128)(2,1)S(1)}, u32[]{:S(2)}, u32[]{:S(2)}) collective-permute-start(bf16[2048,256]{1,0:T(8,128)(2,1)S(1)} %slice.188.refs_0_), channel_id=1, source_target_pairs={{0,16},{4,20},{8,24},{12,28},{16,0},{20,4},{24,8},{28,12},{1,17},{... | collective-permute-start | bytes 3145736 | tf_op jit(solution)/shard_map/cond/branch_1_fun/ppermute | solution.py:39
  75.1 24.6 %collective-permute-start.15 = (bf16[2048,256]{1,0:T(8,128)(2,1)S(1)}, bf16[2048,256]{1,0:T(8,128)(2,1)S(1)}, u32[]{:S(2)}, u32[]{:S(2)}) collective-permute-start(bf16[2048,256]{1,0:T(8,128)(2,1)S(1)} %slice.188.refs_0_), channel_id=1, source_target_pairs={{0,8},{4,12},{8,0},{12,4},{16,24},{20,28},{24,16},{28,20},{1,9},{5... | collective-permute-start | bytes 3145736 | tf_op jit(solution)/shard_map/cond/branch_1_fun/ppermute | solution.py:39
  99.8 14.9 %collective-permute-start.18 = (bf16[1024,256]{1,0:T(8,128)(2,1)S(1)}, bf16[1024,256]{1,0:T(8,128)(2,1)S(1)}, u32[]{:S(2)}, u32[]{:S(2)}) collective-permute-start(bf16[1024,256]{1,0:T(8,128)(2,1)S(1)} %slice.190), channel_id=1, source_target_pairs={{0,8},{4,12},{8,0},{12,4},{16,24},{20,28},{24,16},{28,20},{1,9},{5... | collective-permute-start | bytes 1572872 | tf_op jit(solution)/shard_map/cond/branch_1_fun/ppermute | solution.py:39
  101.1 14.9 %collective-permute-start.17 = (bf16[1024,256]{1,0:T(8,128)(2,1)S(1)}, bf16[1024,256]{1,0:T(8,128)(2,1)S(1)}, u32[]{:S(2)}, u32[]{:S(2)}) collective-permute-start(bf16[1024,256]{1,0:T(8,128)(2,1)S(1)} %slice.189), channel_id=1, source_target_pairs={{0,16},{4,20},{8,24},{12,28},{16,0},{20,4},{24,8},{28,12},{1,17},{... | collective-permute-start | bytes 1572872 | tf_op jit(solution)/shard_map/cond/branch_1_fun/ppermute | solution.py:39
  101.8 22.8 %collective-permute-start.21 = (bf16[128,2048]{1,0:T(8,128)(2,1)S(1)}, bf16[128,2048]{1,0:T(8,128)(2,1)S(1)}, u32[]{:S(2)}, u32[]{:S(2)}) collective-permute-start(bf16[128,2048]{1,0:T(8,128)(2,1)S(1)} %get-tuple-element.146.refs_0_), channel_id=1, source_target_pairs={{0,16},{4,20},{8,24},{12,28},{16,0},{20,4},{24,8},{28,12},{1,17},{... | collective-permute-start | bytes 1572872 | tf_op jit(solution)/shard_map/cond/branch_1_fun/ppermute | solution.py:39
  103.1 21.5 %collective-permute-start.20 = (bf16[128,2048]{1,0:T(8,128)(2,1)S(1)}, bf16[128,2048]{1,0:T(8,128)(2,1)S(1)}, u32[]{:S(2)}, u32[]{:S(2)}) collective-permute-start(bf16[128,2048]{1,0:T(8,128)(2,1)S(1)} %get-tuple-element.146.refs_0_), channel_id=1, source_target_pairs={{0,8},{4,12},{8,0},{12,4},{16,24},{20,28},{24,16},{28,20},{1,9},{5... | collective-permute-start | bytes 1572872 | tf_op jit(solution)/shard_map/cond/branch_1_fun/ppermute | solution.py:39
  126.9 17.8 %collective-permute-start.22 = (bf16[4,2048,256]{2,1,0:T(8,128)(2,1)}, bf16[4,2048,256]{2,1,0:T(8,128)(2,1)}, u32[]{:S(2)}, u32[]{:S(2)}) collective-permute-start(bf16[4,2048,256]{2,1,0:T(8,128)(2,1)} %branch_1_fun.29.even_ref), channel_id=1, source_target_pairs={{0,4},{4,0},{8,12},{12,8},{16,20},{20,16},{24,28},{28,24},{1,5},{5... | collective-permute-start | bytes 12582920 | tf_op jit(solution)/shard_map/cond/branch_1_fun/ppermute | solution.py:39
  129.6 15.0 %collective-permute-start.27 = (bf16[64,2048]{1,0:T(8,128)(2,1)S(1)}, bf16[64,2048]{1,0:T(8,128)(2,1)S(1)}, u32[]{:S(2)}, u32[]{:S(2)}) collective-permute-start(bf16[64,2048]{1,0:T(8,128)(2,1)S(1)} %slice.192), channel_id=1, source_target_pairs={{0,8},{4,12},{8,0},{12,4},{16,24},{20,28},{24,16},{28,20},{1,9},{5... | collective-permute-start | bytes 786440 | tf_op jit(solution)/shard_map/cond/branch_1_fun/ppermute | solution.py:39
  130.8 13.8 %collective-permute-start.26 = (bf16[64,2048]{1,0:T(8,128)(2,1)S(1)}, bf16[64,2048]{1,0:T(8,128)(2,1)S(1)}, u32[]{:S(2)}, u32[]{:S(2)}) collective-permute-start(bf16[64,2048]{1,0:T(8,128)(2,1)S(1)} %slice.191), channel_id=1, source_target_pairs={{0,16},{4,20},{8,24},{12,28},{16,0},{20,4},{24,8},{28,12},{1,17},{... | collective-permute-start | bytes 786440 | tf_op jit(solution)/shard_map/cond/branch_1_fun/ppermute | solution.py:39
  131.6 13.0 %collective-permute-start.24 = (bf16[2,128,256]{2,1,0:T(8,128)(2,1)}, bf16[2,128,256]{2,1,0:T(8,128)(2,1)S(1)}, u32[]{:S(2)}, u32[]{:S(2)}) collective-permute-start(bf16[2,128,256]{2,1,0:T(8,128)(2,1)} %get-tuple-element.153), channel_id=1, source_target_pairs={{0,16},{4,20},{8,24},{12,28},{16,0},{20,4},{24,8},{28,12},{1,17},{... | collective-permute-start | bytes 393224 | tf_op jit(solution)/shard_map/cond/branch_1_fun/ppermute | solution.py:39
  146.8 30.5 %collective-permute-start.30 = (bf16[4,128,2048]{2,1,0:T(8,128)(2,1)S(1)}, bf16[4,128,2048]{2,1,0:T(8,128)(2,1)}, u32[]{:S(2)}, u32[]{:S(2)}) collective-permute-start(bf16[4,128,2048]{2,1,0:T(8,128)(2,1)S(1)} %branch_1_fun.33.mine_ref), channel_id=1, source_target_pairs={{0,4},{4,0},{8,12},{12,8},{16,20},{20,16},{24,28},{28,24},{1,5},{5... | collective-permute-start | bytes 6291464 | tf_op jit(solution)/shard_map/cond/branch_1_fun/ppermute | solution.py:39
  163.2 13.6 %collective-permute-start.29 = (bf16[128,2048]{1,0:T(8,128)(2,1)S(1)}, bf16[128,2048]{1,0:T(8,128)(2,1)S(1)}, u32[]{:S(2)}, u32[]{:S(2)}) collective-permute-start(bf16[128,2048]{1,0:T(8,128)(2,1)S(1)} %multiply_convert_fusion.refs_0_), channel_id=1, source_target_pairs={{0,16},{4,20},{8,24},{12,28},{16,0},{20,4},{24,8},{28,12},{1,17},{... | collective-permute-start | bytes 1572872 | tf_op jit(solution)/shard_map/cond/branch_1_fun/ppermute | solution.py:39
  164.0 13.3 %collective-permute-start.28 = (bf16[128,2048]{1,0:T(8,128)(2,1)S(1)}, bf16[128,2048]{1,0:T(8,128)(2,1)S(1)}, u32[]{:S(2)}, u32[]{:S(2)}) collective-permute-start(bf16[128,2048]{1,0:T(8,128)(2,1)S(1)} %multiply_convert_fusion.refs_0_), channel_id=1, source_target_pairs={{0,8},{4,12},{8,0},{12,4},{16,24},{20,28},{24,16},{28,20},{1,9},{5... | collective-permute-start | bytes 1572872 | tf_op jit(solution)/shard_map/cond/branch_1_fun/ppermute | solution.py:39
  195.7 14.5 %collective-permute-start.35 = (bf16[128,2048]{1,0:T(8,128)(2,1)}, bf16[128,2048]{1,0:T(8,128)(2,1)S(1)}, u32[]{:S(2)}, u32[]{:S(2)}) collective-permute-start(bf16[128,2048]{1,0:T(8,128)(2,1)} %get-tuple-element.179.refs_0_), channel_id=1, source_target_pairs={{0,16},{4,20},{8,24},{12,28},{16,0},{20,4},{24,8},{28,12},{1,17},{... | collective-permute-start | bytes 1572872 | tf_op jit(solution)/shard_map/cond/branch_1_fun/ppermute | solution.py:39
  197.2 13.6 %collective-permute-start.34 = (bf16[128,2048]{1,0:T(8,128)(2,1)}, bf16[128,2048]{1,0:T(8,128)(2,1)S(1)}, u32[]{:S(2)}, u32[]{:S(2)}) collective-permute-start(bf16[128,2048]{1,0:T(8,128)(2,1)} %get-tuple-element.179.refs_0_), channel_id=1, source_target_pairs={{0,8},{4,12},{8,0},{12,4},{16,24},{20,28},{24,16},{28,20},{1,9},{5... | collective-permute-start | bytes 1572872 | tf_op jit(solution)/shard_map/cond/branch_1_fun/ppermute | solution.py:39
  231.7 168.0 %reduce-scatter.6.cloned.1.call-start = ((), (), s32[]{:S(2)}) async-start(), calls=%async_computation.7 | async-start | bytes 7208960 | tf_op jit(solution)/shard_map/reduce_scatter | solution.py:715
  263.2 13.0 %collective-permute-start.42 = (bf16[128,2048]{1,0:T(8,128)(2,1)S(1)}, bf16[128,2048]{1,0:T(8,128)(2,1)S(1)}, u32[]{:S(2)}, u32[]{:S(2)}) collective-permute-start(bf16[128,2048]{1,0:T(8,128)(2,1)S(1)} %pad_maximum_fusion), channel_id=1, source_target_pairs={{0,8},{4,12},{8,0},{12,4},{16,24},{20,28},{24,16},{28,20},{1,9},{5... | collective-permute-start | bytes 1572872 | tf_op jit(solution)/shard_map/cond/branch_1_fun/ppermute | solution.py:39
  264.8 12.7 %collective-permute-start.43 = (bf16[128,2048]{1,0:T(8,128)(2,1)S(1)}, bf16[128,2048]{1,0:T(8,128)(2,1)S(1)}, u32[]{:S(2)}, u32[]{:S(2)}) collective-permute-start(bf16[128,2048]{1,0:T(8,128)(2,1)S(1)} %pad_maximum_fusion.1), channel_id=1, source_target_pairs={{0,16},{4,20},{8,24},{12,28},{16,0},{20,4},{24,8},{28,12},{1,17},{... | collective-permute-start | bytes 1572872 | tf_op jit(solution)/shard_map/cond/branch_1_fun/ppermute | solution.py:39
  291.1 162.0 %reduce-scatter.8.cloned.1.call-start = ((), (), s32[]{:S(2)}) async-start(), calls=%async_computation.8 | async-start | bytes 3276800 | tf_op jit(solution)/shard_map/reduce_scatter | solution.py:715
  298.9 13.9 %collective-permute-start.46 = (bf16[2,128,512]{2,1,0:T(8,128)(2,1)}, bf16[2,128,512]{2,1,0:T(8,128)(2,1)S(1)}, u32[]{:S(2)}, u32[]{:S(2)}) collective-permute-start(bf16[2,128,512]{2,1,0:T(8,128)(2,1)} %get-tuple-element.226), channel_id=1, source_target_pairs={{0,16},{4,20},{8,24},{12,28},{16,0},{20,4},{24,8},{28,12},{1,17},{... | collective-permute-start | bytes 786440 | tf_op jit(solution)/shard_map/cond/branch_1_fun/ppermute | solution.py:39
  300.4 12.4 %collective-permute-start.47 = (bf16[2,128,512]{2,1,0:T(8,128)(2,1)}, bf16[2,128,512]{2,1,0:T(8,128)(2,1)S(1)}, u32[]{:S(2)}, u32[]{:S(2)}) collective-permute-start(bf16[2,128,512]{2,1,0:T(8,128)(2,1)} %get-tuple-element.227), channel_id=1, source_target_pairs={{0,24},{4,28},{8,16},{12,20},{16,8},{20,12},{24,0},{28,4},{1,25},{... | collective-permute-start | bytes 786440 | tf_op jit(solution)/shard_map/cond/branch_1_fun/ppermute | solution.py:39
  316.8 19.8 %collective-permute-start.50 = (bf16[4,128,2048]{2,1,0:T(8,128)(2,1)S(1)}, bf16[4,128,2048]{2,1,0:T(8,128)(2,1)S(1)}, u32[]{:S(2)}, u32[]{:S(2)}) collective-permute-start(bf16[4,128,2048]{2,1,0:T(8,128)(2,1)S(1)} %bitcast.186), channel_id=1, source_target_pairs={{0,4},{4,0},{8,12},{12,8},{16,20},{20,16},{24,28},{28,24},{1,5},{5... | collective-permute-start | bytes 6291464 | tf_op jit(solution)/shard_map/cond/branch_1_fun/ppermute | solution.py:39
  316.9 18.5 %collective-permute-start.49 = (bf16[176,2048]{1,0:T(8,128)(2,1)S(1)}, bf16[176,2048]{1,0:T(8,128)(2,1)S(1)}, u32[]{:S(2)}, u32[]{:S(2)}) collective-permute-start(bf16[176,2048]{1,0:T(8,128)(2,1)S(1)} %copy-done.25), channel_id=1, source_target_pairs={{0,16},{4,20},{8,24},{12,28},{16,0},{20,4},{24,8},{28,12},{1,17},{... | collective-permute-start | bytes 2162696 | tf_op jit(solution)/shard_map/cond/branch_1_fun/ppermute | solution.py:39
  318.4 18.2 %collective-permute-start.48 = (bf16[176,2048]{1,0:T(8,128)(2,1)S(1)}, bf16[176,2048]{1,0:T(8,128)(2,1)S(1)}, u32[]{:S(2)}, u32[]{:S(2)}) collective-permute-start(bf16[176,2048]{1,0:T(8,128)(2,1)S(1)} %copy-done.25), channel_id=1, source_target_pairs={{0,8},{4,12},{8,0},{12,4},{16,24},{20,28},{24,16},{28,20},{1,9},{5... | collective-permute-start | bytes 2162696 | tf_op jit(solution)/shard_map/cond/branch_1_fun/ppermute | solution.py:39
  337.4 16.5 %collective-permute-start.51 = (bf16[80,2048]{1,0:T(8,128)(2,1)}, bf16[80,2048]{1,0:T(8,128)(2,1)S(1)}, u32[]{:S(2)}, u32[]{:S(2)}) collective-permute-start(bf16[80,2048]{1,0:T(8,128)(2,1)} %slice.214), channel_id=1, source_target_pairs={{0,16},{4,20},{8,24},{12,28},{16,0},{20,4},{24,8},{28,12},{1,17},{... | collective-permute-start | bytes 983048 | tf_op jit(solution)/shard_map/cond/branch_1_fun/ppermute | solution.py:39
  338.0 15.9 %collective-permute-start.52 = (bf16[96,2048]{1,0:T(8,128)(2,1)S(1)}, bf16[96,2048]{1,0:T(8,128)(2,1)S(1)}, u32[]{:S(2)}, u32[]{:S(2)}) collective-permute-start(bf16[96,2048]{1,0:T(8,128)(2,1)S(1)} %slice.215), channel_id=1, source_target_pairs={{0,8},{4,12},{8,0},{12,4},{16,24},{20,28},{24,16},{28,20},{1,9},{5... | collective-permute-start | bytes 1179656 | tf_op jit(solution)/shard_map/cond/branch_1_fun/ppermute | solution.py:39
  340.3 12.0 %collective-permute-start.54 = (bf16[64,2048]{1,0:T(8,128)(2,1)S(1)}, bf16[64,2048]{1,0:T(8,128)(2,1)S(1)}, u32[]{:S(2)}, u32[]{:S(2)}) collective-permute-start(bf16[64,2048]{1,0:T(8,128)(2,1)S(1)} %get-tuple-element.413), channel_id=1, source_target_pairs={{0,16},{4,20},{8,24},{12,28},{16,0},{20,4},{24,8},{28,12},{1,17},{... | collective-permute-start | bytes 786440 | tf_op jit(solution)/shard_map/cond/branch_1_fun/ppermute | solution.py:39
  341.3 12.6 %collective-permute-start.53 = (bf16[64,2048]{1,0:T(8,128)(2,1)S(1)}, bf16[64,2048]{1,0:T(8,128)(2,1)S(1)}, u32[]{:S(2)}, u32[]{:S(2)}) collective-permute-start(bf16[64,2048]{1,0:T(8,128)(2,1)S(1)} %get-tuple-element.414), channel_id=1, source_target_pairs={{0,8},{4,12},{8,0},{12,4},{16,24},{20,28},{24,16},{28,20},{1,9},{5... | collective-permute-start | bytes 786440 | tf_op jit(solution)/shard_map/cond/branch_1_fun/ppermute | solution.py:39
  356.1 17.0 %collective-permute-start.56 = (bf16[4,176,2048]{2,1,0:T(8,128)(2,1)}, bf16[4,176,2048]{2,1,0:T(8,128)(2,1)}, u32[]{:S(2)}, u32[]{:S(2)}) collective-permute-start(bf16[4,176,2048]{2,1,0:T(8,128)(2,1)} %branch_1_fun.45), channel_id=1, source_target_pairs={{0,4},{4,0},{8,12},{12,8},{16,20},{20,16},{24,28},{28,24},{1,5},{5... | collective-permute-start | bytes 8650760 | tf_op jit(solution)/shard_map/cond/branch_1_fun/ppermute | solution.py:39
  357.5 15.6 %collective-permute-start.55 = (bf16[4,128,2048]{2,1,0:T(8,128)(2,1)S(1)}, bf16[4,128,2048]{2,1,0:T(8,128)(2,1)S(1)}, u32[]{:S(2)}, u32[]{:S(2)}) collective-permute-start(bf16[4,128,2048]{2,1,0:T(8,128)(2,1)S(1)} %bitcast.163), channel_id=1, source_target_pairs={{0,4},{4,0},{8,12},{12,8},{16,20},{20,16},{24,28},{28,24},{1,5},{5... | collective-permute-start | bytes 6291464 | tf_op jit(solution)/shard_map/cond/branch_1_fun/ppermute | solution.py:39
  358.2 13.9 %collective-permute-start.57 = (bf16[128,2048]{1,0:T(8,128)(2,1)S(1)}, bf16[128,2048]{1,0:T(8,128)(2,1)S(1)}, u32[]{:S(2)}, u32[]{:S(2)}) collective-permute-start(bf16[128,2048]{1,0:T(8,128)(2,1)S(1)} %pad_maximum_fusion.2), channel_id=1, source_target_pairs={{0,8},{4,12},{8,0},{12,4},{16,24},{20,28},{24,16},{28,20},{1,9},{5... | collective-permute-start | bytes 1572872 | tf_op jit(solution)/shard_map/cond/branch_1_fun/ppermute | solution.py:39
  359.5 13.6 %collective-permute-start.58 = (bf16[128,2048]{1,0:T(8,128)(2,1)S(1)}, bf16[128,2048]{1,0:T(8,128)(2,1)S(1)}, u32[]{:S(2)}, u32[]{:S(2)}) collective-permute-start(bf16[128,2048]{1,0:T(8,128)(2,1)S(1)} %pad_maximum_fusion.3), channel_id=1, source_target_pairs={{0,16},{4,20},{8,24},{12,28},{16,0},{20,4},{24,8},{28,12},{1,17},{... | collective-permute-start | bytes 1572872 | tf_op jit(solution)/shard_map/cond/branch_1_fun/ppermute | solution.py:39
  382.2 11.8 %collective-permute-start.61 = (bf16[128,2048]{1,0:T(8,128)(2,1)S(1)}, bf16[128,2048]{1,0:T(8,128)(2,1)S(1)}, u32[]{:S(2)}, u32[]{:S(2)}) collective-permute-start(bf16[128,2048]{1,0:T(8,128)(2,1)S(1)} %pad_maximum_fusion.4), channel_id=1, source_target_pairs={{0,8},{4,12},{8,0},{12,4},{16,24},{20,28},{24,16},{28,20},{1,9},{5... | collective-permute-start | bytes 1572872 | tf_op jit(solution)/shard_map/cond/branch_1_fun/ppermute | solution.py:39
  399.7 31.5 %collective-permute-start.1 = (bf16[512,1408]{1,0:T(8,128)(2,1)}, bf16[512,1408]{1,0:T(8,128)(2,1)S(1)}, u32[]{:S(2)}, u32[]{:S(2)}) collective-permute-start(bf16[512,1408]{1,0:T(8,128)(2,1)} %get-tuple-element.269.refs_0_), channel_id=1, source_target_pairs={{0,16},{4,20},{8,24},{12,28},{16,0},{20,4},{24,8},{28,12},{1,17},{... | collective-permute-start | bytes 4325384 | tf_op jit(solution)/shard_map/cond/branch_1_fun/ppermute | solution.py:39
  400.4 32.1 %collective-permute-start = (bf16[512,1408]{1,0:T(8,128)(2,1)}, bf16[512,1408]{1,0:T(8,128)(2,1)S(1)}, u32[]{:S(2)}, u32[]{:S(2)}) collective-permute-start(bf16[512,1408]{1,0:T(8,128)(2,1)} %get-tuple-element.269.refs_0_), channel_id=1, source_target_pairs={{0,8},{4,12},{8,0},{12,4},{16,24},{20,28},{24,16},{28,20},{1,9},{5... | collective-permute-start | bytes 4325384 | tf_op jit(solution)/shard_map/cond/branch_1_fun/ppermute | solution.py:39
  432.6 15.7 %collective-permute-start.3 = (bf16[256,1408]{1,0:T(8,128)(2,1)S(1)}, bf16[256,1408]{1,0:T(8,128)(2,1)S(1)}, u32[]{:S(2)}, u32[]{:S(2)}) collective-permute-start(bf16[256,1408]{1,0:T(8,128)(2,1)S(1)} %slice.247), channel_id=1, source_target_pairs={{0,8},{4,12},{8,0},{12,4},{16,24},{20,28},{24,16},{28,20},{1,9},{5... | collective-permute-start | bytes 2162696 | tf_op jit(solution)/shard_map/cond/branch_1_fun/ppermute | solution.py:39
  434.1 15.6 %collective-permute-start.2 = (bf16[256,1408]{1,0:T(8,128)(2,1)S(1)}, bf16[256,1408]{1,0:T(8,128)(2,1)S(1)}, u32[]{:S(2)}, u32[]{:S(2)}) collective-permute-start(bf16[256,1408]{1,0:T(8,128)(2,1)S(1)} %slice.246), channel_id=1, source_target_pairs={{0,16},{4,20},{8,24},{12,28},{16,0},{20,4},{24,8},{28,12},{1,17},{... | collective-permute-start | bytes 2162696 | tf_op jit(solution)/shard_map/cond/branch_1_fun/ppermute | solution.py:39
  453.1 18.6 %collective-permute-start.63 = (bf16[4,512,1408]{2,1,0:T(8,128)(2,1)}, bf16[4,512,1408]{2,1,0:T(8,128)(2,1)S(1)}, u32[]{:S(2)}, u32[]{:S(2)}) collective-permute-start(bf16[4,512,1408]{2,1,0:T(8,128)(2,1)} %get-tuple-element.281.even_ref), channel_id=1, source_target_pairs={{0,4},{4,0},{8,12},{12,8},{16,20},{20,16},{24,28},{28,24},{1,5},{5... | collective-permute-start | bytes 17301512 | tf_op jit(solution)/shard_map/cond/branch_1_fun/ppermute | solution.py:39
  453.2 17.4 %collective-permute-start.65 = (bf16[512,640]{1,0:T(8,128)(2,1)}, bf16[512,640]{1,0:T(8,128)(2,1)S(1)}, u32[]{:S(2)}, u32[]{:S(2)}) collective-permute-start(bf16[512,640]{1,0:T(8,128)(2,1)} %get-tuple-element.277.refs_0_), channel_id=1, source_target_pairs={{0,16},{4,20},{8,24},{12,28},{16,0},{20,4},{24,8},{28,12},{1,17},{... | collective-permute-start | bytes 1966088 | tf_op jit(solution)/shard_map/cond/branch_1_fun/ppermute | solution.py:39
  454.7 17.0 %collective-permute-start.64 = (bf16[512,640]{1,0:T(8,128)(2,1)}, bf16[512,640]{1,0:T(8,128)(2,1)S(1)}, u32[]{:S(2)}, u32[]{:S(2)}) collective-permute-start(bf16[512,640]{1,0:T(8,128)(2,1)} %get-tuple-element.277.refs_0_), channel_id=1, source_target_pairs={{0,8},{4,12},{8,0},{12,4},{16,24},{20,28},{24,16},{28,20},{1,9},{5... | collective-permute-start | bytes 1966088 | tf_op jit(solution)/shard_map/cond/branch_1_fun/ppermute | solution.py:39
  471.8 12.1 %collective-permute-start.68 = (bf16[256,640]{1,0:T(8,128)(2,1)S(1)}, bf16[256,640]{1,0:T(8,128)(2,1)S(1)}, u32[]{:S(2)}, u32[]{:S(2)}) collective-permute-start(bf16[256,640]{1,0:T(8,128)(2,1)S(1)} %slice.251), channel_id=1, source_target_pairs={{0,8},{4,12},{8,0},{12,4},{16,24},{20,28},{24,16},{28,20},{1,9},{5... | collective-permute-start | bytes 983048 | tf_op jit(solution)/shard_map/cond/branch_1_fun/ppermute | solution.py:39
  (68 other events, 765.1 us)
Sparse Core Ops, SparseCore 0:
  10.6 58.5 all-gather.3
  70.7 105.3 all-gather.5
  178.3 57.4 all-gather.7
  237.9 54.8 reduce-scatter.3
  295.5 102.1 reduce-scatter.5
  400.4 52.6 reduce-scatter.7

commit v4 on v3

--- a/solution.py
+++ b/solution.py
@@ -182,33 +182,38 @@
     pl.when(core == 1)(lambda: body(odd, even))
 
 
-def put_columns(even, odd, place, pieces, second):
+def put_columns(even, odd, place, pieces, part, parts, earlier=()):
     half, rows, cols = even.shape
     n, w = 2 * half, cols // (2 * pieces)
     tile = 64
-
-    def kernel(place_ref, even_ref, odd_ref, out_ref):
+    steps = rows // parts // tile
+
+    def kernel(place_ref, even_ref, odd_ref, *refs):
         chip = place_ref[0] // 2
 
         def body(first, other):
             blocks = [(other if t % 2 else first)[(t // 2) ^ chip] for t in range(n)]
-            for f in range(pieces):
-                at = (second * pieces + f) * w
-                row = jnp.concatenate([block[:, at : at + w] for block in blocks], axis=1)
-                out_ref[:, f * n * w : (f + 1) * n * w] = row.astype(jnp.float32)
+            for target, start in zip(refs[-2:], (0, cols // 2)):
+                for f in range(pieces):
+                    at = start + f * w
+                    row = jnp.concatenate([block[:, at : at + w] for block in blocks], axis=1)
+                    target[:, f * n * w : (f + 1) * n * w] = row.astype(jnp.float32)
 
         ordered(place_ref[0], even_ref, odd_ref, body)
 
-    spec = pl.BlockSpec((half, tile, cols), lambda i: (0, i, 0))
-    return pl.pallas_call(
-        kernel,
-        grid=(rows // tile,),
-        out_shape=jax.ShapeDtypeStruct((rows, pieces * n * w), jnp.float32),
-        in_specs=[pl.BlockSpec(memory_space=pltpu.SMEM), spec, spec],
-        out_specs=pl.BlockSpec((tile, pieces * n * w), lambda i: (i, 0)),
+    spec = pl.BlockSpec((half, tile, cols), lambda i: (0, i + part * steps, 0))
+    whole = jax.ShapeDtypeStruct((rows, pieces * n * w), jnp.float32)
+    return pl.pallas_call(
+        kernel,
+        grid=(steps,),
+        out_shape=(whole, whole),
+        in_specs=[pl.BlockSpec(memory_space=pltpu.SMEM), spec, spec]
+        + [pl.BlockSpec(memory_space=pl.ANY)] * len(earlier),
+        out_specs=[pl.BlockSpec((tile, pieces * n * w), lambda i: (i + part * steps, 0))] * 2,
+        input_output_aliases={3 + i: i for i in range(len(earlier))},
         compiler_params=pltpu.CompilerParams(vmem_limit_bytes=48 * 2**20),
-        cost_estimate=pl.CostEstimate(flops=0, bytes_accessed=even.size * 8, transcendentals=0),
-    )(place, even, odd)
+        cost_estimate=pl.CostEstimate(flops=0, bytes_accessed=even.size * 6, transcendentals=0),
+    )(place, even, odd, *earlier)
 
 
 def put_rows(even, odd, place):
@@ -893,10 +898,12 @@
 
     def last_stage(mine, mlp_sum, mlp_own, attn_sum, attn_own):
         def columns_put():
-            even, odd = yield from core_chain(mine)
-            gate = yield put_columns(even, odd, place_arg, shards, 0)
-            up = yield put_columns(even, odd, place_arg, shards, 1)
-            return gate, up
+            halves_all, filled = (mine, swap(mine, 1)), ()
+            for part in range(4):
+                filled = put_columns(*halves_all, place_arg, shards, part, 4, filled)
+                if part:
+                    filled = yield filled
+            return filled
 
         def sums_chain():
             pairs = ((attn_sum[:, :-out_cols], attn_own[:, :-out_cols]), (mlp_sum, mlp_own))

time: 517 us -> 510 us (0.986)
  waiting for transfers between devices: 192 us -> 186 us
    ppermute x69, waiting for transfers between devices: 182 us -> 177 us  [swap(): lax.ppermute(value, 'seq', [(i, i ^ mask) for i in range(lax.axis_size('s...]
    pallas_call x2 -> x4, Pallas kernels: 18.8 us -> 17 us  [put_columns(): pl.pallas_call(kernel, grid=(steps,), out_shape=(whole, whole), in_specs=...]
  transfers between devices with their start and end apart: 78 -> 78, of which waited for: 47 -> 48; matrix products, arithmetic and copies ran while one was open for 16% -> 16% of each run, Pallas kernels for 27% -> 27%
where the time goes in v4:
time: 510 us; the launch traced here: 502 us
  waiting for transfers between devices  186 us (36%)
  Pallas kernels  140 us (27%)
  starting transfers between devices  69.1 us (14%)
  matrix products  42.7 us (8%)
  other arithmetic  29.1 us (6%)
  local copies, waits for them, and re-layouts  18.4 us (4%)
  between operations  14.8 us (3%)
    ppermute x69, waiting for transfers between devices, swap(): lax.ppermute(value, 'seq', [(i, i ^ mask) for i in range(lax.axis_size('s...  177 us
    ppermute x69, starting transfers between devices, swap(): lax.ppermute(value, 'seq', [(i, i ^ mask) for i in range(lax.axis_size('s...  64 us
    dot_general x6, matrix products, dot(): lax.dot_general(left, right, ((dims[0], dims[1]), ((), ())), preferred_el...  24.8 us
    pallas_call x4, Pallas kernels, gather_chain(): pl.pallas_call(kernel, grid=(cols // tile,), out_shape=jax.ShapeDtypeStru...  19.6 us
    pallas_call x2, Pallas kernels, row_products(): pl.pallas_call(kernel, grid=(width // tile,), out_shape=jax.ShapeDtypeStr...  17.1 us
    pallas_call x4, Pallas kernels, put_columns(): pl.pallas_call(kernel, grid=(steps,), out_shape=(whole, whole), in_specs=...  17 us
    pallas_call x8, Pallas kernels, place_pieces(): pl.pallas_call(kernel, grid=(cols // tile,), out_shape=jax.ShapeDtypeStru...  14.6 us
    pallas_call x1, Pallas kernels, attention_back(): pl.pallas_call(kernel, out_shape=[jax.ShapeDtypeStruct((n, rows, cols), l...  12.8 us
  transfers between devices with their start and end apart: 78, of which 48 were waited for; matrix products, arithmetic and copies ran while one was open for 16% of the time, Pallas kernels for 27%

profile of v4, /device:TPU:0, one launch (start us, length us, event | category | flops | bytes accessed | tf_op | source)
XLA Modules:
  0.0 502.3 jit_solution(831686705137145770)
XLA Ops:
  18.2 50.2 %conditional.7 = (f32[2,2048]{1,0:T(2,128)}, f32[8,128,128]{2,1,0:T(8,128)}, f32[8,128,128]{2,1,0:T(8,128)}, bf16[1024,2048]{1,0:T(8,128)(2,1)}, f32[1,2048]{1,0:T(1,128)S(1)}, /*index=5*/f32[1,2048]{1,0:T(1,128)}) conditional(s32[]{:T(128)} %bitcast.47, () %tuple.104, (s32[]{:T(128)}, f32[2,512]{1,0:T(2,128)S(1)}, s32[1,128]{1,0:T(1,128)S(1)}, ...), branch_computations={%region_0.1_spmd, %region_1.3_spmd} | conditional | flops 14957828 | bytes 78052016 | solution.py:672
  24.9 9.8 %collective-permute-done.5 = s32[1,1,128]{2,1,0:T(1,128)S(1)} collective-permute-done((s32[1,1,128]{2,1,0:T(1,128)S(1)}, s32[1,1,128]{2,1,0:T(1,128)S(1)}, u32[]{:S(2)}, u32[]{:S(2)}) %collective-permute-start.5) | collective-permute-done | bytes 544 | tf_op jit(solution)/shard_map/cond/branch_1_fun/ppermute | solution.py:39
  53.5 4.7 branch_1_fun.29
  61.6 3.7 fusion.1
  71.9 123.6 %conditional.8 = (bf16[128,2048]{1,0:T(8,128)(2,1)}, bf16[2048,2048]{1,0:T(8,128)(2,1)}, f32[128,2048]{1,0:T(8,128)}, bf16[1024,2048]{1,0:T(8,128)(2,1)}, f32[10...) conditional(s32[]{:T(128)} %bitcast.47, () %tuple.103, ...), branch_computations={%region_3.4_spmd, %region_4.6_spmd} | conditional | flops 3759931648 | bytes 181939232 | solution.py:672
  76.3 5.0 fusion.49
  81.3 9.7 %branch_1_fun.30 = (bf16[4,128,256]{2,1,0:T(8,128)(2,1)S(1)}, bf16[4,128,256]{2,1,0:T(8,128)(2,1)S(1)}, f32[1024,256]{1,0:T(8,128)}, bf16[1024,384]{1,0:T(8,128)...) custom-call(s32[1]{0:T(128)} %get-tuple-element.130.place_ref, f32[8,128,384]{2,1,0:T(8,128)S(1)} %bitcast.156, ...), custom_call_target="tpu_custom_call" | custom-call | flops 1073741824 | bytes 3145728 | tf_op jit(solution)/shard_map/cond/branch_1_fun/pallas_call | solution.py:458
  91.0 7.4 %collective-permute-done.16.refs_2_ = bf16[2048,256]{1,0:T(8,128)(2,1)S(1)} collective-permute-done((bf16[2048,256]{1,0:T(8,128)(2,1)S(1)}, bf16[2048,256]{1,0:T(8,128)(2,1)S(1)}, u32[]{:S(2)}, u32[]{:S(2)}) %collective-permute-start.16) | collective-permute-done | bytes 1048608 | tf_op jit(solution)/shard_map/cond/branch_1_fun/ppermute | solution.py:39
  105.4 9.3 %collective-permute-done.18.refs_4_ = bf16[1024,256]{1,0:T(8,128)(2,1)S(1)} collective-permute-done((bf16[1024,256]{1,0:T(8,128)(2,1)S(1)}, bf16[1024,256]{1,0:T(8,128)(2,1)S(1)}, u32[]{:S(2)}, u32[]{:S(2)}) %collective-permute-start.18) | collective-permute-done | bytes 524320 | tf_op jit(solution)/shard_map/cond/branch_1_fun/ppermute | solution.py:39
  115.9 8.6 %collective-permute-done.21.refs_2_ = bf16[128,2048]{1,0:T(8,128)(2,1)S(1)} collective-permute-done((bf16[128,2048]{1,0:T(8,128)(2,1)S(1)}, bf16[128,2048]{1,0:T(8,128)(2,1)S(1)}, u32[]{:S(2)}, u32[]{:S(2)}) %collective-permute-start.21) | collective-permute-done | bytes 524320 | tf_op jit(solution)/shard_map/cond/branch_1_fun/ppermute | solution.py:39
  136.1 8.5 %collective-permute-done.24.refs_2_ = bf16[2,128,256]{2,1,0:T(8,128)(2,1)S(1)} collective-permute-done((bf16[2,128,256]{2,1,0:T(8,128)(2,1)}, bf16[2,128,256]{2,1,0:T(8,128)(2,1)S(1)}, u32[]{:S(2)}, u32[]{:S(2)}) %collective-permute-start.24) | collective-permute-done | bytes 131104 | tf_op jit(solution)/shard_map/cond/branch_1_fun/ppermute | solution.py:39
  146.9 7.1 %branch_1_fun.34 = bf16[2048,2048]{1,0:T(8,128)(2,1)} custom-call(s32[1]{0:T(128)} %get-tuple-element.130.place_ref, bf16[4,2048,256]{2,1,0:T(8,128)(2,1)S(1)} %copy-done, bf16[4,2048,256]{2,1,0:T(8,128)(2,1)} %collective-permute-done.22.odd_ref), custom_call_target="tpu_custom_call" | custom-call | bytes 16777216 | tf_op jit(solution)/shard_map/cond/branch_1_fun/pallas_call | solution.py:357
  155.9 5.8 %multiply_reduce_fusion.1 = (f32[128]{0:T(128)S(1)}, f32[128,2048]{1,0:T(8,128)}) fusion(bf16[128,2048]{1,0:T(8,128)(2,1)} %branch_1_fun.33, bf16[2048,2048]{1,0:T(8,128)(2,1)} %branch_1_fun.34, bf16[128,2048]{1,0:T(8,128)(2,1)S(1)} %copy-done.13), kind=kOutput, calls=%fused_computation.22 | convolution fusion | flops 1074790272 | bytes 10486272 | tf_op jit(solution)/shard_map/cond/branch_1_fun/dot_general | solution.py:791
  164.7 12.1 %collective-permute-done.29.refs_2_ = bf16[128,2048]{1,0:T(8,128)(2,1)S(1)} collective-permute-done((bf16[128,2048]{1,0:T(8,128)(2,1)S(1)}, bf16[128,2048]{1,0:T(8,128)(2,1)S(1)}, u32[]{:S(2)}, u32[]{:S(2)}) %collective-permute-start.29) | collective-permute-done | bytes 524320 | tf_op jit(solution)/shard_map/cond/branch_1_fun/ppermute | solution.py:39
  179.6 4.7 collective-permute-done.32.refs_4_
  185.4 5.4 %branch_1_fun.38 = bf16[8,128,2048]{2,1,0:T(8,128)(2,1)} custom-call(bf16[4,128,2048]{2,1,0:T(8,128)(2,1)} %copy-done.1, bf16[4,128,2048]{2,1,0:T(8,128)(2,1)} %collective-permute-done.30.other_ref), custom_call_target="tpu_custom_call" | custom-call | bytes 8388608 | tf_op jit(solution)/shard_map/cond/branch_1_fun/pallas_call | solution.py:134
  190.8 4.7 branch_1_fun.37
  195.5 36.2 %conditional.9 = (bf16[1024,2048]{1,0:T(8,128)(2,1)}, f32[1024,1408]{1,0:T(8,128)}, bf16[1024,704]{1,0:T(8,128)(2,1)}, bf16[704,2048]{1,0:T(8,128)(2,1)}) conditional(s32[]{:T(128)} %bitcast.47, () %tuple.107, (bf16[1024,2048]{1,0:T(8,128)(2,1)}, bf16[2048,1408]{1,0:T(8,128)(2,1)}, bf16[128,2048]{1,0:T(8,128)(2,1)}, ...), branch_computations={%region_6.7_spmd, %region_7.8_spmd} | conditional | flops 8859811840 | bytes 56754436 | solution.py:672
  198.3 11.9 %branch_1_fun.39 = (f32[1024,1408]{1,0:T(8,128)}, bf16[1024,704]{1,0:T(8,128)(2,1)}) custom-call(bf16[1024,2048]{1,0:T(8,128)(2,1)} %get-tuple-element.180.normed_ref, bf16[2048,1408]{1,0:T(8,128)(2,1)} %get-tuple-element.181.weights_ref), custom_call_target="tpu_custom_call" | custom-call | flops 5905580032 | bytes 11534336 | tf_op jit(solution)/shard_map/cond/branch_1_fun/pallas_call | solution.py:582
  212.8 7.6 %convolution_convert_fusion = bf16[704,2048]{1,0:T(8,128)(2,1)} fusion(bf16[1024,704]{1,0:T(8,128)(2,1)} %get-tuple-element.491, bf16[1024,2048]{1,0:T(8,128)(2,1)} %get-tuple-element.187), kind=kOutput, calls=%fused_computation.24 | convolution fusion | flops 2954231808 | bytes 8519680 | tf_op jit(solution)/shard_map/cond/branch_1_fun/dot_general | solution.py:35
  222.6 4.3 collective-permute-done.38.other_ref
  226.9 4.8 branch_1_fun.41
  231.7 4.0 all-gather.8.cloned.1.call-done.down_ref
  235.8 8.3 %shard_map.203 = bf16[1024,1408]{1,0:T(8,128)(2,1)S(1)} custom-call(bf16[1024,2048]{1,0:T(8,128)(2,1)} %get-tuple-element.368.dy_ref, bf16[704,2048]{1,0:T(8,128)(2,1)} %all-gather.8.cloned.1.call-done.down_ref, f32[1024,1408]{1,0:T(8,128)} %get-tuple-element.369.pre_ref), custom_call_target="tpu_custom_call" | custom-call | flops 2952790016 | bytes 11534336 | tf_op jit(solution)/shard_map/pallas_call | solution.py:617
  244.1 46.1 %conditional.10 = (f32[128,2048]{1,0:T(8,128)S(1)}, bf16[4,128,512]{2,1,0:T(8,128)(2,1)S(1)}, bf16[4,128,512]{2,1,0:T(8,128)(2,1)}, bf16[2048,1408]{1,0:T(8,128)(2,1)}) conditional(s32[]{:T(128)} %bitcast.47, () %tuple.102, (f32[128,2048]{1,0:T(8,128)}, bf16[1024,1408]{1,0:T(8,128)(2,1)S(1)}, bf16[2048,1408]{1,0:T(8,128)(2,1)S(1)}, ...), branch_computations={%region_8.9_spmd, %region_9.12_spmd} | conditional | flops 12900106240 | bytes 79450888 | solution.py:672
  248.3 3.7 convolution_convert_fusion.2
  257.8 4.1 collective-permute-done.41
  265.4 9.6 %branch_1_fun.42 = bf16[2048,1408]{1,0:T(8,128)(2,1)} custom-call(bf16[1024,2048]{1,0:T(8,128)(2,1)} %get-tuple-element.201.refs_0_, bf16[1024,1408]{1,0:T(8,128)(2,1)S(1)} %get-tuple-element.195.refs_1_), custom_call_target="tpu_custom_call" | custom-call | flops 5905580032 | bytes 8388608 | tf_op jit(solution)/shard_map/cond/branch_1_fun/pallas_call | solution.py:646
  280.8 7.3 %convolution_convert_fusion.3.refs_0_ = bf16[128,2048]{1,0:T(8,128)(2,1)} fusion(bf16[128,2048]{1,0:T(8,128)(2,1)S(1)} %get-tuple-element.399.refs_1_, bf16[2048,2048]{1,0:T(8,128)(2,1)} %get-tuple-element.207), kind=kOutput, calls=%fused_computation.28 | convolution fusion | flops 1074003968 | bytes 9437184 | tf_op jit(solution)/shard_map/cond/branch_1_fun/dot_general | solution.py:35
  292.8 106.8 %conditional.11 = (bf16[2048,640]{1,0:T(8,128)(2,1)}, bf16[4,176,2048]{2,1,0:T(8,128)(2,1)}, bf16[4,176,2048]{2,1,0:T(8,128)(2,1)}, f32[1,128,2048]{2,1,0:T(8,128)}, bf16[1,128,2048]{2,1,0:T(8,128)(2,1)}) conditional(s32[]{:T(128)} %bitcast.47, () %tuple.101, (bf16[4,128,512]{2,1,0:T(8,128)(2,1)}, bf16[176,2048]{1,0:T(8,128)(2,1)}, ...), branch_computations={%region_13.14_spmd, %region_14.17_spmd} | conditional | flops 9958064128 | bytes 155342144 | solution.py:672
  301.0 5.9 %collective-permute-done.45.refs_1_ = bf16[2,128,512]{2,1,0:T(8,128)(2,1)S(1)} collective-permute-done((bf16[2,128,512]{2,1,0:T(8,128)(2,1)}, bf16[2,128,512]{2,1,0:T(8,128)(2,1)S(1)}, u32[]{:S(2)}, u32[]{:S(2)}) %collective-permute-start.45) | collective-permute-done | bytes 262176 | tf_op jit(solution)/shard_map/cond/branch_1_fun/ppermute | solution.py:39
  306.8 6.0 %collective-permute-done.46.refs_2_ = bf16[2,128,512]{2,1,0:T(8,128)(2,1)S(1)} collective-permute-done((bf16[2,128,512]{2,1,0:T(8,128)(2,1)}, bf16[2,128,512]{2,1,0:T(8,128)(2,1)S(1)}, u32[]{:S(2)}, u32[]{:S(2)}) %collective-permute-start.46) | collective-permute-done | bytes 262176 | tf_op jit(solution)/shard_map/cond/branch_1_fun/ppermute | solution.py:39
  312.8 3.9 convolution_convert_fusion.6
  319.1 12.8 %branch_1_fun.45 = (bf16[8,128,384]{2,1,0:T(8,128)(2,1)S(1)}, bf16[8,128,256]{2,1,0:T(8,128)(2,1)S(1)}) custom-call(s32[1]{0:T(128)} %get-tuple-element.212.place_ref, bf16[1024,384]{1,0:T(8,128)(2,1)} %get-tuple-element.213.rot_ref, f32[1024,256]{1,0:T(8,128)} %get-tuple-element.214.out_ref, f32[4,1024,1]{2,1,0:T(8,128)} %get-tuple-element.215.top_ref, ...), custom_call_target="tpu_custom_call" | custom-call | flops 2684354560 | bytes 3145728 | tf_op jit(solution)/shard_map/cond/branch_1_fun/pallas_call | solution.py:544
  342.6 7.4 %branch_1_fun.46 = bf16[2048,640]{1,0:T(8,128)(2,1)} custom-call(bf16[1024,2048]{1,0:T(8,128)(2,1)} %get-tuple-element.211.refs_0_, bf16[1024,384]{1,0:T(8,128)(2,1)S(1)} %bitcast.154, bf16[1024,2048]{1,0:T(8,128)(2,1)} %get-tuple-element.240.refs_2_, bf16[1024,256]{1,0:T(8,128)(2,1)S(1)} %bitcast.155), custom_call_target="tpu_custom_call" | custom-call | flops 2684354560 | bytes 8388608 | tf_op jit(solution)/shard_map/cond/branch_1_fun/pallas_call | solution.py:646
  361.8 10.4 %collective-permute-done.57 = bf16[128,2048]{1,0:T(8,128)(2,1)S(1)} collective-permute-done((bf16[128,2048]{1,0:T(8,128)(2,1)S(1)}, bf16[128,2048]{1,0:T(8,128)(2,1)S(1)}, u32[]{:S(2)}, u32[]{:S(2)}) %collective-permute-start.57) | collective-permute-done | bytes 524320 | tf_op jit(solution)/shard_map/cond/branch_1_fun/ppermute | solution.py:39
  376.5 4.9 collective-permute-done.60
  384.5 9.4 %collective-permute-done.61 = bf16[128,2048]{1,0:T(8,128)(2,1)S(1)} collective-permute-done((bf16[128,2048]{1,0:T(8,128)(2,1)S(1)}, bf16[128,2048]{1,0:T(8,128)(2,1)S(1)}, u32[]{:S(2)}, u32[]{:S(2)}) %collective-permute-start.61) | collective-permute-done | bytes 524320 | tf_op jit(solution)/shard_map/cond/branch_1_fun/ppermute | solution.py:39
  399.7 52.9 %conditional.12 = (f32[1408,2048]{1,0:T(8,128)}, bf16[4,512,1408]{2,1,0:T(8,128)(2,1)}) conditional(s32[]{:T(128)} %bitcast.47, () %tuple.114, (s32[1]{0:T(128)}, bf16[4,176,2048]{2,1,0:T(8,128)(2,1)}, bf16[4,176,2048]{2,1,0:T(8,128)(2,1)}, bf16[512,1408]{1,0:T(8,128)(2,1)}) %tuple.116), branch_computations={%region_18.19_spmd, %region_19.20_spmd} | conditional | bytes 54788300 | solution.py:672
  401.6 8.5 %branch_1_fun.48 = f32[1408,2048]{1,0:T(8,128)} custom-call(s32[1]{0:T(128)} %get-tuple-element.266.place_ref, bf16[4,176,2048]{2,1,0:T(8,128)(2,1)} %get-tuple-element.267.even_ref, bf16[4,176,2048]{2,1,0:T(8,128)(2,1)} %get-tuple-element.268.odd_ref), custom_call_target="tpu_custom_call" | custom-call | bytes 17301504 | tf_op jit(solution)/shard_map/cond/branch_1_fun/pallas_call | solution.py:234
  410.1 21.2 %collective-permute-done.1.refs_2_ = bf16[512,1408]{1,0:T(8,128)(2,1)S(1)} collective-permute-done((bf16[512,1408]{1,0:T(8,128)(2,1)}, bf16[512,1408]{1,0:T(8,128)(2,1)S(1)}, u32[]{:S(2)}, u32[]{:S(2)}) %collective-permute-start.1) | collective-permute-done | bytes 1441824 | tf_op jit(solution)/shard_map/cond/branch_1_fun/ppermute | solution.py:39
  434.7 13.6 %collective-permute-done.3.refs_4_ = bf16[256,1408]{1,0:T(8,128)(2,1)S(1)} collective-permute-done((bf16[256,1408]{1,0:T(8,128)(2,1)S(1)}, bf16[256,1408]{1,0:T(8,128)(2,1)S(1)}, u32[]{:S(2)}, u32[]{:S(2)}) %collective-permute-start.3) | collective-permute-done | bytes 720928 | tf_op jit(solution)/shard_map/cond/branch_1_fun/ppermute | solution.py:39
  453.1 40.7 %conditional.13 = (f32[512,5632]{1,0:T(8,128)}, f32[512,5632]{1,0:T(8,128)}, f32[2,512]{1,0:T(2,128)S(1)}, f32[512,2048]{1,0:T(8,128)}, f32[512,256]{1,0:T(8,128...) conditional(s32[]{:T(128)} %bitcast.47, () %tuple.113, (bf16[4,512,1408]{2,1,0:T(8,128)(2,1)}, s32[1]{0:T(128)}, ...), branch_computations={%region_21.22_spmd, %region_22.25_spmd} | conditional | flops 3676160 | bytes 139301312 | solution.py:672
  462.8 4.2 branch_1_fun.50
  467.0 4.2 branch_1_fun.51
  475.0 4.2 branch_1_fun.52
  484.2 4.2 branch_1_fun.53
  488.5 5.3 %branch_1_fun.55 = (f32[512,2048]{1,0:T(8,128)}, f32[512,256]{1,0:T(8,128)}, f32[512,256]{1,0:T(8,128)}, f32[512,2048]{1,0:T(8,128)}) custom-call(s32[1]{0:T(128)} %get-tuple-element.275.place_ref, bf16[4,512,640]{2,1,0:T(8,128)(2,1)S(1)} %branch_1_fun.54.even_ref, bf16[4,512,640]{2,1,0:T(8,128)(2,1)S(1)} %collective-permute-done.70.odd_ref), custom_call_target="tpu_custom_call" | custom-call | bytes 15728640 | tf_op jit(solution)/shard_map/cond/branch_1_fun/pallas_call | solution.py:271
  (314 shorter events, 187.2 us)
Async XLA Ops:
  7.2 62.0 %all-gather.4.cloned.1.call-start = ((), (), s32[]{:S(2)}) async-start(), calls=%async_computation.3 | async-start | bytes 3276800 | tf_op jit(solution)/shard_map/all_gather | solution.py:717
  10.5 185.0 %all-gather.6.cloned.1.call-start = ((), (), s32[]{:S(2)}) async-start(), calls=%async_computation.4 | async-start | bytes 7208960 | tf_op jit(solution)/shard_map/all_gather | solution.py:717
  15.9 219.9 %all-gather.8.cloned.1.call-start = ((), (), s32[]{:S(2)}) async-start(), calls=%async_computation.5 | async-start | bytes 3604480 | tf_op jit(solution)/shard_map/all_gather | solution.py:717
  18.0 274.8 %reduce-scatter.4.cloned.1.call-start = ((), (), s32[]{:S(2)}) async-start(), calls=%async_computation.6 | async-start | bytes 3604480 | tf_op jit(solution)/shard_map/reduce_scatter | solution.py:720
  18.2 16.5 %collective-permute-start.7 = (bf16[128,2048]{1,0:T(8,128)(2,1)S(1)}, bf16[128,2048]{1,0:T(8,128)(2,1)S(1)}, u32[]{:S(2)}, u32[]{:S(2)}) collective-permute-start(bf16[128,2048]{1,0:T(8,128)(2,1)S(1)} %get-tuple-element.116.refs_0_), channel_id=1, source_target_pairs={{0,16},{4,20},{8,24},{12,28},{16,0},{20,4},{24,8},{28,12},{1,17},{... | collective-permute-start | bytes 1572872 | tf_op jit(solution)/shard_map/cond/branch_1_fun/ppermute | solution.py:39
  21.3 13.4 %collective-permute-start.6 = (bf16[128,2048]{1,0:T(8,128)(2,1)S(1)}, bf16[128,2048]{1,0:T(8,128)(2,1)S(1)}, u32[]{:S(2)}, u32[]{:S(2)}) collective-permute-start(bf16[128,2048]{1,0:T(8,128)(2,1)S(1)} %get-tuple-element.116.refs_0_), channel_id=1, source_target_pairs={{0,8},{4,12},{8,0},{12,4},{16,24},{20,28},{24,16},{28,20},{1,9},{5... | collective-permute-start | bytes 1572872 | tf_op jit(solution)/shard_map/cond/branch_1_fun/ppermute | solution.py:39
  22.7 11.9 %collective-permute-start.4 = (f32[2,2048]{1,0:T(2,128)S(1)}, f32[2,2048]{1,0:T(2,128)S(1)}, u32[]{:S(2)}, u32[]{:S(2)}) collective-permute-start(f32[2,2048]{1,0:T(2,128)S(1)} %constant_dynamic-update-slice_fusion), channel_id=1, source_target_pairs={{0,1},{1,2},{2,3},{3,0},{4,5},{5,6},{6,7},{7,4},{8,9},{9,10},{10,1... | collective-permute-start | bytes 49160 | tf_op jit(solution)/shard_map/cond/branch_1_fun/ppermute | solution.py:148
  73.5 24.9 %collective-permute-start.16 = (bf16[2048,256]{1,0:T(8,128)(2,1)S(1)}, bf16[2048,256]{1,0:T(8,128)(2,1)S(1)}, u32[]{:S(2)}, u32[]{:S(2)}) collective-permute-start(bf16[2048,256]{1,0:T(8,128)(2,1)S(1)} %slice.188.refs_0_), channel_id=1, source_target_pairs={{0,16},{4,20},{8,24},{12,28},{16,0},{20,4},{24,8},{28,12},{1,17},{... | collective-permute-start | bytes 3145736 | tf_op jit(solution)/shard_map/cond/branch_1_fun/ppermute | solution.py:39
  75.0 24.6 %collective-permute-start.15 = (bf16[2048,256]{1,0:T(8,128)(2,1)S(1)}, bf16[2048,256]{1,0:T(8,128)(2,1)S(1)}, u32[]{:S(2)}, u32[]{:S(2)}) collective-permute-start(bf16[2048,256]{1,0:T(8,128)(2,1)S(1)} %slice.188.refs_0_), channel_id=1, source_target_pairs={{0,8},{4,12},{8,0},{12,4},{16,24},{20,28},{24,16},{28,20},{1,9},{5... | collective-permute-start | bytes 3145736 | tf_op jit(solution)/shard_map/cond/branch_1_fun/ppermute | solution.py:39
  99.8 14.9 %collective-permute-start.18 = (bf16[1024,256]{1,0:T(8,128)(2,1)S(1)}, bf16[1024,256]{1,0:T(8,128)(2,1)S(1)}, u32[]{:S(2)}, u32[]{:S(2)}) collective-permute-start(bf16[1024,256]{1,0:T(8,128)(2,1)S(1)} %slice.190), channel_id=1, source_target_pairs={{0,8},{4,12},{8,0},{12,4},{16,24},{20,28},{24,16},{28,20},{1,9},{5... | collective-permute-start | bytes 1572872 | tf_op jit(solution)/shard_map/cond/branch_1_fun/ppermute | solution.py:39
  101.1 14.9 %collective-permute-start.17 = (bf16[1024,256]{1,0:T(8,128)(2,1)S(1)}, bf16[1024,256]{1,0:T(8,128)(2,1)S(1)}, u32[]{:S(2)}, u32[]{:S(2)}) collective-permute-start(bf16[1024,256]{1,0:T(8,128)(2,1)S(1)} %slice.189), channel_id=1, source_target_pairs={{0,16},{4,20},{8,24},{12,28},{16,0},{20,4},{24,8},{28,12},{1,17},{... | collective-permute-start | bytes 1572872 | tf_op jit(solution)/shard_map/cond/branch_1_fun/ppermute | solution.py:39
  101.8 22.8 %collective-permute-start.21 = (bf16[128,2048]{1,0:T(8,128)(2,1)S(1)}, bf16[128,2048]{1,0:T(8,128)(2,1)S(1)}, u32[]{:S(2)}, u32[]{:S(2)}) collective-permute-start(bf16[128,2048]{1,0:T(8,128)(2,1)S(1)} %get-tuple-element.146.refs_0_), channel_id=1, source_target_pairs={{0,16},{4,20},{8,24},{12,28},{16,0},{20,4},{24,8},{28,12},{1,17},{... | collective-permute-start | bytes 1572872 | tf_op jit(solution)/shard_map/cond/branch_1_fun/ppermute | solution.py:39
  103.1 21.5 %collective-permute-start.20 = (bf16[128,2048]{1,0:T(8,128)(2,1)S(1)}, bf16[128,2048]{1,0:T(8,128)(2,1)S(1)}, u32[]{:S(2)}, u32[]{:S(2)}) collective-permute-start(bf16[128,2048]{1,0:T(8,128)(2,1)S(1)} %get-tuple-element.146.refs_0_), channel_id=1, source_target_pairs={{0,8},{4,12},{8,0},{12,4},{16,24},{20,28},{24,16},{28,20},{1,9},{5... | collective-permute-start | bytes 1572872 | tf_op jit(solution)/shard_map/cond/branch_1_fun/ppermute | solution.py:39
  126.8 17.8 %collective-permute-start.22 = (bf16[4,2048,256]{2,1,0:T(8,128)(2,1)}, bf16[4,2048,256]{2,1,0:T(8,128)(2,1)}, u32[]{:S(2)}, u32[]{:S(2)}) collective-permute-start(bf16[4,2048,256]{2,1,0:T(8,128)(2,1)} %branch_1_fun.31.even_ref), channel_id=1, source_target_pairs={{0,4},{4,0},{8,12},{12,8},{16,20},{20,16},{24,28},{28,24},{1,5},{5... | collective-permute-start | bytes 12582920 | tf_op jit(solution)/shard_map/cond/branch_1_fun/ppermute | solution.py:39
  129.6 15.0 %collective-permute-start.27 = (bf16[64,2048]{1,0:T(8,128)(2,1)S(1)}, bf16[64,2048]{1,0:T(8,128)(2,1)S(1)}, u32[]{:S(2)}, u32[]{:S(2)}) collective-permute-start(bf16[64,2048]{1,0:T(8,128)(2,1)S(1)} %slice.192), channel_id=1, source_target_pairs={{0,8},{4,12},{8,0},{12,4},{16,24},{20,28},{24,16},{28,20},{1,9},{5... | collective-permute-start | bytes 786440 | tf_op jit(solution)/shard_map/cond/branch_1_fun/ppermute | solution.py:39
  130.8 13.8 %collective-permute-start.26 = (bf16[64,2048]{1,0:T(8,128)(2,1)S(1)}, bf16[64,2048]{1,0:T(8,128)(2,1)S(1)}, u32[]{:S(2)}, u32[]{:S(2)}) collective-permute-start(bf16[64,2048]{1,0:T(8,128)(2,1)S(1)} %slice.191), channel_id=1, source_target_pairs={{0,16},{4,20},{8,24},{12,28},{16,0},{20,4},{24,8},{28,12},{1,17},{... | collective-permute-start | bytes 786440 | tf_op jit(solution)/shard_map/cond/branch_1_fun/ppermute | solution.py:39
  131.5 13.0 %collective-permute-start.24 = (bf16[2,128,256]{2,1,0:T(8,128)(2,1)}, bf16[2,128,256]{2,1,0:T(8,128)(2,1)S(1)}, u32[]{:S(2)}, u32[]{:S(2)}) collective-permute-start(bf16[2,128,256]{2,1,0:T(8,128)(2,1)} %get-tuple-element.153), channel_id=1, source_target_pairs={{0,16},{4,20},{8,24},{12,28},{16,0},{20,4},{24,8},{28,12},{1,17},{... | collective-permute-start | bytes 393224 | tf_op jit(solution)/shard_map/cond/branch_1_fun/ppermute | solution.py:39
  146.8 30.5 %collective-permute-start.30 = (bf16[4,128,2048]{2,1,0:T(8,128)(2,1)S(1)}, bf16[4,128,2048]{2,1,0:T(8,128)(2,1)}, u32[]{:S(2)}, u32[]{:S(2)}) collective-permute-start(bf16[4,128,2048]{2,1,0:T(8,128)(2,1)S(1)} %branch_1_fun.35.mine_ref), channel_id=1, source_target_pairs={{0,4},{4,0},{8,12},{12,8},{16,20},{20,16},{24,28},{28,24},{1,5},{5... | collective-permute-start | bytes 6291464 | tf_op jit(solution)/shard_map/cond/branch_1_fun/ppermute | solution.py:39
  163.2 13.6 %collective-permute-start.29 = (bf16[128,2048]{1,0:T(8,128)(2,1)S(1)}, bf16[128,2048]{1,0:T(8,128)(2,1)S(1)}, u32[]{:S(2)}, u32[]{:S(2)}) collective-permute-start(bf16[128,2048]{1,0:T(8,128)(2,1)S(1)} %multiply_convert_fusion.refs_0_), channel_id=1, source_target_pairs={{0,16},{4,20},{8,24},{12,28},{16,0},{20,4},{24,8},{28,12},{1,17},{... | collective-permute-start | bytes 1572872 | tf_op jit(solution)/shard_map/cond/branch_1_fun/ppermute | solution.py:39
  164.0 13.3 %collective-permute-start.28 = (bf16[128,2048]{1,0:T(8,128)(2,1)S(1)}, bf16[128,2048]{1,0:T(8,128)(2,1)S(1)}, u32[]{:S(2)}, u32[]{:S(2)}) collective-permute-start(bf16[128,2048]{1,0:T(8,128)(2,1)S(1)} %multiply_convert_fusion.refs_0_), channel_id=1, source_target_pairs={{0,8},{4,12},{8,0},{12,4},{16,24},{20,28},{24,16},{28,20},{1,9},{5... | collective-permute-start | bytes 1572872 | tf_op jit(solution)/shard_map/cond/branch_1_fun/ppermute | solution.py:39
  195.7 14.5 %collective-permute-start.35 = (bf16[128,2048]{1,0:T(8,128)(2,1)}, bf16[128,2048]{1,0:T(8,128)(2,1)S(1)}, u32[]{:S(2)}, u32[]{:S(2)}) collective-permute-start(bf16[128,2048]{1,0:T(8,128)(2,1)} %get-tuple-element.179.refs_0_), channel_id=1, source_target_pairs={{0,16},{4,20},{8,24},{12,28},{16,0},{20,4},{24,8},{28,12},{1,17},{... | collective-permute-start | bytes 1572872 | tf_op jit(solution)/shard_map/cond/branch_1_fun/ppermute | solution.py:39
  197.2 13.6 %collective-permute-start.34 = (bf16[128,2048]{1,0:T(8,128)(2,1)}, bf16[128,2048]{1,0:T(8,128)(2,1)S(1)}, u32[]{:S(2)}, u32[]{:S(2)}) collective-permute-start(bf16[128,2048]{1,0:T(8,128)(2,1)} %get-tuple-element.179.refs_0_), channel_id=1, source_target_pairs={{0,8},{4,12},{8,0},{12,4},{16,24},{20,28},{24,16},{28,20},{1,9},{5... | collective-permute-start | bytes 1572872 | tf_op jit(solution)/shard_map/cond/branch_1_fun/ppermute | solution.py:39
  231.7 168.0 %reduce-scatter.6.cloned.1.call-start = ((), (), s32[]{:S(2)}) async-start(), calls=%async_computation.7 | async-start | bytes 7208960 | tf_op jit(solution)/shard_map/reduce_scatter | solution.py:720
  263.2 13.0 %collective-permute-start.42 = (bf16[128,2048]{1,0:T(8,128)(2,1)S(1)}, bf16[128,2048]{1,0:T(8,128)(2,1)S(1)}, u32[]{:S(2)}, u32[]{:S(2)}) collective-permute-start(bf16[128,2048]{1,0:T(8,128)(2,1)S(1)} %pad_maximum_fusion), channel_id=1, source_target_pairs={{0,8},{4,12},{8,0},{12,4},{16,24},{20,28},{24,16},{28,20},{1,9},{5... | collective-permute-start | bytes 1572872 | tf_op jit(solution)/shard_map/cond/branch_1_fun/ppermute | solution.py:39
  264.8 12.7 %collective-permute-start.43 = (bf16[128,2048]{1,0:T(8,128)(2,1)S(1)}, bf16[128,2048]{1,0:T(8,128)(2,1)S(1)}, u32[]{:S(2)}, u32[]{:S(2)}) collective-permute-start(bf16[128,2048]{1,0:T(8,128)(2,1)S(1)} %pad_maximum_fusion.1), channel_id=1, source_target_pairs={{0,16},{4,20},{8,24},{12,28},{16,0},{20,4},{24,8},{28,12},{1,17},{... | collective-permute-start | bytes 1572872 | tf_op jit(solution)/shard_map/cond/branch_1_fun/ppermute | solution.py:39
  291.0 162.0 %reduce-scatter.8.cloned.1.call-start = ((), (), s32[]{:S(2)}) async-start(), calls=%async_computation.8 | async-start | bytes 3276800 | tf_op jit(solution)/shard_map/reduce_scatter | solution.py:720
  298.9 13.9 %collective-permute-start.46 = (bf16[2,128,512]{2,1,0:T(8,128)(2,1)}, bf16[2,128,512]{2,1,0:T(8,128)(2,1)S(1)}, u32[]{:S(2)}, u32[]{:S(2)}) collective-permute-start(bf16[2,128,512]{2,1,0:T(8,128)(2,1)} %get-tuple-element.226), channel_id=1, source_target_pairs={{0,16},{4,20},{8,24},{12,28},{16,0},{20,4},{24,8},{28,12},{1,17},{... | collective-permute-start | bytes 786440 | tf_op jit(solution)/shard_map/cond/branch_1_fun/ppermute | solution.py:39
  300.4 12.4 %collective-permute-start.47 = (bf16[2,128,512]{2,1,0:T(8,128)(2,1)}, bf16[2,128,512]{2,1,0:T(8,128)(2,1)S(1)}, u32[]{:S(2)}, u32[]{:S(2)}) collective-permute-start(bf16[2,128,512]{2,1,0:T(8,128)(2,1)} %get-tuple-element.227), channel_id=1, source_target_pairs={{0,24},{4,28},{8,16},{12,20},{16,8},{20,12},{24,0},{28,4},{1,25},{... | collective-permute-start | bytes 786440 | tf_op jit(solution)/shard_map/cond/branch_1_fun/ppermute | solution.py:39
  316.8 19.8 %collective-permute-start.50 = (bf16[4,128,2048]{2,1,0:T(8,128)(2,1)S(1)}, bf16[4,128,2048]{2,1,0:T(8,128)(2,1)S(1)}, u32[]{:S(2)}, u32[]{:S(2)}) collective-permute-start(bf16[4,128,2048]{2,1,0:T(8,128)(2,1)S(1)} %bitcast.186), channel_id=1, source_target_pairs={{0,4},{4,0},{8,12},{12,8},{16,20},{20,16},{24,28},{28,24},{1,5},{5... | collective-permute-start | bytes 6291464 | tf_op jit(solution)/shard_map/cond/branch_1_fun/ppermute | solution.py:39
  316.9 18.5 %collective-permute-start.49 = (bf16[176,2048]{1,0:T(8,128)(2,1)S(1)}, bf16[176,2048]{1,0:T(8,128)(2,1)S(1)}, u32[]{:S(2)}, u32[]{:S(2)}) collective-permute-start(bf16[176,2048]{1,0:T(8,128)(2,1)S(1)} %copy-done.25), channel_id=1, source_target_pairs={{0,16},{4,20},{8,24},{12,28},{16,0},{20,4},{24,8},{28,12},{1,17},{... | collective-permute-start | bytes 2162696 | tf_op jit(solution)/shard_map/cond/branch_1_fun/ppermute | solution.py:39
  318.4 18.2 %collective-permute-start.48 = (bf16[176,2048]{1,0:T(8,128)(2,1)S(1)}, bf16[176,2048]{1,0:T(8,128)(2,1)S(1)}, u32[]{:S(2)}, u32[]{:S(2)}) collective-permute-start(bf16[176,2048]{1,0:T(8,128)(2,1)S(1)} %copy-done.25), channel_id=1, source_target_pairs={{0,8},{4,12},{8,0},{12,4},{16,24},{20,28},{24,16},{28,20},{1,9},{5... | collective-permute-start | bytes 2162696 | tf_op jit(solution)/shard_map/cond/branch_1_fun/ppermute | solution.py:39
  337.4 16.5 %collective-permute-start.51 = (bf16[80,2048]{1,0:T(8,128)(2,1)}, bf16[80,2048]{1,0:T(8,128)(2,1)S(1)}, u32[]{:S(2)}, u32[]{:S(2)}) collective-permute-start(bf16[80,2048]{1,0:T(8,128)(2,1)} %slice.214), channel_id=1, source_target_pairs={{0,16},{4,20},{8,24},{12,28},{16,0},{20,4},{24,8},{28,12},{1,17},{... | collective-permute-start | bytes 983048 | tf_op jit(solution)/shard_map/cond/branch_1_fun/ppermute | solution.py:39
  338.0 15.9 %collective-permute-start.52 = (bf16[96,2048]{1,0:T(8,128)(2,1)S(1)}, bf16[96,2048]{1,0:T(8,128)(2,1)S(1)}, u32[]{:S(2)}, u32[]{:S(2)}) collective-permute-start(bf16[96,2048]{1,0:T(8,128)(2,1)S(1)} %slice.215), channel_id=1, source_target_pairs={{0,8},{4,12},{8,0},{12,4},{16,24},{20,28},{24,16},{28,20},{1,9},{5... | collective-permute-start | bytes 1179656 | tf_op jit(solution)/shard_map/cond/branch_1_fun/ppermute | solution.py:39
  340.3 12.0 %collective-permute-start.54 = (bf16[64,2048]{1,0:T(8,128)(2,1)S(1)}, bf16[64,2048]{1,0:T(8,128)(2,1)S(1)}, u32[]{:S(2)}, u32[]{:S(2)}) collective-permute-start(bf16[64,2048]{1,0:T(8,128)(2,1)S(1)} %get-tuple-element.423), channel_id=1, source_target_pairs={{0,16},{4,20},{8,24},{12,28},{16,0},{20,4},{24,8},{28,12},{1,17},{... | collective-permute-start | bytes 786440 | tf_op jit(solution)/shard_map/cond/branch_1_fun/ppermute | solution.py:39
  341.3 12.6 %collective-permute-start.53 = (bf16[64,2048]{1,0:T(8,128)(2,1)S(1)}, bf16[64,2048]{1,0:T(8,128)(2,1)S(1)}, u32[]{:S(2)}, u32[]{:S(2)}) collective-permute-start(bf16[64,2048]{1,0:T(8,128)(2,1)S(1)} %get-tuple-element.424), channel_id=1, source_target_pairs={{0,8},{4,12},{8,0},{12,4},{16,24},{20,28},{24,16},{28,20},{1,9},{5... | collective-permute-start | bytes 786440 | tf_op jit(solution)/shard_map/cond/branch_1_fun/ppermute | solution.py:39
  356.1 17.0 %collective-permute-start.56 = (bf16[4,176,2048]{2,1,0:T(8,128)(2,1)}, bf16[4,176,2048]{2,1,0:T(8,128)(2,1)}, u32[]{:S(2)}, u32[]{:S(2)}) collective-permute-start(bf16[4,176,2048]{2,1,0:T(8,128)(2,1)} %branch_1_fun.47), channel_id=1, source_target_pairs={{0,4},{4,0},{8,12},{12,8},{16,20},{20,16},{24,28},{28,24},{1,5},{5... | collective-permute-start | bytes 8650760 | tf_op jit(solution)/shard_map/cond/branch_1_fun/ppermute | solution.py:39
  357.5 15.6 %collective-permute-start.55 = (bf16[4,128,2048]{2,1,0:T(8,128)(2,1)S(1)}, bf16[4,128,2048]{2,1,0:T(8,128)(2,1)S(1)}, u32[]{:S(2)}, u32[]{:S(2)}) collective-permute-start(bf16[4,128,2048]{2,1,0:T(8,128)(2,1)S(1)} %bitcast.163), channel_id=1, source_target_pairs={{0,4},{4,0},{8,12},{12,8},{16,20},{20,16},{24,28},{28,24},{1,5},{5... | collective-permute-start | bytes 6291464 | tf_op jit(solution)/shard_map/cond/branch_1_fun/ppermute | solution.py:39
  358.2 13.9 %collective-permute-start.57 = (bf16[128,2048]{1,0:T(8,128)(2,1)S(1)}, bf16[128,2048]{1,0:T(8,128)(2,1)S(1)}, u32[]{:S(2)}, u32[]{:S(2)}) collective-permute-start(bf16[128,2048]{1,0:T(8,128)(2,1)S(1)} %pad_maximum_fusion.2), channel_id=1, source_target_pairs={{0,8},{4,12},{8,0},{12,4},{16,24},{20,28},{24,16},{28,20},{1,9},{5... | collective-permute-start | bytes 1572872 | tf_op jit(solution)/shard_map/cond/branch_1_fun/ppermute | solution.py:39
  359.5 13.6 %collective-permute-start.58 = (bf16[128,2048]{1,0:T(8,128)(2,1)S(1)}, bf16[128,2048]{1,0:T(8,128)(2,1)S(1)}, u32[]{:S(2)}, u32[]{:S(2)}) collective-permute-start(bf16[128,2048]{1,0:T(8,128)(2,1)S(1)} %pad_maximum_fusion.3), channel_id=1, source_target_pairs={{0,16},{4,20},{8,24},{12,28},{16,0},{20,4},{24,8},{28,12},{1,17},{... | collective-permute-start | bytes 1572872 | tf_op jit(solution)/shard_map/cond/branch_1_fun/ppermute | solution.py:39
  382.2 11.8 %collective-permute-start.61 = (bf16[128,2048]{1,0:T(8,128)(2,1)S(1)}, bf16[128,2048]{1,0:T(8,128)(2,1)S(1)}, u32[]{:S(2)}, u32[]{:S(2)}) collective-permute-start(bf16[128,2048]{1,0:T(8,128)(2,1)S(1)} %pad_maximum_fusion.4), channel_id=1, source_target_pairs={{0,8},{4,12},{8,0},{12,4},{16,24},{20,28},{24,16},{28,20},{1,9},{5... | collective-permute-start | bytes 1572872 | tf_op jit(solution)/shard_map/cond/branch_1_fun/ppermute | solution.py:39
  383.7 11.5 %collective-permute-start.62 = (bf16[128,2048]{1,0:T(8,128)(2,1)S(1)}, bf16[128,2048]{1,0:T(8,128)(2,1)S(1)}, u32[]{:S(2)}, u32[]{:S(2)}) collective-permute-start(bf16[128,2048]{1,0:T(8,128)(2,1)S(1)} %pad_maximum_fusion.5), channel_id=1, source_target_pairs={{0,16},{4,20},{8,24},{12,28},{16,0},{20,4},{24,8},{28,12},{1,17},{... | collective-permute-start | bytes 1572872 | tf_op jit(solution)/shard_map/cond/branch_1_fun/ppermute | solution.py:39
  399.7 31.5 %collective-permute-start.1 = (bf16[512,1408]{1,0:T(8,128)(2,1)}, bf16[512,1408]{1,0:T(8,128)(2,1)S(1)}, u32[]{:S(2)}, u32[]{:S(2)}) collective-permute-start(bf16[512,1408]{1,0:T(8,128)(2,1)} %get-tuple-element.269.refs_0_), channel_id=1, source_target_pairs={{0,16},{4,20},{8,24},{12,28},{16,0},{20,4},{24,8},{28,12},{1,17},{... | collective-permute-start | bytes 4325384 | tf_op jit(solution)/shard_map/cond/branch_1_fun/ppermute | solution.py:39
  400.4 32.1 %collective-permute-start = (bf16[512,1408]{1,0:T(8,128)(2,1)}, bf16[512,1408]{1,0:T(8,128)(2,1)S(1)}, u32[]{:S(2)}, u32[]{:S(2)}) collective-permute-start(bf16[512,1408]{1,0:T(8,128)(2,1)} %get-tuple-element.269.refs_0_), channel_id=1, source_target_pairs={{0,8},{4,12},{8,0},{12,4},{16,24},{20,28},{24,16},{28,20},{1,9},{5... | collective-permute-start | bytes 4325384 | tf_op jit(solution)/shard_map/cond/branch_1_fun/ppermute | solution.py:39
  432.6 15.7 %collective-permute-start.3 = (bf16[256,1408]{1,0:T(8,128)(2,1)S(1)}, bf16[256,1408]{1,0:T(8,128)(2,1)S(1)}, u32[]{:S(2)}, u32[]{:S(2)}) collective-permute-start(bf16[256,1408]{1,0:T(8,128)(2,1)S(1)} %slice.247), channel_id=1, source_target_pairs={{0,8},{4,12},{8,0},{12,4},{16,24},{20,28},{24,16},{28,20},{1,9},{5... | collective-permute-start | bytes 2162696 | tf_op jit(solution)/shard_map/cond/branch_1_fun/ppermute | solution.py:39
  434.1 15.6 %collective-permute-start.2 = (bf16[256,1408]{1,0:T(8,128)(2,1)S(1)}, bf16[256,1408]{1,0:T(8,128)(2,1)S(1)}, u32[]{:S(2)}, u32[]{:S(2)}) collective-permute-start(bf16[256,1408]{1,0:T(8,128)(2,1)S(1)} %slice.246), channel_id=1, source_target_pairs={{0,16},{4,20},{8,24},{12,28},{16,0},{20,4},{24,8},{28,12},{1,17},{... | collective-permute-start | bytes 2162696 | tf_op jit(solution)/shard_map/cond/branch_1_fun/ppermute | solution.py:39
  453.2 18.1 %collective-permute-start.65 = (bf16[512,640]{1,0:T(8,128)(2,1)}, bf16[512,640]{1,0:T(8,128)(2,1)S(1)}, u32[]{:S(2)}, u32[]{:S(2)}) collective-permute-start(bf16[512,640]{1,0:T(8,128)(2,1)} %get-tuple-element.281.refs_0_), channel_id=1, source_target_pairs={{0,16},{4,20},{8,24},{12,28},{16,0},{20,4},{24,8},{28,12},{1,17},{... | collective-permute-start | bytes 1966088 | tf_op jit(solution)/shard_map/cond/branch_1_fun/ppermute | solution.py:39
  454.7 17.0 %collective-permute-start.64 = (bf16[512,640]{1,0:T(8,128)(2,1)}, bf16[512,640]{1,0:T(8,128)(2,1)S(1)}, u32[]{:S(2)}, u32[]{:S(2)}) collective-permute-start(bf16[512,640]{1,0:T(8,128)(2,1)} %get-tuple-element.281.refs_0_), channel_id=1, source_target_pairs={{0,8},{4,12},{8,0},{12,4},{16,24},{20,28},{24,16},{28,20},{1,9},{5... | collective-permute-start | bytes 1966088 | tf_op jit(solution)/shard_map/cond/branch_1_fun/ppermute | solution.py:39
  459.2 12.1 %collective-permute-start.66 = (f32[2,512]{1,0:T(2,128)S(1)}, f32[2,512]{1,0:T(2,128)S(1)}, u32[]{:S(2)}, u32[]{:S(2)}) collective-permute-start(f32[2,512]{1,0:T(2,128)S(1)} %pad_maximum_fusion.6), channel_id=1, source_target_pairs={{0,4},{4,0},{8,12},{12,8},{16,20},{20,16},{24,28},{28,24},{1,5},{5... | collective-permute-start | bytes 12296 | tf_op jit(solution)/shard_map/cond/branch_1_fun/ppermute | solution.py:39
  (68 other events, 739.8 us)
Sparse Core Ops, SparseCore 0:
  10.6 58.5 all-gather.3
  70.7 105.3 all-gather.5
  178.2 57.4 all-gather.7
  237.9 54.8 reduce-scatter.3
  295.5 102.1 reduce-scatter.5
  400.4 52.6 reduce-scatter.7

commit v5 on v4

--- a/solution.py
+++ b/solution.py
@@ -672,6 +672,40 @@
     return lax.cond(sure, body, nothing, *args)
 
 
+def own_columns(place, w_query, w_key, w_value, w_out, n):
+    rows, q_cols, out_cols = w_query.shape[0], w_query.shape[1] // n, w_out.shape[1] // n
+    cols = q_cols + 2 * HEAD_DIM + out_cols
+
+    def kernel(place_ref, query_ref, key_ref, value_ref, out_ref, result_ref):
+        result_ref[:, :q_cols] = query_ref[...]
+        result_ref[:, cols - out_cols :] = out_ref[...]
+        for head in range(KV_HEADS):
+            at = slice(head * HEAD_DIM, (head + 1) * HEAD_DIM)
+
+            @pl.when(place_ref[0] // (n // KV_HEADS) == head)
+            def _(at=at):
+                both = jnp.concatenate([key_ref[:, at], value_ref[:, at]], axis=1)
+                result_ref[:, q_cols : q_cols + 2 * HEAD_DIM] = both
+
+    tile = rows // 2
+    return pl.pallas_call(
+        kernel,
+        grid_spec=pltpu.PrefetchScalarGridSpec(
+            num_scalar_prefetch=1,
+            grid=(2,),
+            in_specs=[
+                pl.BlockSpec((tile, q_cols), lambda i, place_ref: (i, place_ref[0])),
+                pl.BlockSpec((tile, w_key.shape[1]), lambda i, place_ref: (i, 0)),
+                pl.BlockSpec((tile, w_value.shape[1]), lambda i, place_ref: (i, 0)),
+                pl.BlockSpec((tile, out_cols), lambda i, place_ref: (i, place_ref[0])),
+            ],
+            out_specs=pl.BlockSpec((tile, cols), lambda i, place_ref: (i, 0)),
+        ),
+        out_shape=jax.ShapeDtypeStruct((rows, cols), w_query.dtype),
+        cost_estimate=pl.CostEstimate(flops=0, bytes_accessed=rows * cols * 6, transcendentals=0),
+    )(place, w_query, w_key, w_value, w_out)
+
+
 def columns_of(weight, place, groups, shards):
     width = weight.shape[1] // (groups * shards)
     return jnp.concatenate(
@@ -705,13 +739,9 @@
     tok_rows, width = tokens.shape[1:]
     shard_rows = w_query.shape[0]
     heads_dev = HEADS // groups
-    kv_copies = groups // KV_HEADS
     seq_len = tok_rows * groups
     q_cols = heads_dev * HEAD_DIM
     out_cols = width // groups
-    ff = w_gate.shape[1]
-    ff_dev = ff // groups
-    scale = HEAD_DIM ** (-0.5)
 
     def z_gather(part):
         return lax.all_gather(part, "fsdp", axis=0, tiled=True)
@@ -723,16 +753,7 @@
         return lax.dynamic_slice_in_dim(weight, start, count, 1)
 
     place_arg = place.reshape(1).astype(jnp.int32)
-    kv_head = place // kv_copies
-    attn_own = jnp.concatenate(
-        [
-            columns(w_query, place * q_cols, q_cols),
-            columns(w_key, kv_head * HEAD_DIM, HEAD_DIM),
-            columns(w_value, kv_head * HEAD_DIM, HEAD_DIM),
-            columns(w_out, place * out_cols, out_cols),
-        ],
-        axis=1,
-    )
+    attn_own = own_columns(place_arg, w_query, w_key, w_value, w_out, groups)
     attn_full = z_gather(attn_own)
     attn_full, out_part = attn_full[:, :-out_cols], attn_full[:, -out_cols:]
     mlp_own = jnp.concatenate(
@@ -747,11 +768,13 @@
 
     halves = (slice(seq_len // 2, None), slice(0, seq_len // 2))
 
+    def half_of(product, at):
+        return product(at).astype(low).reshape(groups // 2, tok_rows, width)
+
     def by_halves(product):
-        def half(at):
-            return product(at).astype(low).reshape(groups // 2, tok_rows, width)
-
-        return scatter_chain(lambda: half(halves[0]), lambda: half(halves[1]))
+        return scatter_chain(
+            lambda: half_of(product, halves[0]), lambda: half_of(product, halves[1])
+        )
 
     def inputs_stage(own, positions, gains_own):
         gains = lax.dynamic_update_slice(
@@ -865,15 +888,19 @@
             )
             return grad_normed_in, terms
 
+        def down_terms():
+            later = yield from held(hidden, 1)
+
+            def product(at):
+                return jnp.dot(later[at], down_full, preferred_element_type=wide)
+
+            odd, even = yield [half_of(product, at) for at in halves]
+            return (yield from scatter_chain(lambda: odd, lambda: even))
+
         (grad_normed_in, attn_terms), down_halves, down_term = together(
             in_turn(lambda _: exchange_chain(grad_even, grad_odd), back),
             in_turn(lambda _: held(down_sum, 2), halves_chain),
-            in_turn(
-                lambda _: held(hidden, 2),
-                lambda later: by_halves(
-                    lambda at: jnp.dot(later[at], down_full, preferred_element_type=wide)
-                ),
-            ),
+            down_terms(),
         )
         stream_own = own.astype(wide)
         inverse_in = lax.rsqrt(jnp.mean(stream_own * stream_own, axis=-1, keepdims=True) + EPS)

time: 510 us -> 509 us (level)
  transfers between devices with their start and end apart: 78 -> 78, of which waited for: 48 -> 45; matrix products, arithmetic and copies ran while one was open for 16% -> 17% of each run, Pallas kernels for 27% -> 27%
where the time goes in v5:
time: 509 us; the launch traced here: 501 us
  waiting for transfers between devices  184 us (36%)
  Pallas kernels  142 us (28%)
  starting transfers between devices  69.3 us (14%)
  matrix products  43.3 us (9%)
  other arithmetic  29.8 us (6%)
  local copies, waits for them, and re-layouts  16 us (3%)
  between operations  14.8 us (3%)
    ppermute x69, waiting for transfers between devices, swap(): lax.ppermute(value, 'seq', [(i, i ^ mask) for i in range(lax.axis_size('s...  173 us
    ppermute x69, starting transfers between devices, swap(): lax.ppermute(value, 'seq', [(i, i ^ mask) for i in range(lax.axis_size('s...  64.3 us
    dot_general x6, matrix products, dot(): lax.dot_general(left, right, ((dims[0], dims[1]), ((), ())), preferred_el...  24.8 us
    pallas_call x4, Pallas kernels, gather_chain(): pl.pallas_call(kernel, grid=(cols // tile,), out_shape=jax.ShapeDtypeStru...  19.6 us
    pallas_call x2, Pallas kernels, row_products(): pl.pallas_call(kernel, grid=(width // tile,), out_shape=jax.ShapeDtypeStr...  17.1 us
    pallas_call x4, Pallas kernels, put_columns(): pl.pallas_call(kernel, grid=(steps,), out_shape=(whole, whole), in_specs=...  17 us
    pallas_call x8, Pallas kernels, place_pieces(): pl.pallas_call(kernel, grid=(cols // tile,), out_shape=jax.ShapeDtypeStru...  14.6 us
    pallas_call x1, Pallas kernels, attention_back(): pl.pallas_call(kernel, out_shape=[jax.ShapeDtypeStruct((n, rows, cols), l...  12.8 us
  transfers between devices with their start and end apart: 78, of which 45 were waited for; matrix products, arithmetic and copies ran while one was open for 17% of the time, Pallas kernels for 27%

profile of v5, /device:TPU:0, one launch (start us, length us, event | category | flops | bytes accessed | tf_op | source)
XLA Modules:
  0.0 501.3 jit_solution(13661546403515182674)
XLA Ops:
  17.1 50.2 %conditional.7 = (f32[2,2048]{1,0:T(2,128)}, f32[8,128,128]{2,1,0:T(8,128)}, f32[8,128,128]{2,1,0:T(8,128)}, bf16[1024,2048]{1,0:T(8,128)(2,1)}, f32[1,2048]{1,0:T(1,128)S(1)}, /*index=5*/f32[1,2048]{1,0:T(1,128)}) conditional(s32[]{:T(128)} %bitcast.47, () %tuple.104, (s32[]{:T(128)}, f32[2,512]{1,0:T(2,128)S(1)}, s32[1,128]{1,0:T(1,128)S(1)}, ...), branch_computations={%region_0.0_spmd, %region_1.3_spmd} | conditional | flops 14957828 | bytes 78052016 | solution.py:672
  23.9 9.8 %collective-permute-done.5 = s32[1,1,128]{2,1,0:T(1,128)S(1)} collective-permute-done((s32[1,1,128]{2,1,0:T(1,128)S(1)}, s32[1,1,128]{2,1,0:T(1,128)S(1)}, u32[]{:S(2)}, u32[]{:S(2)}) %collective-permute-start.5) | collective-permute-done | bytes 544 | tf_op jit(solution)/shard_map/cond/branch_1_fun/ppermute | solution.py:39
  52.4 4.7 branch_1_fun.29
  60.6 3.7 fusion.1
  70.8 123.4 %conditional.8 = (bf16[128,2048]{1,0:T(8,128)(2,1)}, bf16[2048,2048]{1,0:T(8,128)(2,1)}, f32[128,2048]{1,0:T(8,128)}, bf16[1024,2048]{1,0:T(8,128)(2,1)}, f32[10...) conditional(s32[]{:T(128)} %bitcast.47, () %tuple.103, ...), branch_computations={%region_3.4_spmd, %region_4.6_spmd} | conditional | flops 3759931648 | bytes 181939232 | solution.py:672
  75.1 5.0 %fusion.49 = f32[1024,384]{1,0:T(8,128)S(1)} fusion(bf16[1024,2048]{1,0:T(8,128)(2,1)} %get-tuple-element.132, bf16[2048,384]{1,0:T(8,128)(2,1)S(1)} %get-tuple-element.133), kind=kOutput, calls=%fused_computation.129 | convolution fusion | flops 1610612736 | bytes 7340032 | tf_op jit(solution)/shard_map/cond/branch_1_fun/dot_general | solution.py:798
  80.1 9.8 %branch_1_fun.30 = (bf16[4,128,256]{2,1,0:T(8,128)(2,1)S(1)}, bf16[4,128,256]{2,1,0:T(8,128)(2,1)S(1)}, f32[1024,256]{1,0:T(8,128)}, bf16[1024,384]{1,0:T(8,128)...) custom-call(s32[1]{0:T(128)} %get-tuple-element.130.place_ref, f32[8,128,384]{2,1,0:T(8,128)S(1)} %bitcast.156, ...), custom_call_target="tpu_custom_call" | custom-call | flops 1073741824 | bytes 3145728 | tf_op jit(solution)/shard_map/cond/branch_1_fun/pallas_call | solution.py:458
  89.9 7.3 %collective-permute-done.16.refs_2_ = bf16[2048,256]{1,0:T(8,128)(2,1)S(1)} collective-permute-done((bf16[2048,256]{1,0:T(8,128)(2,1)S(1)}, bf16[2048,256]{1,0:T(8,128)(2,1)S(1)}, u32[]{:S(2)}, u32[]{:S(2)}) %collective-permute-start.16) | collective-permute-done | bytes 1048608 | tf_op jit(solution)/shard_map/cond/branch_1_fun/ppermute | solution.py:39
  104.2 9.3 %collective-permute-done.18.refs_4_ = bf16[1024,256]{1,0:T(8,128)(2,1)S(1)} collective-permute-done((bf16[1024,256]{1,0:T(8,128)(2,1)S(1)}, bf16[1024,256]{1,0:T(8,128)(2,1)S(1)}, u32[]{:S(2)}, u32[]{:S(2)}) %collective-permute-start.18) | collective-permute-done | bytes 524320 | tf_op jit(solution)/shard_map/cond/branch_1_fun/ppermute | solution.py:39
  114.7 8.6 %collective-permute-done.21.refs_2_ = bf16[128,2048]{1,0:T(8,128)(2,1)S(1)} collective-permute-done((bf16[128,2048]{1,0:T(8,128)(2,1)S(1)}, bf16[128,2048]{1,0:T(8,128)(2,1)S(1)}, u32[]{:S(2)}, u32[]{:S(2)}) %collective-permute-start.21) | collective-permute-done | bytes 524320 | tf_op jit(solution)/shard_map/cond/branch_1_fun/ppermute | solution.py:39
  134.9 8.5 %collective-permute-done.24.refs_2_ = bf16[2,128,256]{2,1,0:T(8,128)(2,1)S(1)} collective-permute-done((bf16[2,128,256]{2,1,0:T(8,128)(2,1)}, bf16[2,128,256]{2,1,0:T(8,128)(2,1)S(1)}, u32[]{:S(2)}, u32[]{:S(2)}) %collective-permute-start.24) | collective-permute-done | bytes 131104 | tf_op jit(solution)/shard_map/cond/branch_1_fun/ppermute | solution.py:39
  145.7 7.1 %branch_1_fun.34 = bf16[2048,2048]{1,0:T(8,128)(2,1)} custom-call(s32[1]{0:T(128)} %get-tuple-element.130.place_ref, bf16[4,2048,256]{2,1,0:T(8,128)(2,1)S(1)} %copy-done, bf16[4,2048,256]{2,1,0:T(8,128)(2,1)} %collective-permute-done.22.odd_ref), custom_call_target="tpu_custom_call" | custom-call | bytes 16777216 | tf_op jit(solution)/shard_map/cond/branch_1_fun/pallas_call | solution.py:357
  154.7 5.9 %multiply_reduce_fusion.1 = (f32[128]{0:T(128)S(1)}, f32[128,2048]{1,0:T(8,128)}) fusion(bf16[128,2048]{1,0:T(8,128)(2,1)} %branch_1_fun.33, bf16[2048,2048]{1,0:T(8,128)(2,1)} %branch_1_fun.34, bf16[128,2048]{1,0:T(8,128)(2,1)S(1)} %copy-done.13), kind=kOutput, calls=%fused_computation.22 | convolution fusion | flops 1074790272 | bytes 10486272 | tf_op jit(solution)/shard_map/cond/branch_1_fun/dot_general | solution.py:814
  163.5 12.1 %collective-permute-done.29.refs_2_ = bf16[128,2048]{1,0:T(8,128)(2,1)S(1)} collective-permute-done((bf16[128,2048]{1,0:T(8,128)(2,1)S(1)}, bf16[128,2048]{1,0:T(8,128)(2,1)S(1)}, u32[]{:S(2)}, u32[]{:S(2)}) %collective-permute-start.29) | collective-permute-done | bytes 524320 | tf_op jit(solution)/shard_map/cond/branch_1_fun/ppermute | solution.py:39
  178.3 4.7 collective-permute-done.32.refs_4_
  184.1 5.4 %branch_1_fun.38 = bf16[8,128,2048]{2,1,0:T(8,128)(2,1)} custom-call(bf16[4,128,2048]{2,1,0:T(8,128)(2,1)} %copy-done.1, bf16[4,128,2048]{2,1,0:T(8,128)(2,1)} %collective-permute-done.30.other_ref), custom_call_target="tpu_custom_call" | custom-call | bytes 8388608 | tf_op jit(solution)/shard_map/cond/branch_1_fun/pallas_call | solution.py:134
  189.5 4.7 branch_1_fun.37
  194.3 36.2 %conditional.9 = (bf16[1024,2048]{1,0:T(8,128)(2,1)}, f32[1024,1408]{1,0:T(8,128)}, bf16[1024,704]{1,0:T(8,128)(2,1)}, bf16[704,2048]{1,0:T(8,128)(2,1)}) conditional(s32[]{:T(128)} %bitcast.47, () %tuple.107, (bf16[1024,2048]{1,0:T(8,128)(2,1)}, bf16[2048,1408]{1,0:T(8,128)(2,1)}, bf16[128,2048]{1,0:T(8,128)(2,1)}, ...), branch_computations={%region_6.7_spmd, %region_7.8_spmd} | conditional | flops 8859811840 | bytes 56754436 | solution.py:672
  197.1 11.9 %branch_1_fun.39 = (f32[1024,1408]{1,0:T(8,128)}, bf16[1024,704]{1,0:T(8,128)(2,1)}) custom-call(bf16[1024,2048]{1,0:T(8,128)(2,1)} %get-tuple-element.180.normed_ref, bf16[2048,1408]{1,0:T(8,128)(2,1)} %get-tuple-element.181.weights_ref), custom_call_target="tpu_custom_call" | custom-call | flops 5905580032 | bytes 11534336 | tf_op jit(solution)/shard_map/cond/branch_1_fun/pallas_call | solution.py:582
  211.6 7.6 %convolution_convert_fusion = bf16[704,2048]{1,0:T(8,128)(2,1)} fusion(bf16[1024,704]{1,0:T(8,128)(2,1)} %get-tuple-element.488, bf16[1024,2048]{1,0:T(8,128)(2,1)} %get-tuple-element.187), kind=kOutput, calls=%fused_computation.24 | convolution fusion | flops 2954231808 | bytes 8519680 | tf_op jit(solution)/shard_map/cond/branch_1_fun/dot_general | solution.py:35
  221.4 4.3 collective-permute-done.38.other_ref
  225.7 4.8 branch_1_fun.41
  230.5 4.2 all-gather.8.cloned.1.call-done.down_ref
  234.7 8.3 %shard_map.204 = bf16[1024,1408]{1,0:T(8,128)(2,1)S(1)} custom-call(bf16[1024,2048]{1,0:T(8,128)(2,1)} %get-tuple-element.369.dy_ref, bf16[704,2048]{1,0:T(8,128)(2,1)} %all-gather.8.cloned.1.call-done.down_ref, f32[1024,1408]{1,0:T(8,128)} %get-tuple-element.370.pre_ref), custom_call_target="tpu_custom_call" | custom-call | flops 2952790016 | bytes 11534336 | tf_op jit(solution)/shard_map/pallas_call | solution.py:617
  243.1 46.3 %conditional.10 = (f32[128,2048]{1,0:T(8,128)S(1)}, bf16[4,128,512]{2,1,0:T(8,128)(2,1)}, bf16[4,128,512]{2,1,0:T(8,128)(2,1)}, bf16[2048,1408]{1,0:T(8,128)(2,1)}) conditional(s32[]{:T(128)} %bitcast.47, () %tuple.102, (f32[128,2048]{1,0:T(8,128)}, bf16[1024,1408]{1,0:T(8,128)(2,1)S(1)}, bf16[2048,1408]{1,0:T(8,128)(2,1)S(1)}, ...), branch_computations={%region_8.9_spmd, %region_9.12_spmd} | conditional | flops 12900106240 | bytes 79450888 | solution.py:672
  247.3 3.7 convolution_convert_fusion.2
  256.8 4.1 collective-permute-done.41
  264.4 9.6 %branch_1_fun.42 = bf16[2048,1408]{1,0:T(8,128)(2,1)} custom-call(bf16[1024,2048]{1,0:T(8,128)(2,1)} %get-tuple-element.201.refs_0_, bf16[1024,1408]{1,0:T(8,128)(2,1)S(1)} %get-tuple-element.195.refs_1_), custom_call_target="tpu_custom_call" | custom-call | flops 5905580032 | bytes 8388608 | tf_op jit(solution)/shard_map/cond/branch_1_fun/pallas_call | solution.py:646
  279.8 7.3 %convolution_convert_fusion.3.refs_0_ = bf16[128,2048]{1,0:T(8,128)(2,1)} fusion(bf16[128,2048]{1,0:T(8,128)(2,1)S(1)} %get-tuple-element.400.refs_1_, bf16[2048,2048]{1,0:T(8,128)(2,1)} %get-tuple-element.207), kind=kOutput, calls=%fused_computation.28 | convolution fusion | flops 1074003968 | bytes 9437184 | tf_op jit(solution)/shard_map/cond/branch_1_fun/dot_general | solution.py:35
  291.8 103.8 %conditional.11 = (bf16[2048,640]{1,0:T(8,128)(2,1)}, bf16[4,176,2048]{2,1,0:T(8,128)(2,1)}, bf16[4,176,2048]{2,1,0:T(8,128)(2,1)}, f32[1,128,2048]{2,1,0:T(8,128)}, bf16[1,128,2048]{2,1,0:T(8,128)(2,1)}) conditional(s32[]{:T(128)} %bitcast.47, () %tuple.101, (bf16[4,128,512]{2,1,0:T(8,128)(2,1)}, bf16[176,2048]{1,0:T(8,128)(2,1)}, ...), branch_computations={%region_13.14_spmd, %region_14.17_spmd} | conditional | flops 9958064128 | bytes 163730784 | solution.py:672
  300.0 4.7 convolution_convert_fusion.6
  307.7 4.1 collective-permute-done.46.refs_2_
  313.9 12.8 %branch_1_fun.45 = (bf16[8,128,384]{2,1,0:T(8,128)(2,1)S(1)}, bf16[8,128,256]{2,1,0:T(8,128)(2,1)S(1)}) custom-call(s32[1]{0:T(128)} %get-tuple-element.212.place_ref, bf16[1024,384]{1,0:T(8,128)(2,1)} %get-tuple-element.213.rot_ref, f32[1024,256]{1,0:T(8,128)} %get-tuple-element.214.out_ref, f32[4,1024,1]{2,1,0:T(8,128)} %get-tuple-element.215.top_ref, ...), custom_call_target="tpu_custom_call" | custom-call | flops 2684354560 | bytes 3145728 | tf_op jit(solution)/shard_map/cond/branch_1_fun/pallas_call | solution.py:544
  340.1 7.4 %branch_1_fun.46 = bf16[2048,640]{1,0:T(8,128)(2,1)} custom-call(bf16[1024,2048]{1,0:T(8,128)(2,1)} %get-tuple-element.211.refs_0_, bf16[1024,384]{1,0:T(8,128)(2,1)S(1)} %bitcast.154, bf16[1024,2048]{1,0:T(8,128)(2,1)} %get-tuple-element.241.refs_2_, bf16[1024,256]{1,0:T(8,128)(2,1)S(1)} %bitcast.155), custom_call_target="tpu_custom_call" | custom-call | flops 2684354560 | bytes 8388608 | tf_op jit(solution)/shard_map/cond/branch_1_fun/pallas_call | solution.py:646
  357.6 10.5 %collective-permute-done.57 = bf16[128,2048]{1,0:T(8,128)(2,1)S(1)} collective-permute-done((bf16[128,2048]{1,0:T(8,128)(2,1)S(1)}, bf16[128,2048]{1,0:T(8,128)(2,1)S(1)}, u32[]{:S(2)}, u32[]{:S(2)}) %collective-permute-start.57) | collective-permute-done | bytes 524320 | tf_op jit(solution)/shard_map/cond/branch_1_fun/ppermute | solution.py:39
  372.5 4.9 collective-permute-done.60
  380.5 9.3 %collective-permute-done.61 = bf16[128,2048]{1,0:T(8,128)(2,1)S(1)} collective-permute-done((bf16[128,2048]{1,0:T(8,128)(2,1)S(1)}, bf16[128,2048]{1,0:T(8,128)(2,1)S(1)}, u32[]{:S(2)}, u32[]{:S(2)}) %collective-permute-start.61) | collective-permute-done | bytes 524320 | tf_op jit(solution)/shard_map/cond/branch_1_fun/ppermute | solution.py:39
  396.7 55.9 %conditional.12 = (f32[1408,2048]{1,0:T(8,128)}, bf16[4,512,1408]{2,1,0:T(8,128)(2,1)}) conditional(s32[]{:T(128)} %bitcast.47, () %tuple.114, (s32[1]{0:T(128)}, bf16[4,176,2048]{2,1,0:T(8,128)(2,1)}, bf16[4,176,2048]{2,1,0:T(8,128)(2,1)}, bf16[512,1408]{1,0:T(8,128)(2,1)}) %tuple.116), branch_computations={%region_18.19_spmd, %region_19.20_spmd} | conditional | bytes 54788300 | solution.py:672
  399.6 8.7 %branch_1_fun.48 = f32[1408,2048]{1,0:T(8,128)} custom-call(s32[1]{0:T(128)} %get-tuple-element.267.place_ref, bf16[4,176,2048]{2,1,0:T(8,128)(2,1)} %get-tuple-element.268.even_ref, bf16[4,176,2048]{2,1,0:T(8,128)(2,1)} %get-tuple-element.269.odd_ref), custom_call_target="tpu_custom_call" | custom-call | bytes 17301504 | tf_op jit(solution)/shard_map/cond/branch_1_fun/pallas_call | solution.py:234
  408.4 21.9 %collective-permute-done.1.refs_2_ = bf16[512,1408]{1,0:T(8,128)(2,1)S(1)} collective-permute-done((bf16[512,1408]{1,0:T(8,128)(2,1)}, bf16[512,1408]{1,0:T(8,128)(2,1)S(1)}, u32[]{:S(2)}, u32[]{:S(2)}) %collective-permute-start.1) | collective-permute-done | bytes 1441824 | tf_op jit(solution)/shard_map/cond/branch_1_fun/ppermute | solution.py:39
  433.7 14.8 %collective-permute-done.3.refs_4_ = bf16[256,1408]{1,0:T(8,128)(2,1)S(1)} collective-permute-done((bf16[256,1408]{1,0:T(8,128)(2,1)S(1)}, bf16[256,1408]{1,0:T(8,128)(2,1)S(1)}, u32[]{:S(2)}, u32[]{:S(2)}) %collective-permute-start.3) | collective-permute-done | bytes 720928 | tf_op jit(solution)/shard_map/cond/branch_1_fun/ppermute | solution.py:39
  452.6 40.2 %conditional.13 = (f32[512,5632]{1,0:T(8,128)}, f32[512,5632]{1,0:T(8,128)}, f32[2,512]{1,0:T(2,128)S(1)}, f32[512,2048]{1,0:T(8,128)}, f32[512,256]{1,0:T(8,128...) conditional(s32[]{:T(128)} %bitcast.47, () %tuple.113, (bf16[4,512,1408]{2,1,0:T(8,128)(2,1)}, s32[1]{0:T(128)}, ...), branch_computations={%region_21.22_spmd, %region_22.25_spmd} | conditional | flops 3676160 | bytes 139301312 | solution.py:672
  458.3 4.0 collective-permute-done.63.odd_ref
  462.3 4.2 branch_1_fun.50
  466.6 4.2 branch_1_fun.51
  474.1 4.2 branch_1_fun.52
  483.2 4.2 branch_1_fun.53
  487.5 5.3 %branch_1_fun.55 = (f32[512,2048]{1,0:T(8,128)}, f32[512,256]{1,0:T(8,128)}, f32[512,256]{1,0:T(8,128)}, f32[512,2048]{1,0:T(8,128)}) custom-call(s32[1]{0:T(128)} %get-tuple-element.276.place_ref, bf16[4,512,640]{2,1,0:T(8,128)(2,1)S(1)} %branch_1_fun.54.even_ref, bf16[4,512,640]{2,1,0:T(8,128)(2,1)S(1)} %collective-permute-done.70.odd_ref), custom_call_target="tpu_custom_call" | custom-call | bytes 15728640 | tf_op jit(solution)/shard_map/cond/branch_1_fun/pallas_call | solution.py:271
  (310 shorter events, 186.9 us)
Async XLA Ops:
  7.2 61.0 %all-gather.4.cloned.1.call-start = ((), (), s32[]{:S(2)}) async-start(), calls=%async_computation.3 | async-start | bytes 3276800 | tf_op jit(solution)/shard_map/all_gather | solution.py:747
  9.4 184.8 %all-gather.6.cloned.1.call-start = ((), (), s32[]{:S(2)}) async-start(), calls=%async_computation.4 | async-start | bytes 7208960 | tf_op jit(solution)/shard_map/all_gather | solution.py:747
  14.9 219.9 %all-gather.8.cloned.1.call-start = ((), (), s32[]{:S(2)}) async-start(), calls=%async_computation.5 | async-start | bytes 3604480 | tf_op jit(solution)/shard_map/all_gather | solution.py:747
  17.0 274.8 %reduce-scatter.4.cloned.1.call-start = ((), (), s32[]{:S(2)}) async-start(), calls=%async_computation.6 | async-start | bytes 3604480 | tf_op jit(solution)/shard_map/reduce_scatter | solution.py:750
  17.2 16.5 %collective-permute-start.7 = (bf16[128,2048]{1,0:T(8,128)(2,1)S(1)}, bf16[128,2048]{1,0:T(8,128)(2,1)S(1)}, u32[]{:S(2)}, u32[]{:S(2)}) collective-permute-start(bf16[128,2048]{1,0:T(8,128)(2,1)S(1)} %get-tuple-element.116.refs_0_), channel_id=1, source_target_pairs={{0,16},{4,20},{8,24},{12,28},{16,0},{20,4},{24,8},{28,12},{1,17},{... | collective-permute-start | bytes 1572872 | tf_op jit(solution)/shard_map/cond/branch_1_fun/ppermute | solution.py:39
  20.2 13.4 %collective-permute-start.6 = (bf16[128,2048]{1,0:T(8,128)(2,1)S(1)}, bf16[128,2048]{1,0:T(8,128)(2,1)S(1)}, u32[]{:S(2)}, u32[]{:S(2)}) collective-permute-start(bf16[128,2048]{1,0:T(8,128)(2,1)S(1)} %get-tuple-element.116.refs_0_), channel_id=1, source_target_pairs={{0,8},{4,12},{8,0},{12,4},{16,24},{20,28},{24,16},{28,20},{1,9},{5... | collective-permute-start | bytes 1572872 | tf_op jit(solution)/shard_map/cond/branch_1_fun/ppermute | solution.py:39
  21.7 11.9 %collective-permute-start.4 = (f32[2,2048]{1,0:T(2,128)S(1)}, f32[2,2048]{1,0:T(2,128)S(1)}, u32[]{:S(2)}, u32[]{:S(2)}) collective-permute-start(f32[2,2048]{1,0:T(2,128)S(1)} %constant_dynamic-update-slice_fusion), channel_id=1, source_target_pairs={{0,1},{1,2},{2,3},{3,0},{4,5},{5,6},{6,7},{7,4},{8,9},{9,10},{10,1... | collective-permute-start | bytes 49160 | tf_op jit(solution)/shard_map/cond/branch_1_fun/ppermute | solution.py:148
  72.3 24.9 %collective-permute-start.16 = (bf16[2048,256]{1,0:T(8,128)(2,1)S(1)}, bf16[2048,256]{1,0:T(8,128)(2,1)S(1)}, u32[]{:S(2)}, u32[]{:S(2)}) collective-permute-start(bf16[2048,256]{1,0:T(8,128)(2,1)S(1)} %slice.188.refs_0_), channel_id=1, source_target_pairs={{0,16},{4,20},{8,24},{12,28},{16,0},{20,4},{24,8},{28,12},{1,17},{... | collective-permute-start | bytes 3145736 | tf_op jit(solution)/shard_map/cond/branch_1_fun/ppermute | solution.py:39
  73.8 24.6 %collective-permute-start.15 = (bf16[2048,256]{1,0:T(8,128)(2,1)S(1)}, bf16[2048,256]{1,0:T(8,128)(2,1)S(1)}, u32[]{:S(2)}, u32[]{:S(2)}) collective-permute-start(bf16[2048,256]{1,0:T(8,128)(2,1)S(1)} %slice.188.refs_0_), channel_id=1, source_target_pairs={{0,8},{4,12},{8,0},{12,4},{16,24},{20,28},{24,16},{28,20},{1,9},{5... | collective-permute-start | bytes 3145736 | tf_op jit(solution)/shard_map/cond/branch_1_fun/ppermute | solution.py:39
  98.5 14.9 %collective-permute-start.18 = (bf16[1024,256]{1,0:T(8,128)(2,1)S(1)}, bf16[1024,256]{1,0:T(8,128)(2,1)S(1)}, u32[]{:S(2)}, u32[]{:S(2)}) collective-permute-start(bf16[1024,256]{1,0:T(8,128)(2,1)S(1)} %slice.190), channel_id=1, source_target_pairs={{0,8},{4,12},{8,0},{12,4},{16,24},{20,28},{24,16},{28,20},{1,9},{5... | collective-permute-start | bytes 1572872 | tf_op jit(solution)/shard_map/cond/branch_1_fun/ppermute | solution.py:39
  99.8 14.9 %collective-permute-start.17 = (bf16[1024,256]{1,0:T(8,128)(2,1)S(1)}, bf16[1024,256]{1,0:T(8,128)(2,1)S(1)}, u32[]{:S(2)}, u32[]{:S(2)}) collective-permute-start(bf16[1024,256]{1,0:T(8,128)(2,1)S(1)} %slice.189), channel_id=1, source_target_pairs={{0,16},{4,20},{8,24},{12,28},{16,0},{20,4},{24,8},{28,12},{1,17},{... | collective-permute-start | bytes 1572872 | tf_op jit(solution)/shard_map/cond/branch_1_fun/ppermute | solution.py:39
  100.6 22.8 %collective-permute-start.21 = (bf16[128,2048]{1,0:T(8,128)(2,1)S(1)}, bf16[128,2048]{1,0:T(8,128)(2,1)S(1)}, u32[]{:S(2)}, u32[]{:S(2)}) collective-permute-start(bf16[128,2048]{1,0:T(8,128)(2,1)S(1)} %copy-done.22), channel_id=1, source_target_pairs={{0,16},{4,20},{8,24},{12,28},{16,0},{20,4},{24,8},{28,12},{1,17},{... | collective-permute-start | bytes 1572872 | tf_op jit(solution)/shard_map/cond/branch_1_fun/ppermute | solution.py:39
  101.9 21.5 %collective-permute-start.20 = (bf16[128,2048]{1,0:T(8,128)(2,1)S(1)}, bf16[128,2048]{1,0:T(8,128)(2,1)S(1)}, u32[]{:S(2)}, u32[]{:S(2)}) collective-permute-start(bf16[128,2048]{1,0:T(8,128)(2,1)S(1)} %copy-done.22), channel_id=1, source_target_pairs={{0,8},{4,12},{8,0},{12,4},{16,24},{20,28},{24,16},{28,20},{1,9},{5... | collective-permute-start | bytes 1572872 | tf_op jit(solution)/shard_map/cond/branch_1_fun/ppermute | solution.py:39
  125.6 17.8 %collective-permute-start.22 = (bf16[4,2048,256]{2,1,0:T(8,128)(2,1)}, bf16[4,2048,256]{2,1,0:T(8,128)(2,1)}, u32[]{:S(2)}, u32[]{:S(2)}) collective-permute-start(bf16[4,2048,256]{2,1,0:T(8,128)(2,1)} %branch_1_fun.31.even_ref), channel_id=1, source_target_pairs={{0,4},{4,0},{8,12},{12,8},{16,20},{20,16},{24,28},{28,24},{1,5},{5... | collective-permute-start | bytes 12582920 | tf_op jit(solution)/shard_map/cond/branch_1_fun/ppermute | solution.py:39
  128.4 15.0 %collective-permute-start.27 = (bf16[64,2048]{1,0:T(8,128)(2,1)S(1)}, bf16[64,2048]{1,0:T(8,128)(2,1)S(1)}, u32[]{:S(2)}, u32[]{:S(2)}) collective-permute-start(bf16[64,2048]{1,0:T(8,128)(2,1)S(1)} %slice.192), channel_id=1, source_target_pairs={{0,8},{4,12},{8,0},{12,4},{16,24},{20,28},{24,16},{28,20},{1,9},{5... | collective-permute-start | bytes 786440 | tf_op jit(solution)/shard_map/cond/branch_1_fun/ppermute | solution.py:39
  129.6 13.8 %collective-permute-start.26 = (bf16[64,2048]{1,0:T(8,128)(2,1)S(1)}, bf16[64,2048]{1,0:T(8,128)(2,1)S(1)}, u32[]{:S(2)}, u32[]{:S(2)}) collective-permute-start(bf16[64,2048]{1,0:T(8,128)(2,1)S(1)} %slice.191), channel_id=1, source_target_pairs={{0,16},{4,20},{8,24},{12,28},{16,0},{20,4},{24,8},{28,12},{1,17},{... | collective-permute-start | bytes 786440 | tf_op jit(solution)/shard_map/cond/branch_1_fun/ppermute | solution.py:39
  130.3 13.0 %collective-permute-start.24 = (bf16[2,128,256]{2,1,0:T(8,128)(2,1)}, bf16[2,128,256]{2,1,0:T(8,128)(2,1)S(1)}, u32[]{:S(2)}, u32[]{:S(2)}) collective-permute-start(bf16[2,128,256]{2,1,0:T(8,128)(2,1)} %get-tuple-element.153), channel_id=1, source_target_pairs={{0,16},{4,20},{8,24},{12,28},{16,0},{20,4},{24,8},{28,12},{1,17},{... | collective-permute-start | bytes 393224 | tf_op jit(solution)/shard_map/cond/branch_1_fun/ppermute | solution.py:39
  145.6 30.5 %collective-permute-start.30 = (bf16[4,128,2048]{2,1,0:T(8,128)(2,1)S(1)}, bf16[4,128,2048]{2,1,0:T(8,128)(2,1)}, u32[]{:S(2)}, u32[]{:S(2)}) collective-permute-start(bf16[4,128,2048]{2,1,0:T(8,128)(2,1)S(1)} %branch_1_fun.35.mine_ref), channel_id=1, source_target_pairs={{0,4},{4,0},{8,12},{12,8},{16,20},{20,16},{24,28},{28,24},{1,5},{5... | collective-permute-start | bytes 6291464 | tf_op jit(solution)/shard_map/cond/branch_1_fun/ppermute | solution.py:39
  162.0 13.6 %collective-permute-start.29 = (bf16[128,2048]{1,0:T(8,128)(2,1)S(1)}, bf16[128,2048]{1,0:T(8,128)(2,1)S(1)}, u32[]{:S(2)}, u32[]{:S(2)}) collective-permute-start(bf16[128,2048]{1,0:T(8,128)(2,1)S(1)} %multiply_convert_fusion.refs_0_), channel_id=1, source_target_pairs={{0,16},{4,20},{8,24},{12,28},{16,0},{20,4},{24,8},{28,12},{1,17},{... | collective-permute-start | bytes 1572872 | tf_op jit(solution)/shard_map/cond/branch_1_fun/ppermute | solution.py:39
  162.8 13.3 %collective-permute-start.28 = (bf16[128,2048]{1,0:T(8,128)(2,1)S(1)}, bf16[128,2048]{1,0:T(8,128)(2,1)S(1)}, u32[]{:S(2)}, u32[]{:S(2)}) collective-permute-start(bf16[128,2048]{1,0:T(8,128)(2,1)S(1)} %multiply_convert_fusion.refs_0_), channel_id=1, source_target_pairs={{0,8},{4,12},{8,0},{12,4},{16,24},{20,28},{24,16},{28,20},{1,9},{5... | collective-permute-start | bytes 1572872 | tf_op jit(solution)/shard_map/cond/branch_1_fun/ppermute | solution.py:39
  194.5 14.5 %collective-permute-start.35 = (bf16[128,2048]{1,0:T(8,128)(2,1)}, bf16[128,2048]{1,0:T(8,128)(2,1)S(1)}, u32[]{:S(2)}, u32[]{:S(2)}) collective-permute-start(bf16[128,2048]{1,0:T(8,128)(2,1)} %get-tuple-element.179.refs_0_), channel_id=1, source_target_pairs={{0,16},{4,20},{8,24},{12,28},{16,0},{20,4},{24,8},{28,12},{1,17},{... | collective-permute-start | bytes 1572872 | tf_op jit(solution)/shard_map/cond/branch_1_fun/ppermute | solution.py:39
  195.9 13.7 %collective-permute-start.34 = (bf16[128,2048]{1,0:T(8,128)(2,1)}, bf16[128,2048]{1,0:T(8,128)(2,1)S(1)}, u32[]{:S(2)}, u32[]{:S(2)}) collective-permute-start(bf16[128,2048]{1,0:T(8,128)(2,1)} %get-tuple-element.179.refs_0_), channel_id=1, source_target_pairs={{0,8},{4,12},{8,0},{12,4},{16,24},{20,28},{24,16},{28,20},{1,9},{5... | collective-permute-start | bytes 1572872 | tf_op jit(solution)/shard_map/cond/branch_1_fun/ppermute | solution.py:39
  230.5 166.2 %reduce-scatter.6.cloned.1.call-start = ((), (), s32[]{:S(2)}) async-start(), calls=%async_computation.7 | async-start | bytes 7208960 | tf_op jit(solution)/shard_map/reduce_scatter | solution.py:750
  262.2 13.0 %collective-permute-start.42 = (bf16[128,2048]{1,0:T(8,128)(2,1)S(1)}, bf16[128,2048]{1,0:T(8,128)(2,1)S(1)}, u32[]{:S(2)}, u32[]{:S(2)}) collective-permute-start(bf16[128,2048]{1,0:T(8,128)(2,1)S(1)} %pad_maximum_fusion), channel_id=1, source_target_pairs={{0,8},{4,12},{8,0},{12,4},{16,24},{20,28},{24,16},{28,20},{1,9},{5... | collective-permute-start | bytes 1572872 | tf_op jit(solution)/shard_map/cond/branch_1_fun/ppermute | solution.py:39
  263.8 12.7 %collective-permute-start.43 = (bf16[128,2048]{1,0:T(8,128)(2,1)S(1)}, bf16[128,2048]{1,0:T(8,128)(2,1)S(1)}, u32[]{:S(2)}, u32[]{:S(2)}) collective-permute-start(bf16[128,2048]{1,0:T(8,128)(2,1)S(1)} %pad_maximum_fusion.1), channel_id=1, source_target_pairs={{0,16},{4,20},{8,24},{12,28},{16,0},{20,4},{24,8},{28,12},{1,17},{... | collective-permute-start | bytes 1572872 | tf_op jit(solution)/shard_map/cond/branch_1_fun/ppermute | solution.py:39
  289.4 163.2 %reduce-scatter.8.cloned.1.call-start = ((), (), s32[]{:S(2)}) async-start(), calls=%async_computation.8 | async-start | bytes 3276800 | tf_op jit(solution)/shard_map/reduce_scatter | solution.py:750
  296.5 11.2 %collective-permute-start.45 = (bf16[2,128,512]{2,1,0:T(8,128)(2,1)}, bf16[2,128,512]{2,1,0:T(8,128)(2,1)S(1)}, u32[]{:S(2)}, u32[]{:S(2)}) collective-permute-start(bf16[2,128,512]{2,1,0:T(8,128)(2,1)} %get-tuple-element.225), channel_id=1, source_target_pairs={{0,8},{4,12},{8,0},{12,4},{16,24},{20,28},{24,16},{28,20},{1,9},{5... | collective-permute-start | bytes 786440 | tf_op jit(solution)/shard_map/cond/branch_1_fun/ppermute | solution.py:39
  297.9 13.9 %collective-permute-start.46 = (bf16[2,128,512]{2,1,0:T(8,128)(2,1)}, bf16[2,128,512]{2,1,0:T(8,128)(2,1)S(1)}, u32[]{:S(2)}, u32[]{:S(2)}) collective-permute-start(bf16[2,128,512]{2,1,0:T(8,128)(2,1)} %get-tuple-element.226), channel_id=1, source_target_pairs={{0,16},{4,20},{8,24},{12,28},{16,0},{20,4},{24,8},{28,12},{1,17},{... | collective-permute-start | bytes 786440 | tf_op jit(solution)/shard_map/cond/branch_1_fun/ppermute | solution.py:39
  299.4 12.4 %collective-permute-start.47 = (bf16[2,128,512]{2,1,0:T(8,128)(2,1)}, bf16[2,128,512]{2,1,0:T(8,128)(2,1)S(1)}, u32[]{:S(2)}, u32[]{:S(2)}) collective-permute-start(bf16[2,128,512]{2,1,0:T(8,128)(2,1)} %get-tuple-element.227), channel_id=1, source_target_pairs={{0,24},{4,28},{8,16},{12,20},{16,8},{20,12},{24,0},{28,4},{1,25},{... | collective-permute-start | bytes 786440 | tf_op jit(solution)/shard_map/cond/branch_1_fun/ppermute | solution.py:39
  311.8 19.8 %collective-permute-start.50 = (bf16[4,128,2048]{2,1,0:T(8,128)(2,1)S(1)}, bf16[4,128,2048]{2,1,0:T(8,128)(2,1)S(1)}, u32[]{:S(2)}, u32[]{:S(2)}) collective-permute-start(bf16[4,128,2048]{2,1,0:T(8,128)(2,1)S(1)} %bitcast.186), channel_id=1, source_target_pairs={{0,4},{4,0},{8,12},{12,8},{16,20},{20,16},{24,28},{28,24},{1,5},{5... | collective-permute-start | bytes 6291464 | tf_op jit(solution)/shard_map/cond/branch_1_fun/ppermute | solution.py:39
  311.8 18.5 %collective-permute-start.49 = (bf16[176,2048]{1,0:T(8,128)(2,1)S(1)}, bf16[176,2048]{1,0:T(8,128)(2,1)S(1)}, u32[]{:S(2)}, u32[]{:S(2)}) collective-permute-start(bf16[176,2048]{1,0:T(8,128)(2,1)S(1)} %copy-done.24), channel_id=1, source_target_pairs={{0,16},{4,20},{8,24},{12,28},{16,0},{20,4},{24,8},{28,12},{1,17},{... | collective-permute-start | bytes 2162696 | tf_op jit(solution)/shard_map/cond/branch_1_fun/ppermute | solution.py:39
  313.4 18.2 %collective-permute-start.48 = (bf16[176,2048]{1,0:T(8,128)(2,1)S(1)}, bf16[176,2048]{1,0:T(8,128)(2,1)S(1)}, u32[]{:S(2)}, u32[]{:S(2)}) collective-permute-start(bf16[176,2048]{1,0:T(8,128)(2,1)S(1)} %copy-done.24), channel_id=1, source_target_pairs={{0,8},{4,12},{8,0},{12,4},{16,24},{20,28},{24,16},{28,20},{1,9},{5... | collective-permute-start | bytes 2162696 | tf_op jit(solution)/shard_map/cond/branch_1_fun/ppermute | solution.py:39
  332.4 17.4 %collective-permute-start.51 = (bf16[80,2048]{1,0:T(8,128)(2,1)}, bf16[80,2048]{1,0:T(8,128)(2,1)S(1)}, u32[]{:S(2)}, u32[]{:S(2)}) collective-permute-start(bf16[80,2048]{1,0:T(8,128)(2,1)} %slice.214), channel_id=1, source_target_pairs={{0,16},{4,20},{8,24},{12,28},{16,0},{20,4},{24,8},{28,12},{1,17},{... | collective-permute-start | bytes 983048 | tf_op jit(solution)/shard_map/cond/branch_1_fun/ppermute | solution.py:39
  333.7 16.1 %collective-permute-start.52 = (bf16[96,2048]{1,0:T(8,128)(2,1)}, bf16[96,2048]{1,0:T(8,128)(2,1)S(1)}, u32[]{:S(2)}, u32[]{:S(2)}) collective-permute-start(bf16[96,2048]{1,0:T(8,128)(2,1)} %slice.215), channel_id=1, source_target_pairs={{0,8},{4,12},{8,0},{12,4},{16,24},{20,28},{24,16},{28,20},{1,9},{5... | collective-permute-start | bytes 1179656 | tf_op jit(solution)/shard_map/cond/branch_1_fun/ppermute | solution.py:39
  338.6 11.2 %collective-permute-start.53 = (bf16[64,2048]{1,0:T(8,128)(2,1)S(1)}, bf16[64,2048]{1,0:T(8,128)(2,1)S(1)}, u32[]{:S(2)}, u32[]{:S(2)}) collective-permute-start(bf16[64,2048]{1,0:T(8,128)(2,1)S(1)} %get-tuple-element.425), channel_id=1, source_target_pairs={{0,8},{4,12},{8,0},{12,4},{16,24},{20,28},{24,16},{28,20},{1,9},{5... | collective-permute-start | bytes 786440 | tf_op jit(solution)/shard_map/cond/branch_1_fun/ppermute | solution.py:39
  352.1 17.1 %collective-permute-start.56 = (bf16[4,176,2048]{2,1,0:T(8,128)(2,1)}, bf16[4,176,2048]{2,1,0:T(8,128)(2,1)}, u32[]{:S(2)}, u32[]{:S(2)}) collective-permute-start(bf16[4,176,2048]{2,1,0:T(8,128)(2,1)} %branch_1_fun.47), channel_id=1, source_target_pairs={{0,4},{4,0},{8,12},{12,8},{16,20},{20,16},{24,28},{28,24},{1,5},{5... | collective-permute-start | bytes 8650760 | tf_op jit(solution)/shard_map/cond/branch_1_fun/ppermute | solution.py:39
  353.4 15.7 %collective-permute-start.55 = (bf16[4,128,2048]{2,1,0:T(8,128)(2,1)S(1)}, bf16[4,128,2048]{2,1,0:T(8,128)(2,1)S(1)}, u32[]{:S(2)}, u32[]{:S(2)}) collective-permute-start(bf16[4,128,2048]{2,1,0:T(8,128)(2,1)S(1)} %bitcast.163), channel_id=1, source_target_pairs={{0,4},{4,0},{8,12},{12,8},{16,20},{20,16},{24,28},{28,24},{1,5},{5... | collective-permute-start | bytes 6291464 | tf_op jit(solution)/shard_map/cond/branch_1_fun/ppermute | solution.py:39
  354.2 13.9 %collective-permute-start.57 = (bf16[128,2048]{1,0:T(8,128)(2,1)S(1)}, bf16[128,2048]{1,0:T(8,128)(2,1)S(1)}, u32[]{:S(2)}, u32[]{:S(2)}) collective-permute-start(bf16[128,2048]{1,0:T(8,128)(2,1)S(1)} %pad_maximum_fusion.2), channel_id=1, source_target_pairs={{0,8},{4,12},{8,0},{12,4},{16,24},{20,28},{24,16},{28,20},{1,9},{5... | collective-permute-start | bytes 1572872 | tf_op jit(solution)/shard_map/cond/branch_1_fun/ppermute | solution.py:39
  355.5 13.6 %collective-permute-start.58 = (bf16[128,2048]{1,0:T(8,128)(2,1)S(1)}, bf16[128,2048]{1,0:T(8,128)(2,1)S(1)}, u32[]{:S(2)}, u32[]{:S(2)}) collective-permute-start(bf16[128,2048]{1,0:T(8,128)(2,1)S(1)} %pad_maximum_fusion.3), channel_id=1, source_target_pairs={{0,16},{4,20},{8,24},{12,28},{16,0},{20,4},{24,8},{28,12},{1,17},{... | collective-permute-start | bytes 1572872 | tf_op jit(solution)/shard_map/cond/branch_1_fun/ppermute | solution.py:39
  378.0 11.8 %collective-permute-start.61 = (bf16[128,2048]{1,0:T(8,128)(2,1)S(1)}, bf16[128,2048]{1,0:T(8,128)(2,1)S(1)}, u32[]{:S(2)}, u32[]{:S(2)}) collective-permute-start(bf16[128,2048]{1,0:T(8,128)(2,1)S(1)} %pad_maximum_fusion.4), channel_id=1, source_target_pairs={{0,8},{4,12},{8,0},{12,4},{16,24},{20,28},{24,16},{28,20},{1,9},{5... | collective-permute-start | bytes 1572872 | tf_op jit(solution)/shard_map/cond/branch_1_fun/ppermute | solution.py:39
  379.6 11.5 %collective-permute-start.62 = (bf16[128,2048]{1,0:T(8,128)(2,1)S(1)}, bf16[128,2048]{1,0:T(8,128)(2,1)S(1)}, u32[]{:S(2)}, u32[]{:S(2)}) collective-permute-start(bf16[128,2048]{1,0:T(8,128)(2,1)S(1)} %pad_maximum_fusion.5), channel_id=1, source_target_pairs={{0,16},{4,20},{8,24},{12,28},{16,0},{20,4},{24,8},{28,12},{1,17},{... | collective-permute-start | bytes 1572872 | tf_op jit(solution)/shard_map/cond/branch_1_fun/ppermute | solution.py:39
  396.7 33.6 %collective-permute-start.1 = (bf16[512,1408]{1,0:T(8,128)(2,1)}, bf16[512,1408]{1,0:T(8,128)(2,1)S(1)}, u32[]{:S(2)}, u32[]{:S(2)}) collective-permute-start(bf16[512,1408]{1,0:T(8,128)(2,1)} %get-tuple-element.270.refs_0_), channel_id=1, source_target_pairs={{0,16},{4,20},{8,24},{12,28},{16,0},{20,4},{24,8},{28,12},{1,17},{... | collective-permute-start | bytes 4325384 | tf_op jit(solution)/shard_map/cond/branch_1_fun/ppermute | solution.py:39
  398.2 33.3 %collective-permute-start = (bf16[512,1408]{1,0:T(8,128)(2,1)}, bf16[512,1408]{1,0:T(8,128)(2,1)S(1)}, u32[]{:S(2)}, u32[]{:S(2)}) collective-permute-start(bf16[512,1408]{1,0:T(8,128)(2,1)} %get-tuple-element.270.refs_0_), channel_id=1, source_target_pairs={{0,8},{4,12},{8,0},{12,4},{16,24},{20,28},{24,16},{28,20},{1,9},{5... | collective-permute-start | bytes 4325384 | tf_op jit(solution)/shard_map/cond/branch_1_fun/ppermute | solution.py:39
  431.6 16.9 %collective-permute-start.3 = (bf16[256,1408]{1,0:T(8,128)(2,1)S(1)}, bf16[256,1408]{1,0:T(8,128)(2,1)S(1)}, u32[]{:S(2)}, u32[]{:S(2)}) collective-permute-start(bf16[256,1408]{1,0:T(8,128)(2,1)S(1)} %slice.247), channel_id=1, source_target_pairs={{0,8},{4,12},{8,0},{12,4},{16,24},{20,28},{24,16},{28,20},{1,9},{5... | collective-permute-start | bytes 2162696 | tf_op jit(solution)/shard_map/cond/branch_1_fun/ppermute | solution.py:39
  433.1 16.6 %collective-permute-start.2 = (bf16[256,1408]{1,0:T(8,128)(2,1)S(1)}, bf16[256,1408]{1,0:T(8,128)(2,1)S(1)}, u32[]{:S(2)}, u32[]{:S(2)}) collective-permute-start(bf16[256,1408]{1,0:T(8,128)(2,1)S(1)} %slice.246), channel_id=1, source_target_pairs={{0,16},{4,20},{8,24},{12,28},{16,0},{20,4},{24,8},{28,12},{1,17},{... | collective-permute-start | bytes 2162696 | tf_op jit(solution)/shard_map/cond/branch_1_fun/ppermute | solution.py:39
  452.7 18.1 %collective-permute-start.65 = (bf16[512,640]{1,0:T(8,128)(2,1)}, bf16[512,640]{1,0:T(8,128)(2,1)S(1)}, u32[]{:S(2)}, u32[]{:S(2)}) collective-permute-start(bf16[512,640]{1,0:T(8,128)(2,1)} %get-tuple-element.282.refs_0_), channel_id=1, source_target_pairs={{0,16},{4,20},{8,24},{12,28},{16,0},{20,4},{24,8},{28,12},{1,17},{... | collective-permute-start | bytes 1966088 | tf_op jit(solution)/shard_map/cond/branch_1_fun/ppermute | solution.py:39
  453.7 17.1 %collective-permute-start.64 = (bf16[512,640]{1,0:T(8,128)(2,1)}, bf16[512,640]{1,0:T(8,128)(2,1)S(1)}, u32[]{:S(2)}, u32[]{:S(2)}) collective-permute-start(bf16[512,640]{1,0:T(8,128)(2,1)} %get-tuple-element.282.refs_0_), channel_id=1, source_target_pairs={{0,8},{4,12},{8,0},{12,4},{16,24},{20,28},{24,16},{28,20},{1,9},{5... | collective-permute-start | bytes 1966088 | tf_op jit(solution)/shard_map/cond/branch_1_fun/ppermute | solution.py:39
  458.2 12.6 %collective-permute-start.66 = (f32[2,512]{1,0:T(2,128)S(1)}, f32[2,512]{1,0:T(2,128)S(1)}, u32[]{:S(2)}, u32[]{:S(2)}) collective-permute-start(f32[2,512]{1,0:T(2,128)S(1)} %pad_maximum_fusion.6), channel_id=1, source_target_pairs={{0,4},{4,0},{8,12},{12,8},{16,20},{20,16},{24,28},{28,24},{1,5},{5... | collective-permute-start | bytes 12296 | tf_op jit(solution)/shard_map/cond/branch_1_fun/ppermute | solution.py:39
  (67 other events, 743.4 us)
Sparse Core Ops, SparseCore 0:
  9.6 58.5 all-gather.3
  69.7 105.3 all-gather.5
  177.2 57.4 all-gather.7
  236.9 54.8 reduce-scatter.3
  294.5 102.1 reduce-scatter.5
  399.4 52.6 reduce-scatter.7

commit v6 on v5

--- a/solution.py
+++ b/solution.py
@@ -118,6 +118,22 @@
 
 def halves_chain(part):
     return in_turn(lambda _: near_chain(part), core_chain)
+
+
+def pieces_chain(part):
+    if lax.axis_size("seq") == 8 and part.shape[0] % 32 == 0:
+        half = part.shape[0] // 2
+        by_x, by_y = yield swap(part, 2), swap(part, 4)
+        near = part, by_x, by_y
+        far, other = yield (
+            (swap(by_x[:half], 4), swap(by_y[half:], 2)),
+            tuple(swap(piece, 1) for piece in near),
+        )
+        other_far = yield tuple(swap(piece, 1) for piece in far)
+        places = ((0, 0), (1, 0), (2, 0), (3, 0), (3, half))
+        return (*near, *far), (*other, *other_far), places
+    mine, other = yield from halves_chain(part)
+    return tuple(mine), tuple(other), tuple((k, 0) for k in range(mine.shape[0]))
 
 
 def gather_chain(part):
@@ -242,13 +258,24 @@
     )(place, even, odd)
 
 
-def put_attention(even, odd, place, q_cols, out_cols):
-    half, rows, cols = even.shape
+def put_attention(even, odd, places, place, q_cols, out_cols):
+    half = max(slot for slot, _ in places) + 1
+    rows, cols = even[0].shape
     n, tile = 2 * half, 64
     copies = n // KV_HEADS
     sizes = (n * q_cols, KV_HEADS * HEAD_DIM, KV_HEADS * HEAD_DIM, n * out_cols)
 
-    def kernel(place_ref, even_ref, odd_ref, query_ref, key_ref, value_ref, out_ref):
+    def kernel(place_ref, *refs):
+        count, step = len(places), pl.program_id(0)
+        query_ref, key_ref, value_ref, out_ref, even_ref, odd_ref = refs[2 * count :]
+        for held_ref, piece_refs in ((even_ref, refs[:count]), (odd_ref, refs[count : 2 * count])):
+            for (slot, row), piece, ref in zip(places, even, piece_refs):
+                first, steps = row // tile, piece.shape[0] // tile
+
+                @pl.when((step >= first) & (step < first + steps))
+                def _(held_ref=held_ref, slot=slot, ref=ref):
+                    held_ref[slot] = ref[...]
+
         chip = place_ref[0] // 2
 
         def body(first, second):
@@ -267,16 +294,21 @@
 
         ordered(place_ref[0], even_ref, odd_ref, body)
 
-    spec = pl.BlockSpec((half, tile, cols), lambda i: (0, i, 0))
+    def spec(row, piece):
+        first, last = row // tile, piece.shape[0] // tile - 1
+        return pl.BlockSpec((tile, cols), lambda i: (jnp.clip(i - first, 0, last), 0))
+
+    specs = [spec(row, piece) for (_, row), piece in zip(places, even)]
     return pl.pallas_call(
         kernel,
         grid=(rows // tile,),
         out_shape=[jax.ShapeDtypeStruct((rows, size), jnp.float32) for size in sizes],
-        in_specs=[pl.BlockSpec(memory_space=pltpu.SMEM), spec, spec],
+        in_specs=[pl.BlockSpec(memory_space=pltpu.SMEM)] + specs * 2,
         out_specs=[pl.BlockSpec((tile, size), lambda i: (i, 0)) for size in sizes],
+        scratch_shapes=[pltpu.VMEM((half, tile, cols), even[0].dtype)] * 2,
         compiler_params=pltpu.CompilerParams(vmem_limit_bytes=48 * 2**20),
-        cost_estimate=pl.CostEstimate(flops=0, bytes_accessed=even.size * 12, transcendentals=0),
-    )(place, even, odd)
+        cost_estimate=pl.CostEstimate(flops=0, bytes_accessed=half * rows * cols * 12, transcendentals=0),
+    )(place, *even, *odd)
 
 
 def slot_of(mask, n):
@@ -941,8 +973,8 @@
                 mask *= 2
             return sums
 
-        puts, attn_halves, sums = together(columns_put(), halves_chain(attn_sum), sums_chain())
-        return *puts, sums, *put_attention(*attn_halves, place_arg, q_cols, out_cols)
+        puts, attn_pieces, sums = together(columns_put(), pieces_chain(attn_sum), sums_chain())
+        return *puts, sums, *put_attention(*attn_pieces, place_arg, q_cols, out_cols)
 
     grad_gate, grad_up, row_sums, grad_query, grad_key, grad_value, grad_out = stage(
         sure, last_stage, mine, mlp_sum, mlp_own, after(attn_sum, grad_down), attn_own

time: 509 us -> 510 us (level)
    ppermute x69 -> x73, starting transfers between devices: 64.3 us -> 65.5 us  [swap(): lax.ppermute(value, 'seq', [(i, i ^ mask) for i in range(lax.axis_size('s...]
    ppermute x69 -> x73, waiting for transfers between devices: 173 us -> 173 us  [swap(): lax.ppermute(value, 'seq', [(i, i ^ mask) for i in range(lax.axis_size('s...]
    pallas_call x8 -> x7, Pallas kernels: 14.6 us -> 14.4 us  [place_pieces(): pl.pallas_call(kernel, grid=(cols // tile,), out_shape=jax.ShapeDtypeStru...]
  transfers between devices with their start and end apart: 78 -> 82, of which waited for: 45 -> 45; matrix products, arithmetic and copies ran while one was open for 17% -> 17% of each run, Pallas kernels for 27% -> 27%
where the time goes in v6:
time: 510 us; the launch traced here: 502 us
  waiting for transfers between devices  183 us (36%)
  Pallas kernels  142 us (28%)
  starting transfers between devices  70.5 us (14%)
  matrix products  43.3 us (8%)
  other arithmetic  29.8 us (6%)
  local copies, waits for them, and re-layouts  16 us (3%)
  between operations  14.8 us (3%)
    ppermute x73, waiting for transfers between devices, swap(): lax.ppermute(value, 'seq', [(i, i ^ mask) for i in range(lax.axis_size('s...  173 us
    ppermute x73, starting transfers between devices, swap(): lax.ppermute(value, 'seq', [(i, i ^ mask) for i in range(lax.axis_size('s...  65.5 us
    dot_general x6, matrix products, dot(): lax.dot_general(left, right, ((dims[0], dims[1]), ((), ())), preferred_el...  24.8 us
    pallas_call x4, Pallas kernels, gather_chain(): pl.pallas_call(kernel, grid=(cols // tile,), out_shape=jax.ShapeDtypeStru...  19.5 us
    pallas_call x2, Pallas kernels, row_products(): pl.pallas_call(kernel, grid=(width // tile,), out_shape=jax.ShapeDtypeStr...  17.1 us
    pallas_call x4, Pallas kernels, put_columns(): pl.pallas_call(kernel, grid=(steps,), out_shape=(whole, whole), in_specs=...  17 us
    pallas_call x7, Pallas kernels, place_pieces(): pl.pallas_call(kernel, grid=(cols // tile,), out_shape=jax.ShapeDtypeStru...  14.4 us
    pallas_call x1, Pallas kernels, attention_back(): pl.pallas_call(kernel, out_shape=[jax.ShapeDtypeStruct((n, rows, cols), l...  12.8 us
  transfers between devices with their start and end apart: 82, of which 45 were waited for; matrix products, arithmetic and copies ran while one was open for 17% of the time, Pallas kernels for 27%

profile of v6, /device:TPU:0, one launch (start us, length us, event | category | flops | bytes accessed | tf_op | source)
XLA Modules:
  0.0 502.1 jit_solution(9208025812566055758)
XLA Ops:
  17.1 50.2 %conditional.7 = (f32[2,2048]{1,0:T(2,128)}, f32[8,128,128]{2,1,0:T(8,128)}, f32[8,128,128]{2,1,0:T(8,128)}, bf16[1024,2048]{1,0:T(8,128)(2,1)}, f32[1,2048]{1,0:T(1,128)S(1)}, /*index=5*/f32[1,2048]{1,0:T(1,128)}) conditional(s32[]{:T(128)} %bitcast.47, () %tuple.104, (s32[]{:T(128)}, f32[2,512]{1,0:T(2,128)S(1)}, s32[1,128]{1,0:T(1,128)S(1)}, ...), branch_computations={%region_0.0_spmd, %region_1.3_spmd} | conditional | flops 14957828 | bytes 78052016 | solution.py:704
  23.9 9.8 %collective-permute-done.5 = s32[1,1,128]{2,1,0:T(1,128)S(1)} collective-permute-done((s32[1,1,128]{2,1,0:T(1,128)S(1)}, s32[1,1,128]{2,1,0:T(1,128)S(1)}, u32[]{:S(2)}, u32[]{:S(2)}) %collective-permute-start.5) | collective-permute-done | bytes 544 | tf_op jit(solution)/shard_map/cond/branch_1_fun/ppermute | solution.py:39
  52.4 4.7 branch_1_fun.28
  60.6 3.7 fusion.1
  70.9 123.4 %conditional.8 = (bf16[128,2048]{1,0:T(8,128)(2,1)}, bf16[2048,2048]{1,0:T(8,128)(2,1)}, f32[128,2048]{1,0:T(8,128)}, bf16[1024,2048]{1,0:T(8,128)(2,1)}, f32[10...) conditional(s32[]{:T(128)} %bitcast.47, () %tuple.103, ...), branch_computations={%region_3.4_spmd, %region_4.6_spmd} | conditional | flops 3759931648 | bytes 181939232 | solution.py:704
  75.1 5.0 fusion.49
  80.2 9.7 %branch_1_fun.29 = (bf16[4,128,256]{2,1,0:T(8,128)(2,1)S(1)}, bf16[4,128,256]{2,1,0:T(8,128)(2,1)S(1)}, f32[1024,256]{1,0:T(8,128)}, bf16[1024,384]{1,0:T(8,128)...) custom-call(s32[1]{0:T(128)} %get-tuple-element.130.place_ref, f32[8,128,384]{2,1,0:T(8,128)S(1)} %bitcast.156, ...), custom_call_target="tpu_custom_call" | custom-call | flops 1073741824 | bytes 3145728 | tf_op jit(solution)/shard_map/cond/branch_1_fun/pallas_call | solution.py:490
  89.9 7.3 %collective-permute-done.16.refs_2_ = bf16[2048,256]{1,0:T(8,128)(2,1)S(1)} collective-permute-done((bf16[2048,256]{1,0:T(8,128)(2,1)S(1)}, bf16[2048,256]{1,0:T(8,128)(2,1)S(1)}, u32[]{:S(2)}, u32[]{:S(2)}) %collective-permute-start.16) | collective-permute-done | bytes 1048608 | tf_op jit(solution)/shard_map/cond/branch_1_fun/ppermute | solution.py:39
  104.2 9.3 %collective-permute-done.18.refs_4_ = bf16[1024,256]{1,0:T(8,128)(2,1)S(1)} collective-permute-done((bf16[1024,256]{1,0:T(8,128)(2,1)S(1)}, bf16[1024,256]{1,0:T(8,128)(2,1)S(1)}, u32[]{:S(2)}, u32[]{:S(2)}) %collective-permute-start.18) | collective-permute-done | bytes 524320 | tf_op jit(solution)/shard_map/cond/branch_1_fun/ppermute | solution.py:39
  114.7 8.6 %collective-permute-done.21.refs_2_ = bf16[128,2048]{1,0:T(8,128)(2,1)S(1)} collective-permute-done((bf16[128,2048]{1,0:T(8,128)(2,1)S(1)}, bf16[128,2048]{1,0:T(8,128)(2,1)S(1)}, u32[]{:S(2)}, u32[]{:S(2)}) %collective-permute-start.21) | collective-permute-done | bytes 524320 | tf_op jit(solution)/shard_map/cond/branch_1_fun/ppermute | solution.py:39
  134.9 8.5 %collective-permute-done.24.refs_2_ = bf16[2,128,256]{2,1,0:T(8,128)(2,1)S(1)} collective-permute-done((bf16[2,128,256]{2,1,0:T(8,128)(2,1)}, bf16[2,128,256]{2,1,0:T(8,128)(2,1)S(1)}, u32[]{:S(2)}, u32[]{:S(2)}) %collective-permute-start.24) | collective-permute-done | bytes 131104 | tf_op jit(solution)/shard_map/cond/branch_1_fun/ppermute | solution.py:39
  145.7 7.1 %branch_1_fun.33 = bf16[2048,2048]{1,0:T(8,128)(2,1)} custom-call(s32[1]{0:T(128)} %get-tuple-element.130.place_ref, bf16[4,2048,256]{2,1,0:T(8,128)(2,1)S(1)} %copy-done, bf16[4,2048,256]{2,1,0:T(8,128)(2,1)} %collective-permute-done.22.odd_ref), custom_call_target="tpu_custom_call" | custom-call | bytes 16777216 | tf_op jit(solution)/shard_map/cond/branch_1_fun/pallas_call | solution.py:389
  154.7 5.8 %multiply_reduce_fusion.1 = (f32[128]{0:T(128)S(1)}, f32[128,2048]{1,0:T(8,128)}) fusion(bf16[128,2048]{1,0:T(8,128)(2,1)} %branch_1_fun.32, bf16[2048,2048]{1,0:T(8,128)(2,1)} %branch_1_fun.33, bf16[128,2048]{1,0:T(8,128)(2,1)S(1)} %copy-done.13), kind=kOutput, calls=%fused_computation.22 | convolution fusion | flops 1074790272 | bytes 10486272 | tf_op jit(solution)/shard_map/cond/branch_1_fun/dot_general | solution.py:846
  163.5 12.1 %collective-permute-done.29.refs_2_ = bf16[128,2048]{1,0:T(8,128)(2,1)S(1)} collective-permute-done((bf16[128,2048]{1,0:T(8,128)(2,1)S(1)}, bf16[128,2048]{1,0:T(8,128)(2,1)S(1)}, u32[]{:S(2)}, u32[]{:S(2)}) %collective-permute-start.29) | collective-permute-done | bytes 524320 | tf_op jit(solution)/shard_map/cond/branch_1_fun/ppermute | solution.py:39
  178.4 4.7 collective-permute-done.32.refs_4_
  184.1 5.4 %branch_1_fun.37 = bf16[8,128,2048]{2,1,0:T(8,128)(2,1)} custom-call(bf16[4,128,2048]{2,1,0:T(8,128)(2,1)} %copy-done.1, bf16[4,128,2048]{2,1,0:T(8,128)(2,1)} %collective-permute-done.30.other_ref), custom_call_target="tpu_custom_call" | custom-call | bytes 8388608 | tf_op jit(solution)/shard_map/cond/branch_1_fun/pallas_call | solution.py:150
  189.6 4.7 branch_1_fun.36
  194.3 36.2 %conditional.9 = (bf16[1024,2048]{1,0:T(8,128)(2,1)}, f32[1024,1408]{1,0:T(8,128)}, bf16[1024,704]{1,0:T(8,128)(2,1)}, bf16[704,2048]{1,0:T(8,128)(2,1)}) conditional(s32[]{:T(128)} %bitcast.47, () %tuple.107, (bf16[1024,2048]{1,0:T(8,128)(2,1)}, bf16[2048,1408]{1,0:T(8,128)(2,1)}, bf16[128,2048]{1,0:T(8,128)(2,1)}, ...), branch_computations={%region_6.7_spmd, %region_7.8_spmd} | conditional | flops 8859811840 | bytes 56754436 | solution.py:704
  197.1 11.9 %branch_1_fun.38 = (f32[1024,1408]{1,0:T(8,128)}, bf16[1024,704]{1,0:T(8,128)(2,1)}) custom-call(bf16[1024,2048]{1,0:T(8,128)(2,1)} %get-tuple-element.180.normed_ref, bf16[2048,1408]{1,0:T(8,128)(2,1)} %get-tuple-element.181.weights_ref), custom_call_target="tpu_custom_call" | custom-call | flops 5905580032 | bytes 11534336 | tf_op jit(solution)/shard_map/cond/branch_1_fun/pallas_call | solution.py:614
  211.6 7.6 %convolution_convert_fusion = bf16[704,2048]{1,0:T(8,128)(2,1)} fusion(bf16[1024,704]{1,0:T(8,128)(2,1)} %get-tuple-element.491, bf16[1024,2048]{1,0:T(8,128)(2,1)} %get-tuple-element.187), kind=kOutput, calls=%fused_computation.24 | convolution fusion | flops 2954231808 | bytes 8519680 | tf_op jit(solution)/shard_map/cond/branch_1_fun/dot_general | solution.py:35
  221.4 4.3 collective-permute-done.38.other_ref
  225.7 4.7 branch_1_fun.40
  230.5 4.2 all-gather.8.cloned.1.call-done.down_ref
  234.8 8.3 %shard_map.204 = bf16[1024,1408]{1,0:T(8,128)(2,1)S(1)} custom-call(bf16[1024,2048]{1,0:T(8,128)(2,1)} %get-tuple-element.372.dy_ref, bf16[704,2048]{1,0:T(8,128)(2,1)} %all-gather.8.cloned.1.call-done.down_ref, f32[1024,1408]{1,0:T(8,128)} %get-tuple-element.373.pre_ref), custom_call_target="tpu_custom_call" | custom-call | flops 2952790016 | bytes 11534336 | tf_op jit(solution)/shard_map/pallas_call | solution.py:649
  243.1 46.2 %conditional.10 = (f32[128,2048]{1,0:T(8,128)S(1)}, bf16[4,128,512]{2,1,0:T(8,128)(2,1)}, bf16[4,128,512]{2,1,0:T(8,128)(2,1)}, bf16[2048,1408]{1,0:T(8,128)(2,1)}) conditional(s32[]{:T(128)} %bitcast.47, () %tuple.102, (f32[128,2048]{1,0:T(8,128)}, bf16[1024,1408]{1,0:T(8,128)(2,1)S(1)}, bf16[2048,1408]{1,0:T(8,128)(2,1)S(1)}, ...), branch_computations={%region_8.9_spmd, %region_9.12_spmd} | conditional | flops 12900106240 | bytes 79450888 | solution.py:704
  243.5 3.7 convolution_convert_fusion.1
  247.3 3.7 convolution_convert_fusion.2
  256.8 4.1 collective-permute-done.41
  264.4 9.6 %branch_1_fun.41 = bf16[2048,1408]{1,0:T(8,128)(2,1)} custom-call(bf16[1024,2048]{1,0:T(8,128)(2,1)} %get-tuple-element.201.refs_0_, bf16[1024,1408]{1,0:T(8,128)(2,1)S(1)} %get-tuple-element.195.refs_1_), custom_call_target="tpu_custom_call" | custom-call | flops 5905580032 | bytes 8388608 | tf_op jit(solution)/shard_map/cond/branch_1_fun/pallas_call | solution.py:678
  279.8 7.3 %convolution_convert_fusion.3.refs_0_ = bf16[128,2048]{1,0:T(8,128)(2,1)} fusion(bf16[128,2048]{1,0:T(8,128)(2,1)S(1)} %get-tuple-element.403.refs_1_, bf16[2048,2048]{1,0:T(8,128)(2,1)} %get-tuple-element.207), kind=kOutput, calls=%fused_computation.28 | convolution fusion | flops 1074003968 | bytes 9437184 | tf_op jit(solution)/shard_map/cond/branch_1_fun/dot_general | solution.py:35
  291.8 103.7 %conditional.11 = (bf16[2048,640]{1,0:T(8,128)(2,1)}, bf16[4,176,2048]{2,1,0:T(8,128)(2,1)}, bf16[4,176,2048]{2,1,0:T(8,128)(2,1)}, f32[1,128,2048]{2,1,0:T(8,128)}, bf16[1,128,2048]{2,1,0:T(8,128)(2,1)}) conditional(s32[]{:T(128)} %bitcast.47, () %tuple.101, (bf16[4,128,512]{2,1,0:T(8,128)(2,1)}, bf16[176,2048]{1,0:T(8,128)(2,1)}, ...), branch_computations={%region_13.14_spmd, %region_14.17_spmd} | conditional | flops 9958064128 | bytes 163730784 | solution.py:704
  300.0 4.7 convolution_convert_fusion.6
  307.7 4.1 collective-permute-done.46.refs_2_
  314.0 12.8 %branch_1_fun.44 = (bf16[8,128,384]{2,1,0:T(8,128)(2,1)S(1)}, bf16[8,128,256]{2,1,0:T(8,128)(2,1)S(1)}) custom-call(s32[1]{0:T(128)} %get-tuple-element.212.place_ref, bf16[1024,384]{1,0:T(8,128)(2,1)} %get-tuple-element.213.rot_ref, f32[1024,256]{1,0:T(8,128)} %get-tuple-element.214.out_ref, f32[4,1024,1]{2,1,0:T(8,128)} %get-tuple-element.215.top_ref, ...), custom_call_target="tpu_custom_call" | custom-call | flops 2684354560 | bytes 3145728 | tf_op jit(solution)/shard_map/cond/branch_1_fun/pallas_call | solution.py:576
  340.0 7.4 %branch_1_fun.45 = bf16[2048,640]{1,0:T(8,128)(2,1)} custom-call(bf16[1024,2048]{1,0:T(8,128)(2,1)} %get-tuple-element.211.refs_0_, bf16[1024,384]{1,0:T(8,128)(2,1)S(1)} %bitcast.154, bf16[1024,2048]{1,0:T(8,128)(2,1)} %get-tuple-element.241.refs_2_, bf16[1024,256]{1,0:T(8,128)(2,1)S(1)} %bitcast.155), custom_call_target="tpu_custom_call" | custom-call | flops 2684354560 | bytes 8388608 | tf_op jit(solution)/shard_map/cond/branch_1_fun/pallas_call | solution.py:678
  357.6 10.4 %collective-permute-done.57 = bf16[128,2048]{1,0:T(8,128)(2,1)S(1)} collective-permute-done((bf16[128,2048]{1,0:T(8,128)(2,1)S(1)}, bf16[128,2048]{1,0:T(8,128)(2,1)S(1)}, u32[]{:S(2)}, u32[]{:S(2)}) %collective-permute-start.57) | collective-permute-done | bytes 524320 | tf_op jit(solution)/shard_map/cond/branch_1_fun/ppermute | solution.py:39
  372.4 4.9 collective-permute-done.60
  380.5 9.3 %collective-permute-done.61 = bf16[128,2048]{1,0:T(8,128)(2,1)S(1)} collective-permute-done((bf16[128,2048]{1,0:T(8,128)(2,1)S(1)}, bf16[128,2048]{1,0:T(8,128)(2,1)S(1)}, u32[]{:S(2)}, u32[]{:S(2)}) %collective-permute-start.61) | collective-permute-done | bytes 524320 | tf_op jit(solution)/shard_map/cond/branch_1_fun/ppermute | solution.py:39
  396.7 55.9 %conditional.12 = (f32[1408,2048]{1,0:T(8,128)}, bf16[4,512,1408]{2,1,0:T(8,128)(2,1)}) conditional(s32[]{:T(128)} %bitcast.47, () %tuple.114, (s32[1]{0:T(128)}, bf16[4,176,2048]{2,1,0:T(8,128)(2,1)}, bf16[4,176,2048]{2,1,0:T(8,128)(2,1)}, bf16[512,1408]{1,0:T(8,128)(2,1)}) %tuple.116), branch_computations={%region_18.19_spmd, %region_19.20_spmd} | conditional | bytes 54788300 | solution.py:704
  399.6 8.7 %branch_1_fun.47 = f32[1408,2048]{1,0:T(8,128)} custom-call(s32[1]{0:T(128)} %get-tuple-element.267.place_ref, bf16[4,176,2048]{2,1,0:T(8,128)(2,1)} %get-tuple-element.268.even_ref, bf16[4,176,2048]{2,1,0:T(8,128)(2,1)} %get-tuple-element.269.odd_ref), custom_call_target="tpu_custom_call" | custom-call | bytes 17301504 | tf_op jit(solution)/shard_map/cond/branch_1_fun/pallas_call | solution.py:250
  408.4 21.9 %collective-permute-done.1.refs_2_ = bf16[512,1408]{1,0:T(8,128)(2,1)S(1)} collective-permute-done((bf16[512,1408]{1,0:T(8,128)(2,1)}, bf16[512,1408]{1,0:T(8,128)(2,1)S(1)}, u32[]{:S(2)}, u32[]{:S(2)}) %collective-permute-start.1) | collective-permute-done | bytes 1441824 | tf_op jit(solution)/shard_map/cond/branch_1_fun/ppermute | solution.py:39
  433.7 14.8 %collective-permute-done.3.refs_4_ = bf16[256,1408]{1,0:T(8,128)(2,1)S(1)} collective-permute-done((bf16[256,1408]{1,0:T(8,128)(2,1)S(1)}, bf16[256,1408]{1,0:T(8,128)(2,1)S(1)}, u32[]{:S(2)}, u32[]{:S(2)}) %collective-permute-start.3) | collective-permute-done | bytes 720928 | tf_op jit(solution)/shard_map/cond/branch_1_fun/ppermute | solution.py:39
  452.6 41.0 %conditional.13 = (f32[512,5632]{1,0:T(8,128)}, f32[512,5632]{1,0:T(8,128)}, f32[2,512]{1,0:T(2,128)S(1)}, f32[512,2048]{1,0:T(8,128)}, f32[512,256]{1,0:T(8,128...) conditional(s32[]{:T(128)} %bitcast.47, () %tuple.113, (bf16[4,512,1408]{2,1,0:T(8,128)(2,1)}, s32[1]{0:T(128)}, ...), branch_computations={%region_21.22_spmd, %region_22.25_spmd} | conditional | flops 3676160 | bytes 134058584 | solution.py:704
  462.3 4.2 branch_1_fun.49
  466.6 4.2 branch_1_fun.50
  474.6 4.2 branch_1_fun.51
  484.0 4.2 branch_1_fun.52
  488.3 5.3 %branch_1_fun.53 = (f32[512,2048]{1,0:T(8,128)}, f32[512,256]{1,0:T(8,128)}, f32[512,256]{1,0:T(8,128)}, f32[512,2048]{1,0:T(8,128)}) custom-call(s32[1]{0:T(128)} %get-tuple-element.276.place_ref, bf16[512,640]{1,0:T(8,128)(2,1)S(1)} %copy-done.23, bf16[512,640]{1,0:T(8,128)(2,1)S(1)} %collective-permute-done.64.refs_1_, ...), custom_call_target="tpu_custom_call" | custom-call | bytes 15728640 | tf_op jit(solution)/shard_map/cond/branch_1_fun/pallas_call | solution.py:302
  (317 shorter events, 188.1 us)
Async XLA Ops:
  7.2 61.0 %all-gather.4.cloned.1.call-start = ((), (), s32[]{:S(2)}) async-start(), calls=%async_computation.3 | async-start | bytes 3276800 | tf_op jit(solution)/shard_map/all_gather | solution.py:779
  9.4 184.8 %all-gather.6.cloned.1.call-start = ((), (), s32[]{:S(2)}) async-start(), calls=%async_computation.4 | async-start | bytes 7208960 | tf_op jit(solution)/shard_map/all_gather | solution.py:779
  14.8 219.9 %all-gather.8.cloned.1.call-start = ((), (), s32[]{:S(2)}) async-start(), calls=%async_computation.5 | async-start | bytes 3604480 | tf_op jit(solution)/shard_map/all_gather | solution.py:779
  17.0 274.8 %reduce-scatter.4.cloned.1.call-start = ((), (), s32[]{:S(2)}) async-start(), calls=%async_computation.6 | async-start | bytes 3604480 | tf_op jit(solution)/shard_map/reduce_scatter | solution.py:782
  17.2 16.5 %collective-permute-start.7 = (bf16[128,2048]{1,0:T(8,128)(2,1)S(1)}, bf16[128,2048]{1,0:T(8,128)(2,1)S(1)}, u32[]{:S(2)}, u32[]{:S(2)}) collective-permute-start(bf16[128,2048]{1,0:T(8,128)(2,1)S(1)} %get-tuple-element.116.refs_0_), channel_id=1, source_target_pairs={{0,16},{4,20},{8,24},{12,28},{16,0},{20,4},{24,8},{28,12},{1,17},{... | collective-permute-start | bytes 1572872 | tf_op jit(solution)/shard_map/cond/branch_1_fun/ppermute | solution.py:39
  20.2 13.4 %collective-permute-start.6 = (bf16[128,2048]{1,0:T(8,128)(2,1)S(1)}, bf16[128,2048]{1,0:T(8,128)(2,1)S(1)}, u32[]{:S(2)}, u32[]{:S(2)}) collective-permute-start(bf16[128,2048]{1,0:T(8,128)(2,1)S(1)} %get-tuple-element.116.refs_0_), channel_id=1, source_target_pairs={{0,8},{4,12},{8,0},{12,4},{16,24},{20,28},{24,16},{28,20},{1,9},{5... | collective-permute-start | bytes 1572872 | tf_op jit(solution)/shard_map/cond/branch_1_fun/ppermute | solution.py:39
  21.7 11.9 %collective-permute-start.4 = (f32[2,2048]{1,0:T(2,128)S(1)}, f32[2,2048]{1,0:T(2,128)S(1)}, u32[]{:S(2)}, u32[]{:S(2)}) collective-permute-start(f32[2,2048]{1,0:T(2,128)S(1)} %constant_dynamic-update-slice_fusion), channel_id=1, source_target_pairs={{0,1},{1,2},{2,3},{3,0},{4,5},{5,6},{6,7},{7,4},{8,9},{9,10},{10,1... | collective-permute-start | bytes 49160 | tf_op jit(solution)/shard_map/cond/branch_1_fun/ppermute | solution.py:164
  72.3 24.9 %collective-permute-start.16 = (bf16[2048,256]{1,0:T(8,128)(2,1)S(1)}, bf16[2048,256]{1,0:T(8,128)(2,1)S(1)}, u32[]{:S(2)}, u32[]{:S(2)}) collective-permute-start(bf16[2048,256]{1,0:T(8,128)(2,1)S(1)} %slice.188.refs_0_), channel_id=1, source_target_pairs={{0,16},{4,20},{8,24},{12,28},{16,0},{20,4},{24,8},{28,12},{1,17},{... | collective-permute-start | bytes 3145736 | tf_op jit(solution)/shard_map/cond/branch_1_fun/ppermute | solution.py:39
  73.8 24.6 %collective-permute-start.15 = (bf16[2048,256]{1,0:T(8,128)(2,1)S(1)}, bf16[2048,256]{1,0:T(8,128)(2,1)S(1)}, u32[]{:S(2)}, u32[]{:S(2)}) collective-permute-start(bf16[2048,256]{1,0:T(8,128)(2,1)S(1)} %slice.188.refs_0_), channel_id=1, source_target_pairs={{0,8},{4,12},{8,0},{12,4},{16,24},{20,28},{24,16},{28,20},{1,9},{5... | collective-permute-start | bytes 3145736 | tf_op jit(solution)/shard_map/cond/branch_1_fun/ppermute | solution.py:39
  98.6 14.9 %collective-permute-start.18 = (bf16[1024,256]{1,0:T(8,128)(2,1)S(1)}, bf16[1024,256]{1,0:T(8,128)(2,1)S(1)}, u32[]{:S(2)}, u32[]{:S(2)}) collective-permute-start(bf16[1024,256]{1,0:T(8,128)(2,1)S(1)} %slice.190), channel_id=1, source_target_pairs={{0,8},{4,12},{8,0},{12,4},{16,24},{20,28},{24,16},{28,20},{1,9},{5... | collective-permute-start | bytes 1572872 | tf_op jit(solution)/shard_map/cond/branch_1_fun/ppermute | solution.py:39
  99.8 14.9 %collective-permute-start.17 = (bf16[1024,256]{1,0:T(8,128)(2,1)S(1)}, bf16[1024,256]{1,0:T(8,128)(2,1)S(1)}, u32[]{:S(2)}, u32[]{:S(2)}) collective-permute-start(bf16[1024,256]{1,0:T(8,128)(2,1)S(1)} %slice.189), channel_id=1, source_target_pairs={{0,16},{4,20},{8,24},{12,28},{16,0},{20,4},{24,8},{28,12},{1,17},{... | collective-permute-start | bytes 1572872 | tf_op jit(solution)/shard_map/cond/branch_1_fun/ppermute | solution.py:39
  100.6 22.8 %collective-permute-start.21 = (bf16[128,2048]{1,0:T(8,128)(2,1)S(1)}, bf16[128,2048]{1,0:T(8,128)(2,1)S(1)}, u32[]{:S(2)}, u32[]{:S(2)}) collective-permute-start(bf16[128,2048]{1,0:T(8,128)(2,1)S(1)} %copy-done.22), channel_id=1, source_target_pairs={{0,16},{4,20},{8,24},{12,28},{16,0},{20,4},{24,8},{28,12},{1,17},{... | collective-permute-start | bytes 1572872 | tf_op jit(solution)/shard_map/cond/branch_1_fun/ppermute | solution.py:39
  101.9 21.5 %collective-permute-start.20 = (bf16[128,2048]{1,0:T(8,128)(2,1)S(1)}, bf16[128,2048]{1,0:T(8,128)(2,1)S(1)}, u32[]{:S(2)}, u32[]{:S(2)}) collective-permute-start(bf16[128,2048]{1,0:T(8,128)(2,1)S(1)} %copy-done.22), channel_id=1, source_target_pairs={{0,8},{4,12},{8,0},{12,4},{16,24},{20,28},{24,16},{28,20},{1,9},{5... | collective-permute-start | bytes 1572872 | tf_op jit(solution)/shard_map/cond/branch_1_fun/ppermute | solution.py:39
  125.6 17.8 %collective-permute-start.22 = (bf16[4,2048,256]{2,1,0:T(8,128)(2,1)}, bf16[4,2048,256]{2,1,0:T(8,128)(2,1)}, u32[]{:S(2)}, u32[]{:S(2)}) collective-permute-start(bf16[4,2048,256]{2,1,0:T(8,128)(2,1)} %branch_1_fun.30.even_ref), channel_id=1, source_target_pairs={{0,4},{4,0},{8,12},{12,8},{16,20},{20,16},{24,28},{28,24},{1,5},{5... | collective-permute-start | bytes 12582920 | tf_op jit(solution)/shard_map/cond/branch_1_fun/ppermute | solution.py:39
  128.4 15.0 %collective-permute-start.27 = (bf16[64,2048]{1,0:T(8,128)(2,1)S(1)}, bf16[64,2048]{1,0:T(8,128)(2,1)S(1)}, u32[]{:S(2)}, u32[]{:S(2)}) collective-permute-start(bf16[64,2048]{1,0:T(8,128)(2,1)S(1)} %slice.192), channel_id=1, source_target_pairs={{0,8},{4,12},{8,0},{12,4},{16,24},{20,28},{24,16},{28,20},{1,9},{5... | collective-permute-start | bytes 786440 | tf_op jit(solution)/shard_map/cond/branch_1_fun/ppermute | solution.py:39
  129.6 13.8 %collective-permute-start.26 = (bf16[64,2048]{1,0:T(8,128)(2,1)S(1)}, bf16[64,2048]{1,0:T(8,128)(2,1)S(1)}, u32[]{:S(2)}, u32[]{:S(2)}) collective-permute-start(bf16[64,2048]{1,0:T(8,128)(2,1)S(1)} %slice.191), channel_id=1, source_target_pairs={{0,16},{4,20},{8,24},{12,28},{16,0},{20,4},{24,8},{28,12},{1,17},{... | collective-permute-start | bytes 786440 | tf_op jit(solution)/shard_map/cond/branch_1_fun/ppermute | solution.py:39
  130.3 13.0 %collective-permute-start.24 = (bf16[2,128,256]{2,1,0:T(8,128)(2,1)}, bf16[2,128,256]{2,1,0:T(8,128)(2,1)S(1)}, u32[]{:S(2)}, u32[]{:S(2)}) collective-permute-start(bf16[2,128,256]{2,1,0:T(8,128)(2,1)} %get-tuple-element.153), channel_id=1, source_target_pairs={{0,16},{4,20},{8,24},{12,28},{16,0},{20,4},{24,8},{28,12},{1,17},{... | collective-permute-start | bytes 393224 | tf_op jit(solution)/shard_map/cond/branch_1_fun/ppermute | solution.py:39
  145.6 30.4 %collective-permute-start.30 = (bf16[4,128,2048]{2,1,0:T(8,128)(2,1)S(1)}, bf16[4,128,2048]{2,1,0:T(8,128)(2,1)}, u32[]{:S(2)}, u32[]{:S(2)}) collective-permute-start(bf16[4,128,2048]{2,1,0:T(8,128)(2,1)S(1)} %branch_1_fun.34.mine_ref), channel_id=1, source_target_pairs={{0,4},{4,0},{8,12},{12,8},{16,20},{20,16},{24,28},{28,24},{1,5},{5... | collective-permute-start | bytes 6291464 | tf_op jit(solution)/shard_map/cond/branch_1_fun/ppermute | solution.py:39
  162.0 13.6 %collective-permute-start.29 = (bf16[128,2048]{1,0:T(8,128)(2,1)S(1)}, bf16[128,2048]{1,0:T(8,128)(2,1)S(1)}, u32[]{:S(2)}, u32[]{:S(2)}) collective-permute-start(bf16[128,2048]{1,0:T(8,128)(2,1)S(1)} %multiply_convert_fusion.refs_0_), channel_id=1, source_target_pairs={{0,16},{4,20},{8,24},{12,28},{16,0},{20,4},{24,8},{28,12},{1,17},{... | collective-permute-start | bytes 1572872 | tf_op jit(solution)/shard_map/cond/branch_1_fun/ppermute | solution.py:39
  162.8 13.3 %collective-permute-start.28 = (bf16[128,2048]{1,0:T(8,128)(2,1)S(1)}, bf16[128,2048]{1,0:T(8,128)(2,1)S(1)}, u32[]{:S(2)}, u32[]{:S(2)}) collective-permute-start(bf16[128,2048]{1,0:T(8,128)(2,1)S(1)} %multiply_convert_fusion.refs_0_), channel_id=1, source_target_pairs={{0,8},{4,12},{8,0},{12,4},{16,24},{20,28},{24,16},{28,20},{1,9},{5... | collective-permute-start | bytes 1572872 | tf_op jit(solution)/shard_map/cond/branch_1_fun/ppermute | solution.py:39
  194.5 14.6 %collective-permute-start.35 = (bf16[128,2048]{1,0:T(8,128)(2,1)}, bf16[128,2048]{1,0:T(8,128)(2,1)S(1)}, u32[]{:S(2)}, u32[]{:S(2)}) collective-permute-start(bf16[128,2048]{1,0:T(8,128)(2,1)} %get-tuple-element.179.refs_0_), channel_id=1, source_target_pairs={{0,16},{4,20},{8,24},{12,28},{16,0},{20,4},{24,8},{28,12},{1,17},{... | collective-permute-start | bytes 1572872 | tf_op jit(solution)/shard_map/cond/branch_1_fun/ppermute | solution.py:39
  196.0 13.7 %collective-permute-start.34 = (bf16[128,2048]{1,0:T(8,128)(2,1)}, bf16[128,2048]{1,0:T(8,128)(2,1)S(1)}, u32[]{:S(2)}, u32[]{:S(2)}) collective-permute-start(bf16[128,2048]{1,0:T(8,128)(2,1)} %get-tuple-element.179.refs_0_), channel_id=1, source_target_pairs={{0,8},{4,12},{8,0},{12,4},{16,24},{20,28},{24,16},{28,20},{1,9},{5... | collective-permute-start | bytes 1572872 | tf_op jit(solution)/shard_map/cond/branch_1_fun/ppermute | solution.py:39
  230.5 166.2 %reduce-scatter.6.cloned.1.call-start = ((), (), s32[]{:S(2)}) async-start(), calls=%async_computation.7 | async-start | bytes 7208960 | tf_op jit(solution)/shard_map/reduce_scatter | solution.py:782
  262.2 13.0 %collective-permute-start.42 = (bf16[128,2048]{1,0:T(8,128)(2,1)S(1)}, bf16[128,2048]{1,0:T(8,128)(2,1)S(1)}, u32[]{:S(2)}, u32[]{:S(2)}) collective-permute-start(bf16[128,2048]{1,0:T(8,128)(2,1)S(1)} %pad_maximum_fusion), channel_id=1, source_target_pairs={{0,8},{4,12},{8,0},{12,4},{16,24},{20,28},{24,16},{28,20},{1,9},{5... | collective-permute-start | bytes 1572872 | tf_op jit(solution)/shard_map/cond/branch_1_fun/ppermute | solution.py:39
  263.8 12.7 %collective-permute-start.43 = (bf16[128,2048]{1,0:T(8,128)(2,1)S(1)}, bf16[128,2048]{1,0:T(8,128)(2,1)S(1)}, u32[]{:S(2)}, u32[]{:S(2)}) collective-permute-start(bf16[128,2048]{1,0:T(8,128)(2,1)S(1)} %pad_maximum_fusion.1), channel_id=1, source_target_pairs={{0,16},{4,20},{8,24},{12,28},{16,0},{20,4},{24,8},{28,12},{1,17},{... | collective-permute-start | bytes 1572872 | tf_op jit(solution)/shard_map/cond/branch_1_fun/ppermute | solution.py:39
  289.4 163.2 %reduce-scatter.8.cloned.1.call-start = ((), (), s32[]{:S(2)}) async-start(), calls=%async_computation.8 | async-start | bytes 3276800 | tf_op jit(solution)/shard_map/reduce_scatter | solution.py:782
  297.9 13.9 %collective-permute-start.46 = (bf16[2,128,512]{2,1,0:T(8,128)(2,1)}, bf16[2,128,512]{2,1,0:T(8,128)(2,1)S(1)}, u32[]{:S(2)}, u32[]{:S(2)}) collective-permute-start(bf16[2,128,512]{2,1,0:T(8,128)(2,1)} %get-tuple-element.226), channel_id=1, source_target_pairs={{0,16},{4,20},{8,24},{12,28},{16,0},{20,4},{24,8},{28,12},{1,17},{... | collective-permute-start | bytes 786440 | tf_op jit(solution)/shard_map/cond/branch_1_fun/ppermute | solution.py:39
  299.4 12.4 %collective-permute-start.47 = (bf16[2,128,512]{2,1,0:T(8,128)(2,1)}, bf16[2,128,512]{2,1,0:T(8,128)(2,1)S(1)}, u32[]{:S(2)}, u32[]{:S(2)}) collective-permute-start(bf16[2,128,512]{2,1,0:T(8,128)(2,1)} %get-tuple-element.227), channel_id=1, source_target_pairs={{0,24},{4,28},{8,16},{12,20},{16,8},{20,12},{24,0},{28,4},{1,25},{... | collective-permute-start | bytes 786440 | tf_op jit(solution)/shard_map/cond/branch_1_fun/ppermute | solution.py:39
  311.8 19.8 %collective-permute-start.50 = (bf16[4,128,2048]{2,1,0:T(8,128)(2,1)S(1)}, bf16[4,128,2048]{2,1,0:T(8,128)(2,1)S(1)}, u32[]{:S(2)}, u32[]{:S(2)}) collective-permute-start(bf16[4,128,2048]{2,1,0:T(8,128)(2,1)S(1)} %bitcast.186), channel_id=1, source_target_pairs={{0,4},{4,0},{8,12},{12,8},{16,20},{20,16},{24,28},{28,24},{1,5},{5... | collective-permute-start | bytes 6291464 | tf_op jit(solution)/shard_map/cond/branch_1_fun/ppermute | solution.py:39
  311.8 18.5 %collective-permute-start.49 = (bf16[176,2048]{1,0:T(8,128)(2,1)S(1)}, bf16[176,2048]{1,0:T(8,128)(2,1)S(1)}, u32[]{:S(2)}, u32[]{:S(2)}) collective-permute-start(bf16[176,2048]{1,0:T(8,128)(2,1)S(1)} %copy-done.24), channel_id=1, source_target_pairs={{0,16},{4,20},{8,24},{12,28},{16,0},{20,4},{24,8},{28,12},{1,17},{... | collective-permute-start | bytes 2162696 | tf_op jit(solution)/shard_map/cond/branch_1_fun/ppermute | solution.py:39
  313.4 18.2 %collective-permute-start.48 = (bf16[176,2048]{1,0:T(8,128)(2,1)S(1)}, bf16[176,2048]{1,0:T(8,128)(2,1)S(1)}, u32[]{:S(2)}, u32[]{:S(2)}) collective-permute-start(bf16[176,2048]{1,0:T(8,128)(2,1)S(1)} %copy-done.24), channel_id=1, source_target_pairs={{0,8},{4,12},{8,0},{12,4},{16,24},{20,28},{24,16},{28,20},{1,9},{5... | collective-permute-start | bytes 2162696 | tf_op jit(solution)/shard_map/cond/branch_1_fun/ppermute | solution.py:39
  332.4 17.4 %collective-permute-start.51 = (bf16[80,2048]{1,0:T(8,128)(2,1)}, bf16[80,2048]{1,0:T(8,128)(2,1)S(1)}, u32[]{:S(2)}, u32[]{:S(2)}) collective-permute-start(bf16[80,2048]{1,0:T(8,128)(2,1)} %slice.214), channel_id=1, source_target_pairs={{0,16},{4,20},{8,24},{12,28},{16,0},{20,4},{24,8},{28,12},{1,17},{... | collective-permute-start | bytes 983048 | tf_op jit(solution)/shard_map/cond/branch_1_fun/ppermute | solution.py:39
  333.7 16.1 %collective-permute-start.52 = (bf16[96,2048]{1,0:T(8,128)(2,1)}, bf16[96,2048]{1,0:T(8,128)(2,1)S(1)}, u32[]{:S(2)}, u32[]{:S(2)}) collective-permute-start(bf16[96,2048]{1,0:T(8,128)(2,1)} %slice.215), channel_id=1, source_target_pairs={{0,8},{4,12},{8,0},{12,4},{16,24},{20,28},{24,16},{28,20},{1,9},{5... | collective-permute-start | bytes 1179656 | tf_op jit(solution)/shard_map/cond/branch_1_fun/ppermute | solution.py:39
  352.0 17.1 %collective-permute-start.56 = (bf16[4,176,2048]{2,1,0:T(8,128)(2,1)}, bf16[4,176,2048]{2,1,0:T(8,128)(2,1)}, u32[]{:S(2)}, u32[]{:S(2)}) collective-permute-start(bf16[4,176,2048]{2,1,0:T(8,128)(2,1)} %branch_1_fun.46), channel_id=1, source_target_pairs={{0,4},{4,0},{8,12},{12,8},{16,20},{20,16},{24,28},{28,24},{1,5},{5... | collective-permute-start | bytes 8650760 | tf_op jit(solution)/shard_map/cond/branch_1_fun/ppermute | solution.py:39
  353.4 15.7 %collective-permute-start.55 = (bf16[4,128,2048]{2,1,0:T(8,128)(2,1)S(1)}, bf16[4,128,2048]{2,1,0:T(8,128)(2,1)S(1)}, u32[]{:S(2)}, u32[]{:S(2)}) collective-permute-start(bf16[4,128,2048]{2,1,0:T(8,128)(2,1)S(1)} %bitcast.163), channel_id=1, source_target_pairs={{0,4},{4,0},{8,12},{12,8},{16,20},{20,16},{24,28},{28,24},{1,5},{5... | collective-permute-start | bytes 6291464 | tf_op jit(solution)/shard_map/cond/branch_1_fun/ppermute | solution.py:39
  354.1 13.9 %collective-permute-start.57 = (bf16[128,2048]{1,0:T(8,128)(2,1)S(1)}, bf16[128,2048]{1,0:T(8,128)(2,1)S(1)}, u32[]{:S(2)}, u32[]{:S(2)}) collective-permute-start(bf16[128,2048]{1,0:T(8,128)(2,1)S(1)} %pad_maximum_fusion.2), channel_id=1, source_target_pairs={{0,8},{4,12},{8,0},{12,4},{16,24},{20,28},{24,16},{28,20},{1,9},{5... | collective-permute-start | bytes 1572872 | tf_op jit(solution)/shard_map/cond/branch_1_fun/ppermute | solution.py:39
  355.5 13.6 %collective-permute-start.58 = (bf16[128,2048]{1,0:T(8,128)(2,1)S(1)}, bf16[128,2048]{1,0:T(8,128)(2,1)S(1)}, u32[]{:S(2)}, u32[]{:S(2)}) collective-permute-start(bf16[128,2048]{1,0:T(8,128)(2,1)S(1)} %pad_maximum_fusion.3), channel_id=1, source_target_pairs={{0,16},{4,20},{8,24},{12,28},{16,0},{20,4},{24,8},{28,12},{1,17},{... | collective-permute-start | bytes 1572872 | tf_op jit(solution)/shard_map/cond/branch_1_fun/ppermute | solution.py:39
  378.1 11.8 %collective-permute-start.61 = (bf16[128,2048]{1,0:T(8,128)(2,1)S(1)}, bf16[128,2048]{1,0:T(8,128)(2,1)S(1)}, u32[]{:S(2)}, u32[]{:S(2)}) collective-permute-start(bf16[128,2048]{1,0:T(8,128)(2,1)S(1)} %pad_maximum_fusion.4), channel_id=1, source_target_pairs={{0,8},{4,12},{8,0},{12,4},{16,24},{20,28},{24,16},{28,20},{1,9},{5... | collective-permute-start | bytes 1572872 | tf_op jit(solution)/shard_map/cond/branch_1_fun/ppermute | solution.py:39
  379.6 11.5 %collective-permute-start.62 = (bf16[128,2048]{1,0:T(8,128)(2,1)S(1)}, bf16[128,2048]{1,0:T(8,128)(2,1)S(1)}, u32[]{:S(2)}, u32[]{:S(2)}) collective-permute-start(bf16[128,2048]{1,0:T(8,128)(2,1)S(1)} %pad_maximum_fusion.5), channel_id=1, source_target_pairs={{0,16},{4,20},{8,24},{12,28},{16,0},{20,4},{24,8},{28,12},{1,17},{... | collective-permute-start | bytes 1572872 | tf_op jit(solution)/shard_map/cond/branch_1_fun/ppermute | solution.py:39
  396.7 33.6 %collective-permute-start.1 = (bf16[512,1408]{1,0:T(8,128)(2,1)}, bf16[512,1408]{1,0:T(8,128)(2,1)S(1)}, u32[]{:S(2)}, u32[]{:S(2)}) collective-permute-start(bf16[512,1408]{1,0:T(8,128)(2,1)} %get-tuple-element.270.refs_0_), channel_id=1, source_target_pairs={{0,16},{4,20},{8,24},{12,28},{16,0},{20,4},{24,8},{28,12},{1,17},{... | collective-permute-start | bytes 4325384 | tf_op jit(solution)/shard_map/cond/branch_1_fun/ppermute | solution.py:39
  398.2 33.3 %collective-permute-start = (bf16[512,1408]{1,0:T(8,128)(2,1)}, bf16[512,1408]{1,0:T(8,128)(2,1)S(1)}, u32[]{:S(2)}, u32[]{:S(2)}) collective-permute-start(bf16[512,1408]{1,0:T(8,128)(2,1)} %get-tuple-element.270.refs_0_), channel_id=1, source_target_pairs={{0,8},{4,12},{8,0},{12,4},{16,24},{20,28},{24,16},{28,20},{1,9},{5... | collective-permute-start | bytes 4325384 | tf_op jit(solution)/shard_map/cond/branch_1_fun/ppermute | solution.py:39
  431.6 16.9 %collective-permute-start.3 = (bf16[256,1408]{1,0:T(8,128)(2,1)S(1)}, bf16[256,1408]{1,0:T(8,128)(2,1)S(1)}, u32[]{:S(2)}, u32[]{:S(2)}) collective-permute-start(bf16[256,1408]{1,0:T(8,128)(2,1)S(1)} %slice.247), channel_id=1, source_target_pairs={{0,8},{4,12},{8,0},{12,4},{16,24},{20,28},{24,16},{28,20},{1,9},{5... | collective-permute-start | bytes 2162696 | tf_op jit(solution)/shard_map/cond/branch_1_fun/ppermute | solution.py:39
  433.1 16.6 %collective-permute-start.2 = (bf16[256,1408]{1,0:T(8,128)(2,1)S(1)}, bf16[256,1408]{1,0:T(8,128)(2,1)S(1)}, u32[]{:S(2)}, u32[]{:S(2)}) collective-permute-start(bf16[256,1408]{1,0:T(8,128)(2,1)S(1)} %slice.246), channel_id=1, source_target_pairs={{0,16},{4,20},{8,24},{12,28},{16,0},{20,4},{24,8},{28,12},{1,17},{... | collective-permute-start | bytes 2162696 | tf_op jit(solution)/shard_map/cond/branch_1_fun/ppermute | solution.py:39
  452.7 18.1 %collective-permute-start.65 = (bf16[512,640]{1,0:T(8,128)(2,1)}, bf16[512,640]{1,0:T(8,128)(2,1)S(1)}, u32[]{:S(2)}, u32[]{:S(2)}) collective-permute-start(bf16[512,640]{1,0:T(8,128)(2,1)} %get-tuple-element.282.refs_0_), channel_id=1, source_target_pairs={{0,16},{4,20},{8,24},{12,28},{16,0},{20,4},{24,8},{28,12},{1,17},{... | collective-permute-start | bytes 1966088 | tf_op jit(solution)/shard_map/cond/branch_1_fun/ppermute | solution.py:39
  453.7 17.1 %collective-permute-start.64 = (bf16[512,640]{1,0:T(8,128)(2,1)}, bf16[512,640]{1,0:T(8,128)(2,1)S(1)}, u32[]{:S(2)}, u32[]{:S(2)}) collective-permute-start(bf16[512,640]{1,0:T(8,128)(2,1)} %get-tuple-element.282.refs_0_), channel_id=1, source_target_pairs={{0,8},{4,12},{8,0},{12,4},{16,24},{20,28},{24,16},{28,20},{1,9},{5... | collective-permute-start | bytes 1966088 | tf_op jit(solution)/shard_map/cond/branch_1_fun/ppermute | solution.py:39
  458.2 12.6 %collective-permute-start.66 = (f32[2,512]{1,0:T(2,128)S(1)}, f32[2,512]{1,0:T(2,128)S(1)}, u32[]{:S(2)}, u32[]{:S(2)}) collective-permute-start(f32[2,512]{1,0:T(2,128)S(1)} %pad_maximum_fusion.6), channel_id=1, source_target_pairs={{0,4},{4,0},{8,12},{12,8},{16,20},{20,16},{24,28},{28,24},{1,5},{5... | collective-permute-start | bytes 12296 | tf_op jit(solution)/shard_map/cond/branch_1_fun/ppermute | solution.py:39
  458.3 15.7 %collective-permute-start.69 = (bf16[512,640]{1,0:T(8,128)(2,1)}, bf16[512,640]{1,0:T(8,128)(2,1)S(1)}, u32[]{:S(2)}, u32[]{:S(2)}) collective-permute-start(bf16[512,640]{1,0:T(8,128)(2,1)} %get-tuple-element.282.refs_0_), channel_id=1, source_target_pairs={{0,4},{4,0},{8,12},{12,8},{16,20},{20,16},{24,28},{28,24},{1,5},{5... | collective-permute-start | bytes 1966088 | tf_op jit(solution)/shard_map/cond/branch_1_fun/ppermute | solution.py:39
  470.8 11.4 %collective-permute-start.70 = (bf16[512,640]{1,0:T(8,128)(2,1)S(1)}, bf16[512,640]{1,0:T(8,128)(2,1)S(1)}, u32[]{:S(2)}, u32[]{:S(2)}) collective-permute-start(bf16[512,640]{1,0:T(8,128)(2,1)S(1)} %collective-permute-done.64.refs_1_), channel_id=1, source_target_pairs={{0,4},{4,0},{8,12},{12,8},{16,20},{20,16},{24,28},{28,24},{1,5},{5... | collective-permute-start | bytes 1966088 | tf_op jit(solution)/shard_map/cond/branch_1_fun/ppermute | solution.py:39
  (71 other events, 782.6 us)
Sparse Core Ops, SparseCore 0:
  9.6 58.5 all-gather.3
  69.7 105.3 all-gather.5
  177.2 57.4 all-gather.7
  236.9 54.8 reduce-scatter.3
  294.5 102.1 reduce-scatter.5
  399.4 52.6 reduce-scatter.7
